TPU v7x, 32 devices: a whole 2x2x4 slice. The times are simulated.
32 devices in a mesh: dom: 1, expert: 8 (over z, y), dp: 4 (over x, core).
Axes of the slice: x: 2, y: 2, z: 4, core: 2. Of those that a mesh axis runs over, the one named last changes fastest.
Arguments:
- tokens: bfloat16 [1024, 1024], P(('dom', 'expert', 'dp')), may hold values from -6 to 6
- cotangent: bfloat16 [1024, 1024], P(('dom', 'expert', 'dp')), may hold values from -1.5 to 1.5
- expert_ids: int32 [1024, 8], P(('dom', 'expert', 'dp')), may hold values from 0 to 15, all different within a row; in each aligned block of 32 rows (0 to 31, 32 to 63, ...) at most 32 rows name the same one
- gate_probs: bfloat16 [1024, 8], P(('dom', 'expert', 'dp')), may hold values from 0.019897461 to 0.25
- gate_half: bfloat16 [32, 512, 384], P(('dom', 'expert', 'dp')), may hold values from -0.1875 to 0.1875
- up_half: bfloat16 [32, 512, 384], P(('dom', 'expert', 'dp')), may hold values from -0.1875 to 0.1875
- down_half: bfloat16 [32, 384, 512], P(('dom', 'expert', 'dp')), may hold values from -0.3125 to 0.3125
Outputs:
- grad_tokens: bfloat16 [1024, 1024], P(('dom', 'expert', 'dp'))
- grad_gates: bfloat16 [1024, 8], P(('dom', 'expert', 'dp'))
- grad_gate_half: bfloat16 [32, 512, 384], P(('dom', 'expert', 'dp'))
- grad_up_half: bfloat16 [32, 512, 384], P(('dom', 'expert', 'dp'))
- grad_down_half: bfloat16 [32, 384, 512], P(('dom', 'expert', 'dp'))
Inputs may be any that keep to these rules, and one draw needn't show every extreme that they name: `expert_ids`: each row names 8 different experts. In each aligned block of 32 rows (the rows of one device) no expert is named by more than 32 rows, a bound that some block reaches.
All inputs are finite; a program needn't handle non-finite values.
Results may differ from a plain program's by a relative error of at most 0.0064.
Values may be sent and summed in bfloat16 or wider, within the bound.
No kernel may reach another device: no remote copies, remote signals or barrier semaphores. Data moves between devices by JAX's collectives and lax.ppermute only.
A program may use at most 64 MiB of HBM per device.

v0:
```python
import jax
import jax.numpy as jnp
from jax import lax
from jax.sharding import PartitionSpec as P


def partner_2(x, axis, stride):
    return lax.ppermute(x, axis, [(i, i ^ 1 << stride) for i in range(lax.axis_size(axis))])


def silu_parts(pre_gate):
    sigmoid_part = jax.nn.sigmoid(pre_gate)
    active = pre_gate * sigmoid_part
    slope_term = sigmoid_part * (1.0 + pre_gate * (1.0 - sigmoid_part))
    return (active, slope_term)


def expert_pass(expert_rows, expert_dys, expert_gates, gate_w, up_w, down_w):
    pre_gate = jnp.dot(expert_rows, gate_w, preferred_element_type=jnp.float32)
    pre_up = jnp.dot(expert_rows, up_w, preferred_element_type=jnp.float32)
    active, slope_term = silu_parts(pre_gate)
    hidden = (active * pre_up).astype(jnp.bfloat16)
    expert_out = jnp.dot(hidden, down_w, preferred_element_type=jnp.float32)
    gate_grads = jnp.sum(expert_dys.astype(jnp.float32) * expert_out, axis=1).astype(jnp.bfloat16)
    scaled = (expert_gates.astype(jnp.float32)[:, None] * expert_dys.astype(jnp.float32)).astype(
        jnp.bfloat16
    )
    grad_hidden = jnp.dot(scaled, down_w.T, preferred_element_type=jnp.float32)
    grad_up = (grad_hidden * active).astype(jnp.bfloat16)
    grad_gate = (grad_hidden * pre_up * slope_term).astype(jnp.bfloat16)
    row_grad = (
        jnp.dot(grad_gate, gate_w.T, preferred_element_type=jnp.float32)
        + jnp.dot(grad_up, up_w.T, preferred_element_type=jnp.float32)
    ).astype(jnp.bfloat16)
    grad_gate_w = jnp.dot(expert_rows.T, grad_gate, preferred_element_type=jnp.float32)
    grad_up_w = jnp.dot(expert_rows.T, grad_up, preferred_element_type=jnp.float32)
    grad_down_w = jnp.dot(hidden.T, scaled, preferred_element_type=jnp.float32)
    return (row_grad, gate_grads, grad_gate_w, grad_up_w, grad_down_w)


def join_halves(own_part, other_part, is_lower, axis_number):
    lower_part = jnp.where(is_lower, own_part, other_part)
    upper_part = jnp.where(is_lower, other_part, own_part)
    return jnp.concatenate([lower_part, upper_part], axis_number)


def body(tokens, cotangent, expert_ids, gate_probs, gate_half, up_half, down_half):
    column_count = lax.axis_size("expert")
    group_count = lax.axis_size("dp")
    device_count = column_count * group_count
    expert_count = device_count // 2
    tok_rows, feature_count = tokens.shape
    top_count = expert_ids.shape[1]
    assigned = tok_rows * top_count
    most_rows = min(2 * assigned // expert_count, tok_rows)
    capacity = most_rows // 2
    slot_count = device_count * capacity
    half_width = feature_count // 2
    member = lax.axis_index("dp") % 2
    is_lower = member == 0
    own_half = (gate_half[0], up_half[0], down_half[0])
    partner = partner_2((own_half[0], own_half[1], own_half[2]), "dp", 0)
    gate_w = join_halves(own_half[0], partner[0], is_lower, 0)
    up_w = join_halves(own_half[1], partner[1], is_lower, 0)
    down_w = join_halves(own_half[2], partner[2], is_lower, 1)
    flat_ids = expert_ids.reshape(-1)
    onehot = (flat_ids[:, None] == jnp.arange(expert_count, dtype=jnp.int32)[None, :]).astype(
        jnp.int32
    )
    rank_in = jnp.sum((jnp.cumsum(onehot, axis=0) - onehot) * onehot, axis=1)
    position = (2 * flat_ids + rank_in % 2) * capacity + rank_in // 2
    source = jnp.arange(assigned, dtype=jnp.int32) // top_count
    block_shape = (column_count, group_count, capacity, feature_count)
    send_rows = (
        jnp.zeros((slot_count, feature_count), jnp.bfloat16)
        .at[position]
        .set(tokens[source])
        .reshape(block_shape)
    )
    send_dys = (
        jnp.zeros((slot_count, feature_count), jnp.bfloat16)
        .at[position]
        .set(cotangent[source])
        .reshape(block_shape)
    )
    send_gates = (
        jnp.zeros((slot_count,), jnp.bfloat16)
        .at[position]
        .set(gate_probs.reshape(-1))
        .reshape(column_count, group_count, capacity)
    )
    rows_in, dys_in, gates_in = (
        lax.all_to_all(
            lax.all_to_all(send_rows, "expert", split_axis=0, concat_axis=0, tiled=True),
            "dp",
            split_axis=1,
            concat_axis=1,
            tiled=True,
        ),
        lax.all_to_all(
            lax.all_to_all(send_dys, "expert", split_axis=0, concat_axis=0, tiled=True),
            "dp",
            split_axis=1,
            concat_axis=1,
            tiled=True,
        ),
        lax.all_to_all(
            lax.all_to_all(send_gates, "expert", split_axis=0, concat_axis=0, tiled=True),
            "dp",
            split_axis=1,
            concat_axis=1,
            tiled=True,
        ),
    )
    row_grad, gate_grads, grad_gate_w, grad_up_w, grad_down_w = expert_pass(
        rows_in.reshape(slot_count, feature_count),
        dys_in.reshape(slot_count, feature_count),
        gates_in.reshape(slot_count),
        gate_w,
        up_w,
        down_w,
    )
    back_rows, back_gates = (
        lax.all_to_all(
            lax.all_to_all(
                row_grad.reshape(block_shape), "expert", split_axis=0, concat_axis=0, tiled=True
            ),
            "dp",
            split_axis=1,
            concat_axis=1,
            tiled=True,
        ),
        lax.all_to_all(
            lax.all_to_all(
                gate_grads.reshape(column_count, group_count, capacity),
                "expert",
                split_axis=0,
                concat_axis=0,
                tiled=True,
            ),
            "dp",
            split_axis=1,
            concat_axis=1,
            tiled=True,
        ),
    )
    picked = back_rows.reshape(slot_count, feature_count)[position]
    grad_tokens = jnp.sum(
        picked.reshape(tok_rows, top_count, feature_count).astype(jnp.float32), axis=1
    ).astype(jnp.bfloat16)
    grad_gates = back_gates.reshape(slot_count)[position].reshape(tok_rows, top_count)
    give_start = (1 - member) * half_width
    keep_start = member * half_width
    outgoing = (
        lax.dynamic_slice_in_dim(grad_gate_w, give_start, half_width, 0),
        lax.dynamic_slice_in_dim(grad_up_w, give_start, half_width, 0),
        lax.dynamic_slice_in_dim(grad_down_w, give_start, half_width, 1),
    )
    incoming = partner_2((outgoing[0], outgoing[1], outgoing[2]), "dp", 0)
    grad_gate_half = (
        lax.dynamic_slice_in_dim(grad_gate_w, keep_start, half_width, 0) + incoming[0]
    ).astype(jnp.bfloat16)
    grad_up_half = (
        lax.dynamic_slice_in_dim(grad_up_w, keep_start, half_width, 0) + incoming[1]
    ).astype(jnp.bfloat16)
    grad_down_half = (
        lax.dynamic_slice_in_dim(grad_down_w, keep_start, half_width, 1) + incoming[2]
    ).astype(jnp.bfloat16)
    return (grad_tokens, grad_gates, grad_gate_half[None], grad_up_half[None], grad_down_half[None])


def solution(mesh):
    in_specs = (
        P(("dom", "expert", "dp"), None),
        P(("dom", "expert", "dp"), None),
        P(("dom", "expert", "dp"), None),
        P(("dom", "expert", "dp"), None),
        P(("dom", "expert", "dp"), None, None),
        P(("dom", "expert", "dp"), None, None),
        P(("dom", "expert", "dp"), None, None),
    )
    out_specs = (
        P(("dom", "expert", "dp"), None),
        P(("dom", "expert", "dp"), None),
        P(("dom", "expert", "dp"), None, None),
        P(("dom", "expert", "dp"), None, None),
        P(("dom", "expert", "dp"), None, None),
    )
    return jax.shard_map(body, mesh=mesh, in_specs=in_specs, out_specs=out_specs, check_vma=False)
```

profile of v0, /device:TPU:0, one launch (start us, length us, event | category | flops | bytes accessed | tf_op | source)
XLA Modules:
  0.0 201.3 jit_solution(8716854576701397598)
XLA Ops:
  4.3 2.2 %scatter_custom_fusion = bf16[512]{0:T(512)(128)(2,1)S(1)} fusion(s32[256]{0:T(256)S(1)} %bitcast.74, bf16[256]{0:T(256)(128)(2,1)S(1)} %reshape.262, bf16[]{:T(256)} %constant.60.clone.1), kind=kCustom, calls=%fused_computation.70 | custom fusion | bytes 1026 | tf_op jit(solution)/shard_map/scatter | solution.py:89
  6.6 13.6 %all_to_all.50 = bf16[8,4,16]{2,1,0:T(4,128)(2,1)S(1)} all-to-all(bf16[8,4,16]{2,1,0:T(4,128)(2,1)S(1)} %reshape.215), channel_id=1, replica_groups=mesh['dom'=1,'expert'=8,'dp'=4] {'expert'}, dimensions={0} | all-to-all | bytes 2048 | tf_op jit(solution)/shard_map/all_to_all | solution.py:108
  20.7 3.2 %all-to-all-start.1 = ((bf16[8,4,16]{2,0,1:T(8,128)(2,1)}), bf16[8,4,16]{2,0,1:T(8,128)(2,1)S(1)}, u32[]{:S(2)}, u32[]{:S(2)}) async-start(bf16[8,4,16]{2,0,1:T(8,128)(2,1)} %copy.48), calls=%async_computation.1 | async-start | bytes 16384 | tf_op jit(solution)/shard_map/all_to_all | solution.py:107
  24.0 4.5 %scatter_custom_fusion.1 = bf16[512,1024]{1,0:T(8,128)(2,1)} fusion(s32[256]{0:T(256)S(1)} %bitcast.75, bf16[32,1024]{1,0:T(8,128)(2,1)S(1)} %copy-done, s32[1024]{0:T(1024)S(1)} %pad_clamp_fusion.1, bf16[]{:T(256)} %constant.60.clone.1), kind=kCustom, calls=%fused_computation.26 | custom fusion | bytes 1048578 | tf_op jit(solution)/shard_map/scatter | solution.py:83
  28.5 3.6 %all-to-all-start.2 = ((bf16[8,4,16,1024]{3,2,1,0:T(8,128)(2,1)}), bf16[8,4,16,1024]{3,2,1,0:T(8,128)(2,1)S(1)}, u32[]{:S(2)}, u32[]{:S(2)}) async-start(bf16[8,4,16,1024]{3,2,1,0:T(8,128)(2,1)} %bitcast.4), calls=%async_computation.2 | async-start | bytes 2097152 | tf_op jit(solution)/shard_map/all_to_all | solution.py:101
  32.1 5.6 %scatter_custom_fusion.2 = bf16[512,1024]{1,0:T(8,128)(2,1)} fusion(s32[256]{0:T(256)S(1)} %bitcast.76, bf16[32,1024]{1,0:T(8,128)(2,1)} %param.7, s32[1024]{0:T(1024)S(1)} %pad_clamp_fusion.1, bf16[]{:T(256)} %constant.60.clone.1), kind=kCustom, calls=%fused_computation.24 | custom fusion | bytes 1049088 | tf_op jit(solution)/shard_map/scatter | solution.py:77
  37.6 21.0 %all-to-all-done.2 = bf16[8,4,16,1024]{3,2,1,0:T(8,128)(2,1)S(1)} async-done(((bf16[8,4,16,1024]{3,2,1,0:T(8,128)(2,1)}), bf16[8,4,16,1024]{3,2,1,0:T(8,128)(2,1)S(1)}, u32[]{:S(2)}, u32[]{:S(2)}) %all-to-all-start.2) | async-done | bytes 1048608 | tf_op jit(solution)/shard_map/all_to_all | solution.py:101
  58.6 3.6 %all-to-all-start.4 = ((bf16[8,4,16,1024]{3,2,1,0:T(8,128)(2,1)}), bf16[8,4,16,1024]{3,2,1,0:T(8,128)(2,1)S(1)}, u32[]{:S(2)}, u32[]{:S(2)}) async-start(bf16[8,4,16,1024]{3,2,1,0:T(8,128)(2,1)} %bitcast.7), calls=%async_computation.4 | async-start | bytes 2097152 | tf_op jit(solution)/shard_map/all_to_all | solution.py:94
  63.4 24.9 %all-to-all-done.4 = bf16[8,4,16,1024]{3,2,1,0:T(8,128)(2,1)S(1)} async-done(((bf16[8,4,16,1024]{3,2,1,0:T(8,128)(2,1)}), bf16[8,4,16,1024]{3,2,1,0:T(8,128)(2,1)S(1)}, u32[]{:S(2)}, u32[]{:S(2)}) %all-to-all-start.4) | async-done | bytes 1048608 | tf_op jit(solution)/shard_map/all_to_all | solution.py:94
  88.3 3.5 %all-to-all-start.3 = ((bf16[8,4,16,1024]{3,2,0,1:T(8,128)(2,1)}), bf16[8,4,16,1024]{3,2,0,1:T(8,128)(2,1)S(1)}, u32[]{:S(2)}, u32[]{:S(2)}) async-start(bf16[8,4,16,1024]{3,2,0,1:T(8,128)(2,1)} %copy.50), calls=%async_computation.3 | async-start | bytes 2097152 | tf_op jit(solution)/shard_map/all_to_all | solution.py:100
  94.0 1.9 broadcast_select_fusion.5
  96.9 9.3 %all-to-all-done.3 = bf16[8,4,16,1024]{3,2,0,1:T(8,128)(2,1)S(1)} async-done(((bf16[8,4,16,1024]{3,2,0,1:T(8,128)(2,1)}), bf16[8,4,16,1024]{3,2,0,1:T(8,128)(2,1)S(1)}, u32[]{:S(2)}, u32[]{:S(2)}) %all-to-all-start.3) | async-done | bytes 1048608 | tf_op jit(solution)/shard_map/all_to_all | solution.py:100
  106.2 4.4 %all-to-all-start.5 = ((bf16[8,4,16,1024]{3,2,0,1:T(8,128)(2,1)}), bf16[8,4,16,1024]{3,2,0,1:T(8,128)(2,1)}, u32[]{:S(2)}, u32[]{:S(2)}) async-start(bf16[8,4,16,1024]{3,2,0,1:T(8,128)(2,1)} %copy.52), calls=%async_computation.5 | async-start | bytes 2097152 | tf_op jit(solution)/shard_map/all_to_all | solution.py:93
  110.7 2.0 broadcast_select_fusion.3
  112.6 1.9 broadcast_select_fusion.1
  116.0 9.0 %all-to-all-done.5 = bf16[8,4,16,1024]{3,2,0,1:T(8,128)(2,1)} async-done(((bf16[8,4,16,1024]{3,2,0,1:T(8,128)(2,1)}), bf16[8,4,16,1024]{3,2,0,1:T(8,128)(2,1)}, u32[]{:S(2)}, u32[]{:S(2)}) %all-to-all-start.5) | async-done | bytes 1048608 | tf_op jit(solution)/shard_map/all_to_all | solution.py:93
  129.0 1.8 multiply_convert_fusion
  133.1 3.6 %all-to-all-start.8 = ((bf16[8,4,16]{2,1,0:T(4,128)(2,1)}), bf16[8,4,16]{2,1,0:T(4,128)(2,1)S(1)}, u32[]{:S(2)}, u32[]{:S(2)}) async-start(bf16[8,4,16]{2,1,0:T(4,128)(2,1)} %convert_element_type.69), calls=%async_computation.8 | async-start | bytes 16384 | tf_op jit(solution)/shard_map/all_to_all | solution.py:134
  136.7 2.1 %fusion.10 = f32[512,1024]{1,0:T(8,128)S(1)} fusion(bf16[512,384]{1,0:T(8,128)(2,1)} %get-tuple-element.27, bf16[512,384]{1,0:T(8,128)(2,1)} %get-tuple-element.29, bf16[512,384]{1,0:T(8,128)(2,1)} %get-tuple-element.28), kind=kOutput, calls=%fused_computation.31 | convolution fusion | flops 404226048 | bytes 3276800 | tf_op jit(solution)/shard_map/dot_general | solution.py:33
  138.8 1.8 add_convert_fusion
  140.6 2.6 %all-to-all-done.8 = bf16[8,4,16]{2,1,0:T(4,128)(2,1)S(1)} async-done(((bf16[8,4,16]{2,1,0:T(4,128)(2,1)}), bf16[8,4,16]{2,1,0:T(4,128)(2,1)S(1)}, u32[]{:S(2)}, u32[]{:S(2)}) %all-to-all-start.8) | async-done | bytes 1056 | tf_op jit(solution)/shard_map/all_to_all | solution.py:134
  143.2 4.2 %all-to-all-start.6 = ((bf16[8,4,16,1024]{3,2,1,0:T(8,128)(2,1)}), bf16[8,4,16,1024]{3,2,1,0:T(8,128)(2,1)}, u32[]{:S(2)}, u32[]{:S(2)}) async-start(bf16[8,4,16,1024]{3,2,1,0:T(8,128)(2,1)} %bitcast.11), calls=%async_computation.6 | async-start | bytes 2097152 | tf_op jit(solution)/shard_map/all_to_all | solution.py:125
  147.5 1.8 fusion.31
  155.4 16.7 %all-to-all-done.6 = bf16[8,4,16,1024]{3,2,1,0:T(8,128)(2,1)} async-done(((bf16[8,4,16,1024]{3,2,1,0:T(8,128)(2,1)}), bf16[8,4,16,1024]{3,2,1,0:T(8,128)(2,1)}, u32[]{:S(2)}, u32[]{:S(2)}) %all-to-all-start.6) | async-done | bytes 1048608 | tf_op jit(solution)/shard_map/all_to_all | solution.py:125
  172.0 3.2 %all-to-all-start.9 = ((bf16[8,4,16]{2,0,1:T(8,128)(2,1)}), bf16[8,4,16]{2,0,1:T(8,128)(2,1)S(1)}, u32[]{:S(2)}, u32[]{:S(2)}) async-start(bf16[8,4,16]{2,0,1:T(8,128)(2,1)} %copy.56), calls=%async_computation.9 | async-start | bytes 16384 | tf_op jit(solution)/shard_map/all_to_all | solution.py:133
  175.3 2.3 %copy.54 = bf16[8,4,16,1024]{3,2,0,1:T(8,128)(2,1)} copy(bf16[8,4,16,1024]{3,2,1,0:T(8,128)(2,1)} %all-to-all-done.6) | data formatting | bytes 2097152 | tf_op jit(solution)/shard_map/all_to_all | solution.py:125
  177.6 1.4 all-to-all-done.9
  179.1 4.2 %all-to-all-start.7 = ((bf16[8,4,16,1024]{3,2,0,1:T(8,128)(2,1)}), bf16[8,4,16,1024]{3,2,0,1:T(8,128)(2,1)}, u32[]{:S(2)}, u32[]{:S(2)}) async-start(bf16[8,4,16,1024]{3,2,0,1:T(8,128)(2,1)} %copy.54), calls=%async_computation.7 | async-start | bytes 2097152 | tf_op jit(solution)/shard_map/all_to_all | solution.py:124
  183.4 1.9 gather_fusion.1
  186.2 2.1 %fusion.15 = bf16[1,384,512]{2,1,0:T(8,128)(2,1)} fusion(f32[384,512]{1,0:T(8,128)} %collective-permute-done.5, f32[384,1024]{1,0:T(8,128)S(1)} %fusion.31, s32[]{:T(128)S(6)} %select_n.127), kind=kLoop, calls=%fused_computation.36 | loop fusion | flops 393216 | bytes 1966084 | tf_op jit(solution)/shard_map/broadcast_in_dim | solution.py:169
  188.3 2.0 fusion.13
  191.1 6.8 %all-to-all-done.7 = bf16[8,4,16,1024]{3,2,0,1:T(8,128)(2,1)} async-done(((bf16[8,4,16,1024]{3,2,0,1:T(8,128)(2,1)}), bf16[8,4,16,1024]{3,2,0,1:T(8,128)(2,1)}, u32[]{:S(2)}, u32[]{:S(2)}) %all-to-all-start.7) | async-done | bytes 1048608 | tf_op jit(solution)/shard_map/all_to_all | solution.py:124
  (97 shorter events, 27.5 us)
Async XLA Ops:
  0.6 23.4 %copy-start = (bf16[32,1024]{1,0:T(8,128)(2,1)S(1)}, bf16[32,1024]{1,0:T(8,128)(2,1)}, u32[]{:S(2)}) copy-start(bf16[32,1024]{1,0:T(8,128)(2,1)} %param.8) | copy-start | bytes 196612
  20.7 7.8 %all-to-all-start.1 = ((bf16[8,4,16]{2,0,1:T(8,128)(2,1)}), bf16[8,4,16]{2,0,1:T(8,128)(2,1)S(1)}, u32[]{:S(2)}, u32[]{:S(2)}) async-start(bf16[8,4,16]{2,0,1:T(8,128)(2,1)} %copy.48), calls=%async_computation.1 | async-start | bytes 16384 | tf_op jit(solution)/shard_map/all_to_all | solution.py:107
  28.5 30.2 %all-to-all-start.2 = ((bf16[8,4,16,1024]{3,2,1,0:T(8,128)(2,1)}), bf16[8,4,16,1024]{3,2,1,0:T(8,128)(2,1)S(1)}, u32[]{:S(2)}, u32[]{:S(2)}) async-start(bf16[8,4,16,1024]{3,2,1,0:T(8,128)(2,1)} %bitcast.4), calls=%async_computation.2 | async-start | bytes 2097152 | tf_op jit(solution)/shard_map/all_to_all | solution.py:101
  58.6 29.6 %all-to-all-start.4 = ((bf16[8,4,16,1024]{3,2,1,0:T(8,128)(2,1)}), bf16[8,4,16,1024]{3,2,1,0:T(8,128)(2,1)S(1)}, u32[]{:S(2)}, u32[]{:S(2)}) async-start(bf16[8,4,16,1024]{3,2,1,0:T(8,128)(2,1)} %bitcast.7), calls=%async_computation.4 | async-start | bytes 2097152 | tf_op jit(solution)/shard_map/all_to_all | solution.py:94
  63.3 28.4 %copy-start.13 = (bf16[1,384,512]{2,1,0:T(8,128)(2,1)S(1)}, bf16[1,384,512]{2,1,0:T(8,128)(2,1)}, u32[]{:S(2)}) copy-start(bf16[1,384,512]{2,1,0:T(8,128)(2,1)} %param.13) | copy-start | bytes 1179652
  63.3 28.9 %copy-start.14 = (bf16[1,512,384]{2,1,0:T(8,128)(2,1)S(1)}, bf16[1,512,384]{2,1,0:T(8,128)(2,1)}, u32[]{:S(2)}) copy-start(bf16[1,512,384]{2,1,0:T(8,128)(2,1)} %param.12) | copy-start | bytes 1179652
  63.4 29.0 %copy-start.15 = (bf16[1,512,384]{2,1,0:T(8,128)(2,1)S(1)}, bf16[1,512,384]{2,1,0:T(8,128)(2,1)}, u32[]{:S(2)}) copy-start(bf16[1,512,384]{2,1,0:T(8,128)(2,1)} %param.11) | copy-start | bytes 1179652
  88.3 18.0 %all-to-all-start.3 = ((bf16[8,4,16,1024]{3,2,0,1:T(8,128)(2,1)}), bf16[8,4,16,1024]{3,2,0,1:T(8,128)(2,1)S(1)}, u32[]{:S(2)}, u32[]{:S(2)}) async-start(bf16[8,4,16,1024]{3,2,0,1:T(8,128)(2,1)} %copy.50), calls=%async_computation.3 | async-start | bytes 2097152 | tf_op jit(solution)/shard_map/all_to_all | solution.py:100
  91.8 2.2 %collective-permute-start = (bf16[384,512]{1,0:T(8,128)(2,1)S(1)}, bf16[384,512]{1,0:T(8,128)(2,1)}, u32[]{:S(2)}, u32[]{:S(2)}) collective-permute-start(bf16[384,512]{1,0:T(8,128)(2,1)S(1)} %bitcast.71), channel_id=1, source_target_pairs={{0,1},{1,0},{2,3},{3,2},{4,5},{5,4},{6,7},{7,6},{8,9},{9,8},{10,11... | collective-permute-start | bytes 1179656 | tf_op jit(solution)/shard_map/ppermute | solution.py:8
  92.3 18.4 %collective-permute-start.1 = (bf16[512,384]{1,0:T(8,128)(2,1)S(1)}, bf16[512,384]{1,0:T(8,128)(2,1)}, u32[]{:S(2)}, u32[]{:S(2)}) collective-permute-start(bf16[512,384]{1,0:T(8,128)(2,1)S(1)} %bitcast.72), channel_id=1, source_target_pairs={{0,1},{1,0},{2,3},{3,2},{4,5},{5,4},{6,7},{7,6},{8,9},{9,8},{10,11... | collective-permute-start | bytes 1179656 | tf_op jit(solution)/shard_map/ppermute | solution.py:8
  92.4 20.2 %collective-permute-start.2 = (bf16[512,384]{1,0:T(8,128)(2,1)S(1)}, bf16[512,384]{1,0:T(8,128)(2,1)}, u32[]{:S(2)}, u32[]{:S(2)}) collective-permute-start(bf16[512,384]{1,0:T(8,128)(2,1)S(1)} %bitcast.73), channel_id=1, source_target_pairs={{0,1},{1,0},{2,3},{3,2},{4,5},{5,4},{6,7},{7,6},{8,9},{9,8},{10,11... | collective-permute-start | bytes 1179656 | tf_op jit(solution)/shard_map/ppermute | solution.py:8
  106.2 18.8 %all-to-all-start.5 = ((bf16[8,4,16,1024]{3,2,0,1:T(8,128)(2,1)}), bf16[8,4,16,1024]{3,2,0,1:T(8,128)(2,1)}, u32[]{:S(2)}, u32[]{:S(2)}) async-start(bf16[8,4,16,1024]{3,2,0,1:T(8,128)(2,1)} %copy.52), calls=%async_computation.5 | async-start | bytes 2097152 | tf_op jit(solution)/shard_map/all_to_all | solution.py:93
  125.0 1.4 copy-start.7
  125.0 1.4 copy-start.9
  126.4 1.2 copy-start.4
  126.4 1.3 copy-start.16
  126.4 1.4 copy-start.17
  133.1 10.2 %all-to-all-start.8 = ((bf16[8,4,16]{2,1,0:T(4,128)(2,1)}), bf16[8,4,16]{2,1,0:T(4,128)(2,1)S(1)}, u32[]{:S(2)}, u32[]{:S(2)}) async-start(bf16[8,4,16]{2,1,0:T(4,128)(2,1)} %convert_element_type.69), calls=%async_computation.8 | async-start | bytes 16384 | tf_op jit(solution)/shard_map/all_to_all | solution.py:134
  136.7 2.1 %copy-start.8 = (bf16[512,384]{1,0:T(8,128)(2,1)S(1)}, bf16[512,384]{1,0:T(8,128)(2,1)}, u32[]{:S(2)}) copy-start(bf16[512,384]{1,0:T(8,128)(2,1)} %get-tuple-element.30) | copy-start | bytes 1179652
  136.7 2.1 %copy-start.10 = (bf16[512,384]{1,0:T(8,128)(2,1)S(1)}, bf16[512,384]{1,0:T(8,128)(2,1)}, u32[]{:S(2)}) copy-start(bf16[512,384]{1,0:T(8,128)(2,1)} %get-tuple-element.31) | copy-start | bytes 1179652
  136.7 2.1 %copy-start.12 = (bf16[512,384]{1,0:T(8,128)(2,1)S(1)}, bf16[512,384]{1,0:T(8,128)(2,1)}, u32[]{:S(2)}) copy-start(bf16[512,384]{1,0:T(8,128)(2,1)} %get-tuple-element.26) | copy-start | bytes 1179652
  140.6 6.9 %copy-start.19 = (bf16[512,384]{1,0:T(8,128)(2,1)S(1)}, bf16[512,384]{1,0:T(8,128)(2,1)}, u32[]{:S(2)}) copy-start(bf16[512,384]{1,0:T(8,128)(2,1)} %copy-done.18) | copy-start | bytes 1179652
  143.2 28.8 %all-to-all-start.6 = ((bf16[8,4,16,1024]{3,2,1,0:T(8,128)(2,1)}), bf16[8,4,16,1024]{3,2,1,0:T(8,128)(2,1)}, u32[]{:S(2)}, u32[]{:S(2)}) async-start(bf16[8,4,16,1024]{3,2,1,0:T(8,128)(2,1)} %bitcast.11), calls=%async_computation.6 | async-start | bytes 2097152 | tf_op jit(solution)/shard_map/all_to_all | solution.py:125
  150.2 2.3 %copy-start.11 = (bf16[512,384]{1,0:T(8,128)(2,1)S(1)}, bf16[512,384]{1,0:T(8,128)(2,1)}, u32[]{:S(2)}) copy-start(bf16[512,384]{1,0:T(8,128)(2,1)} %get-tuple-element.27) | copy-start | bytes 1179652
  150.2 35.9 %collective-permute-start.5 = (f32[384,512]{1,0:T(8,128)}, f32[384,512]{1,0:T(8,128)}, u32[]{:S(2)}, u32[]{:S(2)}) collective-permute-start(f32[384,512]{1,0:T(8,128)} %constant_dynamic-slice_fusion), channel_id=1, source_target_pairs={{0,1},{1,0},{2,3},{3,2},{4,5},{5,4},{6,7},{7,6},{8,9},{9,8},{10,11... | collective-permute-start | bytes 2359304 | tf_op jit(solution)/shard_map/ppermute | solution.py:8
  151.0 2.3 %copy-start.1 = (f32[1024,384]{1,0:T(8,128)}, f32[1024,384]{1,0:T(8,128)S(1)}, u32[]{:S(2)}) copy-start(f32[1024,384]{1,0:T(8,128)S(1)} %fusion.29) | copy-start | bytes 4718596
  152.0 36.2 %collective-permute-start.3 = (f32[512,384]{1,0:T(8,128)}, f32[512,384]{1,0:T(8,128)S(1)}, u32[]{:S(2)}, u32[]{:S(2)}) collective-permute-start(f32[512,384]{1,0:T(8,128)} %constant_dynamic-slice_fusion.2), channel_id=1, source_target_pairs={{0,1},{1,0},{2,3},{3,2},{4,5},{5,4},{6,7},{7,6},{8,9},{9,8},{10,11... | collective-permute-start | bytes 2359304 | tf_op jit(solution)/shard_map/ppermute | solution.py:8
  153.3 1.5 copy-start.2
  154.8 35.4 %collective-permute-start.4 = (f32[512,384]{1,0:T(8,128)}, f32[512,384]{1,0:T(8,128)S(1)}, u32[]{:S(2)}, u32[]{:S(2)}) collective-permute-start(f32[512,384]{1,0:T(8,128)} %constant_dynamic-slice_fusion.1), channel_id=1, source_target_pairs={{0,1},{1,0},{2,3},{3,2},{4,5},{5,4},{6,7},{7,6},{8,9},{9,8},{10,11... | collective-permute-start | bytes 2359304 | tf_op jit(solution)/shard_map/ppermute | solution.py:8
  172.0 7.0 %all-to-all-start.9 = ((bf16[8,4,16]{2,0,1:T(8,128)(2,1)}), bf16[8,4,16]{2,0,1:T(8,128)(2,1)S(1)}, u32[]{:S(2)}, u32[]{:S(2)}) async-start(bf16[8,4,16]{2,0,1:T(8,128)(2,1)} %copy.56), calls=%async_computation.9 | async-start | bytes 16384 | tf_op jit(solution)/shard_map/all_to_all | solution.py:133
  179.1 18.8 %all-to-all-start.7 = ((bf16[8,4,16,1024]{3,2,0,1:T(8,128)(2,1)}), bf16[8,4,16,1024]{3,2,0,1:T(8,128)(2,1)}, u32[]{:S(2)}, u32[]{:S(2)}) async-start(bf16[8,4,16,1024]{3,2,0,1:T(8,128)(2,1)} %copy.54), calls=%async_computation.7 | async-start | bytes 2097152 | tf_op jit(solution)/shard_map/all_to_all | solution.py:124
  186.2 4.1 %copy-start.3 = (f32[1024,384]{1,0:T(8,128)S(1)}, f32[1024,384]{1,0:T(8,128)}, u32[]{:S(2)}) copy-start(f32[1024,384]{1,0:T(8,128)} %copy-done.2) | copy-start | bytes 4718596
  (3 other events, 2.9 us)
where the time goes:
time: 203 us; the launch traced here: 201 us
  waiting for transfers between devices  92.8 us (46%)
  starting transfers between devices  35.2 us (17%)
  local copies, waits for them, and re-layouts  33.2 us (16%)
  other arithmetic  14.3 us (7%)
  blocking collectives  13.6 us (7%)
  matrix products  11.2 us (6%)
    all_to_all x1, waiting for transfers between devices, body(): lax.all_to_all(send_rows, 'expert', split_axis=0, concat_axis=0, tiled=True)  24.9 us
    all_to_all x1, waiting for transfers between devices, body(): lax.all_to_all(send_dys, 'expert', split_axis=0, concat_axis=0, tiled=True)  21 us
    all_to_all x1, waiting for transfers between devices, body(): lax.all_to_all(row_grad.reshape(block_shape), 'expert', split_axis=0, con...  16.7 us
    all_to_all x1, blocking collectives, body(): lax.all_to_all(send_gates, 'expert', split_axis=0, concat_axis=0, tiled=T...  13.6 us
    all_to_all x1, waiting for transfers between devices, body(): lax.all_to_all(lax.all_to_all(send_dys, 'expert', split_axis=0, concat_ax...  9.28 us
    all_to_all x1, waiting for transfers between devices, body(): lax.all_to_all(lax.all_to_all(send_rows, 'expert', split_axis=0, concat_a...  8.99 us
    all_to_all x1, waiting for transfers between devices, body(): lax.all_to_all(lax.all_to_all(row_grad.reshape(block_shape), 'expert', sp...  6.79 us
    select_n x3, other arithmetic, join_halves(): lower_part = jnp.where(is_lower, own_part, other_part)  5.81 us
  transfers between devices with their start and end apart: 15, of which 9 were waited for; matrix products, arithmetic and copies ran while one was open for 20% of the time, Pallas kernels for 0%

commit v1 on v0

v1 whole, which is shorter than its diff:
```python
import jax
import jax.numpy as jnp
from jax import lax
from jax.sharding import Mesh, PartitionSpec as P

CHIPS = ("expert", "chip")


def swap_core(x):
    return lax.ppermute(x, "core", [(0, 1), (1, 0)])


def body(tokens, cotangent, expert_ids, gate_probs, gate_half, up_half, down_half):
    f32, bf16 = jnp.float32, jnp.bfloat16
    chip_count = lax.axis_size("expert") * lax.axis_size("chip")
    tok_rows, feature_count = tokens.shape
    top_count = expert_ids.shape[1]
    half_width = feature_count // 2
    member = lax.axis_index("core")
    own_expert = lax.axis_index("expert") * lax.axis_size("chip") + lax.axis_index("chip")

    own_half = (gate_half[0], up_half[0], down_half[0])
    other_half = [swap_core(w) for w in own_half]
    is_lower = member == 0

    def join(own, other, axis):
        return jnp.concatenate(
            [jnp.where(is_lower, own, other), jnp.where(is_lower, other, own)], axis
        )

    gate_w, up_w, down_w = (
        join(own, other, axis) for own, other, axis in zip(own_half, other_half, (0, 0, 1))
    )

    experts = jnp.arange(chip_count, dtype=jnp.int32)
    named = expert_ids[:, :, None] == experts
    weight = jnp.sum(jnp.where(named, gate_probs.astype(f32)[:, :, None], 0.0), axis=1)
    lanes = -(-chip_count // 128) * 128
    weight = jnp.pad(weight, ((0, 0), (0, lanes - chip_count))).astype(bf16)

    rows = lax.all_gather(tokens, CHIPS, axis=0, tiled=True)
    dys_weight = lax.all_gather(
        jnp.concatenate([cotangent, weight], 1), CHIPS, axis=0, tiled=True
    )
    dys = dys_weight[:, :feature_count]
    is_own = jnp.arange(lanes, dtype=jnp.int32) == own_expert
    gates = jnp.sum(
        jnp.where(is_own, dys_weight[:, feature_count:].astype(f32), 0.0), 1, keepdims=True
    )

    pre_gate = jnp.dot(rows, gate_w, preferred_element_type=f32)
    pre_up = jnp.dot(rows, up_w, preferred_element_type=f32)
    sig = jax.nn.sigmoid(pre_gate)
    active = pre_gate * sig
    slope = sig * (1.0 + pre_gate * (1.0 - sig))
    hidden = active * pre_up
    back = lax.dot_general(dys, down_w, (((1,), (1,)), ((), ())), preferred_element_type=f32)
    gate_grads = jnp.sum(hidden * back, 1, keepdims=True)
    back = back * gates
    grad_up = (back * active).astype(bf16)
    grad_gate = (back * pre_up * slope).astype(bf16)
    row_grad = (
        lax.dot_general(grad_gate, gate_w, (((1,), (1,)), ((), ())), preferred_element_type=f32)
        + lax.dot_general(grad_up, up_w, (((1,), (1,)), ((), ())), preferred_element_type=f32)
    ).astype(bf16)
    hidden = (hidden * gates).astype(bf16)

    gate_cols = jnp.where(is_own, gate_grads, 0.0).astype(bf16)
    summed = lax.psum_scatter(
        jnp.concatenate([row_grad, gate_cols], 1), CHIPS, scatter_dimension=0, tiled=True
    )
    grad_tokens = summed[:, :feature_count]
    grad_gates = jnp.sum(
        jnp.where(named, summed[:, None, feature_count : feature_count + chip_count], 0), 2
    ).astype(bf16)

    across = (((0,), (0,)), ((), ()))
    grad_gate_w = lax.dot_general(rows, grad_gate, across, preferred_element_type=f32)
    grad_up_w = lax.dot_general(rows, grad_up, across, preferred_element_type=f32)
    grad_down_w = lax.dot_general(hidden, dys, across, preferred_element_type=f32)

    def settle(whole, axis):
        give = lax.dynamic_slice_in_dim(whole, (1 - member) * half_width, half_width, axis)
        keep = lax.dynamic_slice_in_dim(whole, member * half_width, half_width, axis)
        return (keep + swap_core(give.astype(bf16)).astype(f32)).astype(bf16)[None]

    return (
        grad_tokens,
        grad_gates,
        settle(grad_gate_w, 0),
        settle(grad_up_w, 0),
        settle(grad_down_w, 1),
    )


def solution(mesh):
    shape = mesh.shape
    devices = mesh.devices.reshape(shape["dom"], shape["expert"], shape["dp"] // 2, 2)
    fine = Mesh(devices, ("dom", "expert", "chip", "core"))
    every = ("dom", "expert", "chip", "core")
    flat, cube = P(every, None), P(every, None, None)
    return jax.shard_map(
        body,
        mesh=fine,
        in_specs=(flat, flat, flat, flat, cube, cube, cube),
        out_specs=(flat, flat, cube, cube, cube),
        check_vma=False,
    )
```

time: 203 us -> 267 us (1.32)
  waiting for transfers between devices: 92.8 us -> 224 us
  starting transfers between devices: 35.2 us -> 1.72 us
  local copies, waits for them, and re-layouts: 33.2 us -> 5.91 us
  blocking collectives: 13.6 us -> 0 us
  between operations: 0.97 us -> 13.9 us
  other arithmetic: 14.3 us -> 10.9 us
    reduce_scatter x0 -> x1, waiting for transfers between devices: none -> 114 us  [body(): lax.psum_scatter(jnp.concatenate([row_grad, gate_cols], 1), CHIPS, scatte...]
    all_gather x0 -> x2, waiting for transfers between devices: none -> 108 us  [the longest x1 54 us: body(): lax.all_gather(jnp.concatenate([cotangent, weight], 1), CHIPS, axis=0, ti...]
    all_to_all x9 -> x0, waiting for transfers between devices: 91.7 us -> none  [the longest x1 24.9 us: body(): lax.all_to_all(send_rows, 'expert', split_axis=0, concat_axis=0, tiled=True)]
    all_to_all x9 -> x0, starting transfers between devices: 33.7 us -> none  [the longest x1 4.42 us: body(): lax.all_to_all(lax.all_to_all(send_rows, 'expert', split_axis=0, concat_a...]
    all_to_all x1 -> x0, blocking collectives: 13.6 us -> none  [body(): lax.all_to_all(send_gates, 'expert', split_axis=0, concat_axis=0, tiled=T...]
    scatter x3 -> x0, local copies, waits for them, and re-layouts: 12.2 us -> none  [the longest x1 5.57 us: body(): send_rows = jnp.zeros((slot_count, feature_count), jnp.bfloat16).at[posit...]
    all_to_all x8 -> x0, local copies, waits for them, and re-layouts: 8.34 us -> none  [the longest x1 2.34 us: body(): lax.all_to_all(row_grad.reshape(block_shape), 'expert', split_axis=0, con...]
    select_n x4 -> x3, other arithmetic: 5.83 us -> 2.08 us  [join(): jnp.where(is_lower, own, other)]
  transfers between devices with their start and end apart: 15 -> 9, of which waited for: 9 -> 4; matrix products, arithmetic and copies ran while one was open for 20% -> 7% of each run, Pallas kernels for 0% -> 0%
where the time goes in v1:
time: 267 us
  waiting for transfers between devices  224 us (84%)
  between operations  13.9 us (5%)
  other arithmetic  10.9 us (4%)
  matrix products  10.4 us (4%)
  local copies, waits for them, and re-layouts  5.91 us (2%)
    reduce_scatter x1, waiting for transfers between devices, body(): lax.psum_scatter(jnp.concatenate([row_grad, gate_cols], 1), CHIPS, scatte...  114 us
    all_gather x1, waiting for transfers between devices, body(): lax.all_gather(jnp.concatenate([cotangent, weight], 1), CHIPS, axis=0, ti...  54 us
    all_gather x1, waiting for transfers between devices, body(): rows = lax.all_gather(tokens, CHIPS, axis=0, tiled=True)  53.6 us
  transfers between devices with their start and end apart: 9, of which 4 were waited for; matrix products, arithmetic and copies ran while one was open for 7% of the time, Pallas kernels for 0%

profile of v1, /device:TPU:0, one launch (start us, length us, event | category | flops | bytes accessed | tf_op | source)
XLA Modules:
  0.0 266.6 jit_solution(3930207546364283554)
XLA Ops:
  7.2 0.7 all-gather.5.cloned.1.call-update
  8.0 0.7 convert_element_type.61
  8.6 0.7 select_reduce_fusion.1
  9.4 1.5 fusion.19
  11.0 0.5 collective-permute-start
  11.6 0.4 collective-permute-start.2
  12.0 1.0 collective-permute-done
  13.1 1.9 broadcast_select_fusion.5
  15.2 53.6 %all-gather.5.cloned.1.call-done = bf16[512,1024]{1,0:T(8,128)(2,1)} async-done(((bf16[32,1024]{1,0:T(8,128)(2,1)}), bf16[512,1024]{1,0:T(8,128)(2,1)}) %all-gather.5.cloned.1.call-update) | async-done | bytes 1048592 | tf_op jit(solution)/shard_map/all_gather | solution.py:41
  68.8 2.8 %convolution_bitcast_fusion = f32[512,384]{0,1:T(8,128)} fusion(bf16[512,1024]{1,0:T(8,128)(2,1)} %all-gather.5.cloned.1.call-done, bf16[512,384]{1,0:T(8,128)(2,1)S(1)} %get-tuple-element.24, bf16[512,384]{1,0:T(8,128)(2,1)S(1)} %get-tuple-element.23), kind=kOutput, calls=%fused_computation.1 | convolution fusion | flops 404226048 | bytes 2621440 | tf_op jit(solution)/shard_map/dot_general | solution.py:51
  71.6 1.5 convolution_bitcast_fusion.1
  73.1 54.0 %all-gather.3.cloned.1.call-done = bf16[512,1152]{1,0:T(8,128)(2,1)} async-done(((bf16[32,1152]{1,0:T(8,128)(2,1)}), bf16[512,1152]{1,0:T(8,128)(2,1)}) %all-gather.3.cloned.1.call-update) | async-done | bytes 1179664 | tf_op jit(solution)/shard_map/all_gather | solution.py:42
  127.1 1.0 select_reduce_fusion
  128.1 2.8 %multiply_convert_fusion.2 = (bf16[512,384]{0,1:T(8,128)(2,1)S(1)}, bf16[512]{0:T(512)(128)(2,1)S(1)}, bf16[512,384]{0,1:T(8,128)(2,1)S(1)}) fusion(f32[512,384]{0,1:T(8,128)} %convolution_bitcast_fusion, f32[512,384]{0,1:T(8,128)} %convolution_bitcast_fusion.1, f32[512]{0:T(512)S(1)} %select_reduce_fusion, bf16[384,512]{1,0:T(8,128)(2,1)} %get-tuple-element.28, ...), kind=kOutput, calls=%fused_computation.24 | convolution fusion | flops 407567872 | bytes 4197376 | tf_op jit(solution)/shard_map/dot_general | solution.py:57
  131.0 0.1 select_convert_fusion
  131.1 0.8 fusion.10
  131.9 0.8 add_convert_fusion
  132.6 1.1 pad_maximum_fusion
  133.8 0.6 fusion.28
  134.5 0.6 fusion.29
  135.1 0.8 fusion.12
  135.9 0.5 collective-permute-start.4
  136.4 0.6 fusion
  137.0 0.8 dynamic-slice_convert_fusion
  138.0 0.9 copy.22
  138.9 1.1 fusion.15
  140.1 0.9 copy.23
  141.0 1.9 fusion.13
  142.9 114.3 %reduce-scatter.2.cloned.1.call-done = bf16[32,1152]{1,0:T(8,128)(2,1)} async-done(((bf16[512,1152]{1,0:T(8,128)(2,1)}), bf16[32,1152]{1,0:T(8,128)(2,1)}) %reduce-scatter.2.cloned.1.call-update) | async-done | bytes 73744 | tf_op jit(solution)/shard_map/reduce_scatter | solution.py:69
  257.2 0.7 slice.19
  258.0 0.6 fusion.21
  258.6 1.5 slice.18
  (34 shorter events, 0.9 us)
Async XLA Ops:
  7.2 7.8 %copy-start.1 = (bf16[1,512,384]{2,1,0:T(8,128)(2,1)S(1)}, bf16[1,512,384]{2,1,0:T(8,128)(2,1)}, u32[]{:S(2)}) copy-start(bf16[1,512,384]{2,1,0:T(8,128)(2,1)} %param.12) | copy-start | bytes 1179652
  7.2 61.6 %all-gather.5.cloned.1.call-start = ((), (), s32[]{:S(2)}) async-start(), calls=%async_computation.2 | async-start | bytes 1114112 | tf_op jit(solution)/shard_map/all_gather | solution.py:41
  7.9 119.2 %all-gather.3.cloned.1.call-start = ((), (), s32[]{:S(2)}) async-start(), calls=%async_computation.1 | async-start | bytes 1253376 | tf_op jit(solution)/shard_map/all_gather | solution.py:42
  10.9 246.2 %reduce-scatter.2.cloned.1.call-start = ((), (), s32[]{:S(2)}) async-start(), calls=%async_computation.3 | async-start | bytes 1253376 | tf_op jit(solution)/shard_map/reduce_scatter | solution.py:69
  11.0 2.1 collective-permute-start
  11.5 3.5 %collective-permute-start.1 = (bf16[512,384]{1,0:T(8,128)(2,1)}, bf16[512,384]{1,0:T(8,128)(2,1)S(1)}, u32[]{:S(2)}, u32[]{:S(2)}) collective-permute-start(bf16[512,384]{1,0:T(8,128)(2,1)} %bitcast.44), channel_id=1, source_target_pairs={{0,1},{1,0},{2,3},{3,2},{4,5},{5,4},{6,7},{7,6},{8,9},{9,8},{10,11... | collective-permute-start | bytes 1179656 | tf_op jit(solution)/shard_map/ppermute | solution.py:10
  11.6 3.5 %collective-permute-start.2 = (bf16[512,384]{1,0:T(8,128)(2,1)}, bf16[512,384]{1,0:T(8,128)(2,1)S(1)}, u32[]{:S(2)}, u32[]{:S(2)}) collective-permute-start(bf16[512,384]{1,0:T(8,128)(2,1)} %bitcast.45), channel_id=1, source_target_pairs={{0,1},{1,0},{2,3},{3,2},{4,5},{5,4},{6,7},{7,6},{8,9},{9,8},{10,11... | collective-permute-start | bytes 1179656 | tf_op jit(solution)/shard_map/ppermute | solution.py:10
  12.0 3.1 %copy-start.2 = (bf16[1,512,384]{2,1,0:T(8,128)(2,1)S(1)}, bf16[1,512,384]{2,1,0:T(8,128)(2,1)}, u32[]{:S(2)}) copy-start(bf16[1,512,384]{2,1,0:T(8,128)(2,1)} %param.11) | copy-start | bytes 1179652
  68.8 2.8 %copy-start = (bf16[512,1024]{1,0:T(8,128)(2,1)S(1)}, bf16[512,1024]{1,0:T(8,128)(2,1)}, u32[]{:S(2)}) copy-start(bf16[512,1024]{1,0:T(8,128)(2,1)} %all-gather.5.cloned.1.call-done) | copy-start | bytes 3145732
  134.4 2.0 copy-start.4
  134.4 2.0 copy-start.5
  134.4 2.0 copy-start.6
  134.5 3.4 %collective-permute-start.3 = (bf16[512,384]{0,1:T(8,128)(2,1)S(1)}, bf16[512,384]{0,1:T(8,128)(2,1)S(1)}, u32[]{:S(2)}, u32[]{:S(2)}) collective-permute-start(bf16[512,384]{0,1:T(8,128)(2,1)S(1)} %fusion.11), channel_id=1, source_target_pairs={{0,1},{1,0},{2,3},{3,2},{4,5},{5,4},{6,7},{7,6},{8,9},{9,8},{10,11... | collective-permute-start | bytes 1179656 | tf_op jit(solution)/shard_map/ppermute | solution.py:10
  135.9 3.0 %collective-permute-start.4 = (bf16[512,384]{0,1:T(8,128)(2,1)}, bf16[512,384]{0,1:T(8,128)(2,1)}, u32[]{:S(2)}, u32[]{:S(2)}) collective-permute-start(bf16[512,384]{0,1:T(8,128)(2,1)} %fusion.12), channel_id=1, source_target_pairs={{0,1},{1,0},{2,3},{3,2},{4,5},{5,4},{6,7},{7,6},{8,9},{9,8},{10,11... | collective-permute-start | bytes 1179656 | tf_op jit(solution)/shard_map/ppermute | solution.py:10
  137.9 3.1 %collective-permute-start.5 = (bf16[384,512]{1,0:T(8,128)(2,1)}, bf16[384,512]{1,0:T(8,128)(2,1)}, u32[]{:S(2)}, u32[]{:S(2)}) collective-permute-start(bf16[384,512]{1,0:T(8,128)(2,1)} %dynamic-slice_convert_fusion), channel_id=1, source_target_pairs={{0,1},{1,0},{2,3},{3,2},{4,5},{5,4},{6,7},{7,6},{8,9},{9,8},{10,11... | collective-permute-start | bytes 1179656 | tf_op jit(solution)/shard_map/ppermute | solution.py:10
  140.1 117.9 %copy-start.3 = (s32[32,8]{0,1:T(8,128)S(1)}, s32[32,8]{0,1:T(8,128)}, u32[]{:S(2)}) copy-start(s32[32,8]{0,1:T(8,128)} %param.9) | copy-start | bytes 3076
Sparse Core Ops, SparseCore 0:
  10.8 57.9 all-gather.4
  72.1 54.9 all-gather.2
  133.9 123.2 reduce-scatter.1

commit v2 on v1

v2 whole, which is shorter than its diff:
```python
import jax
import jax.numpy as jnp
from jax import lax
from jax.sharding import Mesh, PartitionSpec as P

DEVICES = ("expert", "chip", "core")


def swap_core(x):
    return lax.ppermute(x, "core", [(0, 1), (1, 0)])


def doubling_pairs(chip_count):
    bits = []
    bit = chip_count // 2
    while bit:
        bits.append(bit)
        bit //= 2
    orders = (bits[:-2] + bits[-2:][::-1], bits)
    return [
        [
            (2 * chip + core, 2 * (chip ^ orders[core][step]) + core)
            for chip in range(chip_count)
            for core in range(2)
        ]
        for step in range(len(bits))
    ]


def gather(block, steps):
    for pairs in steps:
        block = jnp.concatenate([block, lax.ppermute(block, DEVICES, pairs)], 0)
    return block


def scatter_sum(block, steps):
    for pairs in reversed(steps):
        half = block.shape[0] // 2
        given = lax.ppermute(block[half:], DEVICES, pairs)
        block = (block[:half].astype(jnp.float32) + given.astype(jnp.float32)).astype(block.dtype)
    return block


def body(tokens, cotangent, expert_ids, gate_probs, gate_half, up_half, down_half):
    f32, bf16 = jnp.float32, jnp.bfloat16
    chip_count = lax.axis_size("expert") * lax.axis_size("chip")
    tok_rows, feature_count = tokens.shape
    half_width = feature_count // 2
    is_lower = lax.axis_index("core") == 0
    own_expert = lax.axis_index("expert") * lax.axis_size("chip") + lax.axis_index("chip")
    steps = doubling_pairs(chip_count)

    def own_first(rows):
        return jnp.where(is_lower, rows, jnp.roll(rows, half_width, 1))

    gate_w, up_w, down_w = (
        jnp.concatenate([w[0], swap_core(w[0])], axis)
        for w, axis in ((gate_half, 0), (up_half, 0), (down_half, 1))
    )

    experts = jnp.arange(chip_count, dtype=jnp.int32)
    named = expert_ids[:, :, None] == experts
    weight = jnp.sum(jnp.where(named, gate_probs.astype(f32)[:, :, None], 0.0), axis=1)
    lanes = -(-chip_count // 128) * 128
    weight = jnp.pad(weight, ((0, 0), (0, lanes - chip_count))).astype(bf16)

    rows = gather(own_first(tokens), steps)
    dys_weight = gather(jnp.concatenate([own_first(cotangent), weight], 1), steps)
    dys = dys_weight[:, :feature_count]
    is_own = jnp.arange(lanes, dtype=jnp.int32) == own_expert
    gates = jnp.sum(
        jnp.where(is_own, dys_weight[:, feature_count:].astype(f32), 0.0), 1, keepdims=True
    )

    pre_gate = jnp.dot(rows, gate_w, preferred_element_type=f32)
    pre_up = jnp.dot(rows, up_w, preferred_element_type=f32)
    sig = jax.nn.sigmoid(pre_gate)
    active = pre_gate * sig
    slope = sig * (1.0 + pre_gate * (1.0 - sig))
    hidden = active * pre_up
    last = (((1,), (1,)), ((), ()))
    back = lax.dot_general(dys, down_w, last, preferred_element_type=f32)
    gate_grads = jnp.sum(hidden * back, 1, keepdims=True)
    back = back * gates
    grad_up = (back * active).astype(bf16)
    grad_gate = (back * pre_up * slope).astype(bf16)
    row_grad = (
        lax.dot_general(grad_gate, gate_w, last, preferred_element_type=f32)
        + lax.dot_general(grad_up, up_w, last, preferred_element_type=f32)
    ).astype(bf16)
    hidden = (hidden * gates).astype(bf16)

    gate_cols = jnp.where(is_own, gate_grads, 0.0).astype(bf16)
    summed = scatter_sum(jnp.concatenate([row_grad, gate_cols], 1), steps)
    grad_tokens = own_first(summed[:, :feature_count])
    grad_gates = jnp.sum(
        jnp.where(named, summed[:, None, feature_count : feature_count + chip_count], 0), 2
    ).astype(bf16)

    across = (((0,), (0,)), ((), ()))
    grad_gate_w = lax.dot_general(rows, grad_gate, across, preferred_element_type=f32)
    grad_up_w = lax.dot_general(rows, grad_up, across, preferred_element_type=f32)
    grad_down_w = lax.dot_general(hidden, dys, across, preferred_element_type=f32)

    def settle(whole, axis):
        keep, give = jnp.split(whole, 2, axis)
        return (keep + swap_core(give.astype(bf16)).astype(f32)).astype(bf16)[None]

    return (
        grad_tokens,
        grad_gates,
        settle(grad_gate_w, 0),
        settle(grad_up_w, 0),
        settle(grad_down_w, 1),
    )


def solution(mesh):
    shape = mesh.shape
    devices = mesh.devices.reshape(shape["dom"], shape["expert"], shape["dp"] // 2, 2)
    fine = Mesh(devices, ("dom", "expert", "chip", "core"))
    every = ("dom", "expert", "chip", "core")
    flat, cube = P(every, None), P(every, None, None)
    return jax.shard_map(
        body,
        mesh=fine,
        in_specs=(flat, flat, flat, flat, cube, cube, cube),
        out_specs=(flat, flat, cube, cube, cube),
        check_vma=False,
    )
```

time: 267 us -> 76.7 us (0.29)
  waiting for transfers between devices: 224 us -> 33.8 us
  starting transfers between devices: 1.72 us -> 24.6 us
  between operations: 13.9 us -> 0.97 us
  matrix products: 10.4 us -> 6.84 us
  local copies, waits for them, and re-layouts: 5.91 us -> 2.47 us
  other arithmetic: 10.9 us -> 7.65 us
    reduce_scatter x1 -> x0, waiting for transfers between devices: 114 us -> none  [body(): lax.psum_scatter(jnp.concatenate([row_grad, gate_cols], 1), CHIPS, scatte...]
    all_gather x2 -> x0, waiting for transfers between devices: 108 us -> none  [the longest x1 54 us: body(): lax.all_gather(jnp.concatenate([cotangent, weight], 1), CHIPS, axis=0, ti...]
    ppermute x0 -> x12, waiting for transfers between devices: none -> 33.8 us  [the longest x8 19.4 us: gather(): block = jnp.concatenate([block, lax.ppermute(block, DEVICES, pairs)], 0)]
    ppermute x0 -> x12, starting transfers between devices: none -> 22.8 us  [the longest x8 14 us: gather(): block = jnp.concatenate([block, lax.ppermute(block, DEVICES, pairs)], 0)]
  transfers between devices with their start and end apart: 9 -> 18, of which waited for: 4 -> 10; matrix products, arithmetic and copies ran while one was open for 7% -> 15% of each run, Pallas kernels for 0% -> 0%
where the time goes in v2:
time: 76.7 us; the launch traced here: 76.3 us
  waiting for transfers between devices  33.8 us (44%)
  starting transfers between devices  24.6 us (32%)
  other arithmetic  7.65 us (10%)
  matrix products  6.84 us (9%)
  local copies, waits for them, and re-layouts  2.47 us (3%)
  between operations  0.97 us (1%)
    ppermute x8, waiting for transfers between devices, gather(): block = jnp.concatenate([block, lax.ppermute(block, DEVICES, pairs)], 0)  19.4 us
    ppermute x4, waiting for transfers between devices, scatter_sum(): given = lax.ppermute(block[half:], DEVICES, pairs)  14.4 us
    ppermute x8, starting transfers between devices, gather(): block = jnp.concatenate([block, lax.ppermute(block, DEVICES, pairs)], 0)  14 us
    ppermute x4, starting transfers between devices, scatter_sum(): given = lax.ppermute(block[half:], DEVICES, pairs)  8.86 us
    broadcast_in_dim x3, other arithmetic, settle(): return (keep + swap_core(give.astype(bf16)).astype(f32)).astype(bf16)[None]  2.52 us
    dot_general x1, matrix products, body(): back = lax.dot_general(dys, down_w, last, preferred_element_type=f32)  1.93 us
    ppermute x6, starting transfers between devices, swap_core(): return lax.ppermute(x, 'core', [(0, 1), (1, 0)])  1.73 us
    slice x3, local copies, waits for them, and re-layouts, own_first(): return jnp.where(is_lower, rows, jnp.roll(rows, half_width, 1))  1.57 us
  transfers between devices with their start and end apart: 18, of which 10 were waited for; matrix products, arithmetic and copies ran while one was open for 15% of the time, Pallas kernels for 0%

profile of v2, /device:TPU:0, one launch (start us, length us, event | category | flops | bytes accessed | tf_op | source)
XLA Modules:
  0.0 76.3 jit_solution(1966878949071073665)
XLA Ops:
  1.7 0.8 %fusion.29 = (bf16[32,512]{1,0:T(8,128)(2,1)S(1)}, bf16[32,512]{1,0:T(8,128)(2,1)S(1)}) fusion(bf16[32,1024]{1,0:T(8,128)(2,1)} %param.7), kind=kLoop, calls=%fused_computation.74 | loop fusion | bytes 131072 | tf_op jit(solution)/shard_map/jit(_roll_static)/slice | solution.py:54
  2.4 0.9 %constant_dynamic-update-slice_fusion.9 = (bf16[512,1024]{1,0:T(8,128)(2,1)S(1)}, bf16[32,1024]{1,0:T(8,128)(2,1)S(1)}) fusion(bf16[32,1024]{1,0:T(8,128)(2,1)} %param.7, bf16[32,512]{1,0:T(8,128)(2,1)S(1)} %get-tuple-element.15, bf16[32,512]{1,0:T(8,128)(2,1)S(1)} %get-tuple-element.14, pred[]{:T(512)S(6)} %eq.22), kind=kLoop, calls=%fused_computation.66 | loop fusion | flops 163839 | bytes 262145
  3.3 3.7 %collective-permute-start.5 = (bf16[32,1024]{1,0:T(8,128)(2,1)S(1)}, bf16[32,1024]{1,0:T(8,128)(2,1)S(1)}, u32[]{:S(2)}, u32[]{:S(2)}) collective-permute-start(bf16[32,1024]{1,0:T(8,128)(2,1)S(1)} %get-tuple-element.6), channel_id=1, source_target_pairs={{0,16},{1,17},{2,18},{3,19},{4,20},{5,21},{6,22},{7,23},{8,24},{9,... | collective-permute-start | bytes 196616 | tf_op jit(solution)/shard_map/ppermute | solution.py:32
  8.5 0.8 %fusion.30 = (bf16[32,512]{1,0:T(8,128)(2,1)S(1)}, bf16[32,512]{1,0:T(8,128)(2,1)S(1)}) fusion(bf16[32,1024]{1,0:T(8,128)(2,1)} %param.8), kind=kLoop, calls=%fused_computation.75 | loop fusion | bytes 131072 | tf_op jit(solution)/shard_map/jit(_roll_static)/slice | solution.py:54
  9.3 0.9 %maximum_select_fusion = bf16[32,1024]{1,0:T(8,128)(2,1)S(1)} fusion(bf16[32,1024]{1,0:T(8,128)(2,1)} %param.8, bf16[32,512]{1,0:T(8,128)(2,1)S(1)} %get-tuple-element.17, bf16[32,512]{1,0:T(8,128)(2,1)S(1)} %get-tuple-element.16, pred[]{:T(512)S(6)} %eq.22), kind=kLoop, calls=%fused_computation.51 | loop fusion | flops 163840 | bytes 196609 | tf_op jit(solution)/shard_map/jit(_where)/select_n | solution.py:54
  10.3 1.9 %collective-permute-start.6 = (bf16[64,1024]{1,0:T(8,128)(2,1)S(1)}, bf16[64,1024]{1,0:T(8,128)(2,1)S(1)}, u32[]{:S(2)}, u32[]{:S(2)}) collective-permute-start(bf16[64,1024]{1,0:T(8,128)(2,1)S(1)} %pad_maximum_fusion.12), channel_id=1, source_target_pairs={{0,8},{1,9},{2,10},{3,11},{4,12},{5,13},{6,14},{7,15},{8,0},{9,1},... | collective-permute-start | bytes 393224 | tf_op jit(solution)/shard_map/ppermute | solution.py:32
  12.3 3.4 %collective-permute-done = bf16[32,1152]{1,0:T(8,128)(2,1)S(1)} collective-permute-done((bf16[32,1152]{1,0:T(8,128)(2,1)S(1)}, bf16[32,1152]{1,0:T(8,128)(2,1)S(1)}, u32[]{:S(2)}, u32[]{:S(2)}) %collective-permute-start) | collective-permute-done | bytes 73760 | tf_op jit(solution)/shard_map/ppermute | solution.py:32
  15.6 1.9 %collective-permute-start.1 = (bf16[64,1152]{1,0:T(8,128)(2,1)S(1)}, bf16[64,1152]{1,0:T(8,128)(2,1)S(1)}, u32[]{:S(2)}, u32[]{:S(2)}) collective-permute-start(bf16[64,1152]{1,0:T(8,128)(2,1)S(1)} %pad_maximum_fusion.11), channel_id=1, source_target_pairs={{0,8},{1,9},{2,10},{3,11},{4,12},{5,13},{6,14},{7,15},{8,0},{9,1},... | collective-permute-start | bytes 442376 | tf_op jit(solution)/shard_map/ppermute | solution.py:32
  17.6 1.6 %collective-permute-start.7 = (bf16[128,1024]{1,0:T(8,128)(2,1)S(1)}, bf16[128,1024]{1,0:T(8,128)(2,1)S(1)}, u32[]{:S(2)}, u32[]{:S(2)}) collective-permute-start(bf16[128,1024]{1,0:T(8,128)(2,1)S(1)} %pad_maximum_fusion.10), channel_id=1, source_target_pairs={{0,2},{1,5},{2,0},{3,7},{4,6},{5,1},{6,4},{7,3},{8,10},{9,13},{10,... | collective-permute-start | bytes 786440 | tf_op jit(solution)/shard_map/ppermute | solution.py:32
  19.2 1.7 %collective-permute-done.1 = bf16[64,1152]{1,0:T(8,128)(2,1)S(1)} collective-permute-done((bf16[64,1152]{1,0:T(8,128)(2,1)S(1)}, bf16[64,1152]{1,0:T(8,128)(2,1)S(1)}, u32[]{:S(2)}, u32[]{:S(2)}) %collective-permute-start.1) | collective-permute-done | bytes 147488 | tf_op jit(solution)/shard_map/ppermute | solution.py:32
  20.9 1.6 %collective-permute-start.2 = (bf16[128,1152]{1,0:T(8,128)(2,1)S(1)}, bf16[128,1152]{1,0:T(8,128)(2,1)S(1)}, u32[]{:S(2)}, u32[]{:S(2)}) collective-permute-start(bf16[128,1152]{1,0:T(8,128)(2,1)S(1)} %pad_maximum_fusion.9), channel_id=1, source_target_pairs={{0,2},{1,5},{2,0},{3,7},{4,6},{5,1},{6,4},{7,3},{8,10},{9,13},{10,... | collective-permute-start | bytes 884744 | tf_op jit(solution)/shard_map/ppermute | solution.py:32
  22.4 3.1 %collective-permute-done.7 = bf16[128,1024]{1,0:T(8,128)(2,1)S(1)} collective-permute-done((bf16[128,1024]{1,0:T(8,128)(2,1)S(1)}, bf16[128,1024]{1,0:T(8,128)(2,1)S(1)}, u32[]{:S(2)}, u32[]{:S(2)}) %collective-permute-start.7) | collective-permute-done | bytes 262176 | tf_op jit(solution)/shard_map/ppermute | solution.py:32
  25.6 1.6 %collective-permute-start.8 = (bf16[256,1024]{1,0:T(8,128)(2,1)S(1)}, bf16[256,1024]{1,0:T(8,128)(2,1)S(1)}, u32[]{:S(2)}, u32[]{:S(2)}) collective-permute-start(bf16[256,1024]{1,0:T(8,128)(2,1)S(1)} %pad_maximum_fusion.4), channel_id=1, source_target_pairs={{0,4},{1,3},{2,6},{3,1},{4,0},{5,7},{6,2},{7,5},{8,12},{9,11},{10,... | collective-permute-start | bytes 1572872 | tf_op jit(solution)/shard_map/ppermute | solution.py:32
  27.2 4.7 %collective-permute-done.2 = bf16[128,1152]{1,0:T(8,128)(2,1)S(1)} collective-permute-done((bf16[128,1152]{1,0:T(8,128)(2,1)S(1)}, bf16[128,1152]{1,0:T(8,128)(2,1)S(1)}, u32[]{:S(2)}, u32[]{:S(2)}) %collective-permute-start.2) | collective-permute-done | bytes 294944 | tf_op jit(solution)/shard_map/ppermute | solution.py:32
  31.9 1.6 %collective-permute-start.3 = (bf16[256,1152]{1,0:T(8,128)(2,1)S(1)}, bf16[256,1152]{1,0:T(8,128)(2,1)S(1)}, u32[]{:S(2)}, u32[]{:S(2)}) collective-permute-start(bf16[256,1152]{1,0:T(8,128)(2,1)S(1)} %pad_maximum_fusion.3), channel_id=1, source_target_pairs={{0,4},{1,3},{2,6},{3,1},{4,0},{5,7},{6,2},{7,5},{8,12},{9,11},{10,... | collective-permute-start | bytes 1769480 | tf_op jit(solution)/shard_map/ppermute | solution.py:32
  33.5 1.3 %collective-permute-done.8 = bf16[256,1024]{1,0:T(8,128)(2,1)S(1)} collective-permute-done((bf16[256,1024]{1,0:T(8,128)(2,1)S(1)}, bf16[256,1024]{1,0:T(8,128)(2,1)S(1)}, u32[]{:S(2)}, u32[]{:S(2)}) %collective-permute-start.8) | collective-permute-done | bytes 524320 | tf_op jit(solution)/shard_map/ppermute | solution.py:32
  36.5 5.4 %collective-permute-done.3 = bf16[256,1152]{1,0:T(8,128)(2,1)S(1)} collective-permute-done((bf16[256,1152]{1,0:T(8,128)(2,1)S(1)}, bf16[256,1152]{1,0:T(8,128)(2,1)S(1)}, u32[]{:S(2)}, u32[]{:S(2)}) %collective-permute-start.3) | collective-permute-done | bytes 589856 | tf_op jit(solution)/shard_map/ppermute | solution.py:32
  42.0 1.9 %multiply_convert_fusion.2 = (bf16[512,384]{0,1:T(8,128)(2,1)S(1)}, bf16[512]{0:T(512)(128)(2,1)S(1)}, bf16[512,384]{0,1:T(8,128)(2,1)S(1)}) fusion(f32[512,384]{0,1:T(8,128)S(1)} %fusion.12, f32[512,384]{0,1:T(8,128)S(1)} %fusion.14, f32[512]{0:T(512)S(1)} %select_reduce_fusion, bf16[384,512]{1,0:T(8,128)(2,1)} %collective-permute-done.4, ...), kind=kOutput, calls=%fused_computation.25 | convolution fusion | flops 407567872 | bytes 4197376 | tf_op jit(solution)/shard_map/dot_general | solution.py:82
  44.1 0.8 fusion.13
  44.9 0.8 %add_convert_fusion = bf16[512,1024]{1,0:T(8,128)(2,1)S(1)} fusion(f32[512,1024]{1,0:T(8,128)S(1)} %fusion.13, bf16[512,384]{0,1:T(8,128)(2,1)S(1)} %get-tuple-element.7, bf16[512,384]{1,0:T(8,128)(2,1)S(1)} %collective-permute-done.10, bf16[512,384]{1,0:T(8,128)(2,1)S(1)} %bitcast.22), kind=kOutput, calls=%fused_computation | convolution fusion | flops 405274624 | bytes 4325376 | tf_op jit(solution)/shard_map/dot_general | solution.py:88
  45.7 1.6 %collective-permute-start.11 = (bf16[256,1152]{1,0:T(8,128)(2,1)S(1)}, bf16[256,1152]{1,0:T(8,128)(2,1)S(1)}, u32[]{:S(2)}, u32[]{:S(2)}) collective-permute-start(bf16[256,1152]{1,0:T(8,128)(2,1)S(1)} %pad_maximum_fusion.2), channel_id=1, source_target_pairs={{0,4},{1,3},{2,6},{3,1},{4,0},{5,7},{6,2},{7,5},{8,12},{9,11},{10,... | collective-permute-start | bytes 1769480 | tf_op jit(solution)/shard_map/ppermute | solution.py:39
  48.1 0.8 fusion.31
  48.8 7.3 %collective-permute-done.11 = bf16[256,1152]{1,0:T(8,128)(2,1)S(1)} collective-permute-done((bf16[256,1152]{1,0:T(8,128)(2,1)S(1)}, bf16[256,1152]{1,0:T(8,128)(2,1)S(1)}, u32[]{:S(2)}, u32[]{:S(2)}) %collective-permute-start.11) | collective-permute-done | bytes 589856 | tf_op jit(solution)/shard_map/ppermute | solution.py:39
  56.4 1.5 %collective-permute-start.12 = (bf16[128,1152]{1,0:T(8,128)(2,1)S(1)}, bf16[128,1152]{1,0:T(8,128)(2,1)S(1)}, u32[]{:S(2)}, u32[]{:S(2)}) collective-permute-start(bf16[128,1152]{1,0:T(8,128)(2,1)S(1)} %slice.81), channel_id=1, source_target_pairs={{0,2},{1,5},{2,0},{3,7},{4,6},{5,1},{6,4},{7,3},{8,10},{9,13},{10,... | collective-permute-start | bytes 884744 | tf_op jit(solution)/shard_map/ppermute | solution.py:39
  59.4 0.9 %fusion.17 = bf16[1,384,512]{2,1,0:T(8,128)(2,1)} fusion(bf16[384,512]{1,0:T(8,128)(2,1)S(1)} %collective-permute-done.17, f32[384,1024]{1,0:T(8,128)S(1)} %fusion), kind=kLoop, calls=%fused_computation.38 | loop fusion | flops 589824 | bytes 1572864 | tf_op jit(solution)/shard_map/broadcast_in_dim | solution.py:107
  60.3 2.9 %collective-permute-done.12 = bf16[128,1152]{1,0:T(8,128)(2,1)S(1)} collective-permute-done((bf16[128,1152]{1,0:T(8,128)(2,1)S(1)}, bf16[128,1152]{1,0:T(8,128)(2,1)S(1)}, u32[]{:S(2)}, u32[]{:S(2)}) %collective-permute-start.12) | collective-permute-done | bytes 294944 | tf_op jit(solution)/shard_map/ppermute | solution.py:39
  63.2 1.7 %collective-permute-start.13 = (bf16[64,1152]{1,0:T(8,128)(2,1)S(1)}, bf16[64,1152]{1,0:T(8,128)(2,1)S(1)}, u32[]{:S(2)}, u32[]{:S(2)}) collective-permute-start(bf16[64,1152]{1,0:T(8,128)(2,1)S(1)} %slice.83), channel_id=1, source_target_pairs={{0,8},{1,9},{2,10},{3,11},{4,12},{5,13},{6,14},{7,15},{8,0},{9,1},... | collective-permute-start | bytes 442376 | tf_op jit(solution)/shard_map/ppermute | solution.py:39
  65.0 0.8 %fusion.15 = bf16[1,512,384]{2,1,0:T(8,128)(2,1)} fusion(bf16[512,384]{1,0:T(8,128)(2,1)S(1)} %collective-permute-done.15, f32[1024,384]{1,0:T(8,128)S(1)} %fusion.31), kind=kLoop, calls=%fused_computation.36 | loop fusion | flops 589824 | bytes 1572864 | tf_op jit(solution)/shard_map/broadcast_in_dim | solution.py:107
  65.8 2.7 %collective-permute-done.13 = bf16[64,1152]{1,0:T(8,128)(2,1)S(1)} collective-permute-done((bf16[64,1152]{1,0:T(8,128)(2,1)S(1)}, bf16[64,1152]{1,0:T(8,128)(2,1)S(1)}, u32[]{:S(2)}, u32[]{:S(2)}) %collective-permute-start.13) | collective-permute-done | bytes 147488 | tf_op jit(solution)/shard_map/ppermute | solution.py:39
  68.5 4.0 %collective-permute-start.14 = (bf16[32,1152]{1,0:T(8,128)(2,1)S(1)}, bf16[32,1152]{1,0:T(8,128)(2,1)S(1)}, u32[]{:S(2)}, u32[]{:S(2)}) collective-permute-start(bf16[32,1152]{1,0:T(8,128)(2,1)S(1)} %slice.85), channel_id=1, source_target_pairs={{0,16},{1,17},{2,18},{3,19},{4,20},{5,21},{6,22},{7,23},{8,24},{9,... | collective-permute-start | bytes 221192 | tf_op jit(solution)/shard_map/ppermute | solution.py:39
  72.5 0.8 %fusion.16 = bf16[1,512,384]{2,1,0:T(8,128)(2,1)} fusion(bf16[512,384]{1,0:T(8,128)(2,1)S(1)} %collective-permute-done.16, f32[1024,384]{1,0:T(8,128)S(1)} %fusion.32), kind=kLoop, calls=%fused_computation.37 | loop fusion | flops 589824 | bytes 1572864 | tf_op jit(solution)/shard_map/broadcast_in_dim | solution.py:107
  73.4 1.5 %collective-permute-done.14 = bf16[32,1152]{1,0:T(8,128)(2,1)S(1)} collective-permute-done((bf16[32,1152]{1,0:T(8,128)(2,1)S(1)}, bf16[32,1152]{1,0:T(8,128)(2,1)S(1)}, u32[]{:S(2)}, u32[]{:S(2)}) %collective-permute-start.14) | collective-permute-done | bytes 73760 | tf_op jit(solution)/shard_map/ppermute | solution.py:39
  (65 shorter events, 8.8 us)
Async XLA Ops:
  0.6 34.2 %collective-permute-start.10 = (bf16[512,384]{1,0:T(8,128)(2,1)}, bf16[512,384]{1,0:T(8,128)(2,1)S(1)}, u32[]{:S(2)}, u32[]{:S(2)}) collective-permute-start(bf16[512,384]{1,0:T(8,128)(2,1)} %bitcast.20), channel_id=1, source_target_pairs={{0,1},{1,0},{2,3},{3,2},{4,5},{5,4},{6,7},{7,6},{8,9},{9,8},{10,11... | collective-permute-start | bytes 1179656 | tf_op jit(solution)/shard_map/ppermute | solution.py:10
  1.1 34.4 %collective-permute-start.9 = (bf16[512,384]{1,0:T(8,128)(2,1)}, bf16[512,384]{1,0:T(8,128)(2,1)S(1)}, u32[]{:S(2)}, u32[]{:S(2)}) collective-permute-start(bf16[512,384]{1,0:T(8,128)(2,1)} %bitcast.17), channel_id=1, source_target_pairs={{0,1},{1,0},{2,3},{3,2},{4,5},{5,4},{6,7},{7,6},{8,9},{9,8},{10,11... | collective-permute-start | bytes 1179656 | tf_op jit(solution)/shard_map/ppermute | solution.py:10
  1.2 40.8 %collective-permute-start.4 = (bf16[384,512]{1,0:T(8,128)(2,1)}, bf16[384,512]{1,0:T(8,128)(2,1)}, u32[]{:S(2)}, u32[]{:S(2)}) collective-permute-start(bf16[384,512]{1,0:T(8,128)(2,1)} %bitcast.23), channel_id=1, source_target_pairs={{0,1},{1,0},{2,3},{3,2},{4,5},{5,4},{6,7},{7,6},{8,9},{9,8},{10,11... | collective-permute-start | bytes 1179656 | tf_op jit(solution)/shard_map/ppermute | solution.py:10
  3.3 7.0 %collective-permute-start.5 = (bf16[32,1024]{1,0:T(8,128)(2,1)S(1)}, bf16[32,1024]{1,0:T(8,128)(2,1)S(1)}, u32[]{:S(2)}, u32[]{:S(2)}) collective-permute-start(bf16[32,1024]{1,0:T(8,128)(2,1)S(1)} %get-tuple-element.6), channel_id=1, source_target_pairs={{0,16},{1,17},{2,18},{3,19},{4,20},{5,21},{6,22},{7,23},{8,24},{9,... | collective-permute-start | bytes 196616 | tf_op jit(solution)/shard_map/ppermute | solution.py:32
  10.2 5.4 %collective-permute-start = (bf16[32,1152]{1,0:T(8,128)(2,1)S(1)}, bf16[32,1152]{1,0:T(8,128)(2,1)S(1)}, u32[]{:S(2)}, u32[]{:S(2)}) collective-permute-start(bf16[32,1152]{1,0:T(8,128)(2,1)S(1)} %get-tuple-element.12), channel_id=1, source_target_pairs={{0,16},{1,17},{2,18},{3,19},{4,20},{5,21},{6,22},{7,23},{8,24},{9,... | collective-permute-start | bytes 221192 | tf_op jit(solution)/shard_map/ppermute | solution.py:32
  10.3 7.3 %collective-permute-start.6 = (bf16[64,1024]{1,0:T(8,128)(2,1)S(1)}, bf16[64,1024]{1,0:T(8,128)(2,1)S(1)}, u32[]{:S(2)}, u32[]{:S(2)}) collective-permute-start(bf16[64,1024]{1,0:T(8,128)(2,1)S(1)} %pad_maximum_fusion.12), channel_id=1, source_target_pairs={{0,8},{1,9},{2,10},{3,11},{4,12},{5,13},{6,14},{7,15},{8,0},{9,1},... | collective-permute-start | bytes 393224 | tf_op jit(solution)/shard_map/ppermute | solution.py:32
  15.6 5.2 %collective-permute-start.1 = (bf16[64,1152]{1,0:T(8,128)(2,1)S(1)}, bf16[64,1152]{1,0:T(8,128)(2,1)S(1)}, u32[]{:S(2)}, u32[]{:S(2)}) collective-permute-start(bf16[64,1152]{1,0:T(8,128)(2,1)S(1)} %pad_maximum_fusion.11), channel_id=1, source_target_pairs={{0,8},{1,9},{2,10},{3,11},{4,12},{5,13},{6,14},{7,15},{8,0},{9,1},... | collective-permute-start | bytes 442376 | tf_op jit(solution)/shard_map/ppermute | solution.py:32
  17.6 7.9 %collective-permute-start.7 = (bf16[128,1024]{1,0:T(8,128)(2,1)S(1)}, bf16[128,1024]{1,0:T(8,128)(2,1)S(1)}, u32[]{:S(2)}, u32[]{:S(2)}) collective-permute-start(bf16[128,1024]{1,0:T(8,128)(2,1)S(1)} %pad_maximum_fusion.10), channel_id=1, source_target_pairs={{0,2},{1,5},{2,0},{3,7},{4,6},{5,1},{6,4},{7,3},{8,10},{9,13},{10,... | collective-permute-start | bytes 786440 | tf_op jit(solution)/shard_map/ppermute | solution.py:32
  20.9 11.0 %collective-permute-start.2 = (bf16[128,1152]{1,0:T(8,128)(2,1)S(1)}, bf16[128,1152]{1,0:T(8,128)(2,1)S(1)}, u32[]{:S(2)}, u32[]{:S(2)}) collective-permute-start(bf16[128,1152]{1,0:T(8,128)(2,1)S(1)} %pad_maximum_fusion.9), channel_id=1, source_target_pairs={{0,2},{1,5},{2,0},{3,7},{4,6},{5,1},{6,4},{7,3},{8,10},{9,13},{10,... | collective-permute-start | bytes 884744 | tf_op jit(solution)/shard_map/ppermute | solution.py:32
  25.6 9.2 %collective-permute-start.8 = (bf16[256,1024]{1,0:T(8,128)(2,1)S(1)}, bf16[256,1024]{1,0:T(8,128)(2,1)S(1)}, u32[]{:S(2)}, u32[]{:S(2)}) collective-permute-start(bf16[256,1024]{1,0:T(8,128)(2,1)S(1)} %pad_maximum_fusion.4), channel_id=1, source_target_pairs={{0,4},{1,3},{2,6},{3,1},{4,0},{5,7},{6,2},{7,5},{8,12},{9,11},{10,... | collective-permute-start | bytes 1572872 | tf_op jit(solution)/shard_map/ppermute | solution.py:32
  27.2 7.7 %copy-start.1 = (bf16[1,512,384]{2,1,0:T(8,128)(2,1)S(1)}, bf16[1,512,384]{2,1,0:T(8,128)(2,1)}, u32[]{:S(2)}) copy-start(bf16[1,512,384]{2,1,0:T(8,128)(2,1)} %param.11) | copy-start | bytes 1179652
  31.9 9.9 %collective-permute-start.3 = (bf16[256,1152]{1,0:T(8,128)(2,1)S(1)}, bf16[256,1152]{1,0:T(8,128)(2,1)S(1)}, u32[]{:S(2)}, u32[]{:S(2)}) collective-permute-start(bf16[256,1152]{1,0:T(8,128)(2,1)S(1)} %pad_maximum_fusion.3), channel_id=1, source_target_pairs={{0,4},{1,3},{2,6},{3,1},{4,0},{5,7},{6,2},{7,5},{8,12},{9,11},{10,... | collective-permute-start | bytes 1769480 | tf_op jit(solution)/shard_map/ppermute | solution.py:32
  34.8 1.0 %copy-start = (bf16[1,512,384]{2,1,0:T(8,128)(2,1)S(1)}, bf16[1,512,384]{2,1,0:T(8,128)(2,1)}, u32[]{:S(2)}) copy-start(bf16[1,512,384]{2,1,0:T(8,128)(2,1)} %param.12) | copy-start | bytes 1179652
  36.5 5.6 %copy-start.3 = (bf16[1,384,512]{2,1,0:T(8,128)(2,1)S(1)}, bf16[1,384,512]{2,1,0:T(8,128)(2,1)}, u32[]{:S(2)}) copy-start(bf16[1,384,512]{2,1,0:T(8,128)(2,1)} %param.13) | copy-start | bytes 1179652
  45.7 10.4 %collective-permute-start.11 = (bf16[256,1152]{1,0:T(8,128)(2,1)S(1)}, bf16[256,1152]{1,0:T(8,128)(2,1)S(1)}, u32[]{:S(2)}, u32[]{:S(2)}) collective-permute-start(bf16[256,1152]{1,0:T(8,128)(2,1)S(1)} %pad_maximum_fusion.2), channel_id=1, source_target_pairs={{0,4},{1,3},{2,6},{3,1},{4,0},{5,7},{6,2},{7,5},{8,12},{9,11},{10,... | collective-permute-start | bytes 1769480 | tf_op jit(solution)/shard_map/ppermute | solution.py:39
  48.0 11.4 %collective-permute-start.17 = (bf16[384,512]{1,0:T(8,128)(2,1)S(1)}, bf16[384,512]{1,0:T(8,128)(2,1)S(1)}, u32[]{:S(2)}, u32[]{:S(2)}) collective-permute-start(bf16[384,512]{1,0:T(8,128)(2,1)S(1)} %split.51), channel_id=1, source_target_pairs={{0,1},{1,0},{2,3},{3,2},{4,5},{5,4},{6,7},{7,6},{8,9},{9,8},{10,11... | collective-permute-start | bytes 1179656 | tf_op jit(solution)/shard_map/ppermute | solution.py:10
  56.4 6.8 %collective-permute-start.12 = (bf16[128,1152]{1,0:T(8,128)(2,1)S(1)}, bf16[128,1152]{1,0:T(8,128)(2,1)S(1)}, u32[]{:S(2)}, u32[]{:S(2)}) collective-permute-start(bf16[128,1152]{1,0:T(8,128)(2,1)S(1)} %slice.81), channel_id=1, source_target_pairs={{0,2},{1,5},{2,0},{3,7},{4,6},{5,1},{6,4},{7,3},{8,10},{9,13},{10,... | collective-permute-start | bytes 884744 | tf_op jit(solution)/shard_map/ppermute | solution.py:39
  58.7 6.2 %collective-permute-start.15 = (bf16[512,384]{1,0:T(8,128)(2,1)S(1)}, bf16[512,384]{1,0:T(8,128)(2,1)S(1)}, u32[]{:S(2)}, u32[]{:S(2)}) collective-permute-start(bf16[512,384]{1,0:T(8,128)(2,1)S(1)} %split.53), channel_id=1, source_target_pairs={{0,1},{1,0},{2,3},{3,2},{4,5},{5,4},{6,7},{7,6},{8,9},{9,8},{10,11... | collective-permute-start | bytes 1179656 | tf_op jit(solution)/shard_map/ppermute | solution.py:10
  58.9 13.7 %collective-permute-start.16 = (bf16[512,384]{1,0:T(8,128)(2,1)S(1)}, bf16[512,384]{1,0:T(8,128)(2,1)S(1)}, u32[]{:S(2)}, u32[]{:S(2)}) collective-permute-start(bf16[512,384]{1,0:T(8,128)(2,1)S(1)} %split.52), channel_id=1, source_target_pairs={{0,1},{1,0},{2,3},{3,2},{4,5},{5,4},{6,7},{7,6},{8,9},{9,8},{10,11... | collective-permute-start | bytes 1179656 | tf_op jit(solution)/shard_map/ppermute | solution.py:10
  63.2 5.2 %collective-permute-start.13 = (bf16[64,1152]{1,0:T(8,128)(2,1)S(1)}, bf16[64,1152]{1,0:T(8,128)(2,1)S(1)}, u32[]{:S(2)}, u32[]{:S(2)}) collective-permute-start(bf16[64,1152]{1,0:T(8,128)(2,1)S(1)} %slice.83), channel_id=1, source_target_pairs={{0,8},{1,9},{2,10},{3,11},{4,12},{5,13},{6,14},{7,15},{8,0},{9,1},... | collective-permute-start | bytes 442376 | tf_op jit(solution)/shard_map/ppermute | solution.py:39
  65.8 9.2 %copy-start.2 = (s32[32,8]{0,1:T(8,128)S(1)}, s32[32,8]{0,1:T(8,128)}, u32[]{:S(2)}) copy-start(s32[32,8]{0,1:T(8,128)} %param.9) | copy-start | bytes 3076
  68.5 6.3 %collective-permute-start.14 = (bf16[32,1152]{1,0:T(8,128)(2,1)S(1)}, bf16[32,1152]{1,0:T(8,128)(2,1)S(1)}, u32[]{:S(2)}, u32[]{:S(2)}) collective-permute-start(bf16[32,1152]{1,0:T(8,128)(2,1)S(1)} %slice.85), channel_id=1, source_target_pairs={{0,16},{1,17},{2,18},{3,19},{4,20},{5,21},{6,22},{7,23},{8,24},{9,... | collective-permute-start | bytes 221192 | tf_op jit(solution)/shard_map/ppermute | solution.py:39

commit v3 on v1

v3 whole, which is shorter than its diff:
```python
import jax
import jax.numpy as jnp
from jax import lax
from jax.experimental import pallas as pl
from jax.experimental.pallas import tpu as pltpu
from jax.sharding import Mesh, PartitionSpec as P

DEVICES = ("expert", "chip", "core")
F32, BF16 = jnp.float32, jnp.bfloat16
NN = (((1,), (0,)), ((), ()))
NT = (((1,), (1,)), ((), ()))
TN = (((0,), (0,)), ((), ()))
CHUNK = 256


def dot(a, b, dims):
    return lax.dot_general(a, b, dims, preferred_element_type=F32)


def swap_core(x):
    return lax.ppermute(x, "core", [(0, 1), (1, 0)])


def for_chunks(rows, step):
    if rows <= CHUNK:
        step(pl.ds(0, rows))
    else:

        @pl.loop(0, rows // CHUNK)
        def _(i):
            step(pl.ds(pl.multiple_of(i * CHUNK, CHUNK), CHUNK))


def own_other(place_ref, half):
    member = place_ref[0]
    own = pl.ds(pl.multiple_of(member * half, half), half)
    other = pl.ds(pl.multiple_of((1 - member) * half, half), half)
    return own, other


def forward_kernel(place, rows, gate_own, gate_other, up_own, up_other, active, slope_up, hidden):
    own, other = own_other(place, gate_own.shape[0])

    def step(at):
        mine, rest = rows[at, own], rows[at, other]
        pre_gate = dot(mine, gate_own[...], NN) + dot(rest, gate_other[...], NN)
        pre_up = dot(mine, up_own[...], NN) + dot(rest, up_other[...], NN)
        sig = jax.nn.sigmoid(pre_gate)
        act = pre_gate * sig
        active[at, :] = act
        slope_up[at, :] = pre_up * (sig * (1.0 + pre_gate * (1.0 - sig)))
        hidden[at, :] = act * pre_up

    for_chunks(rows.shape[0], step)


def backward_kernel(
    place, dys, active, slope_up, hidden,
    gate_own, gate_other, up_own, up_other, down_own, down_other,
    row_own, row_other, grads, scaled_hidden,
):
    half, width = gate_own.shape
    lanes = dys.shape[1] - 2 * half
    own, other = own_other(place, half)

    def step(at):
        back = dot(dys[at, own], down_own[...], NT) + dot(dys[at, other], down_other[...], NT)
        lane = lax.broadcasted_iota(jnp.int32, (back.shape[0], lanes), 1)
        is_own = lane == place[1]
        gates = jnp.where(is_own, dys[at, pl.ds(2 * half, lanes)].astype(F32), 0.0)
        gates = jnp.sum(gates, 1, keepdims=True)
        hid = hidden[at, :]
        gate_grads = jnp.sum(hid * back, 1, keepdims=True)
        back = back * gates
        grad_gate = (back * slope_up[at, :]).astype(BF16)
        grad_up = (back * active[at, :]).astype(BF16)
        grads[at, pl.ds(0, width)] = grad_gate
        grads[at, pl.ds(width, width)] = grad_up
        scaled_hidden[at, :] = (hid * gates).astype(BF16)
        row_own[at, :] = (
            dot(grad_gate, gate_own[...], NT) + dot(grad_up, up_own[...], NT)
        ).astype(BF16)
        row_other[at, pl.ds(0, half)] = (
            dot(grad_gate, gate_other[...], NT) + dot(grad_up, up_other[...], NT)
        ).astype(BF16)
        row_other[at, pl.ds(half, lanes)] = jnp.where(is_own, gate_grads, 0.0).astype(BF16)

    for_chunks(dys.shape[0], step)


def weight_kernel(
    place, rows_a, rows_b, dys_a, dys_b, grads_a, grads_b, hidden_a, hidden_b,
    keep_in, keep_down, give_in, give_down,
):
    half = keep_in.shape[0]
    count = rows_a.shape[0]
    own, other = own_other(place, half)

    def products(at, cols):
        into = dot(rows_a[at, cols], grads_a[at, :], TN) + dot(rows_b[at, cols], grads_b[at, :], TN)
        down = dot(hidden_a[at, :], dys_a[at, cols], TN) + dot(hidden_b[at, :], dys_b[at, cols], TN)
        return into, down

    if count <= CHUNK:
        at = pl.ds(0, count)
        into, down = products(at, other)
        give_in[...] = into.astype(BF16)
        give_down[...] = down.astype(BF16)
        into, down = products(at, own)
        keep_in[...] = into
        keep_down[...] = down
    else:
        for cols, give in ((other, True), (own, False)):
            keep_in[...] = jnp.zeros_like(keep_in)
            keep_down[...] = jnp.zeros_like(keep_down)

            @pl.loop(0, count // CHUNK)
            def _(i):
                into, down = products(pl.ds(pl.multiple_of(i * CHUNK, CHUNK), CHUNK), cols)
                keep_in[...] += into
                keep_down[...] += down

            if give:
                give_in[...] = keep_in[...].astype(BF16)
                give_down[...] = keep_down[...].astype(BF16)


def call(kernel, outs, flops, place, *args):
    small = max(x.shape[0] for x in args) <= 2 * CHUNK
    if small:
        args = [pltpu.with_memory_space_constraint(x, pltpu.VMEM) for x in args]
        out_shape = [pltpu.VMEM(s, d) for s, d in outs]
    else:
        out_shape = [jax.ShapeDtypeStruct(s, d) for s, d in outs]
    moved = sum(x.size * x.dtype.itemsize for x in args)
    return pl.pallas_call(
        kernel,
        out_shape=out_shape,
        in_specs=[pl.BlockSpec(memory_space=pltpu.SMEM)]
        + [pl.BlockSpec(memory_space=pltpu.VMEM)] * len(args),
        out_specs=[pl.BlockSpec(memory_space=pltpu.VMEM)] * len(outs),
        compiler_params=pltpu.CompilerParams(vmem_limit_bytes=56 * 2**20),
        cost_estimate=pl.CostEstimate(flops=flops, bytes_accessed=moved, transcendentals=0),
    )(place, *args)


def chip_bits(chip_count):
    bits = []
    bit = chip_count // 2
    while bit:
        bits.append(bit)
        bit //= 2
    return (bits[:-2] + bits[-2:][::-1], bits)


def body(tokens, cotangent, expert_ids, gate_probs, gate_half, up_half, down_half):
    chip_count = lax.axis_size("expert") * lax.axis_size("chip")
    tok_rows, feature_count = tokens.shape
    half = feature_count // 2
    width = gate_half.shape[2]
    member = lax.axis_index("core")
    own_expert = lax.axis_index("expert") * lax.axis_size("chip") + lax.axis_index("chip")
    place = jnp.stack([member, own_expert]).astype(jnp.int32)
    is_lower = member == 0
    orders = chip_bits(chip_count)
    far = len(orders[0]) - 2
    pairs = [
        [
            (2 * chip + core, 2 * (chip ^ orders[core][step]) + core)
            for chip in range(chip_count)
            for core in range(2)
        ]
        for step in range(far + 2)
    ]

    def exchange(x, step):
        return lax.ppermute(x, DEVICES, pairs[step])

    rows = tokens
    for step in range(far + 1):
        rows = jnp.concatenate([rows, exchange(rows, step)], 0)
    rows_a, rows_b = rows, exchange(rows, far + 1)

    experts = jnp.arange(chip_count, dtype=jnp.int32)
    named = expert_ids[:, :, None] == experts
    weight = jnp.sum(jnp.where(named, gate_probs.astype(F32)[:, :, None], 0.0), axis=1)
    lanes = -(-chip_count // 128) * 128
    weight = jnp.pad(weight, ((0, 0), (0, lanes - chip_count))).astype(BF16)
    dys = jnp.concatenate([cotangent, weight], 1)
    dys = jnp.stack([dys, exchange(dys, far)], 0)
    for step in range(far):
        dys = jnp.concatenate([dys, exchange(dys, step)], 1)
    dys_a = dys.reshape(-1, feature_count + lanes)
    dys_b = exchange(dys_a, far + 1)

    gate_own, up_own, down_own = gate_half[0], up_half[0], down_half[0]
    gate_other, up_other, down_other = swap_core(gate_own), swap_core(up_own), swap_core(down_own)

    count = rows_a.shape[0]
    unit = 2 * count * feature_count * width

    def forward(rows):
        return call(
            forward_kernel, [((count, width), F32)] * 3, 2 * unit,
            place, rows, gate_own, gate_other, up_own, up_other,
        )

    def backward(dys, forward_outs):
        return call(
            backward_kernel,
            [
                ((count, half), BF16),
                ((count, half + lanes), BF16),
                ((count, 2 * width), BF16),
                ((count, width), BF16),
            ],
            3 * unit,
            place, dys, *forward_outs,
            gate_own, gate_other, up_own, up_other, down_own, down_other,
        )

    mid_a, mid_b = forward(rows_a), forward(rows_b)
    own_a, other_a, grads_a, hidden_a = backward(dys_a, mid_a)
    own_b, other_b, grads_b, hidden_b = backward(dys_b, mid_b)

    def add(x, y):
        return (x.astype(F32) + y.astype(F32)).astype(BF16)

    own, other = add(own_a, exchange(own_b, far + 1)), add(other_a, exchange(other_b, far + 1))
    for step in reversed(range(far + 1)):
        middle = own.shape[0] // 2
        own = add(own[:middle], exchange(own[middle:], step))
        other = add(other[:middle], exchange(other[middle:], step))

    lower = jnp.where(is_lower, own, other[:, :half])
    upper = jnp.where(is_lower, other[:, :half], own)
    grad_tokens = jnp.concatenate([lower, upper], 1)
    gate_cols = other[:, None, half : half + chip_count]
    grad_gates = jnp.sum(jnp.where(named, gate_cols, 0), 2).astype(BF16)

    keep_in, keep_down, give_in, give_down = call(
        weight_kernel,
        [
            ((half, 2 * width), F32),
            ((width, half), F32),
            ((half, 2 * width), BF16),
            ((width, half), BF16),
        ],
        6 * unit,
        place, rows_a, rows_b, dys_a, dys_b, grads_a, grads_b, hidden_a, hidden_b,
    )
    got_in, got_down = swap_core(give_in), swap_core(give_down)
    grad_in = (keep_in + got_in.astype(F32)).astype(BF16)
    grad_down = (keep_down + got_down.astype(F32)).astype(BF16)
    return (
        grad_tokens,
        grad_gates,
        grad_in[None, :, :width],
        grad_in[None, :, width:],
        grad_down[None],
    )


def solution(mesh):
    shape = mesh.shape
    devices = mesh.devices.reshape(shape["dom"], shape["expert"], shape["dp"] // 2, 2)
    fine = Mesh(devices, ("dom", "expert", "chip", "core"))
    every = ("dom", "expert", "chip", "core")
    flat, cube = P(every, None), P(every, None, None)
    return jax.shard_map(
        body,
        mesh=fine,
        in_specs=(flat, flat, flat, flat, cube, cube, cube),
        out_specs=(flat, flat, cube, cube, cube),
        check_vma=False,
    )
```

time: 267 us -> 86.6 us (0.32)
  waiting for transfers between devices: 224 us -> 32.7 us
  starting transfers between devices: 1.72 us -> 25.7 us
  between operations: 13.9 us -> 0.92 us
  Pallas kernels: 0 us -> 11 us
  matrix products: 10.4 us -> 0 us
    reduce_scatter x1 -> x0, waiting for transfers between devices: 114 us -> none  [body(): lax.psum_scatter(jnp.concatenate([row_grad, gate_cols], 1), CHIPS, scatte...]
    all_gather x2 -> x0, waiting for transfers between devices: 108 us -> none  [the longest x1 54 us: body(): lax.all_gather(jnp.concatenate([cotangent, weight], 1), CHIPS, axis=0, ti...]
    ppermute x0 -> x16, waiting for transfers between devices: none -> 31.6 us  [exchange(): return lax.ppermute(x, DEVICES, pairs[step])]
    ppermute x0 -> x16, starting transfers between devices: none -> 24.6 us  [exchange(): return lax.ppermute(x, DEVICES, pairs[step])]
    pallas_call x0 -> x5, Pallas kernels: none -> 11 us  [call(): pl.pallas_call(kernel, out_shape=out_shape, in_specs=[pl.BlockSpec(memory...]
    dot_general x8 -> x0, matrix products: 10.4 us -> none  [the longest x1 2.83 us: body(): lax.dot_general(dys, down_w, (((1,), (1,)), ((), ())), preferred_element_...]
    unnamed x17 -> x44, local copies, waits for them, and re-layouts: 1.96 us -> 5.98 us
  transfers between devices with their start and end apart: 9 -> 21, of which waited for: 4 -> 12; matrix products, arithmetic and copies ran while one was open for 7% -> 7% of each run, Pallas kernels for 0% -> 9%
where the time goes in v3:
time: 86.6 us; the launch traced here: 86 us
  waiting for transfers between devices  32.7 us (38%)
  starting transfers between devices  25.7 us (30%)
  Pallas kernels  11 us (13%)
  other arithmetic  8.58 us (10%)
  local copies, waits for them, and re-layouts  7.08 us (8%)
  between operations  0.92 us (1%)
    ppermute x16, waiting for transfers between devices, exchange(): return lax.ppermute(x, DEVICES, pairs[step])  31.6 us
    ppermute x16, starting transfers between devices, exchange(): return lax.ppermute(x, DEVICES, pairs[step])  24.6 us
    pallas_call x5, Pallas kernels, call(): pl.pallas_call(kernel, out_shape=out_shape, in_specs=[pl.BlockSpec(memory...  11 us
    unnamed x44, local copies, waits for them, and re-layouts  5.98 us
  transfers between devices with their start and end apart: 21, of which 12 were waited for; matrix products, arithmetic and copies ran while one was open for 7% of the time, Pallas kernels for 9%

profile of v3, /device:TPU:0, one launch (start us, length us, event | category | flops | bytes accessed | tf_op | source)
XLA Modules:
  0.0 86.0 jit_solution(8064932921651539376)
XLA Ops:
  3.0 3.0 %collective-permute-start = (bf16[32,1152]{1,0:T(8,128)(2,1)S(1)}, bf16[32,1152]{1,0:T(8,128)(2,1)S(1)}, u32[]{:S(2)}, u32[]{:S(2)}) collective-permute-start(bf16[32,1152]{1,0:T(8,128)(2,1)S(1)} %get-tuple-element.46), channel_id=1, source_target_pairs={{0,2},{1,5},{2,0},{3,7},{4,6},{5,1},{6,4},{7,3},{8,10},{9,13},{10,... | collective-permute-start | bytes 221192 | tf_op jit(solution)/shard_map/ppermute | solution.py:177
  6.0 2.6 %collective-permute-start.3 = (bf16[32,1024]{1,0:T(8,128)(2,1)}, bf16[32,1024]{1,0:T(8,128)(2,1)S(1)}, u32[]{:S(2)}, u32[]{:S(2)}) collective-permute-start(bf16[32,1024]{1,0:T(8,128)(2,1)} %param.7), channel_id=1, source_target_pairs={{0,16},{1,17},{2,18},{3,19},{4,20},{5,21},{6,22},{7,23},{8,24},{9,... | collective-permute-start | bytes 196616 | tf_op jit(solution)/shard_map/ppermute | solution.py:177
  8.6 2.9 %collective-permute-start.1 = (bf16[2,32,1152]{2,1,0:T(8,128)(2,1)S(1)}, bf16[2,32,1152]{2,1,0:T(8,128)(2,1)S(1)}, u32[]{:S(2)}, u32[]{:S(2)}) collective-permute-start(bf16[2,32,1152]{2,1,0:T(8,128)(2,1)S(1)} %pad_maximum_fusion.3), channel_id=1, source_target_pairs={{0,16},{1,17},{2,18},{3,19},{4,20},{5,21},{6,22},{7,23},{8,24},{9,... | collective-permute-start | bytes 442376 | tf_op jit(solution)/shard_map/ppermute | solution.py:177
  12.4 1.9 %collective-permute-done.3 = bf16[32,1024]{1,0:T(8,128)(2,1)S(1)} collective-permute-done((bf16[32,1024]{1,0:T(8,128)(2,1)}, bf16[32,1024]{1,0:T(8,128)(2,1)S(1)}, u32[]{:S(2)}, u32[]{:S(2)}) %collective-permute-start.3) | collective-permute-done | bytes 65568 | tf_op jit(solution)/shard_map/ppermute | solution.py:177
  15.1 2.1 %collective-permute-start.4 = (bf16[64,1024]{1,0:T(8,128)(2,1)S(1)}, bf16[64,1024]{1,0:T(8,128)(2,1)S(1)}, u32[]{:S(2)}, u32[]{:S(2)}) collective-permute-start(bf16[64,1024]{1,0:T(8,128)(2,1)S(1)} %pad_maximum_fusion.4), channel_id=1, source_target_pairs={{0,8},{1,9},{2,10},{3,11},{4,12},{5,13},{6,14},{7,15},{8,0},{9,1},... | collective-permute-start | bytes 393224 | tf_op jit(solution)/shard_map/ppermute | solution.py:177
  17.2 1.5 %collective-permute-done.1 = bf16[2,32,1152]{2,1,0:T(8,128)(2,1)S(1)} collective-permute-done((bf16[2,32,1152]{2,1,0:T(8,128)(2,1)S(1)}, bf16[2,32,1152]{2,1,0:T(8,128)(2,1)S(1)}, u32[]{:S(2)}, u32[]{:S(2)}) %collective-permute-start.1) | collective-permute-done | bytes 147488 | tf_op jit(solution)/shard_map/ppermute | solution.py:177
  19.2 1.1 %collective-permute-done.4 = bf16[64,1024]{1,0:T(8,128)(2,1)S(1)} collective-permute-done((bf16[64,1024]{1,0:T(8,128)(2,1)S(1)}, bf16[64,1024]{1,0:T(8,128)(2,1)S(1)}, u32[]{:S(2)}, u32[]{:S(2)}) %collective-permute-start.4) | collective-permute-done | bytes 131104 | tf_op jit(solution)/shard_map/ppermute | solution.py:177
  20.3 2.5 %collective-permute-start.5 = (bf16[128,1024]{1,0:T(8,128)(2,1)S(1)}, bf16[128,1024]{1,0:T(8,128)(2,1)S(1)}, u32[]{:S(2)}, u32[]{:S(2)}) collective-permute-start(bf16[128,1024]{1,0:T(8,128)(2,1)S(1)} %pad_maximum_fusion.2), channel_id=1, source_target_pairs={{0,2},{1,5},{2,0},{3,7},{4,6},{5,1},{6,4},{7,3},{8,10},{9,13},{10,... | collective-permute-start | bytes 786440 | tf_op jit(solution)/shard_map/ppermute | solution.py:177
  22.9 4.7 %collective-permute-done.2 = bf16[2,64,1152]{2,1,0:T(8,128)(2,1)S(1)} collective-permute-done((bf16[2,64,1152]{2,1,0:T(8,128)(2,1)S(1)}, bf16[2,64,1152]{2,1,0:T(8,128)(2,1)S(1)}, u32[]{:S(2)}, u32[]{:S(2)}) %collective-permute-start.2) | collective-permute-done | bytes 294944 | tf_op jit(solution)/shard_map/ppermute | solution.py:177
  27.7 1.0 %collective-permute-start.9 = (bf16[256,1152]{1,0:T(8,128)(2,1)S(1)}, bf16[256,1152]{1,0:T(8,128)(2,1)}, u32[]{:S(2)}, u32[]{:S(2)}) collective-permute-start(bf16[256,1152]{1,0:T(8,128)(2,1)S(1)} %bitcast.25), channel_id=1, source_target_pairs={{0,4},{1,3},{2,6},{3,1},{4,0},{5,7},{6,2},{7,5},{8,12},{9,11},{10,... | collective-permute-start | bytes 1769480 | tf_op jit(solution)/shard_map/ppermute | solution.py:177
  28.7 1.1 %collective-permute-start.10 = (bf16[256,1024]{1,0:T(8,128)(2,1)S(1)}, bf16[256,1024]{1,0:T(8,128)(2,1)}, u32[]{:S(2)}, u32[]{:S(2)}) collective-permute-start(bf16[256,1024]{1,0:T(8,128)(2,1)S(1)} %constant_dynamic-update-slice_fusion.rows.rows_a), channel_id=1, source_target_pairs={{0,4},{1,3},{2,6},{3,1},{4,0},{5,7},{6,2},{7,5},{8,12},{9,11},{10,... | collective-permute-start | bytes 1572872 | tf_op jit(solution)/shard_map/ppermute | solution.py:177
  32.1 11.2 %collective-permute-done.10.rows.rows_b = bf16[256,1024]{1,0:T(8,128)(2,1)} collective-permute-done((bf16[256,1024]{1,0:T(8,128)(2,1)S(1)}, bf16[256,1024]{1,0:T(8,128)(2,1)}, u32[]{:S(2)}, u32[]{:S(2)}) %collective-permute-start.10) | collective-permute-done | bytes 524320 | tf_op jit(solution)/shard_map/ppermute | solution.py:177
  43.3 1.8 %shard_map.112 = (f32[256,384]{1,0:T(8,128)S(1)}, f32[256,384]{1,0:T(8,128)S(1)}, f32[256,384]{1,0:T(8,128)S(1)}) custom-call(s32[2]{0:T(128)} %pad_add_fusion.place, bf16[256,1024]{1,0:T(8,128)(2,1)} %collective-permute-done.10.rows.rows_b, bf16[512,384]{1,0:T(8,128)(2,1)S(1)} %bitcast.16, bf16[512,384]{1,0:T(8,128)(2,1)S(1)} %collective-permute-done.6.gate_other, ...), custom_call_target="tpu_custom_call" | custom-call | flops 402653184 | bytes 2097152 | tf_op jit(solution)/shard_map/pallas_call | solution.py:136
  45.1 2.9 %shard_map.113 = (bf16[256,512]{1,0:T(8,128)(2,1)}, bf16[256,640]{1,0:T(8,128)(2,1)}, bf16[256,768]{1,0:T(8,128)(2,1)S(1)}, bf16[256,384]{1,0:T(8,128)(2,1)S(1)}) custom-call(s32[2]{0:T(128)} %pad_add_fusion.place, bf16[256,1152]{1,0:T(8,128)(2,1)} %collective-permute-done.9.dys.dys_b, f32[256,384]{1,0:T(8,128)S(1)} %get-tuple-element.27.active, ...), custom_call_target="tpu_custom_call" | custom-call | flops 603979776 | bytes 4128768 | tf_op jit(solution)/shard_map/pallas_call | solution.py:136
  48.8 1.0 %collective-permute-start.11 = (bf16[256,512]{1,0:T(8,128)(2,1)}, bf16[256,512]{1,0:T(8,128)(2,1)}, u32[]{:S(2)}, u32[]{:S(2)}) collective-permute-start(bf16[256,512]{1,0:T(8,128)(2,1)} %get-tuple-element.30), channel_id=1, source_target_pairs={{0,4},{1,3},{2,6},{3,1},{4,0},{5,7},{6,2},{7,5},{8,12},{9,11},{10,... | collective-permute-start | bytes 786440 | tf_op jit(solution)/shard_map/ppermute | solution.py:177
  49.8 1.0 %copy-done.6 = bf16[256,1024]{1,0:T(8,128)(2,1)S(1)} copy-done((bf16[256,1024]{1,0:T(8,128)(2,1)S(1)}, bf16[256,1024]{1,0:T(8,128)(2,1)}, u32[]{:S(2)}) %copy-start.6) | copy-done | bytes 524312
  50.8 1.4 %shard_map.110 = (f32[256,384]{1,0:T(8,128)S(1)}, f32[256,384]{1,0:T(8,128)S(1)}, f32[256,384]{1,0:T(8,128)S(1)}) custom-call(s32[2]{0:T(128)} %pad_add_fusion.place, bf16[256,1024]{1,0:T(8,128)(2,1)S(1)} %copy-done.6, bf16[512,384]{1,0:T(8,128)(2,1)S(1)} %bitcast.18, bf16[512,384]{1,0:T(8,128)(2,1)S(1)} %collective-permute-done.6.gate_other, ...), custom_call_target="tpu_custom_call" | custom-call | flops 402653184 | bytes 2097152 | tf_op jit(solution)/shard_map/pallas_call | solution.py:136
  52.2 1.9 %shard_map.111 = (bf16[256,512]{1,0:T(8,128)(2,1)S(1)}, bf16[256,640]{1,0:T(8,128)(2,1)S(1)}, bf16[256,768]{1,0:T(8,128)(2,1)S(1)}, bf16[256,384]{1,0:T(8,128)(2,1)S(1)}) custom-call(s32[2]{0:T(128)} %pad_add_fusion.place, bf16[256,1152]{1,0:T(8,128)(2,1)S(1)} %bitcast.26, f32[256,384]{1,0:T(8,128)S(1)} %get-tuple-element.23.active, ...), custom_call_target="tpu_custom_call" | custom-call | flops 603979776 | bytes 4128768 | tf_op jit(solution)/shard_map/pallas_call | solution.py:136
  56.3 1.1 %collective-permute-start.15 = (bf16[256,640]{1,0:T(8,128)(2,1)}, bf16[256,640]{1,0:T(8,128)(2,1)S(1)}, u32[]{:S(2)}, u32[]{:S(2)}) collective-permute-start(bf16[256,640]{1,0:T(8,128)(2,1)} %get-tuple-element.32), channel_id=1, source_target_pairs={{0,4},{1,3},{2,6},{3,1},{4,0},{5,7},{6,2},{7,5},{8,12},{9,11},{10,... | collective-permute-start | bytes 983048 | tf_op jit(solution)/shard_map/ppermute | solution.py:177
  57.4 1.0 %copy-done.15 = bf16[256,768]{1,0:T(8,128)(2,1)S(1)} copy-done((bf16[256,768]{1,0:T(8,128)(2,1)S(1)}, bf16[256,768]{1,0:T(8,128)(2,1)}, u32[]{:S(2)}) %copy-start.15) | copy-done | bytes 393240
  58.4 3.1 %shard_map.114 = (f32[512,768]{1,0:T(8,128)S(1)}, f32[384,512]{1,0:T(8,128)S(1)}, bf16[512,768]{1,0:T(8,128)(2,1)}, bf16[384,512]{1,0:T(8,128)(2,1)S(1)}) custom-call(s32[2]{0:T(128)} %pad_add_fusion.place, bf16[256,1024]{1,0:T(8,128)(2,1)S(1)} %copy-done.7, bf16[256,1024]{1,0:T(8,128)(2,1)} %collective-permute-done.10.rows.rows_b, ...), custom_call_target="tpu_custom_call" | custom-call | flops 1207959552 | bytes 3407872 | tf_op jit(solution)/shard_map/pallas_call | solution.py:136
  62.0 1.1 %add_convert_fusion.3 = bf16[256,512]{1,0:T(8,128)(2,1)S(1)} fusion(bf16[256,512]{1,0:T(8,128)(2,1)} %collective-permute-done.11, bf16[256,512]{1,0:T(8,128)(2,1)S(1)} %copy-done.11), kind=kLoop, calls=%fused_computation.4 | loop fusion | flops 524288 | bytes 786432 | tf_op jit(solution)/shard_map/convert_element_type | solution.py:227
  63.2 1.5 %collective-permute-start.12 = (bf16[128,512]{1,0:T(8,128)(2,1)S(1)}, bf16[128,512]{1,0:T(8,128)(2,1)S(1)}, u32[]{:S(2)}, u32[]{:S(2)}) collective-permute-start(bf16[128,512]{1,0:T(8,128)(2,1)S(1)} %slice.66), channel_id=1, source_target_pairs={{0,2},{1,5},{2,0},{3,7},{4,6},{5,1},{6,4},{7,3},{8,10},{9,13},{10,... | collective-permute-start | bytes 393224 | tf_op jit(solution)/shard_map/ppermute | solution.py:177
  65.5 2.8 %collective-permute-done.12 = bf16[128,512]{1,0:T(8,128)(2,1)S(1)} collective-permute-done((bf16[128,512]{1,0:T(8,128)(2,1)S(1)}, bf16[128,512]{1,0:T(8,128)(2,1)S(1)}, u32[]{:S(2)}, u32[]{:S(2)}) %collective-permute-start.12) | collective-permute-done | bytes 131104 | tf_op jit(solution)/shard_map/ppermute | solution.py:177
  68.3 1.0 %collective-permute-start.13 = (bf16[64,512]{1,0:T(8,128)(2,1)S(1)}, bf16[64,512]{1,0:T(8,128)(2,1)S(1)}, u32[]{:S(2)}, u32[]{:S(2)}) collective-permute-start(bf16[64,512]{1,0:T(8,128)(2,1)S(1)} %slice.68), channel_id=1, source_target_pairs={{0,8},{1,9},{2,10},{3,11},{4,12},{5,13},{6,14},{7,15},{8,0},{9,1},... | collective-permute-start | bytes 196616 | tf_op jit(solution)/shard_map/ppermute | solution.py:177
  69.2 1.0 %collective-permute-done.16 = bf16[128,640]{1,0:T(8,128)(2,1)S(1)} collective-permute-done((bf16[128,640]{1,0:T(8,128)(2,1)S(1)}, bf16[128,640]{1,0:T(8,128)(2,1)S(1)}, u32[]{:S(2)}, u32[]{:S(2)}) %collective-permute-start.16) | collective-permute-done | bytes 163872 | tf_op jit(solution)/shard_map/ppermute | solution.py:177
  71.9 2.9 %collective-permute-done.17 = bf16[64,640]{1,0:T(8,128)(2,1)S(1)} collective-permute-done((bf16[64,640]{1,0:T(8,128)(2,1)S(1)}, bf16[64,640]{1,0:T(8,128)(2,1)S(1)}, u32[]{:S(2)}, u32[]{:S(2)}) %collective-permute-start.17) | collective-permute-done | bytes 81952 | tf_op jit(solution)/shard_map/ppermute | solution.py:177
  74.8 2.8 %collective-permute-start.18 = (bf16[32,640]{1,0:T(8,128)(2,1)S(1)}, bf16[32,640]{1,0:T(8,128)(2,1)S(1)}, u32[]{:S(2)}, u32[]{:S(2)}) collective-permute-start(bf16[32,640]{1,0:T(8,128)(2,1)S(1)} %slice.76), channel_id=1, source_target_pairs={{0,16},{1,17},{2,18},{3,19},{4,20},{5,21},{6,22},{7,23},{8,24},{9,... | collective-permute-start | bytes 122888 | tf_op jit(solution)/shard_map/ppermute | solution.py:177
  77.9 2.2 %collective-permute-done.18 = bf16[32,640]{1,0:T(8,128)(2,1)S(1)} collective-permute-done((bf16[32,640]{1,0:T(8,128)(2,1)S(1)}, bf16[32,640]{1,0:T(8,128)(2,1)S(1)}, u32[]{:S(2)}, u32[]{:S(2)}) %collective-permute-start.18) | collective-permute-done | bytes 40992 | tf_op jit(solution)/shard_map/ppermute | solution.py:177
  80.2 2.3 %collective-permute-done.14 = bf16[32,512]{1,0:T(8,128)(2,1)S(1)} collective-permute-done((bf16[32,512]{1,0:T(8,128)(2,1)S(1)}, bf16[32,512]{1,0:T(8,128)(2,1)S(1)}, u32[]{:S(2)}, u32[]{:S(2)}) %collective-permute-start.14) | collective-permute-done | bytes 32800 | tf_op jit(solution)/shard_map/ppermute | solution.py:177
  83.8 1.3 %add_convert_fusion = bf16[512,768]{1,0:T(8,128)(2,1)S(1)} fusion(f32[512,768]{1,0:T(8,128)S(1)} %copy-done.4, bf16[512,768]{1,0:T(8,128)(2,1)} %collective-permute-done.19), kind=kLoop, calls=%fused_computation | loop fusion | flops 1179648 | bytes 3145728 | tf_op jit(solution)/shard_map/convert_element_type | solution.py:253
  85.1 1.0 %slice_bitcast_fusion = (bf16[1,512,384]{2,1,0:T(8,128)(2,1)}, bf16[1,512,384]{2,1,0:T(8,128)(2,1)}) fusion(bf16[512,768]{1,0:T(8,128)(2,1)S(1)} %add_convert_fusion), kind=kLoop, calls=%fused_computation.6 | loop fusion | bytes 1572864 | tf_op jit(solution)/shard_map/broadcast_in_dim | solution.py:259
  (90 shorter events, 14.5 us)
Async XLA Ops:
  0.6 19.7 %copy-start.18 = (bf16[32,1024]{1,0:T(8,128)(2,1)S(1)}, bf16[32,1024]{1,0:T(8,128)(2,1)}, u32[]{:S(2)}) copy-start(bf16[32,1024]{1,0:T(8,128)(2,1)} %param.7) | copy-start | bytes 196612
  3.0 5.6 %collective-permute-start = (bf16[32,1152]{1,0:T(8,128)(2,1)S(1)}, bf16[32,1152]{1,0:T(8,128)(2,1)S(1)}, u32[]{:S(2)}, u32[]{:S(2)}) collective-permute-start(bf16[32,1152]{1,0:T(8,128)(2,1)S(1)} %get-tuple-element.46), channel_id=1, source_target_pairs={{0,2},{1,5},{2,0},{3,7},{4,6},{5,1},{6,4},{7,3},{8,10},{9,13},{10,... | collective-permute-start | bytes 221192 | tf_op jit(solution)/shard_map/ppermute | solution.py:177
  6.0 8.2 %collective-permute-start.3 = (bf16[32,1024]{1,0:T(8,128)(2,1)}, bf16[32,1024]{1,0:T(8,128)(2,1)S(1)}, u32[]{:S(2)}, u32[]{:S(2)}) collective-permute-start(bf16[32,1024]{1,0:T(8,128)(2,1)} %param.7), channel_id=1, source_target_pairs={{0,16},{1,17},{2,18},{3,19},{4,20},{5,21},{6,22},{7,23},{8,24},{9,... | collective-permute-start | bytes 196616 | tf_op jit(solution)/shard_map/ppermute | solution.py:177
  8.6 10.1 %collective-permute-start.1 = (bf16[2,32,1152]{2,1,0:T(8,128)(2,1)S(1)}, bf16[2,32,1152]{2,1,0:T(8,128)(2,1)S(1)}, u32[]{:S(2)}, u32[]{:S(2)}) collective-permute-start(bf16[2,32,1152]{2,1,0:T(8,128)(2,1)S(1)} %pad_maximum_fusion.3), channel_id=1, source_target_pairs={{0,16},{1,17},{2,18},{3,19},{4,20},{5,21},{6,22},{7,23},{8,24},{9,... | collective-permute-start | bytes 442376 | tf_op jit(solution)/shard_map/ppermute | solution.py:177
  15.1 5.2 %collective-permute-start.4 = (bf16[64,1024]{1,0:T(8,128)(2,1)S(1)}, bf16[64,1024]{1,0:T(8,128)(2,1)S(1)}, u32[]{:S(2)}, u32[]{:S(2)}) collective-permute-start(bf16[64,1024]{1,0:T(8,128)(2,1)S(1)} %pad_maximum_fusion.4), channel_id=1, source_target_pairs={{0,8},{1,9},{2,10},{3,11},{4,12},{5,13},{6,14},{7,15},{8,0},{9,1},... | collective-permute-start | bytes 393224 | tf_op jit(solution)/shard_map/ppermute | solution.py:177
  18.8 8.8 %collective-permute-start.2 = (bf16[2,64,1152]{2,1,0:T(8,128)(2,1)S(1)}, bf16[2,64,1152]{2,1,0:T(8,128)(2,1)S(1)}, u32[]{:S(2)}, u32[]{:S(2)}) collective-permute-start(bf16[2,64,1152]{2,1,0:T(8,128)(2,1)S(1)} %pad_maximum_fusion.1), channel_id=1, source_target_pairs={{0,8},{1,9},{2,10},{3,11},{4,12},{5,13},{6,14},{7,15},{8,0},{9,1},... | collective-permute-start | bytes 884744 | tf_op jit(solution)/shard_map/ppermute | solution.py:177
  19.2 10.6 %copy-start = (bf16[1,512,384]{2,1,0:T(8,128)(2,1)S(1)}, bf16[1,512,384]{2,1,0:T(8,128)(2,1)}, u32[]{:S(2)}) copy-start(bf16[1,512,384]{2,1,0:T(8,128)(2,1)} %param.11) | copy-start | bytes 1179652
  19.2 10.7 %copy-start.1 = (bf16[1,512,384]{2,1,0:T(8,128)(2,1)S(1)}, bf16[1,512,384]{2,1,0:T(8,128)(2,1)}, u32[]{:S(2)}) copy-start(bf16[1,512,384]{2,1,0:T(8,128)(2,1)} %param.12) | copy-start | bytes 1179652
  19.2 11.2 %copy-start.2 = (bf16[1,384,512]{2,1,0:T(8,128)(2,1)S(1)}, bf16[1,384,512]{2,1,0:T(8,128)(2,1)}, u32[]{:S(2)}) copy-start(bf16[1,384,512]{2,1,0:T(8,128)(2,1)} %param.13) | copy-start | bytes 1179652
  20.3 8.4 %collective-permute-start.5 = (bf16[128,1024]{1,0:T(8,128)(2,1)S(1)}, bf16[128,1024]{1,0:T(8,128)(2,1)S(1)}, u32[]{:S(2)}, u32[]{:S(2)}) collective-permute-start(bf16[128,1024]{1,0:T(8,128)(2,1)S(1)} %pad_maximum_fusion.2), channel_id=1, source_target_pairs={{0,2},{1,5},{2,0},{3,7},{4,6},{5,1},{6,4},{7,3},{8,10},{9,13},{10,... | collective-permute-start | bytes 786440 | tf_op jit(solution)/shard_map/ppermute | solution.py:177
  27.7 17.4 %collective-permute-start.9 = (bf16[256,1152]{1,0:T(8,128)(2,1)S(1)}, bf16[256,1152]{1,0:T(8,128)(2,1)}, u32[]{:S(2)}, u32[]{:S(2)}) collective-permute-start(bf16[256,1152]{1,0:T(8,128)(2,1)S(1)} %bitcast.25), channel_id=1, source_target_pairs={{0,4},{1,3},{2,6},{3,1},{4,0},{5,7},{6,2},{7,5},{8,12},{9,11},{10,... | collective-permute-start | bytes 1769480 | tf_op jit(solution)/shard_map/ppermute | solution.py:177
  28.7 16.4 %copy-start.5 = (bf16[256,1024]{1,0:T(8,128)(2,1)}, bf16[256,1024]{1,0:T(8,128)(2,1)S(1)}, u32[]{:S(2)}) copy-start(bf16[256,1024]{1,0:T(8,128)(2,1)S(1)} %constant_dynamic-update-slice_fusion.rows.rows_a) | copy-start | bytes 1572868
  28.7 14.6 %collective-permute-start.10 = (bf16[256,1024]{1,0:T(8,128)(2,1)S(1)}, bf16[256,1024]{1,0:T(8,128)(2,1)}, u32[]{:S(2)}, u32[]{:S(2)}) collective-permute-start(bf16[256,1024]{1,0:T(8,128)(2,1)S(1)} %constant_dynamic-update-slice_fusion.rows.rows_a), channel_id=1, source_target_pairs={{0,4},{1,3},{2,6},{3,1},{4,0},{5,7},{6,2},{7,5},{8,12},{9,11},{10,... | collective-permute-start | bytes 1572872 | tf_op jit(solution)/shard_map/ppermute | solution.py:177
  29.9 1.7 %collective-permute-start.6 = (bf16[512,384]{1,0:T(8,128)(2,1)S(1)}, bf16[512,384]{1,0:T(8,128)(2,1)S(1)}, u32[]{:S(2)}, u32[]{:S(2)}) collective-permute-start(bf16[512,384]{1,0:T(8,128)(2,1)S(1)} %bitcast.15), channel_id=1, source_target_pairs={{0,1},{1,0},{2,3},{3,2},{4,5},{5,4},{6,7},{7,6},{8,9},{9,8},{10,11... | collective-permute-start | bytes 1179656 | tf_op jit(solution)/shard_map/ppermute | solution.py:21
  29.9 2.3 %collective-permute-start.7 = (bf16[512,384]{1,0:T(8,128)(2,1)S(1)}, bf16[512,384]{1,0:T(8,128)(2,1)S(1)}, u32[]{:S(2)}, u32[]{:S(2)}) collective-permute-start(bf16[512,384]{1,0:T(8,128)(2,1)S(1)} %bitcast.20), channel_id=1, source_target_pairs={{0,1},{1,0},{2,3},{3,2},{4,5},{5,4},{6,7},{7,6},{8,9},{9,8},{10,11... | collective-permute-start | bytes 1179656 | tf_op jit(solution)/shard_map/ppermute | solution.py:21
  30.4 14.7 %collective-permute-start.8 = (bf16[384,512]{1,0:T(8,128)(2,1)S(1)}, bf16[384,512]{1,0:T(8,128)(2,1)S(1)}, u32[]{:S(2)}, u32[]{:S(2)}) collective-permute-start(bf16[384,512]{1,0:T(8,128)(2,1)S(1)} %bitcast.28), channel_id=1, source_target_pairs={{0,1},{1,0},{2,3},{3,2},{4,5},{5,4},{6,7},{7,6},{8,9},{9,8},{10,11... | collective-permute-start | bytes 1179656 | tf_op jit(solution)/shard_map/ppermute | solution.py:21
  48.8 13.2 %collective-permute-start.11 = (bf16[256,512]{1,0:T(8,128)(2,1)}, bf16[256,512]{1,0:T(8,128)(2,1)}, u32[]{:S(2)}, u32[]{:S(2)}) collective-permute-start(bf16[256,512]{1,0:T(8,128)(2,1)} %get-tuple-element.30), channel_id=1, source_target_pairs={{0,4},{1,3},{2,6},{3,1},{4,0},{5,7},{6,2},{7,5},{8,12},{9,11},{10,... | collective-permute-start | bytes 786440 | tf_op jit(solution)/shard_map/ppermute | solution.py:177
  52.2 5.2 %copy-start.7 = (bf16[256,1024]{1,0:T(8,128)(2,1)S(1)}, bf16[256,1024]{1,0:T(8,128)(2,1)}, u32[]{:S(2)}) copy-start(bf16[256,1024]{1,0:T(8,128)(2,1)} %copy-done.5) | copy-start | bytes 1572868
  52.2 5.2 %copy-start.13 = (bf16[256,768]{1,0:T(8,128)(2,1)S(1)}, bf16[256,768]{1,0:T(8,128)(2,1)}, u32[]{:S(2)}) copy-start(bf16[256,768]{1,0:T(8,128)(2,1)} %copy-done.12) | copy-start | bytes 1179652
  52.2 5.2 %copy-start.17 = (bf16[256,384]{1,0:T(8,128)(2,1)S(1)}, bf16[256,384]{1,0:T(8,128)(2,1)}, u32[]{:S(2)}) copy-start(bf16[256,384]{1,0:T(8,128)(2,1)} %copy-done.16) | copy-start | bytes 589828
  56.3 8.4 %collective-permute-start.15 = (bf16[256,640]{1,0:T(8,128)(2,1)}, bf16[256,640]{1,0:T(8,128)(2,1)S(1)}, u32[]{:S(2)}, u32[]{:S(2)}) collective-permute-start(bf16[256,640]{1,0:T(8,128)(2,1)} %get-tuple-element.32), channel_id=1, source_target_pairs={{0,4},{1,3},{2,6},{3,1},{4,0},{5,7},{6,2},{7,5},{8,12},{9,11},{10,... | collective-permute-start | bytes 983048 | tf_op jit(solution)/shard_map/ppermute | solution.py:177
  58.4 3.6 %copy-start.11 = (bf16[256,512]{1,0:T(8,128)(2,1)S(1)}, bf16[256,512]{1,0:T(8,128)(2,1)}, u32[]{:S(2)}) copy-start(bf16[256,512]{1,0:T(8,128)(2,1)} %copy-done.10) | copy-start | bytes 786436
  61.5 9.5 %collective-permute-start.20 = (bf16[384,512]{1,0:T(8,128)(2,1)S(1)}, bf16[384,512]{1,0:T(8,128)(2,1)S(1)}, u32[]{:S(2)}, u32[]{:S(2)}) collective-permute-start(bf16[384,512]{1,0:T(8,128)(2,1)S(1)} %get-tuple-element.40), channel_id=1, source_target_pairs={{0,1},{1,0},{2,3},{3,2},{4,5},{5,4},{6,7},{7,6},{8,9},{9,8},{10,11... | collective-permute-start | bytes 1179656 | tf_op jit(solution)/shard_map/ppermute | solution.py:21
  61.5 22.3 %collective-permute-start.19 = (bf16[512,768]{1,0:T(8,128)(2,1)}, bf16[512,768]{1,0:T(8,128)(2,1)}, u32[]{:S(2)}, u32[]{:S(2)}) collective-permute-start(bf16[512,768]{1,0:T(8,128)(2,1)} %get-tuple-element.38), channel_id=1, source_target_pairs={{0,1},{1,0},{2,3},{3,2},{4,5},{5,4},{6,7},{7,6},{8,9},{9,8},{10,11... | collective-permute-start | bytes 2359304 | tf_op jit(solution)/shard_map/ppermute | solution.py:21
  63.2 5.0 %collective-permute-start.12 = (bf16[128,512]{1,0:T(8,128)(2,1)S(1)}, bf16[128,512]{1,0:T(8,128)(2,1)S(1)}, u32[]{:S(2)}, u32[]{:S(2)}) collective-permute-start(bf16[128,512]{1,0:T(8,128)(2,1)S(1)} %slice.66), channel_id=1, source_target_pairs={{0,2},{1,5},{2,0},{3,7},{4,6},{5,1},{6,4},{7,3},{8,10},{9,13},{10,... | collective-permute-start | bytes 393224 | tf_op jit(solution)/shard_map/ppermute | solution.py:177
  64.8 5.4 %collective-permute-start.16 = (bf16[128,640]{1,0:T(8,128)(2,1)S(1)}, bf16[128,640]{1,0:T(8,128)(2,1)S(1)}, u32[]{:S(2)}, u32[]{:S(2)}) collective-permute-start(bf16[128,640]{1,0:T(8,128)(2,1)S(1)} %slice.72), channel_id=1, source_target_pairs={{0,2},{1,5},{2,0},{3,7},{4,6},{5,1},{6,4},{7,3},{8,10},{9,13},{10,... | collective-permute-start | bytes 491528 | tf_op jit(solution)/shard_map/ppermute | solution.py:177
  68.3 9.3 %collective-permute-start.13 = (bf16[64,512]{1,0:T(8,128)(2,1)S(1)}, bf16[64,512]{1,0:T(8,128)(2,1)S(1)}, u32[]{:S(2)}, u32[]{:S(2)}) collective-permute-start(bf16[64,512]{1,0:T(8,128)(2,1)S(1)} %slice.68), channel_id=1, source_target_pairs={{0,8},{1,9},{2,10},{3,11},{4,12},{5,13},{6,14},{7,15},{8,0},{9,1},... | collective-permute-start | bytes 196616 | tf_op jit(solution)/shard_map/ppermute | solution.py:177
  70.3 4.5 %collective-permute-start.17 = (bf16[64,640]{1,0:T(8,128)(2,1)S(1)}, bf16[64,640]{1,0:T(8,128)(2,1)S(1)}, u32[]{:S(2)}, u32[]{:S(2)}) collective-permute-start(bf16[64,640]{1,0:T(8,128)(2,1)S(1)} %slice.74), channel_id=1, source_target_pairs={{0,8},{1,9},{2,10},{3,11},{4,12},{5,13},{6,14},{7,15},{8,0},{9,1},... | collective-permute-start | bytes 245768 | tf_op jit(solution)/shard_map/ppermute | solution.py:177
  71.0 12.2 %copy-start.19 = (s32[32,8]{0,1:T(8,128)S(1)}, s32[32,8]{0,1:T(8,128)}, u32[]{:S(2)}) copy-start(s32[32,8]{0,1:T(8,128)} %param.9) | copy-start | bytes 3076
  71.0 12.8 %copy-start.4 = (f32[512,768]{1,0:T(8,128)S(1)}, f32[512,768]{1,0:T(8,128)}, u32[]{:S(2)}) copy-start(f32[512,768]{1,0:T(8,128)} %copy-done.3) | copy-start | bytes 4718596
  74.8 5.3 %collective-permute-start.18 = (bf16[32,640]{1,0:T(8,128)(2,1)S(1)}, bf16[32,640]{1,0:T(8,128)(2,1)S(1)}, u32[]{:S(2)}, u32[]{:S(2)}) collective-permute-start(bf16[32,640]{1,0:T(8,128)(2,1)S(1)} %slice.76), channel_id=1, source_target_pairs={{0,16},{1,17},{2,18},{3,19},{4,20},{5,21},{6,22},{7,23},{8,24},{9,... | collective-permute-start | bytes 122888 | tf_op jit(solution)/shard_map/ppermute | solution.py:177
  77.6 4.9 %collective-permute-start.14 = (bf16[32,512]{1,0:T(8,128)(2,1)S(1)}, bf16[32,512]{1,0:T(8,128)(2,1)S(1)}, u32[]{:S(2)}, u32[]{:S(2)}) collective-permute-start(bf16[32,512]{1,0:T(8,128)(2,1)S(1)} %slice.70), channel_id=1, source_target_pairs={{0,16},{1,17},{2,18},{3,19},{4,20},{5,21},{6,22},{7,23},{8,24},{9,... | collective-permute-start | bytes 98312 | tf_op jit(solution)/shard_map/ppermute | solution.py:177
  (9 other events, 14.9 us)

commit v4 on v3

--- a/solution.py
+++ b/solution.py
@@ -36,6 +36,57 @@
     own = pl.ds(pl.multiple_of(member * half, half), half)
     other = pl.ds(pl.multiple_of((1 - member) * half, half), half)
     return own, other
+
+
+def prepare_kernel(tokens, cotangent, ids, probs, rows, dys):
+    features = tokens.shape[1]
+    rows[0] = tokens[...]
+    dys[0, :, pl.ds(0, features)] = cotangent[...]
+    lanes = dys.shape[2] - features
+    lane = lax.broadcasted_iota(jnp.int32, (tokens.shape[0], lanes), 1)
+    names, given = ids[...], probs[...].astype(F32)
+    weight = jnp.zeros(lane.shape, F32)
+    for k in range(ids.shape[1]):
+        weight = jnp.where(names[:, k : k + 1] == lane, given[:, k : k + 1], weight)
+    dys[0, :, pl.ds(features, lanes)] = weight.astype(BF16)
+
+
+def stack_kernel(first, second, out):
+    out[0] = first[0]
+    out[1] = second[0]
+
+
+def join_kernel(first, second, out):
+    rows = first.shape[1]
+    out[:, pl.ds(0, rows), :] = first[...]
+    out[:, pl.ds(rows, rows), :] = second[...]
+
+
+def split_kernel(kept, got, keep, give):
+    rows = keep.shape[0]
+    upper, lower = pl.ds(0, rows), pl.ds(rows, rows)
+    give[...] = (kept[lower, :].astype(F32) + got[lower, :].astype(F32)).astype(BF16)
+    keep[...] = kept[upper, :].astype(F32) + got[upper, :].astype(F32)
+
+
+def finish_kernel(place, own_kept, own_got, other_kept, other_got, ids, grad_tokens, grad_gates):
+    half = own_kept.shape[1]
+    own, other = own_other(place, half)
+    left = pl.ds(0, half)
+    grad_tokens[:, own] = (own_kept[...].astype(F32) + own_got[...].astype(F32)).astype(BF16)
+    grad_tokens[:, other] = (
+        other_kept[:, left].astype(F32) + other_got[:, left].astype(F32)
+    ).astype(BF16)
+    right = pl.ds(half, other_kept.shape[1] - half)
+    gates = other_kept[:, right].astype(F32) + other_got[:, right].astype(F32)
+    lane = lax.broadcasted_iota(jnp.int32, gates.shape, 1)
+    names = ids[...]
+    column = lax.broadcasted_iota(jnp.int32, names.shape, 1)
+    out = jnp.zeros(names.shape, F32)
+    for k in range(names.shape[1]):
+        picked = jnp.sum(jnp.where(names[:, k : k + 1] == lane, gates, 0.0), 1, keepdims=True)
+        out = jnp.where(column == k, picked, out)
+    grad_gates[...] = out.astype(BF16)
 
 
 def forward_kernel(place, rows, gate_own, gate_other, up_own, up_other, active, slope_up, hidden):
@@ -90,9 +141,10 @@
 
 def weight_kernel(
     place, rows_a, rows_b, dys_a, dys_b, grads_a, grads_b, hidden_a, hidden_b,
-    keep_in, keep_down, give_in, give_down,
+    keep_in, keep_down, give_gate, give_up, give_down,
 ):
-    half = keep_in.shape[0]
+    half, width = give_gate.shape
+    left, right = pl.ds(0, width), pl.ds(width, width)
     count = rows_a.shape[0]
     own, other = own_other(place, half)
 
@@ -104,7 +156,8 @@
     if count <= CHUNK:
         at = pl.ds(0, count)
         into, down = products(at, other)
-        give_in[...] = into.astype(BF16)
+        give_gate[...] = into[:, :width].astype(BF16)
+        give_up[...] = into[:, width:].astype(BF16)
         give_down[...] = down.astype(BF16)
         into, down = products(at, own)
         keep_in[...] = into
@@ -121,27 +174,52 @@
                 keep_down[...] += down
 
             if give:
-                give_in[...] = keep_in[...].astype(BF16)
+                give_gate[...] = keep_in[:, left].astype(BF16)
+                give_up[...] = keep_in[:, right].astype(BF16)
                 give_down[...] = keep_down[...].astype(BF16)
 
 
-def call(kernel, outs, flops, place, *args):
-    small = max(x.shape[0] for x in args) <= 2 * CHUNK
+def settle_kernel(keep_in, keep_down, got_gate, got_up, got_down, gate, up, down, done):
+    width = gate.shape[1]
+    left, right = pl.ds(0, width), pl.ds(width, width)
+    gate[...] = (keep_in[:, left] + got_gate[...].astype(F32)).astype(BF16)
+    up[...] = (keep_in[:, right] + got_up[...].astype(F32)).astype(BF16)
+    down[...] = (keep_down[...] + got_down[...].astype(F32)).astype(BF16)
+    done[...] = jnp.zeros_like(done)
+
+
+def call(kernel, outs, flops, place, *args, after=(), small=True, arrives=0, leaves=0):
+    used = len(args)
+    limit = 10 * 2**20 if small else 56 * 2**20
     if small:
-        args = [pltpu.with_memory_space_constraint(x, pltpu.VMEM) for x in args]
-        out_shape = [pltpu.VMEM(s, d) for s, d in outs]
-    else:
-        out_shape = [jax.ShapeDtypeStruct(s, d) for s, d in outs]
+        args = [
+            pltpu.with_memory_space_constraint(x, pltpu.VMEM) if i < used - arrives else x
+            for i, x in enumerate(args)
+        ]
+    out_shape = [
+        pltpu.VMEM(s, d) if small and i >= leaves else jax.ShapeDtypeStruct(s, d)
+        for i, (s, d) in enumerate(outs)
+    ]
+
+    scalars = () if place is None else (place,)
+    read = len(scalars) + used
+
+    def run(*refs):
+        kernel(*refs[:read], *refs[read + len(after) :])
+
     moved = sum(x.size * x.dtype.itemsize for x in args)
+    vmem = pl.BlockSpec(memory_space=pltpu.VMEM)
     return pl.pallas_call(
-        kernel,
+        run,
         out_shape=out_shape,
-        in_specs=[pl.BlockSpec(memory_space=pltpu.SMEM)]
-        + [pl.BlockSpec(memory_space=pltpu.VMEM)] * len(args),
-        out_specs=[pl.BlockSpec(memory_space=pltpu.VMEM)] * len(outs),
-        compiler_params=pltpu.CompilerParams(vmem_limit_bytes=56 * 2**20),
+        in_specs=[pl.BlockSpec(memory_space=pltpu.SMEM)] * len(scalars)
+        + [vmem] * used
+        + [pl.BlockSpec(memory_space=pl.ANY)] * len(after),
+        out_specs=[vmem] * len(outs),
+        compiler_params=pltpu.CompilerParams(vmem_limit_bytes=limit),
         cost_estimate=pl.CostEstimate(flops=flops, bytes_accessed=moved, transcendentals=0),
-    )(place, *args)
+        name=kernel.__name__,
+    )(*scalars, *args, *after)
 
 
 def chip_bits(chip_count):
@@ -155,13 +233,15 @@
 
 def body(tokens, cotangent, expert_ids, gate_probs, gate_half, up_half, down_half):
     chip_count = lax.axis_size("expert") * lax.axis_size("chip")
-    tok_rows, feature_count = tokens.shape
-    half = feature_count // 2
+    tok_rows, features = tokens.shape
+    half = features // 2
     width = gate_half.shape[2]
+    lanes = -(-chip_count // 128) * 128
+    count = tok_rows * chip_count // 2
+    small = count <= CHUNK
     member = lax.axis_index("core")
     own_expert = lax.axis_index("expert") * lax.axis_size("chip") + lax.axis_index("chip")
     place = jnp.stack([member, own_expert]).astype(jnp.int32)
-    is_lower = member == 0
     orders = chip_bits(chip_count)
     far = len(orders[0]) - 2
     pairs = [
@@ -176,36 +256,43 @@
     def exchange(x, step):
         return lax.ppermute(x, DEVICES, pairs[step])
 
-    rows = tokens
+    def stack(first, second):
+        shape = (2,) + first.shape[1:]
+        return call(stack_kernel, [(shape, BF16)], 0, None, first, second)[0]
+
+    def join(first, second):
+        outer, rows, cols = first.shape
+        shape = (outer, 2 * rows, cols)
+        fits = small or outer * rows < count
+        return call(join_kernel, [(shape, BF16)], 0, None, first, second, small=fits)[0]
+
+    rows, dys = call(
+        prepare_kernel,
+        [((1, tok_rows, features), BF16), ((1, tok_rows, features + lanes), BF16)], 0,
+        None, tokens, cotangent, expert_ids, gate_probs, arrives=4,
+    )
+
+    near = exchange(dys, far)
     for step in range(far + 1):
-        rows = jnp.concatenate([rows, exchange(rows, step)], 0)
-    rows_a, rows_b = rows, exchange(rows, far + 1)
-
-    experts = jnp.arange(chip_count, dtype=jnp.int32)
-    named = expert_ids[:, :, None] == experts
-    weight = jnp.sum(jnp.where(named, gate_probs.astype(F32)[:, :, None], 0.0), axis=1)
-    lanes = -(-chip_count // 128) * 128
-    weight = jnp.pad(weight, ((0, 0), (0, lanes - chip_count))).astype(BF16)
-    dys = jnp.concatenate([cotangent, weight], 1)
-    dys = jnp.stack([dys, exchange(dys, far)], 0)
-    for step in range(far):
-        dys = jnp.concatenate([dys, exchange(dys, step)], 1)
-    dys_a = dys.reshape(-1, feature_count + lanes)
+        rows = join(rows, exchange(rows, step))
+        dys = join(dys, near) if step else stack(dys, near)
+        if step < far:
+            near = exchange(dys, step)
+    rows_a, rows_b = rows[0], exchange(rows[0], far + 1)
+    dys_a = dys.reshape(count, features + lanes)
     dys_b = exchange(dys_a, far + 1)
 
     gate_own, up_own, down_own = gate_half[0], up_half[0], down_half[0]
     gate_other, up_other, down_other = swap_core(gate_own), swap_core(up_own), swap_core(down_own)
-
-    count = rows_a.shape[0]
-    unit = 2 * count * feature_count * width
-
-    def forward(rows):
+    unit = 2 * count * features * width
+
+    def forward(rows, after=()):
         return call(
-            forward_kernel, [((count, width), F32)] * 3, 2 * unit,
-            place, rows, gate_own, gate_other, up_own, up_other,
+            forward_kernel, [((count, width), F32)] * 3, 20 * unit,
+            place, rows, gate_own, gate_other, up_own, up_other, after=after, small=small,
         )
 
-    def backward(dys, forward_outs):
+    def backward(dys, forward_outs, after=()):
         return call(
             backward_kernel,
             [
@@ -216,49 +303,62 @@
             ],
             3 * unit,
             place, dys, *forward_outs,
-            gate_own, gate_other, up_own, up_other, down_own, down_other,
+            gate_own, gate_other, up_own, up_other, down_own, down_other, after=after, small=small,
         )
 
-    mid_a, mid_b = forward(rows_a), forward(rows_b)
+    mid_a = forward(rows_a)
     own_a, other_a, grads_a, hidden_a = backward(dys_a, mid_a)
+    mid_b = forward(rows_b, after=(own_a,))
     own_b, other_b, grads_b, hidden_b = backward(dys_b, mid_b)
 
-    def add(x, y):
-        return (x.astype(F32) + y.astype(F32)).astype(BF16)
-
-    own, other = add(own_a, exchange(own_b, far + 1)), add(other_a, exchange(other_b, far + 1))
-    for step in reversed(range(far + 1)):
-        middle = own.shape[0] // 2
-        own = add(own[:middle], exchange(own[middle:], step))
-        other = add(other[:middle], exchange(other[middle:], step))
-
-    lower = jnp.where(is_lower, own, other[:, :half])
-    upper = jnp.where(is_lower, other[:, :half], own)
-    grad_tokens = jnp.concatenate([lower, upper], 1)
-    gate_cols = other[:, None, half : half + chip_count]
-    grad_gates = jnp.sum(jnp.where(named, gate_cols, 0), 2).astype(BF16)
-
-    keep_in, keep_down, give_in, give_down = call(
+    got_own, got_other = exchange(own_b, far + 1), exchange(other_b, far + 1)
+    keep_in, keep_down, *gives = call(
         weight_kernel,
         [
             ((half, 2 * width), F32),
             ((width, half), F32),
-            ((half, 2 * width), BF16),
+            ((half, width), BF16),
+            ((half, width), BF16),
             ((width, half), BF16),
         ],
         6 * unit,
-        place, rows_a, rows_b, dys_a, dys_b, grads_a, grads_b, hidden_a, hidden_b,
+        place, rows_a, rows_b, dys_a, dys_b, grads_a, grads_b, hidden_a, hidden_b, small=small,
     )
-    got_in, got_down = swap_core(give_in), swap_core(give_down)
-    grad_in = (keep_in + got_in.astype(F32)).astype(BF16)
-    grad_down = (keep_down + got_down.astype(F32)).astype(BF16)
-    return (
-        grad_tokens,
-        grad_gates,
-        grad_in[None, :, :width],
-        grad_in[None, :, width:],
-        grad_down[None],
+    gots = [swap_core(give) for give in gives]
+
+    def split(kept, got, after=()):
+        rows, cols = kept.shape
+        shape = (rows // 2, cols)
+        return call(
+            split_kernel, [(shape, F32), (shape, BF16)], 0,
+            None, kept, got, after=after, small=small,
+        )
+
+    own, other = own_a, other_a
+    for step in reversed(range(far + 1)):
+        after = ()
+        if step == 0:
+            grad_gate, grad_up, grad_down, *after = call(
+                settle_kernel,
+                [
+                    ((half, width), BF16),
+                    ((half, width), BF16),
+                    ((width, half), BF16),
+                    ((8, 128), F32),
+                ],
+                0,
+                None, keep_in, keep_down, *gots, small=small, leaves=3,
+            )
+        other, give_other = split(other, got_other, after)
+        got_other = exchange(give_other, step)
+        own, give_own = split(own, got_own)
+        got_own = exchange(give_own, step)
+    grad_tokens, grad_gates = call(
+        finish_kernel,
+        [((tok_rows, features), BF16), (expert_ids.shape, BF16)], 0,
+        place, own, got_own, other, got_other, expert_ids, arrives=1, leaves=2,
     )
+    return grad_tokens, grad_gates, grad_gate[None], grad_up[None], grad_down[None]
 
 
 def solution(mesh):

time: 86.6 us -> 71.6 us (0.83)
  other arithmetic: 8.58 us -> 0.07 us
  waiting for transfers between devices: 32.7 us -> 28.2 us
  local copies, waits for them, and re-layouts: 7.08 us -> 3.92 us
  starting transfers between devices: 25.7 us -> 27.2 us
    ppermute x16, waiting for transfers between devices: 31.6 us -> 28.1 us  [exchange(): return lax.ppermute(x, DEVICES, pairs[step])]
    convert_element_type x9 -> x0, other arithmetic: 3.36 us -> none  [the longest x7 1.35 us: add(): return (x.astype(F32) + y.astype(F32)).astype(BF16)]
    unnamed x44 -> x13, local copies, waits for them, and re-layouts: 5.98 us -> 3.92 us
    concatenate x5 -> x0, other arithmetic: 1.57 us -> none  [the longest x2 0.87 us: body(): rows = jnp.concatenate([rows, exchange(rows, step)], 0)]
    reduce_sum x2 -> x0, other arithmetic: 1.31 us -> none  [the longest x1 0.7 us: body(): jnp.sum(jnp.where(named, gate_probs.astype(F32)[:, :, None], 0.0), axis=1)]
    ppermute x16, starting transfers between devices: 24.6 us -> 25.9 us  [exchange(): return lax.ppermute(x, DEVICES, pairs[step])]
    ppermute x5 -> x6, waiting for transfers between devices: 1.12 us -> 0.02 us  [swap_core(): return lax.ppermute(x, 'core', [(0, 1), (1, 0)])]
    broadcast_in_dim x1 -> x0, local copies, waits for them, and re-layouts: 0.96 us -> none  [body(): grad_in[None, :, width:]]
  transfers between devices with their start and end apart: 21 -> 22, of which waited for: 12 -> 13; matrix products, arithmetic and copies ran while one was open for 7% -> 0% of each run, Pallas kernels for 9% -> 11%
where the time goes in v4:
time: 71.6 us; the launch traced here: 71.4 us
  waiting for transfers between devices  28.2 us (39%)
  starting transfers between devices  27.2 us (38%)
  Pallas kernels  11.2 us (16%)
  local copies, waits for them, and re-layouts  3.92 us (5%)
  between operations  0.84 us (1%)
    ppermute x16, waiting for transfers between devices, exchange(): return lax.ppermute(x, DEVICES, pairs[step])  28.1 us
    ppermute x16, starting transfers between devices, exchange(): return lax.ppermute(x, DEVICES, pairs[step])  25.9 us
    pallas_call x20, Pallas kernels, call(): pl.pallas_call(run, out_shape=out_shape, in_specs=[pl.BlockSpec(memory_sp...  11.2 us
    unnamed x13, local copies, waits for them, and re-layouts  3.92 us
  transfers between devices with their start and end apart: 22, of which 13 were waited for; matrix products, arithmetic and copies ran while one was open for 0% of the time, Pallas kernels for 11%

profile of v4, /device:TPU:0, one launch (start us, length us, event | category | flops | bytes accessed | tf_op | source)
XLA Modules:
  0.0 71.4 jit_solution(6692668969106494141)
XLA Ops:
  0.6 0.8 %copy.13.refs_3_ = bf16[32,8]{1,0:T(8,128)(2,1)S(1)} copy(bf16[32,8]{0,1:T(8,128)(2,1)} %param.10) | data formatting | bytes 1024 | tf_op args[3]
  1.5 0.8 %copy.12.refs_2_.refs_5_ = s32[32,8]{1,0:T(8,128)S(1)} copy(s32[32,8]{0,1:T(8,128)} %param.9) | data formatting | bytes 2048 | tf_op args[2]
  2.2 0.8 %copy-done.3 = bf16[32,1024]{1,0:T(8,128)(2,1)S(1)} copy-done((bf16[32,1024]{1,0:T(8,128)(2,1)S(1)}, bf16[32,1024]{1,0:T(8,128)(2,1)}, u32[]{:S(2)}) %copy-start.3) | copy-done | bytes 65560
  3.1 0.8 %copy-done.4 = bf16[32,1024]{1,0:T(8,128)(2,1)S(1)} copy-done((bf16[32,1024]{1,0:T(8,128)(2,1)S(1)}, bf16[32,1024]{1,0:T(8,128)(2,1)}, u32[]{:S(2)}) %copy-start.4) | copy-done | bytes 65560
  4.0 4.1 %collective-permute-start.3 = (bf16[1,32,1024]{2,1,0:T(8,128)(2,1)S(1)}, bf16[1,32,1024]{2,1,0:T(8,128)(2,1)S(1)}, u32[]{:S(2)}, u32[]{:S(2)}) collective-permute-start(bf16[1,32,1024]{2,1,0:T(8,128)(2,1)S(1)} %get-tuple-element.45.refs_0_), channel_id=1, source_target_pairs={{0,16},{1,17},{2,18},{3,19},{4,20},{5,21},{6,22},{7,23},{8,24},{9,... | collective-permute-start | bytes 196616 | tf_op jit(solution)/shard_map/ppermute | solution.py:257
  8.1 1.5 %collective-permute-start = (bf16[1,32,1152]{2,1,0:T(8,128)(2,1)S(1)}, bf16[1,32,1152]{2,1,0:T(8,128)(2,1)S(1)}, u32[]{:S(2)}, u32[]{:S(2)}) collective-permute-start(bf16[1,32,1152]{2,1,0:T(8,128)(2,1)S(1)} %get-tuple-element.44.refs_0_), channel_id=1, source_target_pairs={{0,2},{1,5},{2,0},{3,7},{4,6},{5,1},{6,4},{7,3},{8,10},{9,13},{10,... | collective-permute-start | bytes 221192 | tf_op jit(solution)/shard_map/ppermute | solution.py:257
  9.6 2.2 %collective-permute-done.3.refs_1_ = bf16[1,32,1024]{2,1,0:T(8,128)(2,1)S(1)} collective-permute-done((bf16[1,32,1024]{2,1,0:T(8,128)(2,1)S(1)}, bf16[1,32,1024]{2,1,0:T(8,128)(2,1)S(1)}, u32[]{:S(2)}, u32[]{:S(2)}) %collective-permute-start.3) | collective-permute-done | bytes 65568 | tf_op jit(solution)/shard_map/ppermute | solution.py:257
  12.5 3.4 %collective-permute-start.1 = (bf16[2,32,1152]{2,1,0:T(8,128)(2,1)S(1)}, bf16[2,32,1152]{2,1,0:T(8,128)(2,1)S(1)}, u32[]{:S(2)}, u32[]{:S(2)}) collective-permute-start(bf16[2,32,1152]{2,1,0:T(8,128)(2,1)S(1)} %stack_kernel.1.refs_0_), channel_id=1, source_target_pairs={{0,16},{1,17},{2,18},{3,19},{4,20},{5,21},{6,22},{7,23},{8,24},{9,... | collective-permute-start | bytes 442376 | tf_op jit(solution)/shard_map/ppermute | solution.py:257
  16.4 2.4 %collective-permute-done.4.refs_1_ = bf16[1,64,1024]{2,1,0:T(8,128)(2,1)S(1)} collective-permute-done((bf16[1,64,1024]{2,1,0:T(8,128)(2,1)S(1)}, bf16[1,64,1024]{2,1,0:T(8,128)(2,1)S(1)}, u32[]{:S(2)}, u32[]{:S(2)}) %collective-permute-start.4) | collective-permute-done | bytes 131104 | tf_op jit(solution)/shard_map/ppermute | solution.py:257
  18.9 2.0 %collective-permute-start.5 = (bf16[1,128,1024]{2,1,0:T(8,128)(2,1)S(1)}, bf16[1,128,1024]{2,1,0:T(8,128)(2,1)S(1)}, u32[]{:S(2)}, u32[]{:S(2)}) collective-permute-start(bf16[1,128,1024]{2,1,0:T(8,128)(2,1)S(1)} %join_kernel.8.refs_0_), channel_id=1, source_target_pairs={{0,2},{1,5},{2,0},{3,7},{4,6},{5,1},{6,4},{7,3},{8,10},{9,13},{10,... | collective-permute-start | bytes 786440 | tf_op jit(solution)/shard_map/ppermute | solution.py:257
  20.8 1.7 %collective-permute-done.1.refs_1_ = bf16[2,32,1152]{2,1,0:T(8,128)(2,1)S(1)} collective-permute-done((bf16[2,32,1152]{2,1,0:T(8,128)(2,1)S(1)}, bf16[2,32,1152]{2,1,0:T(8,128)(2,1)S(1)}, u32[]{:S(2)}, u32[]{:S(2)}) %collective-permute-start.1) | collective-permute-done | bytes 147488 | tf_op jit(solution)/shard_map/ppermute | solution.py:257
  22.7 2.6 %collective-permute-done.5.refs_1_ = bf16[1,128,1024]{2,1,0:T(8,128)(2,1)S(1)} collective-permute-done((bf16[1,128,1024]{2,1,0:T(8,128)(2,1)S(1)}, bf16[1,128,1024]{2,1,0:T(8,128)(2,1)S(1)}, u32[]{:S(2)}, u32[]{:S(2)}) %collective-permute-start.5) | collective-permute-done | bytes 262176 | tf_op jit(solution)/shard_map/ppermute | solution.py:257
  25.3 2.0 %collective-permute-start.10 = (bf16[256,1024]{1,0:T(8,128)(2,1)S(1)}, bf16[256,1024]{1,0:T(8,128)(2,1)S(1)}, u32[]{:S(2)}, u32[]{:S(2)}) collective-permute-start(bf16[256,1024]{1,0:T(8,128)(2,1)S(1)} %bitcast.26), channel_id=1, source_target_pairs={{0,4},{1,3},{2,6},{3,1},{4,0},{5,7},{6,2},{7,5},{8,12},{9,11},{10,... | collective-permute-start | bytes 1572872 | tf_op jit(solution)/shard_map/ppermute | solution.py:257
  27.4 1.9 %collective-permute-done.2.refs_1_ = bf16[2,64,1152]{2,1,0:T(8,128)(2,1)S(1)} collective-permute-done((bf16[2,64,1152]{2,1,0:T(8,128)(2,1)S(1)}, bf16[2,64,1152]{2,1,0:T(8,128)(2,1)S(1)}, u32[]{:S(2)}, u32[]{:S(2)}) %collective-permute-start.2) | collective-permute-done | bytes 294944 | tf_op jit(solution)/shard_map/ppermute | solution.py:257
  29.4 1.6 %collective-permute-start.9 = (bf16[256,1152]{1,0:T(8,128)(2,1)S(1)}, bf16[256,1152]{1,0:T(8,128)(2,1)S(1)}, u32[]{:S(2)}, u32[]{:S(2)}) collective-permute-start(bf16[256,1152]{1,0:T(8,128)(2,1)S(1)} %bitcast.10), channel_id=1, source_target_pairs={{0,4},{1,3},{2,6},{3,1},{4,0},{5,7},{6,2},{7,5},{8,12},{9,11},{10,... | collective-permute-start | bytes 1769480 | tf_op jit(solution)/shard_map/ppermute | solution.py:257
  31.0 1.3 %forward_kernel.2 = (f32[256,384]{1,0:T(8,128)S(1)}, f32[256,384]{1,0:T(8,128)S(1)}, f32[256,384]{1,0:T(8,128)S(1)}) custom-call(s32[2]{0:T(128)S(1)} %pad_add_fusion.refs_0_, bf16[256,1024]{1,0:T(8,128)(2,1)S(1)} %bitcast.27, bf16[512,384]{1,0:T(8,128)(2,1)S(1)} %bitcast.14, bf16[512,384]{1,0:T(8,128)(2,1)S(1)} %collective-permute-done.6.refs_3_.refs_6_, ...), custom_call_target="tpu_custom_call" | custom-call | flops 4026531840 | bytes 2097152 | tf_op jit(solution)/shard_map/forward_kernel/pallas_call | solution.py:212
  32.3 1.7 %backward_kernel.2 = (bf16[256,512]{1,0:T(8,128)(2,1)S(1)}, bf16[256,640]{1,0:T(8,128)(2,1)S(1)}, bf16[256,768]{1,0:T(8,128)(2,1)S(1)}, bf16[256,384]{1,0:T(8,128)(2,1)S(1)}) custom-call(s32[2]{0:T(128)S(1)} %pad_add_fusion.refs_0_, bf16[256,1152]{1,0:T(8,128)(2,1)S(1)} %bitcast.11, f32[256,384]{1,0:T(8,128)S(1)} %get-tuple-element.46.refs_2_, ...), custom_call_target="tpu_custom_call" | custom-call | flops 603979776 | bytes 4128768 | tf_op jit(solution)/shard_map/backward_kernel/pallas_call | solution.py:212
  34.6 1.3 %forward_kernel.3 = (f32[256,384]{1,0:T(8,128)S(1)}, f32[256,384]{1,0:T(8,128)S(1)}, f32[256,384]{1,0:T(8,128)S(1)}) custom-call(s32[2]{0:T(128)S(1)} %pad_add_fusion.refs_0_, bf16[256,1024]{1,0:T(8,128)(2,1)S(1)} %collective-permute-done.10.refs_1_.refs_2_, bf16[512,384]{1,0:T(8,128)(2,1)S(1)} %bitcast.16, ...), custom_call_target="tpu_custom_call" | custom-call | flops 4026531840 | bytes 2097152 | tf_op jit(solution)/shard_map/forward_kernel/pallas_call | solution.py:212
  35.9 5.1 %collective-permute-done.9.refs_1_.refs_4_ = bf16[256,1152]{1,0:T(8,128)(2,1)S(1)} collective-permute-done((bf16[256,1152]{1,0:T(8,128)(2,1)S(1)}, bf16[256,1152]{1,0:T(8,128)(2,1)S(1)}, u32[]{:S(2)}, u32[]{:S(2)}) %collective-permute-start.9) | collective-permute-done | bytes 589856 | tf_op jit(solution)/shard_map/ppermute | solution.py:257
  40.9 1.7 %backward_kernel.3 = (bf16[256,512]{1,0:T(8,128)(2,1)S(1)}, bf16[256,640]{1,0:T(8,128)(2,1)S(1)}, bf16[256,768]{1,0:T(8,128)(2,1)S(1)}, bf16[256,384]{1,0:T(8,128)(2,1)S(1)}) custom-call(s32[2]{0:T(128)S(1)} %pad_add_fusion.refs_0_, bf16[256,1152]{1,0:T(8,128)(2,1)S(1)} %collective-permute-done.9.refs_1_.refs_4_, f32[256,384]{1,0:T(8,128)S(1)} %get-tuple-element.50.refs_2_, ...), custom_call_target="tpu_custom_call" | custom-call | flops 603979776 | bytes 4128768 | tf_op jit(solution)/shard_map/backward_kernel/pallas_call | solution.py:212
  42.6 2.0 %collective-permute-start.15 = (bf16[256,640]{1,0:T(8,128)(2,1)S(1)}, bf16[256,640]{1,0:T(8,128)(2,1)S(1)}, u32[]{:S(2)}, u32[]{:S(2)}) collective-permute-start(bf16[256,640]{1,0:T(8,128)(2,1)S(1)} %get-tuple-element.61), channel_id=1, source_target_pairs={{0,4},{1,3},{2,6},{3,1},{4,0},{5,7},{6,2},{7,5},{8,12},{9,11},{10,... | collective-permute-start | bytes 983048 | tf_op jit(solution)/shard_map/ppermute | solution.py:257
  44.7 2.0 %weight_kernel.1 = (f32[512,768]{1,0:T(8,128)S(1)}, f32[384,512]{1,0:T(8,128)S(1)}, bf16[512,384]{1,0:T(8,128)(2,1)S(1)}, bf16[512,384]{1,0:T(8,128)(2,1)S(1)}, bf16[384,512]{1,0:T(8,128)(2,1)S(1)}) custom-call(s32[2]{0:T(128)S(1)} %pad_add_fusion.refs_0_, bf16[256,1024]{1,0:T(8,128)(2,1)S(1)} %bitcast.28, ...), custom_call_target="tpu_custom_call" | custom-call | flops 1207959552 | bytes 3407872 | tf_op jit(solution)/shard_map/weight_kernel/pallas_call | solution.py:212
  47.4 2.3 %collective-permute-done.15.refs_1_ = bf16[256,640]{1,0:T(8,128)(2,1)S(1)} collective-permute-done((bf16[256,640]{1,0:T(8,128)(2,1)S(1)}, bf16[256,640]{1,0:T(8,128)(2,1)S(1)}, u32[]{:S(2)}, u32[]{:S(2)}) %collective-permute-start.15) | collective-permute-done | bytes 327712 | tf_op jit(solution)/shard_map/ppermute | solution.py:257
  49.8 2.0 %collective-permute-start.16 = (bf16[128,640]{1,0:T(8,128)(2,1)S(1)}, bf16[128,640]{1,0:T(8,128)(2,1)S(1)}, u32[]{:S(2)}, u32[]{:S(2)}) collective-permute-start(bf16[128,640]{1,0:T(8,128)(2,1)S(1)} %get-tuple-element.63), channel_id=1, source_target_pairs={{0,2},{1,5},{2,0},{3,7},{4,6},{5,1},{6,4},{7,3},{8,10},{9,13},{10,... | collective-permute-start | bytes 491528 | tf_op jit(solution)/shard_map/ppermute | solution.py:257
  51.8 2.5 %collective-permute-done.11.refs_1_ = bf16[256,512]{1,0:T(8,128)(2,1)S(1)} collective-permute-done((bf16[256,512]{1,0:T(8,128)(2,1)S(1)}, bf16[256,512]{1,0:T(8,128)(2,1)S(1)}, u32[]{:S(2)}, u32[]{:S(2)}) %collective-permute-start.11) | collective-permute-done | bytes 262176 | tf_op jit(solution)/shard_map/ppermute | solution.py:257
  54.3 2.2 %collective-permute-start.12 = (bf16[128,512]{1,0:T(8,128)(2,1)S(1)}, bf16[128,512]{1,0:T(8,128)(2,1)S(1)}, u32[]{:S(2)}, u32[]{:S(2)}) collective-permute-start(bf16[128,512]{1,0:T(8,128)(2,1)S(1)} %get-tuple-element.55), channel_id=1, source_target_pairs={{0,2},{1,5},{2,0},{3,7},{4,6},{5,1},{6,4},{7,3},{8,10},{9,13},{10,... | collective-permute-start | bytes 393224 | tf_op jit(solution)/shard_map/ppermute | solution.py:257
  56.6 2.8 %collective-permute-done.12.refs_1_ = bf16[128,512]{1,0:T(8,128)(2,1)S(1)} collective-permute-done((bf16[128,512]{1,0:T(8,128)(2,1)S(1)}, bf16[128,512]{1,0:T(8,128)(2,1)S(1)}, u32[]{:S(2)}, u32[]{:S(2)}) %collective-permute-start.12) | collective-permute-done | bytes 131104 | tf_op jit(solution)/shard_map/ppermute | solution.py:257
  59.6 1.2 %settle_kernel.1 = (bf16[512,384]{1,0:T(8,128)(2,1)}, bf16[512,384]{1,0:T(8,128)(2,1)}, bf16[384,512]{1,0:T(8,128)(2,1)}, f32[8,128]{1,0:T(8,128)S(1)}) custom-call(f32[512,768]{1,0:T(8,128)S(1)} %get-tuple-element.70.refs_0_, f32[384,512]{1,0:T(8,128)S(1)} %get-tuple-element.71.refs_1_, bf16[512,384]{1,0:T(8,128)(2,1)S(1)} %collective-permute-done.18.refs_2_, ...), custom_call_target="tpu_custom_call" | custom-call | bytes 3538944 | tf_op jit(solution)/shard_map/settle_kernel/pallas_call | solution.py:212
  61.0 3.1 %collective-permute-start.21 = (bf16[32,640]{1,0:T(8,128)(2,1)S(1)}, bf16[32,640]{1,0:T(8,128)(2,1)S(1)}, u32[]{:S(2)}, u32[]{:S(2)}) collective-permute-start(bf16[32,640]{1,0:T(8,128)(2,1)S(1)} %get-tuple-element.77), channel_id=1, source_target_pairs={{0,16},{1,17},{2,18},{3,19},{4,20},{5,21},{6,22},{7,23},{8,24},{9,... | collective-permute-start | bytes 122888 | tf_op jit(solution)/shard_map/ppermute | solution.py:257
  64.2 1.2 %collective-permute-start.14 = (bf16[32,512]{1,0:T(8,128)(2,1)S(1)}, bf16[32,512]{1,0:T(8,128)(2,1)S(1)}, u32[]{:S(2)}, u32[]{:S(2)}) collective-permute-start(bf16[32,512]{1,0:T(8,128)(2,1)S(1)} %get-tuple-element.59), channel_id=1, source_target_pairs={{0,16},{1,17},{2,18},{3,19},{4,20},{5,21},{6,22},{7,23},{8,24},{9,... | collective-permute-start | bytes 98312 | tf_op jit(solution)/shard_map/ppermute | solution.py:257
  65.4 3.7 %collective-permute-done.14.refs_2_ = bf16[32,512]{1,0:T(8,128)(2,1)S(1)} collective-permute-done((bf16[32,512]{1,0:T(8,128)(2,1)S(1)}, bf16[32,512]{1,0:T(8,128)(2,1)S(1)}, u32[]{:S(2)}, u32[]{:S(2)}) %collective-permute-start.14) | collective-permute-done | bytes 32800 | tf_op jit(solution)/shard_map/ppermute | solution.py:257
  69.1 1.6 %finish_kernel.1 = (bf16[32,1024]{1,0:T(8,128)(2,1)}, bf16[32,8]{1,0:T(8,128)(2,1)S(1)}) custom-call(s32[2]{0:T(128)S(1)} %pad_add_fusion.refs_0_, f32[32,512]{1,0:T(8,128)S(1)} %get-tuple-element.58.refs_1_, bf16[32,512]{1,0:T(8,128)(2,1)S(1)} %collective-permute-done.14.refs_2_, f32[32,640]{1,0:T(8,128)S(1)} %get-tuple-element.76.refs_3_, ...), custom_call_target="tpu_custom_call" | custom-call | bytes 222208 | tf_op jit(solution)/shard_map/finish_kernel/pallas_call | solution.py:212
  (46 shorter events, 4.4 us)
Async XLA Ops:
  0.6 22.0 %copy-start.2 = (bf16[1,384,512]{2,1,0:T(8,128)(2,1)S(1)}, bf16[1,384,512]{2,1,0:T(8,128)(2,1)}, u32[]{:S(2)}) copy-start(bf16[1,384,512]{2,1,0:T(8,128)(2,1)} %param.13) | copy-start | bytes 1179652
  2.2 0.8 %copy-start.3 = (bf16[32,1024]{1,0:T(8,128)(2,1)S(1)}, bf16[32,1024]{1,0:T(8,128)(2,1)}, u32[]{:S(2)}) copy-start(bf16[32,1024]{1,0:T(8,128)(2,1)} %refs_0_.1) | copy-start | bytes 196612
  3.1 0.8 %copy-start.4 = (bf16[32,1024]{1,0:T(8,128)(2,1)S(1)}, bf16[32,1024]{1,0:T(8,128)(2,1)}, u32[]{:S(2)}) copy-start(bf16[32,1024]{1,0:T(8,128)(2,1)} %refs_1_.1) | copy-start | bytes 196612
  4.0 7.8 %collective-permute-start.3 = (bf16[1,32,1024]{2,1,0:T(8,128)(2,1)S(1)}, bf16[1,32,1024]{2,1,0:T(8,128)(2,1)S(1)}, u32[]{:S(2)}, u32[]{:S(2)}) collective-permute-start(bf16[1,32,1024]{2,1,0:T(8,128)(2,1)S(1)} %get-tuple-element.45.refs_0_), channel_id=1, source_target_pairs={{0,16},{1,17},{2,18},{3,19},{4,20},{5,21},{6,22},{7,23},{8,24},{9,... | collective-permute-start | bytes 196616 | tf_op jit(solution)/shard_map/ppermute | solution.py:257
  8.1 4.4 %collective-permute-start = (bf16[1,32,1152]{2,1,0:T(8,128)(2,1)S(1)}, bf16[1,32,1152]{2,1,0:T(8,128)(2,1)S(1)}, u32[]{:S(2)}, u32[]{:S(2)}) collective-permute-start(bf16[1,32,1152]{2,1,0:T(8,128)(2,1)S(1)} %get-tuple-element.44.refs_0_), channel_id=1, source_target_pairs={{0,2},{1,5},{2,0},{3,7},{4,6},{5,1},{6,4},{7,3},{8,10},{9,13},{10,... | collective-permute-start | bytes 221192 | tf_op jit(solution)/shard_map/ppermute | solution.py:257
  11.8 7.1 %collective-permute-start.4 = (bf16[1,64,1024]{2,1,0:T(8,128)(2,1)S(1)}, bf16[1,64,1024]{2,1,0:T(8,128)(2,1)S(1)}, u32[]{:S(2)}, u32[]{:S(2)}) collective-permute-start(bf16[1,64,1024]{2,1,0:T(8,128)(2,1)S(1)} %join_kernel.7.refs_0_), channel_id=1, source_target_pairs={{0,8},{1,9},{2,10},{3,11},{4,12},{5,13},{6,14},{7,15},{8,0},{9,1},... | collective-permute-start | bytes 393224 | tf_op jit(solution)/shard_map/ppermute | solution.py:257
  12.5 10.0 %collective-permute-start.1 = (bf16[2,32,1152]{2,1,0:T(8,128)(2,1)S(1)}, bf16[2,32,1152]{2,1,0:T(8,128)(2,1)S(1)}, u32[]{:S(2)}, u32[]{:S(2)}) collective-permute-start(bf16[2,32,1152]{2,1,0:T(8,128)(2,1)S(1)} %stack_kernel.1.refs_0_), channel_id=1, source_target_pairs={{0,16},{1,17},{2,18},{3,19},{4,20},{5,21},{6,22},{7,23},{8,24},{9,... | collective-permute-start | bytes 442376 | tf_op jit(solution)/shard_map/ppermute | solution.py:257
  15.9 15.1 %collective-permute-start.6 = (bf16[512,384]{1,0:T(8,128)(2,1)}, bf16[512,384]{1,0:T(8,128)(2,1)S(1)}, u32[]{:S(2)}, u32[]{:S(2)}) collective-permute-start(bf16[512,384]{1,0:T(8,128)(2,1)} %bitcast.13), channel_id=1, source_target_pairs={{0,1},{1,0},{2,3},{3,2},{4,5},{5,4},{6,7},{7,6},{8,9},{9,8},{10,11... | collective-permute-start | bytes 1179656 | tf_op jit(solution)/shard_map/ppermute | solution.py:21
  15.9 15.1 %copy-start = (bf16[1,512,384]{2,1,0:T(8,128)(2,1)S(1)}, bf16[1,512,384]{2,1,0:T(8,128)(2,1)}, u32[]{:S(2)}) copy-start(bf16[1,512,384]{2,1,0:T(8,128)(2,1)} %param.11) | copy-start | bytes 1179652
  15.9 15.1 %copy-start.1 = (bf16[1,512,384]{2,1,0:T(8,128)(2,1)S(1)}, bf16[1,512,384]{2,1,0:T(8,128)(2,1)}, u32[]{:S(2)}) copy-start(bf16[1,512,384]{2,1,0:T(8,128)(2,1)} %param.12) | copy-start | bytes 1179652
  15.9 15.1 %collective-permute-start.7 = (bf16[512,384]{1,0:T(8,128)(2,1)}, bf16[512,384]{1,0:T(8,128)(2,1)S(1)}, u32[]{:S(2)}, u32[]{:S(2)}) collective-permute-start(bf16[512,384]{1,0:T(8,128)(2,1)} %bitcast.18), channel_id=1, source_target_pairs={{0,1},{1,0},{2,3},{3,2},{4,5},{5,4},{6,7},{7,6},{8,9},{9,8},{10,11... | collective-permute-start | bytes 1179656 | tf_op jit(solution)/shard_map/ppermute | solution.py:21
  18.9 6.4 %collective-permute-start.5 = (bf16[1,128,1024]{2,1,0:T(8,128)(2,1)S(1)}, bf16[1,128,1024]{2,1,0:T(8,128)(2,1)S(1)}, u32[]{:S(2)}, u32[]{:S(2)}) collective-permute-start(bf16[1,128,1024]{2,1,0:T(8,128)(2,1)S(1)} %join_kernel.8.refs_0_), channel_id=1, source_target_pairs={{0,2},{1,5},{2,0},{3,7},{4,6},{5,1},{6,4},{7,3},{8,10},{9,13},{10,... | collective-permute-start | bytes 786440 | tf_op jit(solution)/shard_map/ppermute | solution.py:257
  22.5 6.8 %collective-permute-start.2 = (bf16[2,64,1152]{2,1,0:T(8,128)(2,1)S(1)}, bf16[2,64,1152]{2,1,0:T(8,128)(2,1)S(1)}, u32[]{:S(2)}, u32[]{:S(2)}) collective-permute-start(bf16[2,64,1152]{2,1,0:T(8,128)(2,1)S(1)} %join_kernel.5.refs_0_), channel_id=1, source_target_pairs={{0,8},{1,9},{2,10},{3,11},{4,12},{5,13},{6,14},{7,15},{8,0},{9,1},... | collective-permute-start | bytes 884744 | tf_op jit(solution)/shard_map/ppermute | solution.py:257
  22.6 9.6 %collective-permute-start.8 = (bf16[384,512]{1,0:T(8,128)(2,1)S(1)}, bf16[384,512]{1,0:T(8,128)(2,1)S(1)}, u32[]{:S(2)}, u32[]{:S(2)}) collective-permute-start(bf16[384,512]{1,0:T(8,128)(2,1)S(1)} %bitcast.23), channel_id=1, source_target_pairs={{0,1},{1,0},{2,3},{3,2},{4,5},{5,4},{6,7},{7,6},{8,9},{9,8},{10,11... | collective-permute-start | bytes 1179656 | tf_op jit(solution)/shard_map/ppermute | solution.py:21
  25.3 9.2 %collective-permute-start.10 = (bf16[256,1024]{1,0:T(8,128)(2,1)S(1)}, bf16[256,1024]{1,0:T(8,128)(2,1)S(1)}, u32[]{:S(2)}, u32[]{:S(2)}) collective-permute-start(bf16[256,1024]{1,0:T(8,128)(2,1)S(1)} %bitcast.26), channel_id=1, source_target_pairs={{0,4},{1,3},{2,6},{3,1},{4,0},{5,7},{6,2},{7,5},{8,12},{9,11},{10,... | collective-permute-start | bytes 1572872 | tf_op jit(solution)/shard_map/ppermute | solution.py:257
  29.4 11.5 %collective-permute-start.9 = (bf16[256,1152]{1,0:T(8,128)(2,1)S(1)}, bf16[256,1152]{1,0:T(8,128)(2,1)S(1)}, u32[]{:S(2)}, u32[]{:S(2)}) collective-permute-start(bf16[256,1152]{1,0:T(8,128)(2,1)S(1)} %bitcast.10), channel_id=1, source_target_pairs={{0,4},{1,3},{2,6},{3,1},{4,0},{5,7},{6,2},{7,5},{8,12},{9,11},{10,... | collective-permute-start | bytes 1769480 | tf_op jit(solution)/shard_map/ppermute | solution.py:257
  42.6 7.1 %collective-permute-start.15 = (bf16[256,640]{1,0:T(8,128)(2,1)S(1)}, bf16[256,640]{1,0:T(8,128)(2,1)S(1)}, u32[]{:S(2)}, u32[]{:S(2)}) collective-permute-start(bf16[256,640]{1,0:T(8,128)(2,1)S(1)} %get-tuple-element.61), channel_id=1, source_target_pairs={{0,4},{1,3},{2,6},{3,1},{4,0},{5,7},{6,2},{7,5},{8,12},{9,11},{10,... | collective-permute-start | bytes 983048 | tf_op jit(solution)/shard_map/ppermute | solution.py:257
  44.6 9.7 %collective-permute-start.11 = (bf16[256,512]{1,0:T(8,128)(2,1)S(1)}, bf16[256,512]{1,0:T(8,128)(2,1)S(1)}, u32[]{:S(2)}, u32[]{:S(2)}) collective-permute-start(bf16[256,512]{1,0:T(8,128)(2,1)S(1)} %get-tuple-element.53), channel_id=1, source_target_pairs={{0,4},{1,3},{2,6},{3,1},{4,0},{5,7},{6,2},{7,5},{8,12},{9,11},{10,... | collective-permute-start | bytes 786440 | tf_op jit(solution)/shard_map/ppermute | solution.py:257
  46.7 12.8 %collective-permute-start.18 = (bf16[512,384]{1,0:T(8,128)(2,1)S(1)}, bf16[512,384]{1,0:T(8,128)(2,1)S(1)}, u32[]{:S(2)}, u32[]{:S(2)}) collective-permute-start(bf16[512,384]{1,0:T(8,128)(2,1)S(1)} %get-tuple-element.72), channel_id=1, source_target_pairs={{0,1},{1,0},{2,3},{3,2},{4,5},{5,4},{6,7},{7,6},{8,9},{9,8},{10,11... | collective-permute-start | bytes 1179656 | tf_op jit(solution)/shard_map/ppermute | solution.py:21
  46.8 12.7 %collective-permute-start.19 = (bf16[512,384]{1,0:T(8,128)(2,1)S(1)}, bf16[512,384]{1,0:T(8,128)(2,1)S(1)}, u32[]{:S(2)}, u32[]{:S(2)}) collective-permute-start(bf16[512,384]{1,0:T(8,128)(2,1)S(1)} %get-tuple-element.73), channel_id=1, source_target_pairs={{0,1},{1,0},{2,3},{3,2},{4,5},{5,4},{6,7},{7,6},{8,9},{9,8},{10,11... | collective-permute-start | bytes 1179656 | tf_op jit(solution)/shard_map/ppermute | solution.py:21
  47.3 12.3 %collective-permute-start.20 = (bf16[384,512]{1,0:T(8,128)(2,1)S(1)}, bf16[384,512]{1,0:T(8,128)(2,1)S(1)}, u32[]{:S(2)}, u32[]{:S(2)}) collective-permute-start(bf16[384,512]{1,0:T(8,128)(2,1)S(1)} %get-tuple-element.74), channel_id=1, source_target_pairs={{0,1},{1,0},{2,3},{3,2},{4,5},{5,4},{6,7},{7,6},{8,9},{9,8},{10,11... | collective-permute-start | bytes 1179656 | tf_op jit(solution)/shard_map/ppermute | solution.py:21
  49.8 6.7 %collective-permute-start.16 = (bf16[128,640]{1,0:T(8,128)(2,1)S(1)}, bf16[128,640]{1,0:T(8,128)(2,1)S(1)}, u32[]{:S(2)}, u32[]{:S(2)}) collective-permute-start(bf16[128,640]{1,0:T(8,128)(2,1)S(1)} %get-tuple-element.63), channel_id=1, source_target_pairs={{0,2},{1,5},{2,0},{3,7},{4,6},{5,1},{6,4},{7,3},{8,10},{9,13},{10,... | collective-permute-start | bytes 491528 | tf_op jit(solution)/shard_map/ppermute | solution.py:257
  54.3 5.1 %collective-permute-start.12 = (bf16[128,512]{1,0:T(8,128)(2,1)S(1)}, bf16[128,512]{1,0:T(8,128)(2,1)S(1)}, u32[]{:S(2)}, u32[]{:S(2)}) collective-permute-start(bf16[128,512]{1,0:T(8,128)(2,1)S(1)} %get-tuple-element.55), channel_id=1, source_target_pairs={{0,2},{1,5},{2,0},{3,7},{4,6},{5,1},{6,4},{7,3},{8,10},{9,13},{10,... | collective-permute-start | bytes 393224 | tf_op jit(solution)/shard_map/ppermute | solution.py:257
  56.5 4.5 %collective-permute-start.17 = (bf16[64,640]{1,0:T(8,128)(2,1)S(1)}, bf16[64,640]{1,0:T(8,128)(2,1)S(1)}, u32[]{:S(2)}, u32[]{:S(2)}) collective-permute-start(bf16[64,640]{1,0:T(8,128)(2,1)S(1)} %get-tuple-element.65), channel_id=1, source_target_pairs={{0,8},{1,9},{2,10},{3,11},{4,12},{5,13},{6,14},{7,15},{8,0},{9,1},... | collective-permute-start | bytes 245768 | tf_op jit(solution)/shard_map/ppermute | solution.py:257
  59.4 4.7 %collective-permute-start.13 = (bf16[64,512]{1,0:T(8,128)(2,1)S(1)}, bf16[64,512]{1,0:T(8,128)(2,1)S(1)}, u32[]{:S(2)}, u32[]{:S(2)}) collective-permute-start(bf16[64,512]{1,0:T(8,128)(2,1)S(1)} %get-tuple-element.57), channel_id=1, source_target_pairs={{0,8},{1,9},{2,10},{3,11},{4,12},{5,13},{6,14},{7,15},{8,0},{9,1},... | collective-permute-start | bytes 196616 | tf_op jit(solution)/shard_map/ppermute | solution.py:257
  61.0 8.0 %collective-permute-start.21 = (bf16[32,640]{1,0:T(8,128)(2,1)S(1)}, bf16[32,640]{1,0:T(8,128)(2,1)S(1)}, u32[]{:S(2)}, u32[]{:S(2)}) collective-permute-start(bf16[32,640]{1,0:T(8,128)(2,1)S(1)} %get-tuple-element.77), channel_id=1, source_target_pairs={{0,16},{1,17},{2,18},{3,19},{4,20},{5,21},{6,22},{7,23},{8,24},{9,... | collective-permute-start | bytes 122888 | tf_op jit(solution)/shard_map/ppermute | solution.py:257
  64.2 4.9 %collective-permute-start.14 = (bf16[32,512]{1,0:T(8,128)(2,1)S(1)}, bf16[32,512]{1,0:T(8,128)(2,1)S(1)}, u32[]{:S(2)}, u32[]{:S(2)}) collective-permute-start(bf16[32,512]{1,0:T(8,128)(2,1)S(1)} %get-tuple-element.59), channel_id=1, source_target_pairs={{0,16},{1,17},{2,18},{3,19},{4,20},{5,21},{6,22},{7,23},{8,24},{9,... | collective-permute-start | bytes 98312 | tf_op jit(solution)/shard_map/ppermute | solution.py:257

commit v5 on v1

v5 whole, which is shorter than its diff:
```python
import jax
import jax.numpy as jnp
from jax import lax
from jax.experimental import pallas as pl
from jax.experimental.pallas import tpu as pltpu
from jax.sharding import Mesh, PartitionSpec as P

DEVICES = ("expert", "chip", "core")
F32, BF16 = jnp.float32, jnp.bfloat16
NN = (((1,), (0,)), ((), ()))
NT = (((1,), (1,)), ((), ()))
TN = (((0,), (0,)), ((), ()))
CHUNK = 128


def dot(a, b, dims):
    return lax.dot_general(a, b, dims, preferred_element_type=F32)


def swap_core(x):
    return lax.ppermute(x, "core", [(0, 1), (1, 0)])


def for_chunks(rows, step):
    if rows <= CHUNK:
        step(pl.ds(0, rows))
    else:

        @pl.loop(0, rows // CHUNK)
        def _(i):
            step(pl.ds(pl.multiple_of(i * CHUNK, CHUNK), CHUNK))


def own_other(place_ref, half, start=0):
    member = place_ref[0]
    own = pl.ds(pl.multiple_of(start + member * half, half), half)
    other = pl.ds(pl.multiple_of(start + (1 - member) * half, half), half)
    return own, other


def prepare_kernel(tokens, cotangent, ids, probs, out, ids_here, probs_here, sems):
    features = tokens.shape[1]
    lanes = out.shape[1] - 2 * features
    copies = [
        pltpu.make_async_copy(source, target, sems.at[i])
        for i, (source, target) in enumerate(
            (
                (ids, ids_here),
                (probs, probs_here),
                (tokens, out.at[:, pl.ds(0, features)]),
                (cotangent, out.at[:, pl.ds(features, features)]),
            )
        )
    ]
    for copy in copies:
        copy.start()
    copies[0].wait()
    copies[1].wait()
    names, given = ids_here[...], probs_here[...].astype(F32)
    expert = lax.broadcasted_iota(jnp.int32, (lanes, names.shape[1]), 0)
    weight = jnp.zeros(expert.shape, F32)
    for k in range(names.shape[0]):
        weight = jnp.where(names[k : k + 1, :] == expert, given[k : k + 1, :], weight)
    turned = dot(weight.astype(BF16), unit_matrix(lanes), TN)
    out[:, pl.ds(2 * features, lanes)] = turned.astype(BF16)
    copies[2].wait()
    copies[3].wait()


def unit_matrix(size):
    row = lax.broadcasted_iota(jnp.int32, (size, size), 0)
    column = lax.broadcasted_iota(jnp.int32, (size, size), 1)
    return jnp.where(row == column, 1.0, 0.0).astype(BF16)


def join_kernel(first, second, out):
    rows = first.shape[0]
    out[pl.ds(0, rows), :] = first[...]
    out[pl.ds(rows, rows), :] = second[...]


def split_kernel(kept, got, keep, give):
    rows = keep.shape[0]
    upper, lower = pl.ds(0, rows), pl.ds(rows, rows)
    give[...] = (kept[lower, :].astype(F32) + got[lower, :].astype(F32)).astype(BF16)
    keep[...] = kept[upper, :].astype(F32) + got[upper, :].astype(F32)


def add_kernel(kept, got, total):
    total[...] = (kept[...] + got[...].astype(F32)).astype(total.dtype)


def pass_kernel(source, out):
    out[...] = source[...]


def expert_kernel(
    place, first, second, gate_own, gate_other, up_own, up_other, down_own, down_other,
    keep, give, grads, scaled_hidden,
):
    half, width = gate_own.shape
    features = 2 * half
    lanes = first.shape[1] - 2 * features
    own, other = own_other(place, half)
    dys_own, dys_other = own_other(place, half, features)

    def step(at):
        count = at.size

        def take(cols):
            return jnp.concatenate([first[at, cols], second[at, cols]], 0)

        mine, rest = take(own), take(other)
        pre_gate = dot(mine, gate_own[...], NN) + dot(rest, gate_other[...], NN)
        pre_up = dot(mine, up_own[...], NN) + dot(rest, up_other[...], NN)
        back = dot(take(dys_own), down_own[...], NT) + dot(take(dys_other), down_other[...], NT)
        sig = jax.nn.sigmoid(pre_gate)
        active = pre_gate * sig
        slope = sig * (1.0 + pre_gate * (1.0 - sig))
        hidden = active * pre_up
        lane = lax.broadcasted_iota(jnp.int32, (2 * count, lanes), 1)
        is_own = lane == place[1]
        gates = jnp.where(is_own, take(pl.ds(2 * features, lanes)).astype(F32), 0.0)
        gates = jnp.sum(gates, 1, keepdims=True)
        gate_grads = jnp.sum(hidden * back, 1, keepdims=True)
        back = back * gates
        grad_gate = (back * pre_up * slope).astype(BF16)
        grad_up = (back * active).astype(BF16)
        scaled = (hidden * gates).astype(BF16)
        pieces = (
            dot(grad_gate, gate_own[...], NT) + dot(grad_up, up_own[...], NT),
            dot(grad_gate, gate_other[...], NT) + dot(grad_up, up_other[...], NT),
            jnp.where(is_own, gate_grads, 0.0),
        )
        begin = 0
        for piece in pieces:
            cols = pl.ds(begin, piece.shape[1])
            give[at, cols] = piece[count:].astype(BF16)
            keep[at, cols] = piece[:count].astype(BF16)
            begin += piece.shape[1]
        for i in range(2):
            part = slice(i * count, (i + 1) * count)
            grads[i, at, pl.ds(0, width)] = grad_gate[part]
            grads[i, at, pl.ds(width, width)] = grad_up[part]
            scaled_hidden[i, at, :] = scaled[part]

    for_chunks(first.shape[0], step)


def weight_kernel(place, *refs):
    keep_in, keep_down, give_gate, give_up, give_down = refs[-5:]
    pieces = [refs[i : i + 4] for i in range(0, len(refs) - 5, 4)]
    half, width = give_gate.shape
    count = pieces[0][0].shape[0]
    own, other = own_other(place, half)
    dys_own, dys_other = own_other(place, half, 2 * half)
    left, right = pl.ds(0, width), pl.ds(width, width)
    parts = [(p[i], p[2].at[i], p[3].at[i]) for p in pieces for i in range(2)]

    def products(parts, at, cols, dys_cols):
        def gathered(values):
            return values[0] if len(values) == 1 else jnp.concatenate(values, 0)

        rows = gathered([p[0][at, cols] for p in parts])
        dys = gathered([p[0][at, dys_cols] for p in parts])
        grads = gathered([p[1][at, :] for p in parts])
        hidden = gathered([p[2][at, :] for p in parts])
        return dot(rows, grads, TN), dot(hidden, dys, TN)

    def hand_over(into, down):
        give_gate[...] = into[:, left.start : left.start + width].astype(BF16)
        give_up[...] = into[:, width : 2 * width].astype(BF16)
        give_down[...] = down.astype(BF16)

    if count <= CHUNK:
        at = pl.ds(0, count)
        hand_over(*products(parts, at, other, dys_other))
        keep_in[...], keep_down[...] = products(parts, at, own, dys_own)
    else:
        for cols, dys_cols, is_given in ((other, dys_other, True), (own, dys_own, False)):
            keep_in[...] = jnp.zeros_like(keep_in)
            keep_down[...] = jnp.zeros_like(keep_down)

            @pl.loop(0, count // CHUNK)
            def _(i):
                at = pl.ds(pl.multiple_of(i * CHUNK, CHUNK), CHUNK)
                into, down = products(parts, at, cols, dys_cols)
                keep_in[...] += into
                keep_down[...] += down

            if is_given:
                hand_over(keep_in[...], keep_down[...])


def settle_kernel(keep_in, keep_down, got_gate, got_up, got_down, gate, up, down):
    width = gate.shape[1]
    left, right = pl.ds(0, width), pl.ds(width, width)
    gate[...] = (keep_in[:, left] + got_gate[...].astype(F32)).astype(BF16)
    up[...] = (keep_in[:, right] + got_up[...].astype(F32)).astype(BF16)
    down[...] = (keep_down[...] + got_down[...].astype(F32)).astype(BF16)


def finish_kernel(place, *refs):
    ids, grad_tokens, grad_gates, done = refs[-4:]
    done[...] = jnp.zeros_like(done)
    total = refs[0][...].astype(F32)
    for part in refs[1:-4]:
        total = total + part[...].astype(F32)
    half = grad_tokens.shape[1] // 2
    lanes = total.shape[1] - 2 * half
    own, other = own_other(place, half)
    grad_tokens[:, own] = total[:, :half].astype(BF16)
    grad_tokens[:, other] = total[:, half : 2 * half].astype(BF16)
    gates = dot(unit_matrix(lanes), total[:, 2 * half :].astype(BF16), NT)
    names = ids[...]
    expert = lax.broadcasted_iota(jnp.int32, gates.shape, 0)
    row = lax.broadcasted_iota(jnp.int32, names.shape, 0)
    out = jnp.zeros(names.shape, F32)
    for k in range(names.shape[0]):
        picked = jnp.sum(jnp.where(names[k : k + 1, :] == expert, gates, 0.0), 0, keepdims=True)
        out = jnp.where(row == k, picked, out)
    grad_gates[...] = out.astype(BF16)


def call(kernel, outs, place, *args, after=(), small=True, arrives=0, leaves=0, flops=0):
    used = len(args)
    limit = 10 * 2**20 if small else 56 * 2**20
    if small:
        args = [
            pltpu.with_memory_space_constraint(x, pltpu.VMEM) if i < used - arrives else x
            for i, x in enumerate(args)
        ]
    out_shape = [
        pltpu.VMEM(s, d) if small and i >= leaves else jax.ShapeDtypeStruct(s, d)
        for i, (s, d) in enumerate(outs)
    ]

    scalars = () if place is None else (place,)
    read = len(scalars) + used

    def run(*refs):
        kernel(*refs[:read], *refs[read + len(after) :])

    vmem = pl.BlockSpec(memory_space=pltpu.VMEM)
    return pl.pallas_call(
        run,
        out_shape=out_shape,
        in_specs=[pl.BlockSpec(memory_space=pltpu.SMEM)] * len(scalars)
        + [vmem] * used
        + [pl.BlockSpec(memory_space=pl.ANY)] * len(after),
        out_specs=[vmem] * len(outs),
        compiler_params=pltpu.CompilerParams(vmem_limit_bytes=limit),
        cost_estimate=pl.CostEstimate(flops=flops, bytes_accessed=0, transcendentals=0),
        name=kernel.__name__,
    )(*scalars, *args, *after)


def chip_bits(chip_count):
    bits = []
    bit = chip_count // 2
    while bit:
        bits.append(bit)
        bit //= 2
    return (bits[:-2] + bits[-2:][::-1], bits)


def body(tokens, cotangent, expert_ids, gate_probs, gate_half, up_half, down_half):
    chip_count = lax.axis_size("expert") * lax.axis_size("chip")
    tok_rows, features = tokens.shape
    half = features // 2
    width = gate_half.shape[2]
    lanes = -(-chip_count // 128) * 128
    member = lax.axis_index("core")
    own_expert = lax.axis_index("expert") * lax.axis_size("chip") + lax.axis_index("chip")
    place = jnp.stack([member, own_expert]).astype(jnp.int32)
    bits = chip_bits(chip_count)
    far = len(bits[0]) - 4
    small = far == 0

    def exchange(x, offsets):
        pairs = [
            (2 * chip + core, 2 * (chip ^ offsets[core]) + core)
            for chip in range(chip_count)
            for core in range(2)
        ]
        return lax.ppermute(x, DEVICES, pairs)

    steps = list(zip(*bits))
    near_a, near_b = steps[-2:]
    up_two, up_one = steps[far][0], steps[far + 1][0]

    before = []

    def run(kernel, outs, place, *args, **kwargs):
        results = call(kernel, outs, place, *args, after=tuple(before), small=small, **kwargs)
        before[:] = results[-1:]
        return results

    hbm = pl.BlockSpec(memory_space=pltpu.HBM)
    arguments = (tokens, cotangent, expert_ids.T, gate_probs.T)
    block = pl.pallas_call(
        prepare_kernel,
        out_shape=pltpu.VMEM((tok_rows, 2 * features + lanes), BF16),
        in_specs=[hbm] * 4,
        out_specs=pl.BlockSpec(memory_space=pltpu.VMEM),
        scratch_shapes=[
            pltpu.VMEM(expert_ids.shape[::-1], jnp.int32),
            pltpu.VMEM(gate_probs.shape[::-1], BF16),
            pltpu.SemaphoreType.DMA((4,)),
        ],
        name="prepare_kernel",
    )(*(pltpu.with_memory_space_constraint(x, pltpu.HBM) for x in arguments))

    for step in steps[:far]:
        block = jnp.concatenate([block, exchange(block, step)], 0)

    offsets = (0, up_one, up_two, up_one ^ up_two)
    sources = [block] + [exchange(block, (offset, offset)) for offset in offsets[1:]]
    count = 2 * block.shape[0]
    half_shape = (count // 2, features + lanes)
    full_shape = (count, features + lanes)

    gate_own, up_own, down_own = gate_half[0], up_half[0], down_half[0]
    gate_other, up_other, down_other = swap_core(gate_own), swap_core(up_own), swap_core(down_own)
    weights = (gate_own, gate_other, up_own, up_other, down_own, down_other)

    second_blocks = {}
    first, second, kept, got, saved = {}, {}, {}, {}, {}
    returned = {}

    def send(i, ordered=True):
        if ordered:
            (sources[i],) = run(pass_kernel, [(sources[i].shape, BF16)], None, sources[i])
        second_blocks[i] = exchange(sources[i], near_a)

    def join(i):
        shape = (count, 2 * features + lanes)
        (first[i],) = run(join_kernel, [(shape, BF16)], None, sources[i], second_blocks[i])
        second[i] = exchange(first[i], near_b)

    def expert(i):
        kept[i], give, grads, hidden = run(
            expert_kernel,
            [
                (full_shape, BF16),
                (full_shape, BF16),
                ((2, count, 2 * width), BF16),
                ((2, count, width), BF16),
            ],
            place, first[i], second[i], *weights,
        )
        got[i] = exchange(give, near_b)
        saved[i] = (first[i], second[i], grads, hidden)

    def split(i):
        kept[i], give = run(
            split_kernel, [(half_shape, F32), (half_shape, BF16)], None, kept[i], got[i]
        )
        got[i] = exchange(give, near_a)

    def add(i):
        (give,) = run(add_kernel, [(half_shape, BF16)], None, kept[i], got[i])
        returned[i] = exchange(give, (offsets[i], offsets[i]))

    def collect(total, part):
        return run(add_kernel, [(half_shape, F32)], None, total, part)[0]

    send(0, ordered=False)
    send(1, ordered=False)
    join(0)
    join(1)
    send(2)
    expert(0)
    join(2)
    send(3)
    expert(1)
    join(3)
    split(0)
    expert(2)
    split(1)
    total = collect(kept[0], got[0])
    expert(3)
    add(1)
    split(2)
    split(3)
    add(2)
    total = collect(total, returned[1])
    add(3)
    keep_in, keep_down, *gives = run(
        weight_kernel,
        [
            ((half, 2 * width), F32),
            ((width, half), F32),
            ((half, width), BF16),
            ((half, width), BF16),
            ((width, half), BF16),
        ],
        place, *saved[0], *saved[1], *saved[2], *saved[3],
    )
    gots = [swap_core(give) for give in gives]
    total = collect(total, returned[2])

    parts = (total, returned[3])
    if far:
        total = total + returned[3].astype(F32)
        for step in reversed(steps[:far]):
            middle = total.shape[0] // 2
            total = total[:middle] + exchange(total[middle:].astype(BF16), step).astype(F32)
        parts = (total,)
    grad_tokens, grad_gates, _ = run(
        finish_kernel,
        [((tok_rows, features), BF16), (expert_ids.shape[::-1], BF16), ((8, 128), F32)],
        place, *parts, expert_ids.T, arrives=1, leaves=2, flops=6 * 10**9,
    )
    grad_gate, grad_up, grad_down = run(
        settle_kernel,
        [((half, width), BF16), ((half, width), BF16), ((width, half), BF16)],
        None, keep_in, keep_down, *gots, leaves=3,
    )
    return grad_tokens, grad_gates.T, grad_gate[None], grad_up[None], grad_down[None]


def solution(mesh):
    shape = mesh.shape
    devices = mesh.devices.reshape(shape["dom"], shape["expert"], shape["dp"] // 2, 2)
    fine = Mesh(devices, ("dom", "expert", "chip", "core"))
    every = ("dom", "expert", "chip", "core")
    flat, cube = P(every, None), P(every, None, None)
    return jax.shard_map(
        body,
        mesh=fine,
        in_specs=(flat, flat, flat, flat, cube, cube, cube),
        out_specs=(flat, flat, cube, cube, cube),
        check_vma=False,
    )
```

time: 267 us -> 74 us (0.28)
  waiting for transfers between devices: 224 us -> 24.6 us
  starting transfers between devices: 1.72 us -> 32.7 us
  Pallas kernels: 0 us -> 15.7 us
  between operations: 13.9 us -> 0.84 us
  other arithmetic: 10.9 us -> 0.07 us
  matrix products: 10.4 us -> 0 us
  local copies, waits for them, and re-layouts: 5.91 us -> 0.02 us
    reduce_scatter x1 -> x0, waiting for transfers between devices: 114 us -> none  [body(): lax.psum_scatter(jnp.concatenate([row_grad, gate_cols], 1), CHIPS, scatte...]
    all_gather x2 -> x0, waiting for transfers between devices: 108 us -> none  [the longest x1 54 us: body(): lax.all_gather(jnp.concatenate([cotangent, weight], 1), CHIPS, axis=0, ti...]
    ppermute x0 -> x22, starting transfers between devices: none -> 31.5 us  [exchange(): return lax.ppermute(x, DEVICES, pairs)]
    ppermute x0 -> x22, waiting for transfers between devices: none -> 24.5 us  [exchange(): return lax.ppermute(x, DEVICES, pairs)]
    pallas_call x0 -> x24, Pallas kernels: none -> 15.7 us  [the longest x23 14.6 us: call(): pl.pallas_call(run, out_shape=out_shape, in_specs=[pl.BlockSpec(memory_sp...]
    dot_general x8 -> x0, matrix products: 10.4 us -> none  [the longest x1 2.83 us: body(): lax.dot_general(dys, down_w, (((1,), (1,)), ((), ())), preferred_element_...]
    broadcast_in_dim x3 -> x0, other arithmetic: 3.11 us -> none  [settle(): return (keep + swap_core(give.astype(bf16)).astype(f32)).astype(bf16)[None]]
  transfers between devices with their start and end apart: 9 -> 28, of which waited for: 4 -> 12; matrix products, arithmetic and copies ran while one was open for 7% -> 0% of each run, Pallas kernels for 0% -> 18%
where the time goes in v5:
time: 74 us; the launch traced here: 73.8 us
  starting transfers between devices  32.7 us (44%)
  waiting for transfers between devices  24.6 us (33%)
  Pallas kernels  15.7 us (21%)
  between operations  0.84 us (1%)
    ppermute x22, starting transfers between devices, exchange(): return lax.ppermute(x, DEVICES, pairs)  31.5 us
    ppermute x22, waiting for transfers between devices, exchange(): return lax.ppermute(x, DEVICES, pairs)  24.5 us
    pallas_call x23, Pallas kernels, call(): pl.pallas_call(run, out_shape=out_shape, in_specs=[pl.BlockSpec(memory_sp...  14.6 us
  transfers between devices with their start and end apart: 28, of which 12 were waited for; matrix products, arithmetic and copies ran while one was open for 0% of the time, Pallas kernels for 18%

profile of v5, /device:TPU:0, one launch (start us, length us, event | category | flops | bytes accessed | tf_op | source)
XLA Modules:
  0.0 73.8 jit_solution(5864198867194612301)
XLA Ops:
  0.7 1.0 %prepare_kernel.1.refs_0_ = bf16[32,2176]{1,0:T(8,128)(2,1)S(1)} custom-call(bf16[32,1024]{1,0:T(8,128)(2,1)} %tokens.1, bf16[32,1024]{1,0:T(8,128)(2,1)} %cotangent.1, s32[8,32]{1,0:T(8,128)} %bitcast.26, bf16[8,32]{1,0:T(8,128)(2,1)} %bitcast.28), custom_call_target="tpu_custom_call" | custom-call | tf_op jit(solution)/shard_map/prepare_kernel/pallas_call | solution.py:301
  1.7 3.1 %collective-permute-start.6 = (bf16[32,2176]{1,0:T(8,128)(2,1)S(1)}, bf16[32,2176]{1,0:T(8,128)(2,1)S(1)}, u32[]{:S(2)}, u32[]{:S(2)}) collective-permute-start(bf16[32,2176]{1,0:T(8,128)(2,1)S(1)} %prepare_kernel.1.refs_0_), channel_id=1, source_target_pairs={{0,8},{1,9},{2,10},{3,11},{4,12},{5,13},{6,14},{7,15},{8,0},{9,1},... | collective-permute-start | bytes 417800 | tf_op jit(solution)/shard_map/ppermute | solution.py:286
  5.3 1.5 %collective-permute-start = (bf16[32,2176]{1,0:T(8,128)(2,1)S(1)}, bf16[32,2176]{1,0:T(8,128)(2,1)S(1)}, u32[]{:S(2)}, u32[]{:S(2)}) collective-permute-start(bf16[32,2176]{1,0:T(8,128)(2,1)S(1)} %prepare_kernel.1.refs_0_), channel_id=1, source_target_pairs={{0,2},{1,5},{2,0},{3,7},{4,6},{5,1},{6,4},{7,3},{8,10},{9,13},{10,... | collective-permute-start | bytes 417800 | tf_op jit(solution)/shard_map/ppermute | solution.py:286
  6.8 1.7 %collective-permute-done.6.refs_0_ = bf16[32,2176]{1,0:T(8,128)(2,1)S(1)} collective-permute-done((bf16[32,2176]{1,0:T(8,128)(2,1)S(1)}, bf16[32,2176]{1,0:T(8,128)(2,1)S(1)}, u32[]{:S(2)}, u32[]{:S(2)}) %collective-permute-start.6) | collective-permute-done | bytes 139296 | tf_op jit(solution)/shard_map/ppermute | solution.py:286
  8.5 1.7 %collective-permute-start.7 = (bf16[32,2176]{1,0:T(8,128)(2,1)S(1)}, bf16[32,2176]{1,0:T(8,128)(2,1)S(1)}, u32[]{:S(2)}, u32[]{:S(2)}) collective-permute-start(bf16[32,2176]{1,0:T(8,128)(2,1)S(1)} %collective-permute-done.6.refs_0_), channel_id=1, source_target_pairs={{0,2},{1,5},{2,0},{3,7},{4,6},{5,1},{6,4},{7,3},{8,10},{9,13},{10,... | collective-permute-start | bytes 417800 | tf_op jit(solution)/shard_map/ppermute | solution.py:286
  10.4 2.6 %collective-permute-start.5 = (bf16[32,2176]{1,0:T(8,128)(2,1)S(1)}, bf16[32,2176]{1,0:T(8,128)(2,1)S(1)}, u32[]{:S(2)}, u32[]{:S(2)}) collective-permute-start(bf16[32,2176]{1,0:T(8,128)(2,1)S(1)} %prepare_kernel.1.refs_0_), channel_id=1, source_target_pairs={{0,16},{1,17},{2,18},{3,19},{4,20},{5,21},{6,22},{7,23},{8,24},{9,... | collective-permute-start | bytes 417800 | tf_op jit(solution)/shard_map/ppermute | solution.py:286
  13.5 1.7 %collective-permute-start.1 = (bf16[64,2176]{1,0:T(8,128)(2,1)S(1)}, bf16[64,2176]{1,0:T(8,128)(2,1)S(1)}, u32[]{:S(2)}, u32[]{:S(2)}) collective-permute-start(bf16[64,2176]{1,0:T(8,128)(2,1)S(1)} %join_kernel.4.refs_2_.refs_1_), channel_id=1, source_target_pairs={{0,4},{1,3},{2,6},{3,1},{4,0},{5,7},{6,2},{7,5},{8,12},{9,11},{10,... | collective-permute-start | bytes 835592 | tf_op jit(solution)/shard_map/ppermute | solution.py:286
  15.2 4.9 %collective-permute-done.5.refs_0_ = bf16[32,2176]{1,0:T(8,128)(2,1)S(1)} collective-permute-done((bf16[32,2176]{1,0:T(8,128)(2,1)S(1)}, bf16[32,2176]{1,0:T(8,128)(2,1)S(1)}, u32[]{:S(2)}, u32[]{:S(2)}) %collective-permute-start.5) | collective-permute-done | bytes 139296 | tf_op jit(solution)/shard_map/ppermute | solution.py:286
  20.7 1.6 %collective-permute-start.12 = (bf16[64,2176]{1,0:T(8,128)(2,1)S(1)}, bf16[64,2176]{1,0:T(8,128)(2,1)}, u32[]{:S(2)}, u32[]{:S(2)}) collective-permute-start(bf16[64,2176]{1,0:T(8,128)(2,1)S(1)} %join_kernel.5.refs_1_.refs_5_), channel_id=1, source_target_pairs={{0,4},{1,3},{2,6},{3,1},{4,0},{5,7},{6,2},{7,5},{8,12},{9,11},{10,... | collective-permute-start | bytes 835592 | tf_op jit(solution)/shard_map/ppermute | solution.py:286
  22.2 3.5 %collective-permute-start.9 = (bf16[32,2176]{1,0:T(8,128)(2,1)S(1)}, bf16[32,2176]{1,0:T(8,128)(2,1)}, u32[]{:S(2)}, u32[]{:S(2)}) collective-permute-start(bf16[32,2176]{1,0:T(8,128)(2,1)S(1)} %prepare_kernel.1.refs_0_), channel_id=1, source_target_pairs={{0,24},{1,25},{2,26},{3,27},{4,28},{5,29},{6,30},{7,31},{8,16},{9,... | collective-permute-start | bytes 417800 | tf_op jit(solution)/shard_map/ppermute | solution.py:286
  25.8 1.7 %expert_kernel.4 = (bf16[64,1152]{1,0:T(8,128)(2,1)S(1)}, bf16[64,1152]{1,0:T(8,128)(2,1)S(1)}, bf16[2,64,768]{2,1,0:T(8,128)(2,1)S(1)}, bf16[2,64,384]{2,1,0:T(8,128)(2,1)S(1)}) custom-call(s32[2]{0:T(128)S(1)} %pad_add_fusion.refs_0_, bf16[64,2176]{1,0:T(8,128)(2,1)S(1)} %join_kernel.4.refs_2_.refs_1_, ...), custom_call_target="tpu_custom_call" | custom-call | tf_op jit(solution)/shard_map/expert_kernel/pallas_call | solution.py:245
  30.2 1.6 %collective-permute-start.11 = (bf16[32,2176]{1,0:T(8,128)(2,1)S(1)}, bf16[32,2176]{1,0:T(8,128)(2,1)S(1)}, u32[]{:S(2)}, u32[]{:S(2)}) collective-permute-start(bf16[32,2176]{1,0:T(8,128)(2,1)S(1)} %pass_kernel.3.refs_9_.refs_0_), channel_id=1, source_target_pairs={{0,2},{1,5},{2,0},{3,7},{4,6},{5,1},{6,4},{7,3},{8,10},{9,13},{10,... | collective-permute-start | bytes 417800 | tf_op jit(solution)/shard_map/ppermute | solution.py:286
  32.3 2.2 %expert_kernel.5 = (bf16[64,1152]{1,0:T(8,128)(2,1)S(1)}, bf16[64,1152]{1,0:T(8,128)(2,1)S(1)}, bf16[2,64,768]{2,1,0:T(8,128)(2,1)S(1)}, bf16[2,64,384]{2,1,0:T(8,128)(2,1)S(1)}) custom-call(s32[2]{0:T(128)S(1)} %pad_add_fusion.refs_0_, bf16[64,2176]{1,0:T(8,128)(2,1)S(1)} %join_kernel.5.refs_1_.refs_5_, ...), custom_call_target="tpu_custom_call" | custom-call | tf_op jit(solution)/shard_map/expert_kernel/pallas_call | solution.py:245
  34.5 2.4 %collective-permute-done.11.refs_1_ = bf16[32,2176]{1,0:T(8,128)(2,1)S(1)} collective-permute-done((bf16[32,2176]{1,0:T(8,128)(2,1)S(1)}, bf16[32,2176]{1,0:T(8,128)(2,1)S(1)}, u32[]{:S(2)}, u32[]{:S(2)}) %collective-permute-start.11) | collective-permute-done | bytes 139296 | tf_op jit(solution)/shard_map/ppermute | solution.py:286
  37.4 1.6 %collective-permute-start.8 = (bf16[64,1152]{1,0:T(8,128)(2,1)S(1)}, bf16[64,1152]{1,0:T(8,128)(2,1)S(1)}, u32[]{:S(2)}, u32[]{:S(2)}) collective-permute-start(bf16[64,1152]{1,0:T(8,128)(2,1)S(1)} %get-tuple-element.41), channel_id=1, source_target_pairs={{0,4},{1,3},{2,6},{3,1},{4,0},{5,7},{6,2},{7,5},{8,12},{9,11},{10,... | collective-permute-start | bytes 442376 | tf_op jit(solution)/shard_map/ppermute | solution.py:286
  39.5 6.4 %collective-permute-done.8.refs_1_ = bf16[64,1152]{1,0:T(8,128)(2,1)S(1)} collective-permute-done((bf16[64,1152]{1,0:T(8,128)(2,1)S(1)}, bf16[64,1152]{1,0:T(8,128)(2,1)S(1)}, u32[]{:S(2)}, u32[]{:S(2)}) %collective-permute-start.8) | collective-permute-done | bytes 147488 | tf_op jit(solution)/shard_map/ppermute | solution.py:286
  45.9 1.4 %collective-permute-start.13 = (bf16[32,1152]{1,0:T(8,128)(2,1)S(1)}, bf16[32,1152]{1,0:T(8,128)(2,1)S(1)}, u32[]{:S(2)}, u32[]{:S(2)}) collective-permute-start(bf16[32,1152]{1,0:T(8,128)(2,1)S(1)} %get-tuple-element.45.refs_9_), channel_id=1, source_target_pairs={{0,2},{1,5},{2,0},{3,7},{4,6},{5,1},{6,4},{7,3},{8,10},{9,13},{10,... | collective-permute-start | bytes 221192 | tf_op jit(solution)/shard_map/ppermute | solution.py:286
  47.3 1.7 %expert_kernel.6 = (bf16[64,1152]{1,0:T(8,128)(2,1)S(1)}, bf16[64,1152]{1,0:T(8,128)(2,1)S(1)}, bf16[2,64,768]{2,1,0:T(8,128)(2,1)S(1)}, bf16[2,64,384]{2,1,0:T(8,128)(2,1)S(1)}) custom-call(s32[2]{0:T(128)S(1)} %pad_add_fusion.refs_0_, bf16[64,2176]{1,0:T(8,128)(2,1)S(1)} %join_kernel.6.refs_1_.refs_9_, ...), custom_call_target="tpu_custom_call" | custom-call | tf_op jit(solution)/shard_map/expert_kernel/pallas_call | solution.py:245
  49.6 1.4 %collective-permute-done.13.refs_1_ = bf16[32,1152]{1,0:T(8,128)(2,1)S(1)} collective-permute-done((bf16[32,1152]{1,0:T(8,128)(2,1)S(1)}, bf16[32,1152]{1,0:T(8,128)(2,1)S(1)}, u32[]{:S(2)}, u32[]{:S(2)}) %collective-permute-start.13) | collective-permute-done | bytes 73760 | tf_op jit(solution)/shard_map/ppermute | solution.py:286
  51.0 1.8 %expert_kernel.7 = (bf16[64,1152]{1,0:T(8,128)(2,1)S(1)}, bf16[64,1152]{1,0:T(8,128)(2,1)S(1)}, bf16[2,64,768]{2,1,0:T(8,128)(2,1)S(1)}, bf16[2,64,384]{2,1,0:T(8,128)(2,1)S(1)}) custom-call(s32[2]{0:T(128)S(1)} %pad_add_fusion.refs_0_, bf16[64,2176]{1,0:T(8,128)(2,1)S(1)} %join_kernel.7.refs_2_.refs_1_.refs_13_, ...), custom_call_target="tpu_custom_call" | custom-call | tf_op jit(solution)/shard_map/expert_kernel/pallas_call | solution.py:245
  53.1 1.1 %collective-permute-start.16 = (bf16[32,1152]{1,0:T(8,128)(2,1)S(1)}, bf16[32,1152]{1,0:T(8,128)(2,1)S(1)}, u32[]{:S(2)}, u32[]{:S(2)}) collective-permute-start(bf16[32,1152]{1,0:T(8,128)(2,1)S(1)} %get-tuple-element.49.refs_2_), channel_id=1, source_target_pairs={{0,2},{1,5},{2,0},{3,7},{4,6},{5,1},{6,4},{7,3},{8,10},{9,13},{10,... | collective-permute-start | bytes 221192 | tf_op jit(solution)/shard_map/ppermute | solution.py:286
  54.1 3.3 %collective-permute-done.16.refs_1_ = bf16[32,1152]{1,0:T(8,128)(2,1)S(1)} collective-permute-done((bf16[32,1152]{1,0:T(8,128)(2,1)S(1)}, bf16[32,1152]{1,0:T(8,128)(2,1)S(1)}, u32[]{:S(2)}, u32[]{:S(2)}) %collective-permute-start.16) | collective-permute-done | bytes 73760 | tf_op jit(solution)/shard_map/ppermute | solution.py:286
  57.5 1.1 %collective-permute-start.20 = (bf16[32,1152]{1,0:T(8,128)(2,1)S(1)}, bf16[32,1152]{1,0:T(8,128)(2,1)S(1)}, u32[]{:S(2)}, u32[]{:S(2)}) collective-permute-start(bf16[32,1152]{1,0:T(8,128)(2,1)S(1)} %get-tuple-element.55.refs_2_), channel_id=1, source_target_pairs={{0,2},{1,5},{2,0},{3,7},{4,6},{5,1},{6,4},{7,3},{8,10},{9,13},{10,... | collective-permute-start | bytes 221192 | tf_op jit(solution)/shard_map/ppermute | solution.py:286
  58.6 1.9 %collective-permute-start.18 = (bf16[32,1152]{1,0:T(8,128)(2,1)S(1)}, bf16[32,1152]{1,0:T(8,128)(2,1)S(1)}, u32[]{:S(2)}, u32[]{:S(2)}) collective-permute-start(bf16[32,1152]{1,0:T(8,128)(2,1)S(1)} %add_kernel.7.refs_2_), channel_id=1, source_target_pairs={{0,8},{1,9},{2,10},{3,11},{4,12},{5,13},{6,14},{7,15},{8,0},{9,1},... | collective-permute-start | bytes 221192 | tf_op jit(solution)/shard_map/ppermute | solution.py:286
  60.6 1.2 %collective-permute-start.23 = (bf16[32,1152]{1,0:T(8,128)(2,1)S(1)}, bf16[32,1152]{1,0:T(8,128)(2,1)S(1)}, u32[]{:S(2)}, u32[]{:S(2)}) collective-permute-start(bf16[32,1152]{1,0:T(8,128)(2,1)S(1)} %get-tuple-element.58.refs_2_), channel_id=1, source_target_pairs={{0,2},{1,5},{2,0},{3,7},{4,6},{5,1},{6,4},{7,3},{8,10},{9,13},{10,... | collective-permute-start | bytes 221192 | tf_op jit(solution)/shard_map/ppermute | solution.py:286
  62.0 1.7 %collective-permute-start.22 = (bf16[32,1152]{1,0:T(8,128)(2,1)S(1)}, bf16[32,1152]{1,0:T(8,128)(2,1)S(1)}, u32[]{:S(2)}, u32[]{:S(2)}) collective-permute-start(bf16[32,1152]{1,0:T(8,128)(2,1)S(1)} %add_kernel.8.refs_2_), channel_id=1, source_target_pairs={{0,16},{1,17},{2,18},{3,19},{4,20},{5,21},{6,22},{7,23},{8,24},{9,... | collective-permute-start | bytes 221192 | tf_op jit(solution)/shard_map/ppermute | solution.py:286
  63.7 1.3 %collective-permute-done.23.refs_1_ = bf16[32,1152]{1,0:T(8,128)(2,1)S(1)} collective-permute-done((bf16[32,1152]{1,0:T(8,128)(2,1)S(1)}, bf16[32,1152]{1,0:T(8,128)(2,1)S(1)}, u32[]{:S(2)}, u32[]{:S(2)}) %collective-permute-start.23) | collective-permute-done | bytes 73760 | tf_op jit(solution)/shard_map/ppermute | solution.py:286
  65.0 1.6 %collective-permute-start.24 = (bf16[32,1152]{1,0:T(8,128)(2,1)S(1)}, bf16[32,1152]{1,0:T(8,128)(2,1)S(1)}, u32[]{:S(2)}, u32[]{:S(2)}) collective-permute-start(bf16[32,1152]{1,0:T(8,128)(2,1)S(1)} %add_kernel.10.refs_17_), channel_id=1, source_target_pairs={{0,24},{1,25},{2,26},{3,27},{4,28},{5,29},{6,30},{7,31},{8,16},{9,... | collective-permute-start | bytes 221192 | tf_op jit(solution)/shard_map/ppermute | solution.py:286
  66.6 2.4 %weight_kernel.1 = (f32[512,768]{1,0:T(8,128)S(1)}, f32[384,512]{1,0:T(8,128)S(1)}, bf16[512,384]{1,0:T(8,128)(2,1)S(1)}, bf16[512,384]{1,0:T(8,128)(2,1)S(1)}, bf16[384,512]{1,0:T(8,128)(2,1)S(1)}) custom-call(s32[2]{0:T(128)S(1)} %pad_add_fusion.refs_0_, bf16[64,2176]{1,0:T(8,128)(2,1)S(1)} %join_kernel.4.refs_2_.refs_1_, ...), custom_call_target="tpu_custom_call" | custom-call | tf_op jit(solution)/shard_map/weight_kernel/pallas_call | solution.py:245
  69.8 1.4 %collective-permute-done.24.refs_2_ = bf16[32,1152]{1,0:T(8,128)(2,1)S(1)} collective-permute-done((bf16[32,1152]{1,0:T(8,128)(2,1)S(1)}, bf16[32,1152]{1,0:T(8,128)(2,1)S(1)}, u32[]{:S(2)}, u32[]{:S(2)}) %collective-permute-start.24) | collective-permute-done | bytes 73760 | tf_op jit(solution)/shard_map/ppermute | solution.py:286
  71.2 1.4 %finish_kernel.1 = (bf16[32,1024]{1,0:T(8,128)(2,1)}, bf16[8,32]{1,0:T(8,128)(2,1)}, f32[8,128]{1,0:T(8,128)S(1)}) custom-call(s32[2]{0:T(128)S(1)} %pad_add_fusion.refs_0_, f32[32,1152]{1,0:T(8,128)S(1)} %add_kernel.11.refs_1_.refs_4_, bf16[32,1152]{1,0:T(8,128)(2,1)S(1)} %collective-permute-done.24.refs_2_, s32[8,32]{1,0:T(8,128)S(1)} %bitcast.27, ...), custom_call_target="tpu_custom_call" | custom-call | flops 6000000000 | tf_op jit(solution)/shard_map/finish_kernel/pallas_call | solution.py:245
  72.6 1.2 %settle_kernel.1 = (bf16[512,384]{1,0:T(8,128)(2,1)}, bf16[512,384]{1,0:T(8,128)(2,1)}, bf16[384,512]{1,0:T(8,128)(2,1)}) custom-call(f32[512,768]{1,0:T(8,128)S(1)} %get-tuple-element.67.refs_0_, f32[384,512]{1,0:T(8,128)S(1)} %get-tuple-element.68.refs_1_, bf16[512,384]{1,0:T(8,128)(2,1)S(1)} %collective-permute-done.25.refs_2_, ...), custom_call_target="tpu_custom_call" | custom-call | tf_op jit(solution)/shard_map/settle_kernel/pallas_call | solution.py:245
  (57 shorter events, 8.1 us)
Async XLA Ops:
  0.6 25.2 %copy-start = (bf16[1,512,384]{2,1,0:T(8,128)(2,1)S(1)}, bf16[1,512,384]{2,1,0:T(8,128)(2,1)}, u32[]{:S(2)}) copy-start(bf16[1,512,384]{2,1,0:T(8,128)(2,1)} %param.11) | copy-start | bytes 1179652
  0.6 25.2 %copy-start.1 = (bf16[1,512,384]{2,1,0:T(8,128)(2,1)S(1)}, bf16[1,512,384]{2,1,0:T(8,128)(2,1)}, u32[]{:S(2)}) copy-start(bf16[1,512,384]{2,1,0:T(8,128)(2,1)} %param.12) | copy-start | bytes 1179652
  0.7 25.2 %copy-start.2 = (bf16[1,384,512]{2,1,0:T(8,128)(2,1)S(1)}, bf16[1,384,512]{2,1,0:T(8,128)(2,1)}, u32[]{:S(2)}) copy-start(bf16[1,384,512]{2,1,0:T(8,128)(2,1)} %param.13) | copy-start | bytes 1179652
  1.7 6.8 %collective-permute-start.6 = (bf16[32,2176]{1,0:T(8,128)(2,1)S(1)}, bf16[32,2176]{1,0:T(8,128)(2,1)S(1)}, u32[]{:S(2)}, u32[]{:S(2)}) collective-permute-start(bf16[32,2176]{1,0:T(8,128)(2,1)S(1)} %prepare_kernel.1.refs_0_), channel_id=1, source_target_pairs={{0,8},{1,9},{2,10},{3,11},{4,12},{5,13},{6,14},{7,15},{8,0},{9,1},... | collective-permute-start | bytes 417800 | tf_op jit(solution)/shard_map/ppermute | solution.py:286
  4.8 15.9 %collective-permute-start.2 = (bf16[512,384]{1,0:T(8,128)(2,1)}, bf16[512,384]{1,0:T(8,128)(2,1)S(1)}, u32[]{:S(2)}, u32[]{:S(2)}) collective-permute-start(bf16[512,384]{1,0:T(8,128)(2,1)} %bitcast.11), channel_id=1, source_target_pairs={{0,1},{1,0},{2,3},{3,2},{4,5},{5,4},{6,7},{7,6},{8,9},{9,8},{10,11... | collective-permute-start | bytes 1179656 | tf_op jit(solution)/shard_map/ppermute | solution.py:21
  4.8 17.4 %collective-permute-start.3 = (bf16[512,384]{1,0:T(8,128)(2,1)}, bf16[512,384]{1,0:T(8,128)(2,1)S(1)}, u32[]{:S(2)}, u32[]{:S(2)}) collective-permute-start(bf16[512,384]{1,0:T(8,128)(2,1)} %bitcast.16), channel_id=1, source_target_pairs={{0,1},{1,0},{2,3},{3,2},{4,5},{5,4},{6,7},{7,6},{8,9},{9,8},{10,11... | collective-permute-start | bytes 1179656 | tf_op jit(solution)/shard_map/ppermute | solution.py:21
  5.3 5.1 %collective-permute-start = (bf16[32,2176]{1,0:T(8,128)(2,1)S(1)}, bf16[32,2176]{1,0:T(8,128)(2,1)S(1)}, u32[]{:S(2)}, u32[]{:S(2)}) collective-permute-start(bf16[32,2176]{1,0:T(8,128)(2,1)S(1)} %prepare_kernel.1.refs_0_), channel_id=1, source_target_pairs={{0,2},{1,5},{2,0},{3,7},{4,6},{5,1},{6,4},{7,3},{8,10},{9,13},{10,... | collective-permute-start | bytes 417800 | tf_op jit(solution)/shard_map/ppermute | solution.py:286
  8.5 5.1 %collective-permute-start.7 = (bf16[32,2176]{1,0:T(8,128)(2,1)S(1)}, bf16[32,2176]{1,0:T(8,128)(2,1)S(1)}, u32[]{:S(2)}, u32[]{:S(2)}) collective-permute-start(bf16[32,2176]{1,0:T(8,128)(2,1)S(1)} %collective-permute-done.6.refs_0_), channel_id=1, source_target_pairs={{0,2},{1,5},{2,0},{3,7},{4,6},{5,1},{6,4},{7,3},{8,10},{9,13},{10,... | collective-permute-start | bytes 417800 | tf_op jit(solution)/shard_map/ppermute | solution.py:286
  10.1 15.7 %collective-permute-start.4 = (bf16[384,512]{1,0:T(8,128)(2,1)}, bf16[384,512]{1,0:T(8,128)(2,1)S(1)}, u32[]{:S(2)}, u32[]{:S(2)}) collective-permute-start(bf16[384,512]{1,0:T(8,128)(2,1)} %bitcast.21), channel_id=1, source_target_pairs={{0,1},{1,0},{2,3},{3,2},{4,5},{5,4},{6,7},{7,6},{8,9},{9,8},{10,11... | collective-permute-start | bytes 1179656 | tf_op jit(solution)/shard_map/ppermute | solution.py:21
  10.4 9.7 %collective-permute-start.5 = (bf16[32,2176]{1,0:T(8,128)(2,1)S(1)}, bf16[32,2176]{1,0:T(8,128)(2,1)S(1)}, u32[]{:S(2)}, u32[]{:S(2)}) collective-permute-start(bf16[32,2176]{1,0:T(8,128)(2,1)S(1)} %prepare_kernel.1.refs_0_), channel_id=1, source_target_pairs={{0,16},{1,17},{2,18},{3,19},{4,20},{5,21},{6,22},{7,23},{8,24},{9,... | collective-permute-start | bytes 417800 | tf_op jit(solution)/shard_map/ppermute | solution.py:286
  13.5 12.3 %collective-permute-start.1 = (bf16[64,2176]{1,0:T(8,128)(2,1)S(1)}, bf16[64,2176]{1,0:T(8,128)(2,1)S(1)}, u32[]{:S(2)}, u32[]{:S(2)}) collective-permute-start(bf16[64,2176]{1,0:T(8,128)(2,1)S(1)} %join_kernel.4.refs_2_.refs_1_), channel_id=1, source_target_pairs={{0,4},{1,3},{2,6},{3,1},{4,0},{5,7},{6,2},{7,5},{8,12},{9,11},{10,... | collective-permute-start | bytes 835592 | tf_op jit(solution)/shard_map/ppermute | solution.py:286
  20.1 7.5 %collective-permute-start.10 = (bf16[32,2176]{1,0:T(8,128)(2,1)S(1)}, bf16[32,2176]{1,0:T(8,128)(2,1)}, u32[]{:S(2)}, u32[]{:S(2)}) collective-permute-start(bf16[32,2176]{1,0:T(8,128)(2,1)S(1)} %pass_kernel.2.refs_9_.refs_0_), channel_id=1, source_target_pairs={{0,2},{1,5},{2,0},{3,7},{4,6},{5,1},{6,4},{7,3},{8,10},{9,13},{10,... | collective-permute-start | bytes 417800 | tf_op jit(solution)/shard_map/ppermute | solution.py:286
  20.7 11.6 %collective-permute-start.12 = (bf16[64,2176]{1,0:T(8,128)(2,1)S(1)}, bf16[64,2176]{1,0:T(8,128)(2,1)}, u32[]{:S(2)}, u32[]{:S(2)}) collective-permute-start(bf16[64,2176]{1,0:T(8,128)(2,1)S(1)} %join_kernel.5.refs_1_.refs_5_), channel_id=1, source_target_pairs={{0,4},{1,3},{2,6},{3,1},{4,0},{5,7},{6,2},{7,5},{8,12},{9,11},{10,... | collective-permute-start | bytes 835592 | tf_op jit(solution)/shard_map/ppermute | solution.py:286
  22.2 7.0 %collective-permute-start.9 = (bf16[32,2176]{1,0:T(8,128)(2,1)S(1)}, bf16[32,2176]{1,0:T(8,128)(2,1)}, u32[]{:S(2)}, u32[]{:S(2)}) collective-permute-start(bf16[32,2176]{1,0:T(8,128)(2,1)S(1)} %prepare_kernel.1.refs_0_), channel_id=1, source_target_pairs={{0,24},{1,25},{2,26},{3,27},{4,28},{5,29},{6,30},{7,31},{8,16},{9,... | collective-permute-start | bytes 417800 | tf_op jit(solution)/shard_map/ppermute | solution.py:286
  30.2 6.7 %collective-permute-start.11 = (bf16[32,2176]{1,0:T(8,128)(2,1)S(1)}, bf16[32,2176]{1,0:T(8,128)(2,1)S(1)}, u32[]{:S(2)}, u32[]{:S(2)}) collective-permute-start(bf16[32,2176]{1,0:T(8,128)(2,1)S(1)} %pass_kernel.3.refs_9_.refs_0_), channel_id=1, source_target_pairs={{0,2},{1,5},{2,0},{3,7},{4,6},{5,1},{6,4},{7,3},{8,10},{9,13},{10,... | collective-permute-start | bytes 417800 | tf_op jit(solution)/shard_map/ppermute | solution.py:286
  31.8 15.6 %collective-permute-start.15 = (bf16[64,2176]{1,0:T(8,128)(2,1)S(1)}, bf16[64,2176]{1,0:T(8,128)(2,1)S(1)}, u32[]{:S(2)}, u32[]{:S(2)}) collective-permute-start(bf16[64,2176]{1,0:T(8,128)(2,1)S(1)} %join_kernel.6.refs_1_.refs_9_), channel_id=1, source_target_pairs={{0,4},{1,3},{2,6},{3,1},{4,0},{5,7},{6,2},{7,5},{8,12},{9,11},{10,... | collective-permute-start | bytes 835592 | tf_op jit(solution)/shard_map/ppermute | solution.py:286
  36.9 14.1 %collective-permute-start.17 = (bf16[64,2176]{1,0:T(8,128)(2,1)S(1)}, bf16[64,2176]{1,0:T(8,128)(2,1)S(1)}, u32[]{:S(2)}, u32[]{:S(2)}) collective-permute-start(bf16[64,2176]{1,0:T(8,128)(2,1)S(1)} %join_kernel.7.refs_2_.refs_1_.refs_13_), channel_id=1, source_target_pairs={{0,4},{1,3},{2,6},{3,1},{4,0},{5,7},{6,2},{7,5},{8,12},{9,11},{10,... | collective-permute-start | bytes 835592 | tf_op jit(solution)/shard_map/ppermute | solution.py:286
  37.4 8.4 %collective-permute-start.8 = (bf16[64,1152]{1,0:T(8,128)(2,1)S(1)}, bf16[64,1152]{1,0:T(8,128)(2,1)S(1)}, u32[]{:S(2)}, u32[]{:S(2)}) collective-permute-start(bf16[64,1152]{1,0:T(8,128)(2,1)S(1)} %get-tuple-element.41), channel_id=1, source_target_pairs={{0,4},{1,3},{2,6},{3,1},{4,0},{5,7},{6,2},{7,5},{8,12},{9,11},{10,... | collective-permute-start | bytes 442376 | tf_op jit(solution)/shard_map/ppermute | solution.py:286
  39.0 10.6 %collective-permute-start.14 = (bf16[64,1152]{1,0:T(8,128)(2,1)S(1)}, bf16[64,1152]{1,0:T(8,128)(2,1)S(1)}, u32[]{:S(2)}, u32[]{:S(2)}) collective-permute-start(bf16[64,1152]{1,0:T(8,128)(2,1)S(1)} %get-tuple-element.47), channel_id=1, source_target_pairs={{0,4},{1,3},{2,6},{3,1},{4,0},{5,7},{6,2},{7,5},{8,12},{9,11},{10,... | collective-permute-start | bytes 442376 | tf_op jit(solution)/shard_map/ppermute | solution.py:286
  45.9 5.0 %collective-permute-start.13 = (bf16[32,1152]{1,0:T(8,128)(2,1)S(1)}, bf16[32,1152]{1,0:T(8,128)(2,1)S(1)}, u32[]{:S(2)}, u32[]{:S(2)}) collective-permute-start(bf16[32,1152]{1,0:T(8,128)(2,1)S(1)} %get-tuple-element.45.refs_9_), channel_id=1, source_target_pairs={{0,2},{1,5},{2,0},{3,7},{4,6},{5,1},{6,4},{7,3},{8,10},{9,13},{10,... | collective-permute-start | bytes 221192 | tf_op jit(solution)/shard_map/ppermute | solution.py:286
  49.1 8.4 %collective-permute-start.19 = (bf16[64,1152]{1,0:T(8,128)(2,1)S(1)}, bf16[64,1152]{1,0:T(8,128)(2,1)S(1)}, u32[]{:S(2)}, u32[]{:S(2)}) collective-permute-start(bf16[64,1152]{1,0:T(8,128)(2,1)S(1)} %get-tuple-element.53), channel_id=1, source_target_pairs={{0,4},{1,3},{2,6},{3,1},{4,0},{5,7},{6,2},{7,5},{8,12},{9,11},{10,... | collective-permute-start | bytes 442376 | tf_op jit(solution)/shard_map/ppermute | solution.py:286
  52.8 7.8 %collective-permute-start.21 = (bf16[64,1152]{1,0:T(8,128)(2,1)S(1)}, bf16[64,1152]{1,0:T(8,128)(2,1)S(1)}, u32[]{:S(2)}, u32[]{:S(2)}) collective-permute-start(bf16[64,1152]{1,0:T(8,128)(2,1)S(1)} %get-tuple-element.57), channel_id=1, source_target_pairs={{0,4},{1,3},{2,6},{3,1},{4,0},{5,7},{6,2},{7,5},{8,12},{9,11},{10,... | collective-permute-start | bytes 442376 | tf_op jit(solution)/shard_map/ppermute | solution.py:286
  53.1 4.4 %collective-permute-start.16 = (bf16[32,1152]{1,0:T(8,128)(2,1)S(1)}, bf16[32,1152]{1,0:T(8,128)(2,1)S(1)}, u32[]{:S(2)}, u32[]{:S(2)}) collective-permute-start(bf16[32,1152]{1,0:T(8,128)(2,1)S(1)} %get-tuple-element.49.refs_2_), channel_id=1, source_target_pairs={{0,2},{1,5},{2,0},{3,7},{4,6},{5,1},{6,4},{7,3},{8,10},{9,13},{10,... | collective-permute-start | bytes 221192 | tf_op jit(solution)/shard_map/ppermute | solution.py:286
  57.5 4.4 %collective-permute-start.20 = (bf16[32,1152]{1,0:T(8,128)(2,1)S(1)}, bf16[32,1152]{1,0:T(8,128)(2,1)S(1)}, u32[]{:S(2)}, u32[]{:S(2)}) collective-permute-start(bf16[32,1152]{1,0:T(8,128)(2,1)S(1)} %get-tuple-element.55.refs_2_), channel_id=1, source_target_pairs={{0,2},{1,5},{2,0},{3,7},{4,6},{5,1},{6,4},{7,3},{8,10},{9,13},{10,... | collective-permute-start | bytes 221192 | tf_op jit(solution)/shard_map/ppermute | solution.py:286
  58.6 5.0 %collective-permute-start.18 = (bf16[32,1152]{1,0:T(8,128)(2,1)S(1)}, bf16[32,1152]{1,0:T(8,128)(2,1)S(1)}, u32[]{:S(2)}, u32[]{:S(2)}) collective-permute-start(bf16[32,1152]{1,0:T(8,128)(2,1)S(1)} %add_kernel.7.refs_2_), channel_id=1, source_target_pairs={{0,8},{1,9},{2,10},{3,11},{4,12},{5,13},{6,14},{7,15},{8,0},{9,1},... | collective-permute-start | bytes 221192 | tf_op jit(solution)/shard_map/ppermute | solution.py:286
  60.6 4.4 %collective-permute-start.23 = (bf16[32,1152]{1,0:T(8,128)(2,1)S(1)}, bf16[32,1152]{1,0:T(8,128)(2,1)S(1)}, u32[]{:S(2)}, u32[]{:S(2)}) collective-permute-start(bf16[32,1152]{1,0:T(8,128)(2,1)S(1)} %get-tuple-element.58.refs_2_), channel_id=1, source_target_pairs={{0,2},{1,5},{2,0},{3,7},{4,6},{5,1},{6,4},{7,3},{8,10},{9,13},{10,... | collective-permute-start | bytes 221192 | tf_op jit(solution)/shard_map/ppermute | solution.py:286
  62.0 7.8 %collective-permute-start.22 = (bf16[32,1152]{1,0:T(8,128)(2,1)S(1)}, bf16[32,1152]{1,0:T(8,128)(2,1)S(1)}, u32[]{:S(2)}, u32[]{:S(2)}) collective-permute-start(bf16[32,1152]{1,0:T(8,128)(2,1)S(1)} %add_kernel.8.refs_2_), channel_id=1, source_target_pairs={{0,16},{1,17},{2,18},{3,19},{4,20},{5,21},{6,22},{7,23},{8,24},{9,... | collective-permute-start | bytes 221192 | tf_op jit(solution)/shard_map/ppermute | solution.py:286
  65.0 6.2 %collective-permute-start.24 = (bf16[32,1152]{1,0:T(8,128)(2,1)S(1)}, bf16[32,1152]{1,0:T(8,128)(2,1)S(1)}, u32[]{:S(2)}, u32[]{:S(2)}) collective-permute-start(bf16[32,1152]{1,0:T(8,128)(2,1)S(1)} %add_kernel.10.refs_17_), channel_id=1, source_target_pairs={{0,24},{1,25},{2,26},{3,27},{4,28},{5,29},{6,30},{7,31},{8,16},{9,... | collective-permute-start | bytes 221192 | tf_op jit(solution)/shard_map/ppermute | solution.py:286
  66.6 4.6 %copy-start.3 = (s32[32,8]{0,1:T(8,128)S(1)}, s32[32,8]{0,1:T(8,128)}, u32[]{:S(2)}) copy-start(s32[32,8]{0,1:T(8,128)} %param.9) | copy-start | bytes 3076
  69.1 3.5 %collective-permute-start.25 = (bf16[512,384]{1,0:T(8,128)(2,1)S(1)}, bf16[512,384]{1,0:T(8,128)(2,1)S(1)}, u32[]{:S(2)}, u32[]{:S(2)}) collective-permute-start(bf16[512,384]{1,0:T(8,128)(2,1)S(1)} %get-tuple-element.69), channel_id=1, source_target_pairs={{0,1},{1,0},{2,3},{3,2},{4,5},{5,4},{6,7},{7,6},{8,9},{9,8},{10,11... | collective-permute-start | bytes 1179656 | tf_op jit(solution)/shard_map/ppermute | solution.py:21
  69.2 3.4 %collective-permute-start.26 = (bf16[512,384]{1,0:T(8,128)(2,1)S(1)}, bf16[512,384]{1,0:T(8,128)(2,1)S(1)}, u32[]{:S(2)}, u32[]{:S(2)}) collective-permute-start(bf16[512,384]{1,0:T(8,128)(2,1)S(1)} %get-tuple-element.70), channel_id=1, source_target_pairs={{0,1},{1,0},{2,3},{3,2},{4,5},{5,4},{6,7},{7,6},{8,9},{9,8},{10,11... | collective-permute-start | bytes 1179656 | tf_op jit(solution)/shard_map/ppermute | solution.py:21
  69.7 2.9 %collective-permute-start.27 = (bf16[384,512]{1,0:T(8,128)(2,1)S(1)}, bf16[384,512]{1,0:T(8,128)(2,1)S(1)}, u32[]{:S(2)}, u32[]{:S(2)}) collective-permute-start(bf16[384,512]{1,0:T(8,128)(2,1)S(1)} %get-tuple-element.64.refs_2_), channel_id=1, source_target_pairs={{0,1},{1,0},{2,3},{3,2},{4,5},{5,4},{6,7},{7,6},{8,9},{9,8},{10,11... | collective-permute-start | bytes 1179656 | tf_op jit(solution)/shard_map/ppermute | solution.py:21

commit v6 on v5

--- a/solution.py
+++ b/solution.py
@@ -82,8 +82,8 @@
 def split_kernel(kept, got, keep, give):
     rows = keep.shape[0]
     upper, lower = pl.ds(0, rows), pl.ds(rows, rows)
-    give[...] = (kept[lower, :].astype(F32) + got[lower, :].astype(F32)).astype(BF16)
-    keep[...] = kept[upper, :].astype(F32) + got[upper, :].astype(F32)
+    give[...] = (kept[lower, :].astype(F32) + got[lower, :].astype(F32)).astype(give.dtype)
+    keep[...] = (kept[upper, :].astype(F32) + got[upper, :].astype(F32)).astype(keep.dtype)
 
 
 def add_kernel(kept, got, total):
@@ -95,76 +95,61 @@
 
 
 def expert_kernel(
-    place, first, second, gate_own, gate_other, up_own, up_other, down_own, down_other,
-    keep, give, grads, scaled_hidden,
+    place, block, gate_own, gate_other, up_own, up_other, down_own, down_other,
+    row_grads, grads, scaled_hidden,
 ):
     half, width = gate_own.shape
     features = 2 * half
-    lanes = first.shape[1] - 2 * features
+    lanes = block.shape[1] - 2 * features
     own, other = own_other(place, half)
     dys_own, dys_other = own_other(place, half, features)
 
     def step(at):
-        count = at.size
-
-        def take(cols):
-            return jnp.concatenate([first[at, cols], second[at, cols]], 0)
-
-        mine, rest = take(own), take(other)
+        mine, rest = block[at, own], block[at, other]
         pre_gate = dot(mine, gate_own[...], NN) + dot(rest, gate_other[...], NN)
         pre_up = dot(mine, up_own[...], NN) + dot(rest, up_other[...], NN)
-        back = dot(take(dys_own), down_own[...], NT) + dot(take(dys_other), down_other[...], NT)
+        back = dot(block[at, dys_own], down_own[...], NT)
+        back = back + dot(block[at, dys_other], down_other[...], NT)
         sig = jax.nn.sigmoid(pre_gate)
         active = pre_gate * sig
         slope = sig * (1.0 + pre_gate * (1.0 - sig))
         hidden = active * pre_up
-        lane = lax.broadcasted_iota(jnp.int32, (2 * count, lanes), 1)
+        lane = lax.broadcasted_iota(jnp.int32, (back.shape[0], lanes), 1)
         is_own = lane == place[1]
-        gates = jnp.where(is_own, take(pl.ds(2 * features, lanes)).astype(F32), 0.0)
+        gates = jnp.where(is_own, block[at, pl.ds(2 * features, lanes)].astype(F32), 0.0)
         gates = jnp.sum(gates, 1, keepdims=True)
         gate_grads = jnp.sum(hidden * back, 1, keepdims=True)
         back = back * gates
         grad_gate = (back * pre_up * slope).astype(BF16)
         grad_up = (back * active).astype(BF16)
-        scaled = (hidden * gates).astype(BF16)
-        pieces = (
-            dot(grad_gate, gate_own[...], NT) + dot(grad_up, up_own[...], NT),
-            dot(grad_gate, gate_other[...], NT) + dot(grad_up, up_other[...], NT),
-            jnp.where(is_own, gate_grads, 0.0),
-        )
-        begin = 0
-        for piece in pieces:
-            cols = pl.ds(begin, piece.shape[1])
-            give[at, cols] = piece[count:].astype(BF16)
-            keep[at, cols] = piece[:count].astype(BF16)
-            begin += piece.shape[1]
-        for i in range(2):
-            part = slice(i * count, (i + 1) * count)
-            grads[i, at, pl.ds(0, width)] = grad_gate[part]
-            grads[i, at, pl.ds(width, width)] = grad_up[part]
-            scaled_hidden[i, at, :] = scaled[part]
-
-    for_chunks(first.shape[0], step)
+        row_grads[at, pl.ds(0, half)] = (
+            dot(grad_gate, gate_own[...], NT) + dot(grad_up, up_own[...], NT)
+        ).astype(BF16)
+        row_grads[at, pl.ds(half, half)] = (
+            dot(grad_gate, gate_other[...], NT) + dot(grad_up, up_other[...], NT)
+        ).astype(BF16)
+        row_grads[at, pl.ds(features, lanes)] = jnp.where(is_own, gate_grads, 0.0).astype(BF16)
+        grads[at, pl.ds(0, width)] = grad_gate
+        grads[at, pl.ds(width, width)] = grad_up
+        scaled_hidden[at, :] = (hidden * gates).astype(BF16)
+
+    for_chunks(block.shape[0], step)
 
 
 def weight_kernel(place, *refs):
     keep_in, keep_down, give_gate, give_up, give_down = refs[-5:]
-    pieces = [refs[i : i + 4] for i in range(0, len(refs) - 5, 4)]
+    parts = [refs[i : i + 3] for i in range(0, len(refs) - 5, 3)]
     half, width = give_gate.shape
-    count = pieces[0][0].shape[0]
+    count = parts[0][0].shape[0]
     own, other = own_other(place, half)
     dys_own, dys_other = own_other(place, half, 2 * half)
     left, right = pl.ds(0, width), pl.ds(width, width)
-    parts = [(p[i], p[2].at[i], p[3].at[i]) for p in pieces for i in range(2)]
 
     def products(parts, at, cols, dys_cols):
-        def gathered(values):
-            return values[0] if len(values) == 1 else jnp.concatenate(values, 0)
-
-        rows = gathered([p[0][at, cols] for p in parts])
-        dys = gathered([p[0][at, dys_cols] for p in parts])
-        grads = gathered([p[1][at, :] for p in parts])
-        hidden = gathered([p[2][at, :] for p in parts])
+        rows = jnp.concatenate([p[0][at, cols] for p in parts], 0)
+        dys = jnp.concatenate([p[0][at, dys_cols] for p in parts], 0)
+        grads = jnp.concatenate([p[1][at, :] for p in parts], 0)
+        hidden = jnp.concatenate([p[2][at, :] for p in parts], 0)
         return dot(rows, grads, TN), dot(hidden, dys, TN)
 
     def hand_over(into, down):
@@ -222,9 +207,9 @@
     grad_gates[...] = out.astype(BF16)
 
 
-def call(kernel, outs, place, *args, after=(), small=True, arrives=0, leaves=0, flops=0):
+def call(kernel, outs, place, *args, after=(), small=True, arrives=0, leaves=0, flops=0, limit=2):
     used = len(args)
-    limit = 10 * 2**20 if small else 56 * 2**20
+    limit = (limit if small else 56) * 2**20
     if small:
         args = [
             pltpu.with_memory_space_constraint(x, pltpu.VMEM) if i < used - arrives else x
@@ -314,78 +299,65 @@
     for step in steps[:far]:
         block = jnp.concatenate([block, exchange(block, step)], 0)
 
-    offsets = (0, up_one, up_two, up_one ^ up_two)
-    sources = [block] + [exchange(block, (offset, offset)) for offset in offsets[1:]]
-    count = 2 * block.shape[0]
-    half_shape = (count // 2, features + lanes)
-    full_shape = (count, features + lanes)
+    offsets = (up_two, up_one, up_one ^ up_two)
+    rows = block.shape[0]
+    columns = features + lanes
 
     gate_own, up_own, down_own = gate_half[0], up_half[0], down_half[0]
     gate_other, up_other, down_other = swap_core(gate_own), swap_core(up_own), swap_core(down_own)
     weights = (gate_own, gate_other, up_own, up_other, down_own, down_other)
-
-    second_blocks = {}
-    first, second, kept, got, saved = {}, {}, {}, {}, {}
-    returned = {}
-
-    def send(i, ordered=True):
-        if ordered:
-            (sources[i],) = run(pass_kernel, [(sources[i].shape, BF16)], None, sources[i])
-        second_blocks[i] = exchange(sources[i], near_a)
-
-    def join(i):
-        shape = (count, 2 * features + lanes)
-        (first[i],) = run(join_kernel, [(shape, BF16)], None, sources[i], second_blocks[i])
-        second[i] = exchange(first[i], near_b)
-
-    def expert(i):
-        kept[i], give, grads, hidden = run(
+    saved = []
+
+    def at_offset(x, i):
+        return exchange(x, (offsets[i], offsets[i]))
+
+    def join(first, second):
+        shape = (2 * first.shape[0], first.shape[1])
+        return run(join_kernel, [(shape, BF16)], None, first, second)[0]
+
+    def after_all(x, *others):
+        before.extend(others)
+        return run(pass_kernel, [(x.shape, BF16)], None, x)[0]
+
+    def expert(block):
+        count = block.shape[0]
+        row_grads, grads, hidden = run(
             expert_kernel,
-            [
-                (full_shape, BF16),
-                (full_shape, BF16),
-                ((2, count, 2 * width), BF16),
-                ((2, count, width), BF16),
-            ],
-            place, first[i], second[i], *weights,
+            [((count, columns), BF16), ((count, 2 * width), BF16), ((count, width), BF16)],
+            place, block, *weights, limit=6, flops=6 * 10**9,
         )
-        got[i] = exchange(give, near_b)
-        saved[i] = (first[i], second[i], grads, hidden)
-
-    def split(i):
-        kept[i], give = run(
-            split_kernel, [(half_shape, F32), (half_shape, BF16)], None, kept[i], got[i]
-        )
-        got[i] = exchange(give, near_a)
-
-    def add(i):
-        (give,) = run(add_kernel, [(half_shape, BF16)], None, kept[i], got[i])
-        returned[i] = exchange(give, (offsets[i], offsets[i]))
+        saved.extend([block, grads, hidden])
+        return row_grads
+
+    def split(kept, got, types):
+        shape = (kept.shape[0] // 2, columns)
+        return run(split_kernel, [(shape, t) for t in types], None, kept, got)
 
     def collect(total, part):
-        return run(add_kernel, [(half_shape, F32)], None, total, part)[0]
-
-    send(0, ordered=False)
-    send(1, ordered=False)
-    join(0)
-    join(1)
-    send(2)
-    expert(0)
-    join(2)
-    send(3)
-    expert(1)
-    join(3)
-    split(0)
-    expert(2)
-    split(1)
-    total = collect(kept[0], got[0])
-    expert(3)
-    add(1)
-    split(2)
-    split(3)
-    add(2)
-    total = collect(total, returned[1])
-    add(3)
+        return run(add_kernel, [(total.shape, F32)], None, total, part)[0]
+
+    near_0 = join(block, at_offset(block, 0))
+    near_1 = at_offset(near_0, 1)
+    first_0 = join(near_0, exchange(near_0, near_a))
+    second_0 = exchange(first_0, near_b)
+    near_1 = after_all(near_1)
+    got_near = exchange(near_1, near_a)
+    kept_0 = expert(first_0)
+    first_1 = join(near_1, got_near)
+    second_1 = exchange(first_1, near_b)
+    give_0 = expert(second_0)
+    kept_1 = expert(first_1)
+    got_0 = exchange(after_all(give_0, second_1), near_b)
+    got_1 = exchange(expert(second_1), near_b)
+
+    kept_0, give = split(kept_0, got_0, (F32, BF16))
+    got_0 = exchange(give, near_a)
+    kept_1, give = split(kept_1, got_1, (F32, BF16))
+    got_1 = exchange(give, near_a)
+    total, give = split(kept_0, got_0, (F32, BF16))
+    back_two = at_offset(give, 0)
+    give_one, give_both = split(kept_1, got_1, (BF16, BF16))
+    back_one, back_both = at_offset(give_one, 1), at_offset(give_both, 2)
     keep_in, keep_down, *gives = run(
         weight_kernel,
         [
@@ -395,14 +367,15 @@
             ((half, width), BF16),
             ((width, half), BF16),
         ],
-        place, *saved[0], *saved[1], *saved[2], *saved[3],
+        place, *saved, limit=10,
     )
     gots = [swap_core(give) for give in gives]
-    total = collect(total, returned[2])
-
-    parts = (total, returned[3])
+    total = collect(total, back_two)
+    total = collect(total, back_one)
+
+    parts = (total, back_both)
     if far:
-        total = total + returned[3].astype(F32)
+        total = total + back_both.astype(F32)
         for step in reversed(steps[:far]):
             middle = total.shape[0] // 2
             total = total[:middle] + exchange(total[middle:].astype(BF16), step).astype(F32)
@@ -415,7 +388,7 @@
     grad_gate, grad_up, grad_down = run(
         settle_kernel,
         [((half, width), BF16), ((half, width), BF16), ((width, half), BF16)],
-        None, keep_in, keep_down, *gots, leaves=3,
+        None, keep_in, keep_down, *gots, leaves=3, limit=6,
     )
     return grad_tokens, grad_gates.T, grad_gate[None], grad_up[None], grad_down[None]
 

time: 74 us -> 66.3 us (0.90)
  starting transfers between devices: 32.7 us -> 22.9 us
  waiting for transfers between devices: 24.6 us -> 29.4 us
  Pallas kernels: 15.7 us -> 12.8 us
    ppermute x22 -> x13, starting transfers between devices: 31.5 us -> 21.8 us  [exchange(): return lax.ppermute(x, DEVICES, pairs)]
    ppermute x22 -> x13, waiting for transfers between devices: 24.5 us -> 29.2 us  [exchange(): return lax.ppermute(x, DEVICES, pairs)]
    pallas_call x23 -> x18, Pallas kernels: 14.6 us -> 11.9 us  [call(): pl.pallas_call(run, out_shape=out_shape, in_specs=[pl.BlockSpec(memory_sp...]
  transfers between devices with their start and end apart: 28 -> 19, of which waited for: 12 -> 11; matrix products, arithmetic and copies ran while one was open for 0% -> 0% of each run, Pallas kernels for 18% -> 16%
where the time goes in v6:
time: 66.3 us; the launch traced here: 66.1 us
  waiting for transfers between devices  29.4 us (44%)
  starting transfers between devices  22.9 us (35%)
  Pallas kernels  12.8 us (19%)
  between operations  0.8 us (1%)
    ppermute x13, waiting for transfers between devices, exchange(): return lax.ppermute(x, DEVICES, pairs)  29.2 us
    ppermute x13, starting transfers between devices, exchange(): return lax.ppermute(x, DEVICES, pairs)  21.8 us
    pallas_call x18, Pallas kernels, call(): pl.pallas_call(run, out_shape=out_shape, in_specs=[pl.BlockSpec(memory_sp...  11.9 us
  transfers between devices with their start and end apart: 19, of which 11 were waited for; matrix products, arithmetic and copies ran while one was open for 0% of the time, Pallas kernels for 16%

profile of v6, /device:TPU:0, one launch (start us, length us, event | category | flops | bytes accessed | tf_op | source)
XLA Modules:
  0.0 66.1 jit_solution(3762290833802047089)
XLA Ops:
  0.6 0.9 %prepare_kernel.1.refs_0_ = bf16[32,2176]{1,0:T(8,128)(2,1)S(1)} custom-call(bf16[32,1024]{1,0:T(8,128)(2,1)} %tokens.1, bf16[32,1024]{1,0:T(8,128)(2,1)} %cotangent.1, s32[8,32]{1,0:T(8,128)} %bitcast.11, bf16[8,32]{1,0:T(8,128)(2,1)} %bitcast.28), custom_call_target="tpu_custom_call" | custom-call | tf_op jit(solution)/shard_map/prepare_kernel/pallas_call | solution.py:286
  1.6 4.1 %collective-permute-start = (bf16[32,2176]{1,0:T(8,128)(2,1)S(1)}, bf16[32,2176]{1,0:T(8,128)(2,1)S(1)}, u32[]{:S(2)}, u32[]{:S(2)}) collective-permute-start(bf16[32,2176]{1,0:T(8,128)(2,1)S(1)} %prepare_kernel.1.refs_0_), channel_id=1, source_target_pairs={{0,16},{1,17},{2,18},{3,19},{4,20},{5,21},{6,22},{7,23},{8,24},{9,... | collective-permute-start | bytes 417800 | tf_op jit(solution)/shard_map/ppermute | solution.py:271
  5.7 0.5 collective-permute-start.3
  6.2 6.1 %collective-permute-done.refs_1_ = bf16[32,2176]{1,0:T(8,128)(2,1)S(1)} collective-permute-done((bf16[32,2176]{1,0:T(8,128)(2,1)S(1)}, bf16[32,2176]{1,0:T(8,128)(2,1)S(1)}, u32[]{:S(2)}, u32[]{:S(2)}) %collective-permute-start) | collective-permute-done | bytes 139296 | tf_op jit(solution)/shard_map/ppermute | solution.py:271
  12.4 1.6 %collective-permute-start.1 = (bf16[64,2176]{1,0:T(8,128)(2,1)S(1)}, bf16[64,2176]{1,0:T(8,128)(2,1)S(1)}, u32[]{:S(2)}, u32[]{:S(2)}) collective-permute-start(bf16[64,2176]{1,0:T(8,128)(2,1)S(1)} %join_kernel.3.refs_0_.refs_2_), channel_id=1, source_target_pairs={{0,2},{1,5},{2,0},{3,7},{4,6},{5,1},{6,4},{7,3},{8,10},{9,13},{10,... | collective-permute-start | bytes 835592 | tf_op jit(solution)/shard_map/ppermute | solution.py:271
  14.0 0.7 %collective-permute-start.5 = (bf16[64,2176]{1,0:T(8,128)(2,1)S(1)}, bf16[64,2176]{1,0:T(8,128)(2,1)S(1)}, u32[]{:S(2)}, u32[]{:S(2)}) collective-permute-start(bf16[64,2176]{1,0:T(8,128)(2,1)S(1)} %join_kernel.3.refs_0_.refs_2_), channel_id=1, source_target_pairs={{0,8},{1,9},{2,10},{3,11},{4,12},{5,13},{6,14},{7,15},{8,0},{9,1},... | collective-permute-start | bytes 835592 | tf_op jit(solution)/shard_map/ppermute | solution.py:271
  14.8 4.3 %collective-permute-done.1.refs_1_ = bf16[64,2176]{1,0:T(8,128)(2,1)S(1)} collective-permute-done((bf16[64,2176]{1,0:T(8,128)(2,1)S(1)}, bf16[64,2176]{1,0:T(8,128)(2,1)S(1)}, u32[]{:S(2)}, u32[]{:S(2)}) %collective-permute-start.1) | collective-permute-done | bytes 278560 | tf_op jit(solution)/shard_map/ppermute | solution.py:271
  19.1 1.6 %collective-permute-start.6 = (bf16[128,2176]{1,0:T(8,128)(2,1)S(1)}, bf16[128,2176]{1,0:T(8,128)(2,1)S(1)}, u32[]{:S(2)}, u32[]{:S(2)}) collective-permute-start(bf16[128,2176]{1,0:T(8,128)(2,1)S(1)} %join_kernel.4.refs_1_), channel_id=1, source_target_pairs={{0,4},{1,3},{2,6},{3,1},{4,0},{5,7},{6,2},{7,5},{8,12},{9,11},{10,... | collective-permute-start | bytes 1671176 | tf_op jit(solution)/shard_map/ppermute | solution.py:271
  20.7 0.6 collective-permute-done.5.refs_0_
  21.3 1.6 %collective-permute-start.7 = (bf16[64,2176]{1,0:T(8,128)(2,1)S(1)}, bf16[64,2176]{1,0:T(8,128)(2,1)S(1)}, u32[]{:S(2)}, u32[]{:S(2)}) collective-permute-start(bf16[64,2176]{1,0:T(8,128)(2,1)S(1)} %pass_kernel.2.refs_8_.refs_0_), channel_id=1, source_target_pairs={{0,2},{1,5},{2,0},{3,7},{4,6},{5,1},{6,4},{7,3},{8,10},{9,13},{10,... | collective-permute-start | bytes 835592 | tf_op jit(solution)/shard_map/ppermute | solution.py:271
  22.9 1.8 %expert_kernel.4 = (bf16[128,1152]{1,0:T(8,128)(2,1)S(1)}, bf16[128,768]{1,0:T(8,128)(2,1)S(1)}, bf16[128,384]{1,0:T(8,128)(2,1)S(1)}) custom-call(s32[2]{0:T(128)S(1)} %pad_add_fusion.refs_0_, bf16[128,2176]{1,0:T(8,128)(2,1)S(1)} %join_kernel.4.refs_1_, bf16[512,384]{1,0:T(8,128)(2,1)S(1)} %bitcast.14, ...), custom_call_target="tpu_custom_call" | custom-call | flops 6000000000 | tf_op jit(solution)/shard_map/expert_kernel/pallas_call | solution.py:230
  24.7 4.4 %collective-permute-done.7.refs_1_ = bf16[64,2176]{1,0:T(8,128)(2,1)S(1)} collective-permute-done((bf16[64,2176]{1,0:T(8,128)(2,1)S(1)}, bf16[64,2176]{1,0:T(8,128)(2,1)S(1)}, u32[]{:S(2)}, u32[]{:S(2)}) %collective-permute-start.7) | collective-permute-done | bytes 278560 | tf_op jit(solution)/shard_map/ppermute | solution.py:271
  29.1 1.3 %collective-permute-start.8 = (bf16[128,2176]{1,0:T(8,128)(2,1)S(1)}, bf16[128,2176]{1,0:T(8,128)(2,1)S(1)}, u32[]{:S(2)}, u32[]{:S(2)}) collective-permute-start(bf16[128,2176]{1,0:T(8,128)(2,1)S(1)} %join_kernel.5.refs_8_.refs_1_.refs_7_), channel_id=1, source_target_pairs={{0,4},{1,3},{2,6},{3,1},{4,0},{5,7},{6,2},{7,5},{8,12},{9,11},{10,... | collective-permute-start | bytes 1671176 | tf_op jit(solution)/shard_map/ppermute | solution.py:271
  30.5 0.6 collective-permute-done.6.refs_1_.refs_4_
  31.0 1.8 %expert_kernel.5 = (bf16[128,1152]{1,0:T(8,128)(2,1)S(1)}, bf16[128,768]{1,0:T(8,128)(2,1)S(1)}, bf16[128,384]{1,0:T(8,128)(2,1)S(1)}) custom-call(s32[2]{0:T(128)S(1)} %pad_add_fusion.refs_0_, bf16[128,2176]{1,0:T(8,128)(2,1)S(1)} %collective-permute-done.6.refs_1_.refs_4_, bf16[512,384]{1,0:T(8,128)(2,1)S(1)} %bitcast.15, ...), custom_call_target="tpu_custom_call" | custom-call | flops 6000000000 | tf_op jit(solution)/shard_map/expert_kernel/pallas_call | solution.py:230
  32.8 1.7 %expert_kernel.6 = (bf16[128,1152]{1,0:T(8,128)(2,1)S(1)}, bf16[128,768]{1,0:T(8,128)(2,1)S(1)}, bf16[128,384]{1,0:T(8,128)(2,1)S(1)}) custom-call(s32[2]{0:T(128)S(1)} %pad_add_fusion.refs_0_, bf16[128,2176]{1,0:T(8,128)(2,1)S(1)} %join_kernel.5.refs_8_.refs_1_.refs_7_, bf16[512,384]{1,0:T(8,128)(2,1)S(1)} %bitcast.16, ...), custom_call_target="tpu_custom_call" | custom-call | flops 6000000000 | tf_op jit(solution)/shard_map/expert_kernel/pallas_call | solution.py:230
  34.6 4.2 %collective-permute-done.8.refs_2_.refs_1_.refs_10_ = bf16[128,2176]{1,0:T(8,128)(2,1)S(1)} collective-permute-done((bf16[128,2176]{1,0:T(8,128)(2,1)S(1)}, bf16[128,2176]{1,0:T(8,128)(2,1)S(1)}, u32[]{:S(2)}, u32[]{:S(2)}) %collective-permute-start.8) | collective-permute-done | bytes 557088 | tf_op jit(solution)/shard_map/ppermute | solution.py:271
  38.8 1.3 %collective-permute-start.9 = (bf16[128,1152]{1,0:T(8,128)(2,1)S(1)}, bf16[128,1152]{1,0:T(8,128)(2,1)S(1)}, u32[]{:S(2)}, u32[]{:S(2)}) collective-permute-start(bf16[128,1152]{1,0:T(8,128)(2,1)S(1)} %pass_kernel.3.refs_8_), channel_id=1, source_target_pairs={{0,4},{1,3},{2,6},{3,1},{4,0},{5,7},{6,2},{7,5},{8,12},{9,11},{10,... | collective-permute-start | bytes 884744 | tf_op jit(solution)/shard_map/ppermute | solution.py:271
  40.1 1.7 %expert_kernel.7 = (bf16[128,1152]{1,0:T(8,128)(2,1)S(1)}, bf16[128,768]{1,0:T(8,128)(2,1)S(1)}, bf16[128,384]{1,0:T(8,128)(2,1)S(1)}) custom-call(s32[2]{0:T(128)S(1)} %pad_add_fusion.refs_0_, bf16[128,2176]{1,0:T(8,128)(2,1)S(1)} %collective-permute-done.8.refs_2_.refs_1_.refs_10_, bf16[512,384]{1,0:T(8,128)(2,1)S(1)} %bitcast.17, ...), custom_call_target="tpu_custom_call" | custom-call | flops 6000000000 | tf_op jit(solution)/shard_map/expert_kernel/pallas_call | solution.py:230
  41.9 0.8 %collective-permute-start.11 = (bf16[128,1152]{1,0:T(8,128)(2,1)S(1)}, bf16[128,1152]{1,0:T(8,128)(2,1)S(1)}, u32[]{:S(2)}, u32[]{:S(2)}) collective-permute-start(bf16[128,1152]{1,0:T(8,128)(2,1)S(1)} %get-tuple-element.45), channel_id=1, source_target_pairs={{0,4},{1,3},{2,6},{3,1},{4,0},{5,7},{6,2},{7,5},{8,12},{9,11},{10,... | collective-permute-start | bytes 884744 | tf_op jit(solution)/shard_map/ppermute | solution.py:271
  42.7 2.9 %collective-permute-done.9.refs_1_ = bf16[128,1152]{1,0:T(8,128)(2,1)S(1)} collective-permute-done((bf16[128,1152]{1,0:T(8,128)(2,1)S(1)}, bf16[128,1152]{1,0:T(8,128)(2,1)S(1)}, u32[]{:S(2)}, u32[]{:S(2)}) %collective-permute-start.9) | collective-permute-done | bytes 294944 | tf_op jit(solution)/shard_map/ppermute | solution.py:271
  45.6 1.3 %collective-permute-start.10 = (bf16[64,1152]{1,0:T(8,128)(2,1)S(1)}, bf16[64,1152]{1,0:T(8,128)(2,1)S(1)}, u32[]{:S(2)}, u32[]{:S(2)}) collective-permute-start(bf16[64,1152]{1,0:T(8,128)(2,1)S(1)} %get-tuple-element.43.refs_2_), channel_id=1, source_target_pairs={{0,2},{1,5},{2,0},{3,7},{4,6},{5,1},{6,4},{7,3},{8,10},{9,13},{10,... | collective-permute-start | bytes 442376 | tf_op jit(solution)/shard_map/ppermute | solution.py:271
  46.9 3.9 %collective-permute-done.11.refs_1_ = bf16[128,1152]{1,0:T(8,128)(2,1)S(1)} collective-permute-done((bf16[128,1152]{1,0:T(8,128)(2,1)S(1)}, bf16[128,1152]{1,0:T(8,128)(2,1)S(1)}, u32[]{:S(2)}, u32[]{:S(2)}) %collective-permute-start.11) | collective-permute-done | bytes 294944 | tf_op jit(solution)/shard_map/ppermute | solution.py:271
  50.9 1.4 %collective-permute-start.13 = (bf16[64,1152]{1,0:T(8,128)(2,1)S(1)}, bf16[64,1152]{1,0:T(8,128)(2,1)S(1)}, u32[]{:S(2)}, u32[]{:S(2)}) collective-permute-start(bf16[64,1152]{1,0:T(8,128)(2,1)S(1)} %get-tuple-element.46.refs_2_), channel_id=1, source_target_pairs={{0,2},{1,5},{2,0},{3,7},{4,6},{5,1},{6,4},{7,3},{8,10},{9,13},{10,... | collective-permute-start | bytes 442376 | tf_op jit(solution)/shard_map/ppermute | solution.py:271
  52.3 2.2 %collective-permute-start.12 = (bf16[32,1152]{1,0:T(8,128)(2,1)S(1)}, bf16[32,1152]{1,0:T(8,128)(2,1)S(1)}, u32[]{:S(2)}, u32[]{:S(2)}) collective-permute-start(bf16[32,1152]{1,0:T(8,128)(2,1)S(1)} %get-tuple-element.48.refs_2_), channel_id=1, source_target_pairs={{0,16},{1,17},{2,18},{3,19},{4,20},{5,21},{6,22},{7,23},{8,24},{9,... | collective-permute-start | bytes 221192 | tf_op jit(solution)/shard_map/ppermute | solution.py:271
  54.5 1.6 %collective-permute-done.13.refs_1_ = bf16[64,1152]{1,0:T(8,128)(2,1)S(1)} collective-permute-done((bf16[64,1152]{1,0:T(8,128)(2,1)S(1)}, bf16[64,1152]{1,0:T(8,128)(2,1)S(1)}, u32[]{:S(2)}, u32[]{:S(2)}) %collective-permute-start.13) | collective-permute-done | bytes 147488 | tf_op jit(solution)/shard_map/ppermute | solution.py:271
  56.2 0.9 %collective-permute-start.14 = (bf16[32,1152]{1,0:T(8,128)(2,1)S(1)}, bf16[32,1152]{1,0:T(8,128)(2,1)S(1)}, u32[]{:S(2)}, u32[]{:S(2)}) collective-permute-start(bf16[32,1152]{1,0:T(8,128)(2,1)S(1)} %get-tuple-element.56), channel_id=1, source_target_pairs={{0,8},{1,9},{2,10},{3,11},{4,12},{5,13},{6,14},{7,15},{8,0},{9,1},... | collective-permute-start | bytes 221192 | tf_op jit(solution)/shard_map/ppermute | solution.py:271
  57.1 2.9 %collective-permute-start.15 = (bf16[32,1152]{1,0:T(8,128)(2,1)S(1)}, bf16[32,1152]{1,0:T(8,128)(2,1)S(1)}, u32[]{:S(2)}, u32[]{:S(2)}) collective-permute-start(bf16[32,1152]{1,0:T(8,128)(2,1)S(1)} %get-tuple-element.54.refs_13_), channel_id=1, source_target_pairs={{0,24},{1,25},{2,26},{3,27},{4,28},{5,29},{6,30},{7,31},{8,16},{9,... | collective-permute-start | bytes 221192 | tf_op jit(solution)/shard_map/ppermute | solution.py:271
  60.0 2.0 %weight_kernel.1 = (f32[512,768]{1,0:T(8,128)S(1)}, f32[384,512]{1,0:T(8,128)S(1)}, bf16[512,384]{1,0:T(8,128)(2,1)S(1)}, bf16[512,384]{1,0:T(8,128)(2,1)S(1)}, bf16[384,512]{1,0:T(8,128)(2,1)S(1)}) custom-call(s32[2]{0:T(128)S(1)} %pad_add_fusion.refs_0_, bf16[128,2176]{1,0:T(8,128)(2,1)S(1)} %join_kernel.4.refs_1_, ...), custom_call_target="tpu_custom_call" | custom-call | tf_op jit(solution)/shard_map/weight_kernel/pallas_call | solution.py:230
  62.7 0.6 collective-permute-done.15.refs_2_
  63.3 1.4 %finish_kernel.1 = (bf16[32,1024]{1,0:T(8,128)(2,1)}, bf16[8,32]{1,0:T(8,128)(2,1)}, f32[8,128]{1,0:T(8,128)S(1)}) custom-call(s32[2]{0:T(128)S(1)} %pad_add_fusion.refs_0_, f32[32,1152]{1,0:T(8,128)S(1)} %add_kernel.3.refs_1_.refs_4_, bf16[32,1152]{1,0:T(8,128)(2,1)S(1)} %collective-permute-done.15.refs_2_, s32[8,32]{1,0:T(8,128)S(1)} %bitcast.12, ...), custom_call_target="tpu_custom_call" | custom-call | flops 6000000000 | tf_op jit(solution)/shard_map/finish_kernel/pallas_call | solution.py:230
  64.9 1.2 %settle_kernel.1 = (bf16[512,384]{1,0:T(8,128)(2,1)}, bf16[512,384]{1,0:T(8,128)(2,1)}, bf16[384,512]{1,0:T(8,128)(2,1)}) custom-call(f32[512,768]{1,0:T(8,128)S(1)} %get-tuple-element.59.refs_0_, f32[384,512]{1,0:T(8,128)S(1)} %get-tuple-element.60.refs_1_, bf16[512,384]{1,0:T(8,128)(2,1)S(1)} %collective-permute-done.16.refs_2_, ...), custom_call_target="tpu_custom_call" | custom-call | tf_op jit(solution)/shard_map/settle_kernel/pallas_call | solution.py:230
  (34 shorter events, 1.3 us)
Async XLA Ops:
  1.6 21.3 %copy-start.1 = (bf16[1,512,384]{2,1,0:T(8,128)(2,1)S(1)}, bf16[1,512,384]{2,1,0:T(8,128)(2,1)}, u32[]{:S(2)}) copy-start(bf16[1,512,384]{2,1,0:T(8,128)(2,1)} %param.11) | copy-start | bytes 1179652
  1.6 21.3 %copy-start.2 = (bf16[1,512,384]{2,1,0:T(8,128)(2,1)S(1)}, bf16[1,512,384]{2,1,0:T(8,128)(2,1)}, u32[]{:S(2)}) copy-start(bf16[1,512,384]{2,1,0:T(8,128)(2,1)} %param.12) | copy-start | bytes 1179652
  1.6 21.3 %copy-start.3 = (bf16[1,384,512]{2,1,0:T(8,128)(2,1)S(1)}, bf16[1,384,512]{2,1,0:T(8,128)(2,1)}, u32[]{:S(2)}) copy-start(bf16[1,384,512]{2,1,0:T(8,128)(2,1)} %param.13) | copy-start | bytes 1179652
  1.6 10.8 %collective-permute-start = (bf16[32,2176]{1,0:T(8,128)(2,1)S(1)}, bf16[32,2176]{1,0:T(8,128)(2,1)S(1)}, u32[]{:S(2)}, u32[]{:S(2)}) collective-permute-start(bf16[32,2176]{1,0:T(8,128)(2,1)S(1)} %prepare_kernel.1.refs_0_), channel_id=1, source_target_pairs={{0,16},{1,17},{2,18},{3,19},{4,20},{5,21},{6,22},{7,23},{8,24},{9,... | collective-permute-start | bytes 417800 | tf_op jit(solution)/shard_map/ppermute | solution.py:271
  5.7 17.2 %collective-permute-start.2 = (bf16[512,384]{1,0:T(8,128)(2,1)}, bf16[512,384]{1,0:T(8,128)(2,1)S(1)}, u32[]{:S(2)}, u32[]{:S(2)}) collective-permute-start(bf16[512,384]{1,0:T(8,128)(2,1)} %bitcast.13), channel_id=1, source_target_pairs={{0,1},{1,0},{2,3},{3,2},{4,5},{5,4},{6,7},{7,6},{8,9},{9,8},{10,11... | collective-permute-start | bytes 1179656 | tf_op jit(solution)/shard_map/ppermute | solution.py:21
  5.7 17.2 %collective-permute-start.3 = (bf16[512,384]{1,0:T(8,128)(2,1)}, bf16[512,384]{1,0:T(8,128)(2,1)S(1)}, u32[]{:S(2)}, u32[]{:S(2)}) collective-permute-start(bf16[512,384]{1,0:T(8,128)(2,1)} %bitcast.18), channel_id=1, source_target_pairs={{0,1},{1,0},{2,3},{3,2},{4,5},{5,4},{6,7},{7,6},{8,9},{9,8},{10,11... | collective-permute-start | bytes 1179656 | tf_op jit(solution)/shard_map/ppermute | solution.py:21
  6.2 16.7 %collective-permute-start.4 = (bf16[384,512]{1,0:T(8,128)(2,1)}, bf16[384,512]{1,0:T(8,128)(2,1)S(1)}, u32[]{:S(2)}, u32[]{:S(2)}) collective-permute-start(bf16[384,512]{1,0:T(8,128)(2,1)} %bitcast.23), channel_id=1, source_target_pairs={{0,1},{1,0},{2,3},{3,2},{4,5},{5,4},{6,7},{7,6},{8,9},{9,8},{10,11... | collective-permute-start | bytes 1179656 | tf_op jit(solution)/shard_map/ppermute | solution.py:21
  12.4 6.6 %collective-permute-start.1 = (bf16[64,2176]{1,0:T(8,128)(2,1)S(1)}, bf16[64,2176]{1,0:T(8,128)(2,1)S(1)}, u32[]{:S(2)}, u32[]{:S(2)}) collective-permute-start(bf16[64,2176]{1,0:T(8,128)(2,1)S(1)} %join_kernel.3.refs_0_.refs_2_), channel_id=1, source_target_pairs={{0,2},{1,5},{2,0},{3,7},{4,6},{5,1},{6,4},{7,3},{8,10},{9,13},{10,... | collective-permute-start | bytes 835592 | tf_op jit(solution)/shard_map/ppermute | solution.py:271
  14.0 7.3 %collective-permute-start.5 = (bf16[64,2176]{1,0:T(8,128)(2,1)S(1)}, bf16[64,2176]{1,0:T(8,128)(2,1)S(1)}, u32[]{:S(2)}, u32[]{:S(2)}) collective-permute-start(bf16[64,2176]{1,0:T(8,128)(2,1)S(1)} %join_kernel.3.refs_0_.refs_2_), channel_id=1, source_target_pairs={{0,8},{1,9},{2,10},{3,11},{4,12},{5,13},{6,14},{7,15},{8,0},{9,1},... | collective-permute-start | bytes 835592 | tf_op jit(solution)/shard_map/ppermute | solution.py:271
  19.1 12.0 %collective-permute-start.6 = (bf16[128,2176]{1,0:T(8,128)(2,1)S(1)}, bf16[128,2176]{1,0:T(8,128)(2,1)S(1)}, u32[]{:S(2)}, u32[]{:S(2)}) collective-permute-start(bf16[128,2176]{1,0:T(8,128)(2,1)S(1)} %join_kernel.4.refs_1_), channel_id=1, source_target_pairs={{0,4},{1,3},{2,6},{3,1},{4,0},{5,7},{6,2},{7,5},{8,12},{9,11},{10,... | collective-permute-start | bytes 1671176 | tf_op jit(solution)/shard_map/ppermute | solution.py:271
  21.3 7.8 %collective-permute-start.7 = (bf16[64,2176]{1,0:T(8,128)(2,1)S(1)}, bf16[64,2176]{1,0:T(8,128)(2,1)S(1)}, u32[]{:S(2)}, u32[]{:S(2)}) collective-permute-start(bf16[64,2176]{1,0:T(8,128)(2,1)S(1)} %pass_kernel.2.refs_8_.refs_0_), channel_id=1, source_target_pairs={{0,2},{1,5},{2,0},{3,7},{4,6},{5,1},{6,4},{7,3},{8,10},{9,13},{10,... | collective-permute-start | bytes 835592 | tf_op jit(solution)/shard_map/ppermute | solution.py:271
  29.1 9.6 %collective-permute-start.8 = (bf16[128,2176]{1,0:T(8,128)(2,1)S(1)}, bf16[128,2176]{1,0:T(8,128)(2,1)S(1)}, u32[]{:S(2)}, u32[]{:S(2)}) collective-permute-start(bf16[128,2176]{1,0:T(8,128)(2,1)S(1)} %join_kernel.5.refs_8_.refs_1_.refs_7_), channel_id=1, source_target_pairs={{0,4},{1,3},{2,6},{3,1},{4,0},{5,7},{6,2},{7,5},{8,12},{9,11},{10,... | collective-permute-start | bytes 1671176 | tf_op jit(solution)/shard_map/ppermute | solution.py:271
  38.8 6.8 %collective-permute-start.9 = (bf16[128,1152]{1,0:T(8,128)(2,1)S(1)}, bf16[128,1152]{1,0:T(8,128)(2,1)S(1)}, u32[]{:S(2)}, u32[]{:S(2)}) collective-permute-start(bf16[128,1152]{1,0:T(8,128)(2,1)S(1)} %pass_kernel.3.refs_8_), channel_id=1, source_target_pairs={{0,4},{1,3},{2,6},{3,1},{4,0},{5,7},{6,2},{7,5},{8,12},{9,11},{10,... | collective-permute-start | bytes 884744 | tf_op jit(solution)/shard_map/ppermute | solution.py:271
  41.9 9.0 %collective-permute-start.11 = (bf16[128,1152]{1,0:T(8,128)(2,1)S(1)}, bf16[128,1152]{1,0:T(8,128)(2,1)S(1)}, u32[]{:S(2)}, u32[]{:S(2)}) collective-permute-start(bf16[128,1152]{1,0:T(8,128)(2,1)S(1)} %get-tuple-element.45), channel_id=1, source_target_pairs={{0,4},{1,3},{2,6},{3,1},{4,0},{5,7},{6,2},{7,5},{8,12},{9,11},{10,... | collective-permute-start | bytes 884744 | tf_op jit(solution)/shard_map/ppermute | solution.py:271
  45.6 6.7 %collective-permute-start.10 = (bf16[64,1152]{1,0:T(8,128)(2,1)S(1)}, bf16[64,1152]{1,0:T(8,128)(2,1)S(1)}, u32[]{:S(2)}, u32[]{:S(2)}) collective-permute-start(bf16[64,1152]{1,0:T(8,128)(2,1)S(1)} %get-tuple-element.43.refs_2_), channel_id=1, source_target_pairs={{0,2},{1,5},{2,0},{3,7},{4,6},{5,1},{6,4},{7,3},{8,10},{9,13},{10,... | collective-permute-start | bytes 442376 | tf_op jit(solution)/shard_map/ppermute | solution.py:271
  50.9 5.2 %collective-permute-start.13 = (bf16[64,1152]{1,0:T(8,128)(2,1)S(1)}, bf16[64,1152]{1,0:T(8,128)(2,1)S(1)}, u32[]{:S(2)}, u32[]{:S(2)}) collective-permute-start(bf16[64,1152]{1,0:T(8,128)(2,1)S(1)} %get-tuple-element.46.refs_2_), channel_id=1, source_target_pairs={{0,2},{1,5},{2,0},{3,7},{4,6},{5,1},{6,4},{7,3},{8,10},{9,13},{10,... | collective-permute-start | bytes 442376 | tf_op jit(solution)/shard_map/ppermute | solution.py:271
  52.3 10.2 %collective-permute-start.12 = (bf16[32,1152]{1,0:T(8,128)(2,1)S(1)}, bf16[32,1152]{1,0:T(8,128)(2,1)S(1)}, u32[]{:S(2)}, u32[]{:S(2)}) collective-permute-start(bf16[32,1152]{1,0:T(8,128)(2,1)S(1)} %get-tuple-element.48.refs_2_), channel_id=1, source_target_pairs={{0,16},{1,17},{2,18},{3,19},{4,20},{5,21},{6,22},{7,23},{8,24},{9,... | collective-permute-start | bytes 221192 | tf_op jit(solution)/shard_map/ppermute | solution.py:271
  56.2 6.5 %collective-permute-start.14 = (bf16[32,1152]{1,0:T(8,128)(2,1)S(1)}, bf16[32,1152]{1,0:T(8,128)(2,1)S(1)}, u32[]{:S(2)}, u32[]{:S(2)}) collective-permute-start(bf16[32,1152]{1,0:T(8,128)(2,1)S(1)} %get-tuple-element.56), channel_id=1, source_target_pairs={{0,8},{1,9},{2,10},{3,11},{4,12},{5,13},{6,14},{7,15},{8,0},{9,1},... | collective-permute-start | bytes 221192 | tf_op jit(solution)/shard_map/ppermute | solution.py:271
  57.1 6.3 %collective-permute-start.15 = (bf16[32,1152]{1,0:T(8,128)(2,1)S(1)}, bf16[32,1152]{1,0:T(8,128)(2,1)S(1)}, u32[]{:S(2)}, u32[]{:S(2)}) collective-permute-start(bf16[32,1152]{1,0:T(8,128)(2,1)S(1)} %get-tuple-element.54.refs_13_), channel_id=1, source_target_pairs={{0,24},{1,25},{2,26},{3,27},{4,28},{5,29},{6,30},{7,31},{8,16},{9,... | collective-permute-start | bytes 221192 | tf_op jit(solution)/shard_map/ppermute | solution.py:271
  60.0 3.4 %copy-start = (s32[32,8]{0,1:T(8,128)S(1)}, s32[32,8]{0,1:T(8,128)}, u32[]{:S(2)}) copy-start(s32[32,8]{0,1:T(8,128)} %param.9) | copy-start | bytes 3076
  62.0 2.7 %collective-permute-start.16 = (bf16[512,384]{1,0:T(8,128)(2,1)S(1)}, bf16[512,384]{1,0:T(8,128)(2,1)S(1)}, u32[]{:S(2)}, u32[]{:S(2)}) collective-permute-start(bf16[512,384]{1,0:T(8,128)(2,1)S(1)} %get-tuple-element.61), channel_id=1, source_target_pairs={{0,1},{1,0},{2,3},{3,2},{4,5},{5,4},{6,7},{7,6},{8,9},{9,8},{10,11... | collective-permute-start | bytes 1179656 | tf_op jit(solution)/shard_map/ppermute | solution.py:21
  62.1 2.6 %collective-permute-start.17 = (bf16[512,384]{1,0:T(8,128)(2,1)S(1)}, bf16[512,384]{1,0:T(8,128)(2,1)S(1)}, u32[]{:S(2)}, u32[]{:S(2)}) collective-permute-start(bf16[512,384]{1,0:T(8,128)(2,1)S(1)} %get-tuple-element.62), channel_id=1, source_target_pairs={{0,1},{1,0},{2,3},{3,2},{4,5},{5,4},{6,7},{7,6},{8,9},{9,8},{10,11... | collective-permute-start | bytes 1179656 | tf_op jit(solution)/shard_map/ppermute | solution.py:21
  62.6 2.3 %collective-permute-start.18 = (bf16[384,512]{1,0:T(8,128)(2,1)S(1)}, bf16[384,512]{1,0:T(8,128)(2,1)S(1)}, u32[]{:S(2)}, u32[]{:S(2)}) collective-permute-start(bf16[384,512]{1,0:T(8,128)(2,1)S(1)} %get-tuple-element.55.refs_2_), channel_id=1, source_target_pairs={{0,1},{1,0},{2,3},{3,2},{4,5},{5,4},{6,7},{7,6},{8,9},{9,8},{10,11... | collective-permute-start | bytes 1179656 | tf_op jit(solution)/shard_map/ppermute | solution.py:21

commit v7 on v6

--- a/solution.py
+++ b/solution.py
@@ -21,14 +21,14 @@
     return lax.ppermute(x, "core", [(0, 1), (1, 0)])
 
 
-def for_chunks(rows, step):
-    if rows <= CHUNK:
+def for_chunks(rows, step, chunk):
+    if rows <= chunk:
         step(pl.ds(0, rows))
     else:
 
-        @pl.loop(0, rows // CHUNK)
+        @pl.loop(0, rows // chunk)
         def _(i):
-            step(pl.ds(pl.multiple_of(i * CHUNK, CHUNK), CHUNK))
+            step(pl.ds(pl.multiple_of(i * chunk, chunk), chunk))
 
 
 def own_other(place_ref, half, start=0):
@@ -94,82 +94,105 @@
     out[...] = source[...]
 
 
-def expert_kernel(
-    place, block, gate_own, gate_other, up_own, up_other, down_own, down_other,
-    row_grads, grads, scaled_hidden,
-):
+def expert_kernel(place, *refs):
+    blocks, refs = refs[:-9], refs[-9:]
+    gate_own, gate_other, up_own, up_other, down_own, down_other = refs[:6]
+    row_grads, grads, scaled_hidden = refs[6:]
     half, width = gate_own.shape
     features = 2 * half
-    lanes = block.shape[1] - 2 * features
+    number, count = len(blocks), blocks[0].shape[0]
+    lanes = blocks[0].shape[1] - 2 * features
     own, other = own_other(place, half)
     dys_own, dys_other = own_other(place, half, features)
 
     def step(at):
-        mine, rest = block[at, own], block[at, other]
+        def take(cols):
+            return jnp.concatenate([block[at, cols] for block in blocks], 0)
+
+        mine, rest = take(own), take(other)
         pre_gate = dot(mine, gate_own[...], NN) + dot(rest, gate_other[...], NN)
         pre_up = dot(mine, up_own[...], NN) + dot(rest, up_other[...], NN)
-        back = dot(block[at, dys_own], down_own[...], NT)
-        back = back + dot(block[at, dys_other], down_other[...], NT)
+        back = dot(take(dys_own), down_own[...], NT) + dot(take(dys_other), down_other[...], NT)
         sig = jax.nn.sigmoid(pre_gate)
         active = pre_gate * sig
         slope = sig * (1.0 + pre_gate * (1.0 - sig))
         hidden = active * pre_up
         lane = lax.broadcasted_iota(jnp.int32, (back.shape[0], lanes), 1)
         is_own = lane == place[1]
-        gates = jnp.where(is_own, block[at, pl.ds(2 * features, lanes)].astype(F32), 0.0)
+        gates = jnp.where(is_own, take(pl.ds(2 * features, lanes)).astype(F32), 0.0)
         gates = jnp.sum(gates, 1, keepdims=True)
         gate_grads = jnp.sum(hidden * back, 1, keepdims=True)
         back = back * gates
         grad_gate = (back * pre_up * slope).astype(BF16)
         grad_up = (back * active).astype(BF16)
-        row_grads[at, pl.ds(0, half)] = (
-            dot(grad_gate, gate_own[...], NT) + dot(grad_up, up_own[...], NT)
-        ).astype(BF16)
-        row_grads[at, pl.ds(half, half)] = (
-            dot(grad_gate, gate_other[...], NT) + dot(grad_up, up_other[...], NT)
-        ).astype(BF16)
-        row_grads[at, pl.ds(features, lanes)] = jnp.where(is_own, gate_grads, 0.0).astype(BF16)
-        grads[at, pl.ds(0, width)] = grad_gate
-        grads[at, pl.ds(width, width)] = grad_up
-        scaled_hidden[at, :] = (hidden * gates).astype(BF16)
-
-    for_chunks(block.shape[0], step)
-
-
-def weight_kernel(place, *refs):
+        scaled = (hidden * gates).astype(BF16)
+        pieces = (
+            dot(grad_gate, gate_own[...], NT) + dot(grad_up, up_own[...], NT),
+            dot(grad_gate, gate_other[...], NT) + dot(grad_up, up_other[...], NT),
+            jnp.where(is_own, gate_grads, 0.0),
+        )
+        middle = count // 2
+        for i in range(number):
+            part = slice(i * at.size, (i + 1) * at.size)
+            grads[i, at, pl.ds(0, width)] = grad_gate[part]
+            grads[i, at, pl.ds(width, width)] = grad_up[part]
+            scaled_hidden[i, at, :] = scaled[part]
+            begin = 0
+            for piece in pieces:
+                cols = pl.ds(begin, piece.shape[1])
+                begin += piece.shape[1]
+                rows = piece[part].astype(BF16)
+                if at.size == count:
+                    row_grads[pl.ds(i * middle, middle), cols] = rows[:middle]
+                    row_grads[pl.ds((number + i) * middle, middle), cols] = rows[middle:]
+                else:
+                    place_at = at.start + at.start // middle * (number - 1) * middle + i * middle
+                    row_grads[pl.ds(pl.multiple_of(place_at, at.size), at.size), cols] = rows
+
+    for_chunks(count, step, CHUNK // number)
+
+
+def weight_kernel(numbers, place, *refs):
     keep_in, keep_down, give_gate, give_up, give_down = refs[-5:]
-    parts = [refs[i : i + 3] for i in range(0, len(refs) - 5, 3)]
+    parts, begin = [], 0
+    for number in numbers:
+        grads, hidden = refs[begin + number : begin + number + 2]
+        parts += [(refs[begin + i], grads.at[i], hidden.at[i]) for i in range(number)]
+        begin += number + 2
     half, width = give_gate.shape
-    count = parts[0][0].shape[0]
     own, other = own_other(place, half)
     dys_own, dys_other = own_other(place, half, 2 * half)
-    left, right = pl.ds(0, width), pl.ds(width, width)
-
-    def products(parts, at, cols, dys_cols):
-        rows = jnp.concatenate([p[0][at, cols] for p in parts], 0)
-        dys = jnp.concatenate([p[0][at, dys_cols] for p in parts], 0)
-        grads = jnp.concatenate([p[1][at, :] for p in parts], 0)
-        hidden = jnp.concatenate([p[2][at, :] for p in parts], 0)
-        return dot(rows, grads, TN), dot(hidden, dys, TN)
+    steps = max(1, min(p[0].shape[0] for p in parts) // CHUNK)
+
+    def products(i, cols, dys_cols):
+        def gather(which, cols):
+            values = []
+            for part in parts:
+                size = part[0].shape[0] // steps
+                start = i * size
+                at = pl.ds(start if steps == 1 else pl.multiple_of(start, size), size)
+                values.append(part[which][at, cols])
+            return jnp.concatenate(values, 0)
+
+        into = dot(gather(0, cols), gather(1, pl.ds(0, 2 * width)), TN)
+        return into, dot(gather(2, pl.ds(0, width)), gather(0, dys_cols), TN)
 
     def hand_over(into, down):
-        give_gate[...] = into[:, left.start : left.start + width].astype(BF16)
-        give_up[...] = into[:, width : 2 * width].astype(BF16)
+        give_gate[...] = into[:, :width].astype(BF16)
+        give_up[...] = into[:, width:].astype(BF16)
         give_down[...] = down.astype(BF16)
 
-    if count <= CHUNK:
-        at = pl.ds(0, count)
-        hand_over(*products(parts, at, other, dys_other))
-        keep_in[...], keep_down[...] = products(parts, at, own, dys_own)
+    if steps == 1:
+        hand_over(*products(0, other, dys_other))
+        keep_in[...], keep_down[...] = products(0, own, dys_own)
     else:
         for cols, dys_cols, is_given in ((other, dys_other, True), (own, dys_own, False)):
             keep_in[...] = jnp.zeros_like(keep_in)
             keep_down[...] = jnp.zeros_like(keep_down)
 
-            @pl.loop(0, count // CHUNK)
+            @pl.loop(0, steps)
             def _(i):
-                at = pl.ds(pl.multiple_of(i * CHUNK, CHUNK), CHUNK)
-                into, down = products(parts, at, cols, dys_cols)
+                into, down = products(i, cols, dys_cols)
                 keep_in[...] += into
                 keep_down[...] += down
 
@@ -177,19 +200,19 @@
                 hand_over(keep_in[...], keep_down[...])
 
 
-def settle_kernel(keep_in, keep_down, got_gate, got_up, got_down, gate, up, down):
+def settle_kernel(keep_in, keep_down, got_gate, got_up, got_down, gate, up, down, done):
     width = gate.shape[1]
     left, right = pl.ds(0, width), pl.ds(width, width)
     gate[...] = (keep_in[:, left] + got_gate[...].astype(F32)).astype(BF16)
     up[...] = (keep_in[:, right] + got_up[...].astype(F32)).astype(BF16)
     down[...] = (keep_down[...] + got_down[...].astype(F32)).astype(BF16)
+    done[...] = jnp.zeros_like(done)
 
 
 def finish_kernel(place, *refs):
-    ids, grad_tokens, grad_gates, done = refs[-4:]
-    done[...] = jnp.zeros_like(done)
+    ids, grad_tokens, grad_gates = refs[-3:]
     total = refs[0][...].astype(F32)
-    for part in refs[1:-4]:
+    for part in refs[1:-3]:
         total = total + part[...].astype(F32)
     half = grad_tokens.shape[1] // 2
     lanes = total.shape[1] - 2 * half
@@ -236,7 +259,7 @@
         out_specs=[vmem] * len(outs),
         compiler_params=pltpu.CompilerParams(vmem_limit_bytes=limit),
         cost_estimate=pl.CostEstimate(flops=flops, bytes_accessed=0, transcendentals=0),
-        name=kernel.__name__,
+        name=kernel.__name__.replace("<lambda>", "weight_kernel"),
     )(*scalars, *args, *after)
 
 
@@ -306,7 +329,7 @@
     gate_own, up_own, down_own = gate_half[0], up_half[0], down_half[0]
     gate_other, up_other, down_other = swap_core(gate_own), swap_core(up_own), swap_core(down_own)
     weights = (gate_own, gate_other, up_own, up_other, down_own, down_other)
-    saved = []
+    numbers, saved = [], []
 
     def at_offset(x, i):
         return exchange(x, (offsets[i], offsets[i]))
@@ -319,14 +342,19 @@
         before.extend(others)
         return run(pass_kernel, [(x.shape, BF16)], None, x)[0]
 
-    def expert(block):
-        count = block.shape[0]
+    def expert(*blocks):
+        number, count = len(blocks), blocks[0].shape[0]
         row_grads, grads, hidden = run(
             expert_kernel,
-            [((count, columns), BF16), ((count, 2 * width), BF16), ((count, width), BF16)],
-            place, block, *weights, limit=6, flops=6 * 10**9,
+            [
+                ((number * count, columns), BF16),
+                ((number, count, 2 * width), BF16),
+                ((number, count, width), BF16),
+            ],
+            place, *blocks, *weights, limit=6, flops=6 * 10**9,
         )
-        saved.extend([block, grads, hidden])
+        numbers.append(number)
+        saved.extend([*blocks, grads, hidden])
         return row_grads
 
     def split(kept, got, types):
@@ -336,30 +364,27 @@
     def collect(total, part):
         return run(add_kernel, [(total.shape, F32)], None, total, part)[0]
 
-    near_0 = join(block, at_offset(block, 0))
-    near_1 = at_offset(near_0, 1)
-    first_0 = join(near_0, exchange(near_0, near_a))
-    second_0 = exchange(first_0, near_b)
+    far_two = at_offset(block, 0)
+    first_own = join(block, exchange(block, near_a))
+    second_own = exchange(first_own, near_b)
+    near_1 = at_offset(join(block, far_two), 1)
+    second_own = after_all(second_own)
+    first_two = join(far_two, exchange(far_two, near_a))
+    second_two = exchange(first_two, near_b)
     near_1 = after_all(near_1)
     got_near = exchange(near_1, near_a)
-    kept_0 = expert(first_0)
+    got_0 = exchange(expert(second_own, second_two), near_b)
     first_1 = join(near_1, got_near)
     second_1 = exchange(first_1, near_b)
-    give_0 = expert(second_0)
-    kept_1 = expert(first_1)
-    got_0 = exchange(after_all(give_0, second_1), near_b)
-    got_1 = exchange(expert(second_1), near_b)
-
+    kept_0 = expert(first_own, first_two)
     kept_0, give = split(kept_0, got_0, (F32, BF16))
     got_0 = exchange(give, near_a)
-    kept_1, give = split(kept_1, got_1, (F32, BF16))
-    got_1 = exchange(give, near_a)
+    kept_1 = expert(first_1)
+    got_1 = exchange(expert(second_1), near_b)
     total, give = split(kept_0, got_0, (F32, BF16))
     back_two = at_offset(give, 0)
-    give_one, give_both = split(kept_1, got_1, (BF16, BF16))
-    back_one, back_both = at_offset(give_one, 1), at_offset(give_both, 2)
     keep_in, keep_down, *gives = run(
-        weight_kernel,
+        lambda *refs: weight_kernel(tuple(numbers), *refs),
         [
             ((half, 2 * width), F32),
             ((width, half), F32),
@@ -370,7 +395,16 @@
         place, *saved, limit=10,
     )
     gots = [swap_core(give) for give in gives]
+    kept_1, give = split(kept_1, got_1, (F32, BF16))
+    got_1 = exchange(give, near_a)
     total = collect(total, back_two)
+    give_one, give_both = split(kept_1, got_1, (BF16, BF16))
+    back_one, back_both = at_offset(give_one, 1), at_offset(give_both, 2)
+    grad_gate, grad_up, grad_down, _ = run(
+        settle_kernel,
+        [((half, width), BF16), ((half, width), BF16), ((width, half), BF16), ((8, 128), F32)],
+        None, keep_in, keep_down, *gots, leaves=3, limit=6,
+    )
     total = collect(total, back_one)
 
     parts = (total, back_both)
@@ -380,15 +414,10 @@
             middle = total.shape[0] // 2
             total = total[:middle] + exchange(total[middle:].astype(BF16), step).astype(F32)
         parts = (total,)
-    grad_tokens, grad_gates, _ = run(
+    grad_tokens, grad_gates = run(
         finish_kernel,
-        [((tok_rows, features), BF16), (expert_ids.shape[::-1], BF16), ((8, 128), F32)],
-        place, *parts, expert_ids.T, arrives=1, leaves=2, flops=6 * 10**9,
-    )
-    grad_gate, grad_up, grad_down = run(
-        settle_kernel,
-        [((half, width), BF16), ((half, width), BF16), ((width, half), BF16)],
-        None, keep_in, keep_down, *gots, leaves=3, limit=6,
+        [((tok_rows, features), BF16), (expert_ids.shape[::-1], BF16)],
+        place, *parts, expert_ids.T, arrives=1, leaves=2,
     )
     return grad_tokens, grad_gates.T, grad_gate[None], grad_up[None], grad_down[None]
 

time: 66.3 us -> 72.9 us (1.100)
  starting transfers between devices: 22.9 us -> 27.9 us
  Pallas kernels: 12.8 us -> 15.2 us
  waiting for transfers between devices: 29.4 us -> 28.1 us
    ppermute x13 -> x15, starting transfers between devices: 21.8 us -> 26.7 us  [exchange(): return lax.ppermute(x, DEVICES, pairs)]
    pallas_call x18 -> x19, Pallas kernels: 11.9 us -> 14.3 us  [call(): pl.pallas_call(run, out_shape=out_shape, in_specs=[pl.BlockSpec(memory_sp...]
    ppermute x13 -> x15, waiting for transfers between devices: 29.2 us -> 28 us  [exchange(): return lax.ppermute(x, DEVICES, pairs)]
  transfers between devices with their start and end apart: 19 -> 21, of which waited for: 11 -> 9; matrix products, arithmetic and copies ran while one was open for 0% -> 0% of each run, Pallas kernels for 16% -> 18%
where the time goes in v7:
time: 72.9 us; the launch traced here: 72.1 us
  waiting for transfers between devices  28.1 us (39%)
  starting transfers between devices  27.9 us (38%)
  Pallas kernels  15.2 us (21%)
  between operations  0.82 us (1%)
    ppermute x15, waiting for transfers between devices, exchange(): return lax.ppermute(x, DEVICES, pairs)  28 us
    ppermute x15, starting transfers between devices, exchange(): return lax.ppermute(x, DEVICES, pairs)  26.7 us
    pallas_call x19, Pallas kernels, call(): pl.pallas_call(run, out_shape=out_shape, in_specs=[pl.BlockSpec(memory_sp...  14.3 us
  transfers between devices with their start and end apart: 21, of which 9 were waited for; matrix products, arithmetic and copies ran while one was open for 0% of the time, Pallas kernels for 18%

profile of v7, /device:TPU:0, one launch (start us, length us, event | category | flops | bytes accessed | tf_op | source)
XLA Modules:
  0.0 72.1 jit_solution(4856786501874702328)
XLA Ops:
  0.6 0.9 %prepare_kernel.1.refs_0_ = bf16[32,2176]{1,0:T(8,128)(2,1)S(1)} custom-call(bf16[32,1024]{1,0:T(8,128)(2,1)} %tokens.1, bf16[32,1024]{1,0:T(8,128)(2,1)} %cotangent.1, s32[8,32]{1,0:T(8,128)} %bitcast.11, bf16[8,32]{1,0:T(8,128)(2,1)} %bitcast.28), custom_call_target="tpu_custom_call" | custom-call | tf_op jit(solution)/shard_map/prepare_kernel/pallas_call | solution.py:309
  1.6 3.0 %collective-permute-start = (bf16[32,2176]{1,0:T(8,128)(2,1)S(1)}, bf16[32,2176]{1,0:T(8,128)(2,1)S(1)}, u32[]{:S(2)}, u32[]{:S(2)}) collective-permute-start(bf16[32,2176]{1,0:T(8,128)(2,1)S(1)} %prepare_kernel.1.refs_0_), channel_id=1, source_target_pairs={{0,2},{1,5},{2,0},{3,7},{4,6},{5,1},{6,4},{7,3},{8,10},{9,13},{10,... | collective-permute-start | bytes 417800 | tf_op jit(solution)/shard_map/ppermute | solution.py:294
  4.6 3.0 %collective-permute-done.refs_1_ = bf16[32,2176]{1,0:T(8,128)(2,1)S(1)} collective-permute-done((bf16[32,2176]{1,0:T(8,128)(2,1)S(1)}, bf16[32,2176]{1,0:T(8,128)(2,1)S(1)}, u32[]{:S(2)}, u32[]{:S(2)}) %collective-permute-start) | collective-permute-done | bytes 139296 | tf_op jit(solution)/shard_map/ppermute | solution.py:294
  7.6 2.1 %collective-permute-start.3 = (bf16[64,2176]{1,0:T(8,128)(2,1)S(1)}, bf16[64,2176]{1,0:T(8,128)(2,1)S(1)}, u32[]{:S(2)}, u32[]{:S(2)}) collective-permute-start(bf16[64,2176]{1,0:T(8,128)(2,1)S(1)} %join_kernel.4.refs_2_.refs_1_.refs_5_), channel_id=1, source_target_pairs={{0,4},{1,3},{2,6},{3,1},{4,0},{5,7},{6,2},{7,5},{8,12},{9,11},{10,... | collective-permute-start | bytes 835592 | tf_op jit(solution)/shard_map/ppermute | solution.py:294
  9.8 2.6 %collective-permute-start.1 = (bf16[32,2176]{1,0:T(8,128)(2,1)S(1)}, bf16[32,2176]{1,0:T(8,128)(2,1)S(1)}, u32[]{:S(2)}, u32[]{:S(2)}) collective-permute-start(bf16[32,2176]{1,0:T(8,128)(2,1)S(1)} %prepare_kernel.1.refs_0_), channel_id=1, source_target_pairs={{0,16},{1,17},{2,18},{3,19},{4,20},{5,21},{6,22},{7,23},{8,24},{9,... | collective-permute-start | bytes 417800 | tf_op jit(solution)/shard_map/ppermute | solution.py:294
  12.3 5.5 %collective-permute-done.1.refs_1_.refs_0_ = bf16[32,2176]{1,0:T(8,128)(2,1)S(1)} collective-permute-done((bf16[32,2176]{1,0:T(8,128)(2,1)S(1)}, bf16[32,2176]{1,0:T(8,128)(2,1)S(1)}, u32[]{:S(2)}, u32[]{:S(2)}) %collective-permute-start.1) | collective-permute-done | bytes 139296 | tf_op jit(solution)/shard_map/ppermute | solution.py:294
  17.9 0.8 %collective-permute-start.2 = (bf16[32,2176]{1,0:T(8,128)(2,1)S(1)}, bf16[32,2176]{1,0:T(8,128)(2,1)S(1)}, u32[]{:S(2)}, u32[]{:S(2)}) collective-permute-start(bf16[32,2176]{1,0:T(8,128)(2,1)S(1)} %collective-permute-done.1.refs_1_.refs_0_), channel_id=1, source_target_pairs={{0,2},{1,5},{2,0},{3,7},{4,6},{5,1},{6,4},{7,3},{8,10},{9,13},{10,... | collective-permute-start | bytes 417800 | tf_op jit(solution)/shard_map/ppermute | solution.py:294
  19.3 1.1 %collective-permute-start.7 = (bf16[64,2176]{1,0:T(8,128)(2,1)S(1)}, bf16[64,2176]{1,0:T(8,128)(2,1)S(1)}, u32[]{:S(2)}, u32[]{:S(2)}) collective-permute-start(bf16[64,2176]{1,0:T(8,128)(2,1)S(1)} %join_kernel.5.refs_1_), channel_id=1, source_target_pairs={{0,8},{1,9},{2,10},{3,11},{4,12},{5,13},{6,14},{7,15},{8,0},{9,1},... | collective-permute-start | bytes 835592 | tf_op jit(solution)/shard_map/ppermute | solution.py:294
  20.5 2.5 %collective-permute-done.2.refs_1_ = bf16[32,2176]{1,0:T(8,128)(2,1)S(1)} collective-permute-done((bf16[32,2176]{1,0:T(8,128)(2,1)S(1)}, bf16[32,2176]{1,0:T(8,128)(2,1)S(1)}, u32[]{:S(2)}, u32[]{:S(2)}) %collective-permute-start.2) | collective-permute-done | bytes 139296 | tf_op jit(solution)/shard_map/ppermute | solution.py:294
  23.0 1.6 %collective-permute-start.9 = (bf16[64,2176]{1,0:T(8,128)(2,1)S(1)}, bf16[64,2176]{1,0:T(8,128)(2,1)S(1)}, u32[]{:S(2)}, u32[]{:S(2)}) collective-permute-start(bf16[64,2176]{1,0:T(8,128)(2,1)S(1)} %join_kernel.6.refs_1_.refs_2_.refs_6_), channel_id=1, source_target_pairs={{0,4},{1,3},{2,6},{3,1},{4,0},{5,7},{6,2},{7,5},{8,12},{9,11},{10,... | collective-permute-start | bytes 835592 | tf_op jit(solution)/shard_map/ppermute | solution.py:294
  24.6 3.8 %collective-permute-done.7.refs_0_ = bf16[64,2176]{1,0:T(8,128)(2,1)S(1)} collective-permute-done((bf16[64,2176]{1,0:T(8,128)(2,1)S(1)}, bf16[64,2176]{1,0:T(8,128)(2,1)S(1)}, u32[]{:S(2)}, u32[]{:S(2)}) %collective-permute-start.7) | collective-permute-done | bytes 278560 | tf_op jit(solution)/shard_map/ppermute | solution.py:294
  28.4 1.3 %collective-permute-start.8 = (bf16[64,2176]{1,0:T(8,128)(2,1)S(1)}, bf16[64,2176]{1,0:T(8,128)(2,1)S(1)}, u32[]{:S(2)}, u32[]{:S(2)}) collective-permute-start(bf16[64,2176]{1,0:T(8,128)(2,1)S(1)} %pass_kernel.3.refs_9_.refs_0_), channel_id=1, source_target_pairs={{0,2},{1,5},{2,0},{3,7},{4,6},{5,1},{6,4},{7,3},{8,10},{9,13},{10,... | collective-permute-start | bytes 835592 | tf_op jit(solution)/shard_map/ppermute | solution.py:294
  29.7 2.3 %expert_kernel.4 = (bf16[128,1152]{1,0:T(8,128)(2,1)S(1)}, bf16[2,64,768]{2,1,0:T(8,128)(2,1)S(1)}, bf16[2,64,384]{2,1,0:T(8,128)(2,1)S(1)}) custom-call(s32[2]{0:T(128)S(1)} %pad_add_fusion.refs_0_, bf16[64,2176]{1,0:T(8,128)(2,1)S(1)} %pass_kernel.2.refs_2_.refs_1_, bf16[64,2176]{1,0:T(8,128)(2,1)S(1)} %collective-permute-done.9.refs_2_, ...), custom_call_target="tpu_custom_call" | custom-call | flops 6000000000 | tf_op jit(solution)/shard_map/expert_kernel/pallas_call | solution.py:253
  32.1 1.6 %collective-permute-start.10 = (bf16[128,1152]{1,0:T(8,128)(2,1)S(1)}, bf16[128,1152]{1,0:T(8,128)(2,1)S(1)}, u32[]{:S(2)}, u32[]{:S(2)}) collective-permute-start(bf16[128,1152]{1,0:T(8,128)(2,1)S(1)} %get-tuple-element.38), channel_id=1, source_target_pairs={{0,4},{1,3},{2,6},{3,1},{4,0},{5,7},{6,2},{7,5},{8,12},{9,11},{10,... | collective-permute-start | bytes 884744 | tf_op jit(solution)/shard_map/ppermute | solution.py:294
  33.7 2.2 %collective-permute-done.8.refs_1_ = bf16[64,2176]{1,0:T(8,128)(2,1)S(1)} collective-permute-done((bf16[64,2176]{1,0:T(8,128)(2,1)S(1)}, bf16[64,2176]{1,0:T(8,128)(2,1)S(1)}, u32[]{:S(2)}, u32[]{:S(2)}) %collective-permute-start.8) | collective-permute-done | bytes 278560 | tf_op jit(solution)/shard_map/ppermute | solution.py:294
  35.9 1.8 %collective-permute-start.12 = (bf16[128,2176]{1,0:T(8,128)(2,1)S(1)}, bf16[128,2176]{1,0:T(8,128)(2,1)S(1)}, u32[]{:S(2)}, u32[]{:S(2)}) collective-permute-start(bf16[128,2176]{1,0:T(8,128)(2,1)S(1)} %join_kernel.7.refs_9_.refs_1_), channel_id=1, source_target_pairs={{0,4},{1,3},{2,6},{3,1},{4,0},{5,7},{6,2},{7,5},{8,12},{9,11},{10,... | collective-permute-start | bytes 1671176 | tf_op jit(solution)/shard_map/ppermute | solution.py:294
  37.7 2.3 %expert_kernel.5 = (bf16[128,1152]{1,0:T(8,128)(2,1)S(1)}, bf16[2,64,768]{2,1,0:T(8,128)(2,1)S(1)}, bf16[2,64,384]{2,1,0:T(8,128)(2,1)S(1)}) custom-call(s32[2]{0:T(128)S(1)} %pad_add_fusion.refs_0_, bf16[64,2176]{1,0:T(8,128)(2,1)S(1)} %join_kernel.4.refs_2_.refs_1_.refs_5_, bf16[64,2176]{1,0:T(8,128)(2,1)S(1)} %join_kernel.6.refs_1_.refs_2_.refs_6_, ...), custom_call_target="tpu_custom_call" | custom-call | flops 6000000000 | tf_op jit(solution)/shard_map/expert_kernel/pallas_call | solution.py:253
  40.1 1.8 %collective-permute-start.11 = (bf16[64,1152]{1,0:T(8,128)(2,1)S(1)}, bf16[64,1152]{1,0:T(8,128)(2,1)S(1)}, u32[]{:S(2)}, u32[]{:S(2)}) collective-permute-start(bf16[64,1152]{1,0:T(8,128)(2,1)S(1)} %get-tuple-element.41.refs_8_), channel_id=1, source_target_pairs={{0,2},{1,5},{2,0},{3,7},{4,6},{5,1},{6,4},{7,3},{8,10},{9,13},{10,... | collective-permute-start | bytes 442376 | tf_op jit(solution)/shard_map/ppermute | solution.py:294
  42.0 2.3 %expert_kernel.6 = (bf16[128,1152]{1,0:T(8,128)(2,1)S(1)}, bf16[1,128,768]{2,1,0:T(8,128)(2,1)S(1)}, bf16[1,128,384]{2,1,0:T(8,128)(2,1)S(1)}) custom-call(s32[2]{0:T(128)S(1)} %pad_add_fusion.refs_0_, bf16[128,2176]{1,0:T(8,128)(2,1)S(1)} %join_kernel.7.refs_9_.refs_1_, bf16[512,384]{1,0:T(8,128)(2,1)S(1)} %bitcast.16, ...), custom_call_target="tpu_custom_call" | custom-call | flops 6000000000 | tf_op jit(solution)/shard_map/expert_kernel/pallas_call | solution.py:253
  44.3 2.8 %collective-permute-done.12.refs_1_.refs_12_ = bf16[128,2176]{1,0:T(8,128)(2,1)S(1)} collective-permute-done((bf16[128,2176]{1,0:T(8,128)(2,1)S(1)}, bf16[128,2176]{1,0:T(8,128)(2,1)S(1)}, u32[]{:S(2)}, u32[]{:S(2)}) %collective-permute-start.12) | collective-permute-done | bytes 557088 | tf_op jit(solution)/shard_map/ppermute | solution.py:294
  47.1 2.3 %expert_kernel.7 = (bf16[128,1152]{1,0:T(8,128)(2,1)S(1)}, bf16[1,128,768]{2,1,0:T(8,128)(2,1)S(1)}, bf16[1,128,384]{2,1,0:T(8,128)(2,1)S(1)}) custom-call(s32[2]{0:T(128)S(1)} %pad_add_fusion.refs_0_, bf16[128,2176]{1,0:T(8,128)(2,1)S(1)} %collective-permute-done.12.refs_1_.refs_12_, bf16[512,384]{1,0:T(8,128)(2,1)S(1)} %bitcast.17, ...), custom_call_target="tpu_custom_call" | custom-call | flops 6000000000 | tf_op jit(solution)/shard_map/expert_kernel/pallas_call | solution.py:253
  49.4 1.8 %collective-permute-start.14 = (bf16[128,1152]{1,0:T(8,128)(2,1)S(1)}, bf16[128,1152]{1,0:T(8,128)(2,1)S(1)}, u32[]{:S(2)}, u32[]{:S(2)}) collective-permute-start(bf16[128,1152]{1,0:T(8,128)(2,1)S(1)} %get-tuple-element.47), channel_id=1, source_target_pairs={{0,4},{1,3},{2,6},{3,1},{4,0},{5,7},{6,2},{7,5},{8,12},{9,11},{10,... | collective-permute-start | bytes 884744 | tf_op jit(solution)/shard_map/ppermute | solution.py:294
  51.2 2.0 %weight_kernel.1 = (f32[512,768]{1,0:T(8,128)S(1)}, f32[384,512]{1,0:T(8,128)S(1)}, bf16[512,384]{1,0:T(8,128)(2,1)S(1)}, bf16[512,384]{1,0:T(8,128)(2,1)S(1)}, bf16[384,512]{1,0:T(8,128)(2,1)S(1)}) custom-call(s32[2]{0:T(128)S(1)} %pad_add_fusion.refs_0_, bf16[64,2176]{1,0:T(8,128)(2,1)S(1)} %pass_kernel.2.refs_2_.refs_1_, ...), custom_call_target="tpu_custom_call" | custom-call | tf_op jit(solution)/shard_map/weight_kernel/pallas_call | solution.py:253
  53.9 2.3 %collective-permute-done.14.refs_1_ = bf16[128,1152]{1,0:T(8,128)(2,1)S(1)} collective-permute-done((bf16[128,1152]{1,0:T(8,128)(2,1)S(1)}, bf16[128,1152]{1,0:T(8,128)(2,1)S(1)}, u32[]{:S(2)}, u32[]{:S(2)}) %collective-permute-start.14) | collective-permute-done | bytes 294944 | tf_op jit(solution)/shard_map/ppermute | solution.py:294
  56.3 1.6 %collective-permute-start.15 = (bf16[64,1152]{1,0:T(8,128)(2,1)S(1)}, bf16[64,1152]{1,0:T(8,128)(2,1)S(1)}, u32[]{:S(2)}, u32[]{:S(2)}) collective-permute-start(bf16[64,1152]{1,0:T(8,128)(2,1)S(1)} %get-tuple-element.53.refs_2_), channel_id=1, source_target_pairs={{0,2},{1,5},{2,0},{3,7},{4,6},{5,1},{6,4},{7,3},{8,10},{9,13},{10,... | collective-permute-start | bytes 442376 | tf_op jit(solution)/shard_map/ppermute | solution.py:294
  57.9 2.1 %collective-permute-start.13 = (bf16[32,1152]{1,0:T(8,128)(2,1)S(1)}, bf16[32,1152]{1,0:T(8,128)(2,1)S(1)}, u32[]{:S(2)}, u32[]{:S(2)}) collective-permute-start(bf16[32,1152]{1,0:T(8,128)(2,1)S(1)} %get-tuple-element.45.refs_15_), channel_id=1, source_target_pairs={{0,16},{1,17},{2,18},{3,19},{4,20},{5,21},{6,22},{7,23},{8,24},{9,... | collective-permute-start | bytes 221192 | tf_op jit(solution)/shard_map/ppermute | solution.py:294
  59.9 4.0 %collective-permute-done.13.refs_1_ = bf16[32,1152]{1,0:T(8,128)(2,1)S(1)} collective-permute-done((bf16[32,1152]{1,0:T(8,128)(2,1)S(1)}, bf16[32,1152]{1,0:T(8,128)(2,1)S(1)}, u32[]{:S(2)}, u32[]{:S(2)}) %collective-permute-start.13) | collective-permute-done | bytes 73760 | tf_op jit(solution)/shard_map/ppermute | solution.py:294
  64.0 0.5 collective-permute-start.16
  64.5 3.0 %collective-permute-start.20 = (bf16[32,1152]{1,0:T(8,128)(2,1)S(1)}, bf16[32,1152]{1,0:T(8,128)(2,1)S(1)}, u32[]{:S(2)}, u32[]{:S(2)}) collective-permute-start(bf16[32,1152]{1,0:T(8,128)(2,1)S(1)} %get-tuple-element.60.refs_5_), channel_id=1, source_target_pairs={{0,24},{1,25},{2,26},{3,27},{4,28},{5,29},{6,30},{7,31},{8,16},{9,... | collective-permute-start | bytes 221192 | tf_op jit(solution)/shard_map/ppermute | solution.py:294
  67.6 1.2 %settle_kernel.1 = (bf16[512,384]{1,0:T(8,128)(2,1)}, bf16[512,384]{1,0:T(8,128)(2,1)}, bf16[384,512]{1,0:T(8,128)(2,1)}, f32[8,128]{1,0:T(8,128)S(1)}) custom-call(f32[512,768]{1,0:T(8,128)S(1)} %get-tuple-element.56.refs_0_, f32[384,512]{1,0:T(8,128)S(1)} %get-tuple-element.57.refs_1_, bf16[512,384]{1,0:T(8,128)(2,1)S(1)} %collective-permute-done.17.refs_2_, ...), custom_call_target="tpu_custom_call" | custom-call | tf_op jit(solution)/shard_map/settle_kernel/pallas_call | solution.py:253
  68.8 2.0 %collective-permute-done.20.refs_2_ = bf16[32,1152]{1,0:T(8,128)(2,1)S(1)} collective-permute-done((bf16[32,1152]{1,0:T(8,128)(2,1)S(1)}, bf16[32,1152]{1,0:T(8,128)(2,1)S(1)}, u32[]{:S(2)}, u32[]{:S(2)}) %collective-permute-start.20) | collective-permute-done | bytes 73760 | tf_op jit(solution)/shard_map/ppermute | solution.py:294
  70.7 1.4 %finish_kernel.1 = (bf16[32,1024]{1,0:T(8,128)(2,1)}, bf16[8,32]{1,0:T(8,128)(2,1)}) custom-call(s32[2]{0:T(128)S(1)} %pad_add_fusion.refs_0_, f32[32,1152]{1,0:T(8,128)S(1)} %add_kernel.3.refs_1_.refs_4_, bf16[32,1152]{1,0:T(8,128)(2,1)S(1)} %collective-permute-done.20.refs_2_, s32[8,32]{1,0:T(8,128)S(1)} %bitcast.12, f32[32,1152]{1,0:T(8,128)S(1)} %add_kernel.3.refs_1_.refs_4_), custom_call_target="tpu_custom_call" | custom-call | tf_op jit(solution)/shard_map/finish_kernel/pallas_call | solution.py:253
  (39 shorter events, 1.7 us)
Async XLA Ops:
  1.6 6.0 %collective-permute-start = (bf16[32,2176]{1,0:T(8,128)(2,1)S(1)}, bf16[32,2176]{1,0:T(8,128)(2,1)S(1)}, u32[]{:S(2)}, u32[]{:S(2)}) collective-permute-start(bf16[32,2176]{1,0:T(8,128)(2,1)S(1)} %prepare_kernel.1.refs_0_), channel_id=1, source_target_pairs={{0,2},{1,5},{2,0},{3,7},{4,6},{5,1},{6,4},{7,3},{8,10},{9,13},{10,... | collective-permute-start | bytes 417800 | tf_op jit(solution)/shard_map/ppermute | solution.py:294
  7.6 11.7 %collective-permute-start.3 = (bf16[64,2176]{1,0:T(8,128)(2,1)S(1)}, bf16[64,2176]{1,0:T(8,128)(2,1)S(1)}, u32[]{:S(2)}, u32[]{:S(2)}) collective-permute-start(bf16[64,2176]{1,0:T(8,128)(2,1)S(1)} %join_kernel.4.refs_2_.refs_1_.refs_5_), channel_id=1, source_target_pairs={{0,4},{1,3},{2,6},{3,1},{4,0},{5,7},{6,2},{7,5},{8,12},{9,11},{10,... | collective-permute-start | bytes 835592 | tf_op jit(solution)/shard_map/ppermute | solution.py:294
  9.8 8.1 %collective-permute-start.1 = (bf16[32,2176]{1,0:T(8,128)(2,1)S(1)}, bf16[32,2176]{1,0:T(8,128)(2,1)S(1)}, u32[]{:S(2)}, u32[]{:S(2)}) collective-permute-start(bf16[32,2176]{1,0:T(8,128)(2,1)S(1)} %prepare_kernel.1.refs_0_), channel_id=1, source_target_pairs={{0,16},{1,17},{2,18},{3,19},{4,20},{5,21},{6,22},{7,23},{8,24},{9,... | collective-permute-start | bytes 417800 | tf_op jit(solution)/shard_map/ppermute | solution.py:294
  17.9 5.1 %collective-permute-start.2 = (bf16[32,2176]{1,0:T(8,128)(2,1)S(1)}, bf16[32,2176]{1,0:T(8,128)(2,1)S(1)}, u32[]{:S(2)}, u32[]{:S(2)}) collective-permute-start(bf16[32,2176]{1,0:T(8,128)(2,1)S(1)} %collective-permute-done.1.refs_1_.refs_0_), channel_id=1, source_target_pairs={{0,2},{1,5},{2,0},{3,7},{4,6},{5,1},{6,4},{7,3},{8,10},{9,13},{10,... | collective-permute-start | bytes 417800 | tf_op jit(solution)/shard_map/ppermute | solution.py:294
  18.7 11.0 %collective-permute-start.4 = (bf16[512,384]{1,0:T(8,128)(2,1)}, bf16[512,384]{1,0:T(8,128)(2,1)S(1)}, u32[]{:S(2)}, u32[]{:S(2)}) collective-permute-start(bf16[512,384]{1,0:T(8,128)(2,1)} %bitcast.13), channel_id=1, source_target_pairs={{0,1},{1,0},{2,3},{3,2},{4,5},{5,4},{6,7},{7,6},{8,9},{9,8},{10,11... | collective-permute-start | bytes 1179656 | tf_op jit(solution)/shard_map/ppermute | solution.py:21
  18.7 11.0 %collective-permute-start.5 = (bf16[512,384]{1,0:T(8,128)(2,1)}, bf16[512,384]{1,0:T(8,128)(2,1)}, u32[]{:S(2)}, u32[]{:S(2)}) collective-permute-start(bf16[512,384]{1,0:T(8,128)(2,1)} %bitcast.18), channel_id=1, source_target_pairs={{0,1},{1,0},{2,3},{3,2},{4,5},{5,4},{6,7},{7,6},{8,9},{9,8},{10,11... | collective-permute-start | bytes 1179656 | tf_op jit(solution)/shard_map/ppermute | solution.py:21
  19.2 10.5 %copy-start.1 = (bf16[1,512,384]{2,1,0:T(8,128)(2,1)S(1)}, bf16[1,512,384]{2,1,0:T(8,128)(2,1)}, u32[]{:S(2)}) copy-start(bf16[1,512,384]{2,1,0:T(8,128)(2,1)} %param.11) | copy-start | bytes 1179652
  19.2 10.5 %copy-start.2 = (bf16[1,512,384]{2,1,0:T(8,128)(2,1)S(1)}, bf16[1,512,384]{2,1,0:T(8,128)(2,1)}, u32[]{:S(2)}) copy-start(bf16[1,512,384]{2,1,0:T(8,128)(2,1)} %param.12) | copy-start | bytes 1179652
  19.2 10.5 %copy-start.3 = (bf16[1,384,512]{2,1,0:T(8,128)(2,1)S(1)}, bf16[1,384,512]{2,1,0:T(8,128)(2,1)}, u32[]{:S(2)}) copy-start(bf16[1,384,512]{2,1,0:T(8,128)(2,1)} %param.13) | copy-start | bytes 1179652
  19.2 10.5 %collective-permute-start.6 = (bf16[384,512]{1,0:T(8,128)(2,1)}, bf16[384,512]{1,0:T(8,128)(2,1)}, u32[]{:S(2)}, u32[]{:S(2)}) collective-permute-start(bf16[384,512]{1,0:T(8,128)(2,1)} %bitcast.23), channel_id=1, source_target_pairs={{0,1},{1,0},{2,3},{3,2},{4,5},{5,4},{6,7},{7,6},{8,9},{9,8},{10,11... | collective-permute-start | bytes 1179656 | tf_op jit(solution)/shard_map/ppermute | solution.py:21
  19.3 9.1 %collective-permute-start.7 = (bf16[64,2176]{1,0:T(8,128)(2,1)S(1)}, bf16[64,2176]{1,0:T(8,128)(2,1)S(1)}, u32[]{:S(2)}, u32[]{:S(2)}) collective-permute-start(bf16[64,2176]{1,0:T(8,128)(2,1)S(1)} %join_kernel.5.refs_1_), channel_id=1, source_target_pairs={{0,8},{1,9},{2,10},{3,11},{4,12},{5,13},{6,14},{7,15},{8,0},{9,1},... | collective-permute-start | bytes 835592 | tf_op jit(solution)/shard_map/ppermute | solution.py:294
  23.0 6.7 %collective-permute-start.9 = (bf16[64,2176]{1,0:T(8,128)(2,1)S(1)}, bf16[64,2176]{1,0:T(8,128)(2,1)S(1)}, u32[]{:S(2)}, u32[]{:S(2)}) collective-permute-start(bf16[64,2176]{1,0:T(8,128)(2,1)S(1)} %join_kernel.6.refs_1_.refs_2_.refs_6_), channel_id=1, source_target_pairs={{0,4},{1,3},{2,6},{3,1},{4,0},{5,7},{6,2},{7,5},{8,12},{9,11},{10,... | collective-permute-start | bytes 835592 | tf_op jit(solution)/shard_map/ppermute | solution.py:294
  28.4 7.4 %collective-permute-start.8 = (bf16[64,2176]{1,0:T(8,128)(2,1)S(1)}, bf16[64,2176]{1,0:T(8,128)(2,1)S(1)}, u32[]{:S(2)}, u32[]{:S(2)}) collective-permute-start(bf16[64,2176]{1,0:T(8,128)(2,1)S(1)} %pass_kernel.3.refs_9_.refs_0_), channel_id=1, source_target_pairs={{0,2},{1,5},{2,0},{3,7},{4,6},{5,1},{6,4},{7,3},{8,10},{9,13},{10,... | collective-permute-start | bytes 835592 | tf_op jit(solution)/shard_map/ppermute | solution.py:294
  32.1 7.9 %collective-permute-start.10 = (bf16[128,1152]{1,0:T(8,128)(2,1)S(1)}, bf16[128,1152]{1,0:T(8,128)(2,1)S(1)}, u32[]{:S(2)}, u32[]{:S(2)}) collective-permute-start(bf16[128,1152]{1,0:T(8,128)(2,1)S(1)} %get-tuple-element.38), channel_id=1, source_target_pairs={{0,4},{1,3},{2,6},{3,1},{4,0},{5,7},{6,2},{7,5},{8,12},{9,11},{10,... | collective-permute-start | bytes 884744 | tf_op jit(solution)/shard_map/ppermute | solution.py:294
  35.9 11.2 %collective-permute-start.12 = (bf16[128,2176]{1,0:T(8,128)(2,1)S(1)}, bf16[128,2176]{1,0:T(8,128)(2,1)S(1)}, u32[]{:S(2)}, u32[]{:S(2)}) collective-permute-start(bf16[128,2176]{1,0:T(8,128)(2,1)S(1)} %join_kernel.7.refs_9_.refs_1_), channel_id=1, source_target_pairs={{0,4},{1,3},{2,6},{3,1},{4,0},{5,7},{6,2},{7,5},{8,12},{9,11},{10,... | collective-permute-start | bytes 1671176 | tf_op jit(solution)/shard_map/ppermute | solution.py:294
  40.1 11.1 %collective-permute-start.11 = (bf16[64,1152]{1,0:T(8,128)(2,1)S(1)}, bf16[64,1152]{1,0:T(8,128)(2,1)S(1)}, u32[]{:S(2)}, u32[]{:S(2)}) collective-permute-start(bf16[64,1152]{1,0:T(8,128)(2,1)S(1)} %get-tuple-element.41.refs_8_), channel_id=1, source_target_pairs={{0,2},{1,5},{2,0},{3,7},{4,6},{5,1},{6,4},{7,3},{8,10},{9,13},{10,... | collective-permute-start | bytes 442376 | tf_op jit(solution)/shard_map/ppermute | solution.py:294
  49.4 6.8 %collective-permute-start.14 = (bf16[128,1152]{1,0:T(8,128)(2,1)S(1)}, bf16[128,1152]{1,0:T(8,128)(2,1)S(1)}, u32[]{:S(2)}, u32[]{:S(2)}) collective-permute-start(bf16[128,1152]{1,0:T(8,128)(2,1)S(1)} %get-tuple-element.47), channel_id=1, source_target_pairs={{0,4},{1,3},{2,6},{3,1},{4,0},{5,7},{6,2},{7,5},{8,12},{9,11},{10,... | collective-permute-start | bytes 884744 | tf_op jit(solution)/shard_map/ppermute | solution.py:294
  53.3 14.3 %collective-permute-start.17 = (bf16[512,384]{1,0:T(8,128)(2,1)S(1)}, bf16[512,384]{1,0:T(8,128)(2,1)S(1)}, u32[]{:S(2)}, u32[]{:S(2)}) collective-permute-start(bf16[512,384]{1,0:T(8,128)(2,1)S(1)} %get-tuple-element.58), channel_id=1, source_target_pairs={{0,1},{1,0},{2,3},{3,2},{4,5},{5,4},{6,7},{7,6},{8,9},{9,8},{10,11... | collective-permute-start | bytes 1179656 | tf_op jit(solution)/shard_map/ppermute | solution.py:21
  53.3 14.2 %collective-permute-start.18 = (bf16[512,384]{1,0:T(8,128)(2,1)S(1)}, bf16[512,384]{1,0:T(8,128)(2,1)S(1)}, u32[]{:S(2)}, u32[]{:S(2)}) collective-permute-start(bf16[512,384]{1,0:T(8,128)(2,1)S(1)} %get-tuple-element.59), channel_id=1, source_target_pairs={{0,1},{1,0},{2,3},{3,2},{4,5},{5,4},{6,7},{7,6},{8,9},{9,8},{10,11... | collective-permute-start | bytes 1179656 | tf_op jit(solution)/shard_map/ppermute | solution.py:21
  53.8 13.7 %collective-permute-start.19 = (bf16[384,512]{1,0:T(8,128)(2,1)S(1)}, bf16[384,512]{1,0:T(8,128)(2,1)S(1)}, u32[]{:S(2)}, u32[]{:S(2)}) collective-permute-start(bf16[384,512]{1,0:T(8,128)(2,1)S(1)} %get-tuple-element.52.refs_2_), channel_id=1, source_target_pairs={{0,1},{1,0},{2,3},{3,2},{4,5},{5,4},{6,7},{7,6},{8,9},{9,8},{10,11... | collective-permute-start | bytes 1179656 | tf_op jit(solution)/shard_map/ppermute | solution.py:21
  56.3 7.6 %collective-permute-start.15 = (bf16[64,1152]{1,0:T(8,128)(2,1)S(1)}, bf16[64,1152]{1,0:T(8,128)(2,1)S(1)}, u32[]{:S(2)}, u32[]{:S(2)}) collective-permute-start(bf16[64,1152]{1,0:T(8,128)(2,1)S(1)} %get-tuple-element.53.refs_2_), channel_id=1, source_target_pairs={{0,2},{1,5},{2,0},{3,7},{4,6},{5,1},{6,4},{7,3},{8,10},{9,13},{10,... | collective-permute-start | bytes 442376 | tf_op jit(solution)/shard_map/ppermute | solution.py:294
  57.9 6.0 %collective-permute-start.13 = (bf16[32,1152]{1,0:T(8,128)(2,1)S(1)}, bf16[32,1152]{1,0:T(8,128)(2,1)S(1)}, u32[]{:S(2)}, u32[]{:S(2)}) collective-permute-start(bf16[32,1152]{1,0:T(8,128)(2,1)S(1)} %get-tuple-element.45.refs_15_), channel_id=1, source_target_pairs={{0,16},{1,17},{2,18},{3,19},{4,20},{5,21},{6,22},{7,23},{8,24},{9,... | collective-permute-start | bytes 221192 | tf_op jit(solution)/shard_map/ppermute | solution.py:294
  64.0 4.8 %collective-permute-start.16 = (bf16[32,1152]{1,0:T(8,128)(2,1)S(1)}, bf16[32,1152]{1,0:T(8,128)(2,1)S(1)}, u32[]{:S(2)}, u32[]{:S(2)}) collective-permute-start(bf16[32,1152]{1,0:T(8,128)(2,1)S(1)} %get-tuple-element.55), channel_id=1, source_target_pairs={{0,8},{1,9},{2,10},{3,11},{4,12},{5,13},{6,14},{7,15},{8,0},{9,1},... | collective-permute-start | bytes 221192 | tf_op jit(solution)/shard_map/ppermute | solution.py:294
  64.5 6.3 %collective-permute-start.20 = (bf16[32,1152]{1,0:T(8,128)(2,1)S(1)}, bf16[32,1152]{1,0:T(8,128)(2,1)S(1)}, u32[]{:S(2)}, u32[]{:S(2)}) collective-permute-start(bf16[32,1152]{1,0:T(8,128)(2,1)S(1)} %get-tuple-element.60.refs_5_), channel_id=1, source_target_pairs={{0,24},{1,25},{2,26},{3,27},{4,28},{5,29},{6,30},{7,31},{8,16},{9,... | collective-permute-start | bytes 221192 | tf_op jit(solution)/shard_map/ppermute | solution.py:294
  67.5 3.2 %copy-start = (s32[32,8]{0,1:T(8,128)S(1)}, s32[32,8]{0,1:T(8,128)}, u32[]{:S(2)}) copy-start(s32[32,8]{0,1:T(8,128)} %param.9) | copy-start | bytes 3076

commit v8 on v7

--- a/solution.py
+++ b/solution.py
@@ -126,28 +126,28 @@
         grad_gate = (back * pre_up * slope).astype(BF16)
         grad_up = (back * active).astype(BF16)
         scaled = (hidden * gates).astype(BF16)
-        pieces = (
-            dot(grad_gate, gate_own[...], NT) + dot(grad_up, up_own[...], NT),
-            dot(grad_gate, gate_other[...], NT) + dot(grad_up, up_other[...], NT),
-            jnp.where(is_own, gate_grads, 0.0),
-        )
         middle = count // 2
+
+        def put(rows, cols):
+            for i in range(number):
+                part = rows[i * at.size : (i + 1) * at.size]
+                if at.size == count:
+                    row_grads[pl.ds(i * middle, middle), cols] = part[:middle]
+                    row_grads[pl.ds((number + i) * middle, middle), cols] = part[middle:]
+                else:
+                    start = at.start + at.start // middle * (number - 1) * middle + i * middle
+                    row_grads[pl.ds(pl.multiple_of(start, at.size), at.size), cols] = part
+
+        to_own = dot(grad_gate, gate_own[...], NT) + dot(grad_up, up_own[...], NT)
+        put(to_own.astype(BF16), pl.ds(0, half))
+        to_other = dot(grad_gate, gate_other[...], NT) + dot(grad_up, up_other[...], NT)
+        put(to_other.astype(BF16), pl.ds(half, half))
+        put(jnp.where(is_own, gate_grads, 0.0).astype(BF16), pl.ds(features, lanes))
         for i in range(number):
             part = slice(i * at.size, (i + 1) * at.size)
             grads[i, at, pl.ds(0, width)] = grad_gate[part]
             grads[i, at, pl.ds(width, width)] = grad_up[part]
             scaled_hidden[i, at, :] = scaled[part]
-            begin = 0
-            for piece in pieces:
-                cols = pl.ds(begin, piece.shape[1])
-                begin += piece.shape[1]
-                rows = piece[part].astype(BF16)
-                if at.size == count:
-                    row_grads[pl.ds(i * middle, middle), cols] = rows[:middle]
-                    row_grads[pl.ds((number + i) * middle, middle), cols] = rows[middle:]
-                else:
-                    place_at = at.start + at.start // middle * (number - 1) * middle + i * middle
-                    row_grads[pl.ds(pl.multiple_of(place_at, at.size), at.size), cols] = rows
 
     for_chunks(count, step, CHUNK // number)
 
@@ -334,9 +334,9 @@
     def at_offset(x, i):
         return exchange(x, (offsets[i], offsets[i]))
 
-    def join(first, second):
+    def join(first, second, flops=0):
         shape = (2 * first.shape[0], first.shape[1])
-        return run(join_kernel, [(shape, BF16)], None, first, second)[0]
+        return run(join_kernel, [(shape, BF16)], None, first, second, flops=flops)[0]
 
     def after_all(x, *others):
         before.extend(others)
@@ -367,7 +367,7 @@
     far_two = at_offset(block, 0)
     first_own = join(block, exchange(block, near_a))
     second_own = exchange(first_own, near_b)
-    near_1 = at_offset(join(block, far_two), 1)
+    near_1 = at_offset(join(block, far_two, flops=4 * 10**9), 1)
     second_own = after_all(second_own)
     first_two = join(far_two, exchange(far_two, near_a))
     second_two = exchange(first_two, near_b)
@@ -392,14 +392,14 @@
             ((half, width), BF16),
             ((width, half), BF16),
         ],
-        place, *saved, limit=10,
+        place, *saved, limit=10, flops=6 * 10**9,
     )
     gots = [swap_core(give) for give in gives]
     kept_1, give = split(kept_1, got_1, (F32, BF16))
     got_1 = exchange(give, near_a)
-    total = collect(total, back_two)
     give_one, give_both = split(kept_1, got_1, (BF16, BF16))
     back_one, back_both = at_offset(give_one, 1), at_offset(give_both, 2)
+    total = collect(total, back_two)
     grad_gate, grad_up, grad_down, _ = run(
         settle_kernel,
         [((half, width), BF16), ((half, width), BF16), ((width, half), BF16), ((8, 128), F32)],

time: 72.9 us -> 69.1 us (0.948)
  starting transfers between devices: 27.9 us -> 23.2 us
  waiting for transfers between devices: 28.1 us -> 29.5 us
    ppermute x15, starting transfers between devices: 26.7 us -> 22 us  [exchange(): return lax.ppermute(x, DEVICES, pairs)]
    ppermute x15, waiting for transfers between devices: 28 us -> 29.4 us  [exchange(): return lax.ppermute(x, DEVICES, pairs)]
  transfers between devices with their start and end apart: 21 -> 21, of which waited for: 9 -> 10; matrix products, arithmetic and copies ran while one was open for 0% -> 0% of each run, Pallas kernels for 18% -> 19%
where the time goes in v8:
time: 69.1 us; the launch traced here: 68.8 us
  waiting for transfers between devices  29.5 us (43%)
  starting transfers between devices  23.2 us (34%)
  Pallas kernels  15.2 us (22%)
  between operations  0.84 us (1%)
    ppermute x15, waiting for transfers between devices, exchange(): return lax.ppermute(x, DEVICES, pairs)  29.4 us
    ppermute x15, starting transfers between devices, exchange(): return lax.ppermute(x, DEVICES, pairs)  22 us
    pallas_call x19, Pallas kernels, call(): pl.pallas_call(run, out_shape=out_shape, in_specs=[pl.BlockSpec(memory_sp...  14.3 us
  transfers between devices with their start and end apart: 21, of which 10 were waited for; matrix products, arithmetic and copies ran while one was open for 0% of the time, Pallas kernels for 19%

profile of v8, /device:TPU:0, one launch (start us, length us, event | category | flops | bytes accessed | tf_op | source)
XLA Modules:
  0.0 68.8 jit_solution(13223841369589100701)
XLA Ops:
  0.6 0.9 %prepare_kernel.1.refs_0_ = bf16[32,2176]{1,0:T(8,128)(2,1)S(1)} custom-call(bf16[32,1024]{1,0:T(8,128)(2,1)} %tokens.1, bf16[32,1024]{1,0:T(8,128)(2,1)} %cotangent.1, s32[8,32]{1,0:T(8,128)} %bitcast.11, bf16[8,32]{1,0:T(8,128)(2,1)} %bitcast.28), custom_call_target="tpu_custom_call" | custom-call | tf_op jit(solution)/shard_map/prepare_kernel/pallas_call | solution.py:309
  1.6 3.0 %collective-permute-start = (bf16[32,2176]{1,0:T(8,128)(2,1)S(1)}, bf16[32,2176]{1,0:T(8,128)(2,1)S(1)}, u32[]{:S(2)}, u32[]{:S(2)}) collective-permute-start(bf16[32,2176]{1,0:T(8,128)(2,1)S(1)} %prepare_kernel.1.refs_0_), channel_id=1, source_target_pairs={{0,2},{1,5},{2,0},{3,7},{4,6},{5,1},{6,4},{7,3},{8,10},{9,13},{10,... | collective-permute-start | bytes 417800 | tf_op jit(solution)/shard_map/ppermute | solution.py:294
  4.6 2.6 %collective-permute-start.1 = (bf16[32,2176]{1,0:T(8,128)(2,1)S(1)}, bf16[32,2176]{1,0:T(8,128)(2,1)S(1)}, u32[]{:S(2)}, u32[]{:S(2)}) collective-permute-start(bf16[32,2176]{1,0:T(8,128)(2,1)S(1)} %prepare_kernel.1.refs_0_), channel_id=1, source_target_pairs={{0,16},{1,17},{2,18},{3,19},{4,20},{5,21},{6,22},{7,23},{8,24},{9,... | collective-permute-start | bytes 417800 | tf_op jit(solution)/shard_map/ppermute | solution.py:294
  7.2 0.5 collective-permute-start.5
  7.7 2.0 %collective-permute-start.3 = (bf16[64,2176]{1,0:T(8,128)(2,1)S(1)}, bf16[64,2176]{1,0:T(8,128)(2,1)S(1)}, u32[]{:S(2)}, u32[]{:S(2)}) collective-permute-start(bf16[64,2176]{1,0:T(8,128)(2,1)S(1)} %join_kernel.4.refs_2_.refs_1_.refs_5_), channel_id=1, source_target_pairs={{0,4},{1,3},{2,6},{3,1},{4,0},{5,7},{6,2},{7,5},{8,12},{9,11},{10,... | collective-permute-start | bytes 835592 | tf_op jit(solution)/shard_map/ppermute | solution.py:294
  9.8 3.9 %collective-permute-done.1.refs_1_.refs_0_ = bf16[32,2176]{1,0:T(8,128)(2,1)S(1)} collective-permute-done((bf16[32,2176]{1,0:T(8,128)(2,1)S(1)}, bf16[32,2176]{1,0:T(8,128)(2,1)S(1)}, u32[]{:S(2)}, u32[]{:S(2)}) %collective-permute-start.1) | collective-permute-done | bytes 139296 | tf_op jit(solution)/shard_map/ppermute | solution.py:294
  13.6 1.5 %collective-permute-start.2 = (bf16[32,2176]{1,0:T(8,128)(2,1)S(1)}, bf16[32,2176]{1,0:T(8,128)(2,1)S(1)}, u32[]{:S(2)}, u32[]{:S(2)}) collective-permute-start(bf16[32,2176]{1,0:T(8,128)(2,1)S(1)} %collective-permute-done.1.refs_1_.refs_0_), channel_id=1, source_target_pairs={{0,2},{1,5},{2,0},{3,7},{4,6},{5,1},{6,4},{7,3},{8,10},{9,13},{10,... | collective-permute-start | bytes 417800 | tf_op jit(solution)/shard_map/ppermute | solution.py:294
  15.2 1.2 %collective-permute-start.7 = (bf16[64,2176]{1,0:T(8,128)(2,1)S(1)}, bf16[64,2176]{1,0:T(8,128)(2,1)S(1)}, u32[]{:S(2)}, u32[]{:S(2)}) collective-permute-start(bf16[64,2176]{1,0:T(8,128)(2,1)S(1)} %join_kernel.5.refs_1_), channel_id=1, source_target_pairs={{0,8},{1,9},{2,10},{3,11},{4,12},{5,13},{6,14},{7,15},{8,0},{9,1},... | collective-permute-start | bytes 835592 | tf_op jit(solution)/shard_map/ppermute | solution.py:294
  16.4 2.3 %collective-permute-done.2.refs_1_ = bf16[32,2176]{1,0:T(8,128)(2,1)S(1)} collective-permute-done((bf16[32,2176]{1,0:T(8,128)(2,1)S(1)}, bf16[32,2176]{1,0:T(8,128)(2,1)S(1)}, u32[]{:S(2)}, u32[]{:S(2)}) %collective-permute-start.2) | collective-permute-done | bytes 139296 | tf_op jit(solution)/shard_map/ppermute | solution.py:294
  18.7 0.5 collective-permute-start.9
  19.3 3.2 %collective-permute-done.7.refs_0_ = bf16[64,2176]{1,0:T(8,128)(2,1)S(1)} collective-permute-done((bf16[64,2176]{1,0:T(8,128)(2,1)S(1)}, bf16[64,2176]{1,0:T(8,128)(2,1)S(1)}, u32[]{:S(2)}, u32[]{:S(2)}) %collective-permute-start.7) | collective-permute-done | bytes 278560 | tf_op jit(solution)/shard_map/ppermute | solution.py:294
  22.6 1.4 %collective-permute-start.8 = (bf16[64,2176]{1,0:T(8,128)(2,1)S(1)}, bf16[64,2176]{1,0:T(8,128)(2,1)S(1)}, u32[]{:S(2)}, u32[]{:S(2)}) collective-permute-start(bf16[64,2176]{1,0:T(8,128)(2,1)S(1)} %pass_kernel.3.refs_9_.refs_0_), channel_id=1, source_target_pairs={{0,2},{1,5},{2,0},{3,7},{4,6},{5,1},{6,4},{7,3},{8,10},{9,13},{10,... | collective-permute-start | bytes 835592 | tf_op jit(solution)/shard_map/ppermute | solution.py:294
  23.9 3.8 %collective-permute-done.9.refs_2_ = bf16[64,2176]{1,0:T(8,128)(2,1)} collective-permute-done((bf16[64,2176]{1,0:T(8,128)(2,1)S(1)}, bf16[64,2176]{1,0:T(8,128)(2,1)}, u32[]{:S(2)}, u32[]{:S(2)}) %collective-permute-start.9) | collective-permute-done | bytes 278560 | tf_op jit(solution)/shard_map/ppermute | solution.py:294
  27.8 2.3 %expert_kernel.4 = (bf16[128,1152]{1,0:T(8,128)(2,1)S(1)}, bf16[2,64,768]{2,1,0:T(8,128)(2,1)S(1)}, bf16[2,64,384]{2,1,0:T(8,128)(2,1)S(1)}) custom-call(s32[2]{0:T(128)S(1)} %pad_add_fusion.refs_0_, bf16[64,2176]{1,0:T(8,128)(2,1)S(1)} %pass_kernel.2.refs_2_.refs_1_, bf16[64,2176]{1,0:T(8,128)(2,1)} %collective-permute-done.9.refs_2_, ...), custom_call_target="tpu_custom_call" | custom-call | flops 6000000000 | tf_op jit(solution)/shard_map/expert_kernel/pallas_call | solution.py:253
  30.2 2.5 %collective-permute-start.12 = (bf16[128,2176]{1,0:T(8,128)(2,1)S(1)}, bf16[128,2176]{1,0:T(8,128)(2,1)S(1)}, u32[]{:S(2)}, u32[]{:S(2)}) collective-permute-start(bf16[128,2176]{1,0:T(8,128)(2,1)S(1)} %join_kernel.7.refs_9_.refs_1_), channel_id=1, source_target_pairs={{0,4},{1,3},{2,6},{3,1},{4,0},{5,7},{6,2},{7,5},{8,12},{9,11},{10,... | collective-permute-start | bytes 1671176 | tf_op jit(solution)/shard_map/ppermute | solution.py:294
  32.7 2.2 %expert_kernel.5 = (bf16[128,1152]{1,0:T(8,128)(2,1)S(1)}, bf16[2,64,768]{2,1,0:T(8,128)(2,1)S(1)}, bf16[2,64,384]{2,1,0:T(8,128)(2,1)S(1)}) custom-call(s32[2]{0:T(128)S(1)} %pad_add_fusion.refs_0_, bf16[64,2176]{1,0:T(8,128)(2,1)S(1)} %join_kernel.4.refs_2_.refs_1_.refs_5_, bf16[64,2176]{1,0:T(8,128)(2,1)S(1)} %join_kernel.6.refs_1_.refs_2_.refs_6_, ...), custom_call_target="tpu_custom_call" | custom-call | flops 6000000000 | tf_op jit(solution)/shard_map/expert_kernel/pallas_call | solution.py:253
  34.9 3.5 %collective-permute-done.10.refs_1_ = bf16[128,1152]{1,0:T(8,128)(2,1)S(1)} collective-permute-done((bf16[128,1152]{1,0:T(8,128)(2,1)S(1)}, bf16[128,1152]{1,0:T(8,128)(2,1)S(1)}, u32[]{:S(2)}, u32[]{:S(2)}) %collective-permute-start.10) | collective-permute-done | bytes 294944 | tf_op jit(solution)/shard_map/ppermute | solution.py:294
  38.5 1.1 %collective-permute-start.11 = (bf16[64,1152]{1,0:T(8,128)(2,1)S(1)}, bf16[64,1152]{1,0:T(8,128)(2,1)S(1)}, u32[]{:S(2)}, u32[]{:S(2)}) collective-permute-start(bf16[64,1152]{1,0:T(8,128)(2,1)S(1)} %get-tuple-element.41.refs_8_), channel_id=1, source_target_pairs={{0,2},{1,5},{2,0},{3,7},{4,6},{5,1},{6,4},{7,3},{8,10},{9,13},{10,... | collective-permute-start | bytes 442376 | tf_op jit(solution)/shard_map/ppermute | solution.py:294
  39.6 2.2 %expert_kernel.6 = (bf16[128,1152]{1,0:T(8,128)(2,1)S(1)}, bf16[1,128,768]{2,1,0:T(8,128)(2,1)S(1)}, bf16[1,128,384]{2,1,0:T(8,128)(2,1)S(1)}) custom-call(s32[2]{0:T(128)S(1)} %pad_add_fusion.refs_0_, bf16[128,2176]{1,0:T(8,128)(2,1)S(1)} %join_kernel.7.refs_9_.refs_1_, bf16[512,384]{1,0:T(8,128)(2,1)S(1)} %bitcast.16, ...), custom_call_target="tpu_custom_call" | custom-call | flops 6000000000 | tf_op jit(solution)/shard_map/expert_kernel/pallas_call | solution.py:253
  41.8 2.6 %collective-permute-done.12.refs_1_.refs_12_ = bf16[128,2176]{1,0:T(8,128)(2,1)S(1)} collective-permute-done((bf16[128,2176]{1,0:T(8,128)(2,1)S(1)}, bf16[128,2176]{1,0:T(8,128)(2,1)S(1)}, u32[]{:S(2)}, u32[]{:S(2)}) %collective-permute-start.12) | collective-permute-done | bytes 557088 | tf_op jit(solution)/shard_map/ppermute | solution.py:294
  44.4 2.2 %expert_kernel.7 = (bf16[128,1152]{1,0:T(8,128)(2,1)S(1)}, bf16[1,128,768]{2,1,0:T(8,128)(2,1)S(1)}, bf16[1,128,384]{2,1,0:T(8,128)(2,1)S(1)}) custom-call(s32[2]{0:T(128)S(1)} %pad_add_fusion.refs_0_, bf16[128,2176]{1,0:T(8,128)(2,1)S(1)} %collective-permute-done.12.refs_1_.refs_12_, bf16[512,384]{1,0:T(8,128)(2,1)S(1)} %bitcast.17, ...), custom_call_target="tpu_custom_call" | custom-call | flops 6000000000 | tf_op jit(solution)/shard_map/expert_kernel/pallas_call | solution.py:253
  46.8 2.5 %weight_kernel.1 = (f32[512,768]{1,0:T(8,128)S(1)}, f32[384,512]{1,0:T(8,128)S(1)}, bf16[512,384]{1,0:T(8,128)(2,1)S(1)}, bf16[512,384]{1,0:T(8,128)(2,1)S(1)}, bf16[384,512]{1,0:T(8,128)(2,1)S(1)}) custom-call(s32[2]{0:T(128)S(1)} %pad_add_fusion.refs_0_, bf16[64,2176]{1,0:T(8,128)(2,1)S(1)} %pass_kernel.2.refs_2_.refs_1_, ...), custom_call_target="tpu_custom_call" | custom-call | flops 6000000000 | tf_op jit(solution)/shard_map/weight_kernel/pallas_call | solution.py:253
  49.9 3.6 %collective-permute-done.14.refs_1_ = bf16[128,1152]{1,0:T(8,128)(2,1)S(1)} collective-permute-done((bf16[128,1152]{1,0:T(8,128)(2,1)S(1)}, bf16[128,1152]{1,0:T(8,128)(2,1)S(1)}, u32[]{:S(2)}, u32[]{:S(2)}) %collective-permute-start.14) | collective-permute-done | bytes 294944 | tf_op jit(solution)/shard_map/ppermute | solution.py:294
  53.5 1.2 %collective-permute-start.15 = (bf16[64,1152]{1,0:T(8,128)(2,1)S(1)}, bf16[64,1152]{1,0:T(8,128)(2,1)S(1)}, u32[]{:S(2)}, u32[]{:S(2)}) collective-permute-start(bf16[64,1152]{1,0:T(8,128)(2,1)S(1)} %get-tuple-element.54.refs_2_), channel_id=1, source_target_pairs={{0,2},{1,5},{2,0},{3,7},{4,6},{5,1},{6,4},{7,3},{8,10},{9,13},{10,... | collective-permute-start | bytes 442376 | tf_op jit(solution)/shard_map/ppermute | solution.py:294
  54.8 1.5 %collective-permute-start.13 = (bf16[32,1152]{1,0:T(8,128)(2,1)S(1)}, bf16[32,1152]{1,0:T(8,128)(2,1)S(1)}, u32[]{:S(2)}, u32[]{:S(2)}) collective-permute-start(bf16[32,1152]{1,0:T(8,128)(2,1)S(1)} %get-tuple-element.45.refs_15_), channel_id=1, source_target_pairs={{0,16},{1,17},{2,18},{3,19},{4,20},{5,21},{6,22},{7,23},{8,24},{9,... | collective-permute-start | bytes 221192 | tf_op jit(solution)/shard_map/ppermute | solution.py:294
  56.2 2.5 %collective-permute-done.15.refs_1_ = bf16[64,1152]{1,0:T(8,128)(2,1)S(1)} collective-permute-done((bf16[64,1152]{1,0:T(8,128)(2,1)S(1)}, bf16[64,1152]{1,0:T(8,128)(2,1)S(1)}, u32[]{:S(2)}, u32[]{:S(2)}) %collective-permute-start.15) | collective-permute-done | bytes 147488 | tf_op jit(solution)/shard_map/ppermute | solution.py:294
  58.8 0.6 collective-permute-start.16
  59.4 1.8 %collective-permute-done.13.refs_1_ = bf16[32,1152]{1,0:T(8,128)(2,1)S(1)} collective-permute-done((bf16[32,1152]{1,0:T(8,128)(2,1)S(1)}, bf16[32,1152]{1,0:T(8,128)(2,1)S(1)}, u32[]{:S(2)}, u32[]{:S(2)}) %collective-permute-start.13) | collective-permute-done | bytes 73760 | tf_op jit(solution)/shard_map/ppermute | solution.py:294
  61.3 2.7 %collective-permute-start.20 = (bf16[32,1152]{1,0:T(8,128)(2,1)S(1)}, bf16[32,1152]{1,0:T(8,128)(2,1)S(1)}, u32[]{:S(2)}, u32[]{:S(2)}) collective-permute-start(bf16[32,1152]{1,0:T(8,128)(2,1)S(1)} %get-tuple-element.55.refs_2_), channel_id=1, source_target_pairs={{0,24},{1,25},{2,26},{3,27},{4,28},{5,29},{6,30},{7,31},{8,16},{9,... | collective-permute-start | bytes 221192 | tf_op jit(solution)/shard_map/ppermute | solution.py:294
  64.1 1.2 %settle_kernel.1 = (bf16[512,384]{1,0:T(8,128)(2,1)}, bf16[512,384]{1,0:T(8,128)(2,1)}, bf16[384,512]{1,0:T(8,128)(2,1)}, f32[8,128]{1,0:T(8,128)S(1)}) custom-call(f32[512,768]{1,0:T(8,128)S(1)} %get-tuple-element.57.refs_0_, f32[384,512]{1,0:T(8,128)S(1)} %get-tuple-element.58.refs_1_, bf16[512,384]{1,0:T(8,128)(2,1)S(1)} %collective-permute-done.17.refs_2_, ...), custom_call_target="tpu_custom_call" | custom-call | tf_op jit(solution)/shard_map/settle_kernel/pallas_call | solution.py:253
  65.3 2.1 %collective-permute-done.20.refs_2_ = bf16[32,1152]{1,0:T(8,128)(2,1)S(1)} collective-permute-done((bf16[32,1152]{1,0:T(8,128)(2,1)S(1)}, bf16[32,1152]{1,0:T(8,128)(2,1)S(1)}, u32[]{:S(2)}, u32[]{:S(2)}) %collective-permute-start.20) | collective-permute-done | bytes 73760 | tf_op jit(solution)/shard_map/ppermute | solution.py:294
  67.4 1.4 %finish_kernel.1 = (bf16[32,1024]{1,0:T(8,128)(2,1)}, bf16[8,32]{1,0:T(8,128)(2,1)}) custom-call(s32[2]{0:T(128)S(1)} %pad_add_fusion.refs_0_, f32[32,1152]{1,0:T(8,128)S(1)} %add_kernel.3.refs_1_.refs_4_, bf16[32,1152]{1,0:T(8,128)(2,1)S(1)} %collective-permute-done.20.refs_2_, s32[8,32]{1,0:T(8,128)S(1)} %bitcast.12, f32[32,1152]{1,0:T(8,128)S(1)} %add_kernel.3.refs_1_.refs_4_), custom_call_target="tpu_custom_call" | custom-call | tf_op jit(solution)/shard_map/finish_kernel/pallas_call | solution.py:253
  (39 shorter events, 1.3 us)
Async XLA Ops:
  1.6 6.1 %collective-permute-start = (bf16[32,2176]{1,0:T(8,128)(2,1)S(1)}, bf16[32,2176]{1,0:T(8,128)(2,1)S(1)}, u32[]{:S(2)}, u32[]{:S(2)}) collective-permute-start(bf16[32,2176]{1,0:T(8,128)(2,1)S(1)} %prepare_kernel.1.refs_0_), channel_id=1, source_target_pairs={{0,2},{1,5},{2,0},{3,7},{4,6},{5,1},{6,4},{7,3},{8,10},{9,13},{10,... | collective-permute-start | bytes 417800 | tf_op jit(solution)/shard_map/ppermute | solution.py:294
  4.6 9.0 %collective-permute-start.1 = (bf16[32,2176]{1,0:T(8,128)(2,1)S(1)}, bf16[32,2176]{1,0:T(8,128)(2,1)S(1)}, u32[]{:S(2)}, u32[]{:S(2)}) collective-permute-start(bf16[32,2176]{1,0:T(8,128)(2,1)S(1)} %prepare_kernel.1.refs_0_), channel_id=1, source_target_pairs={{0,16},{1,17},{2,18},{3,19},{4,20},{5,21},{6,22},{7,23},{8,24},{9,... | collective-permute-start | bytes 417800 | tf_op jit(solution)/shard_map/ppermute | solution.py:294
  7.2 16.8 %collective-permute-start.4 = (bf16[512,384]{1,0:T(8,128)(2,1)}, bf16[512,384]{1,0:T(8,128)(2,1)S(1)}, u32[]{:S(2)}, u32[]{:S(2)}) collective-permute-start(bf16[512,384]{1,0:T(8,128)(2,1)} %bitcast.13), channel_id=1, source_target_pairs={{0,1},{1,0},{2,3},{3,2},{4,5},{5,4},{6,7},{7,6},{8,9},{9,8},{10,11... | collective-permute-start | bytes 1179656 | tf_op jit(solution)/shard_map/ppermute | solution.py:21
  7.2 16.8 %collective-permute-start.5 = (bf16[512,384]{1,0:T(8,128)(2,1)}, bf16[512,384]{1,0:T(8,128)(2,1)S(1)}, u32[]{:S(2)}, u32[]{:S(2)}) collective-permute-start(bf16[512,384]{1,0:T(8,128)(2,1)} %bitcast.18), channel_id=1, source_target_pairs={{0,1},{1,0},{2,3},{3,2},{4,5},{5,4},{6,7},{7,6},{8,9},{9,8},{10,11... | collective-permute-start | bytes 1179656 | tf_op jit(solution)/shard_map/ppermute | solution.py:21
  7.7 16.3 %collective-permute-start.6 = (bf16[384,512]{1,0:T(8,128)(2,1)}, bf16[384,512]{1,0:T(8,128)(2,1)}, u32[]{:S(2)}, u32[]{:S(2)}) collective-permute-start(bf16[384,512]{1,0:T(8,128)(2,1)} %bitcast.23), channel_id=1, source_target_pairs={{0,1},{1,0},{2,3},{3,2},{4,5},{5,4},{6,7},{7,6},{8,9},{9,8},{10,11... | collective-permute-start | bytes 1179656 | tf_op jit(solution)/shard_map/ppermute | solution.py:21
  7.7 7.5 %collective-permute-start.3 = (bf16[64,2176]{1,0:T(8,128)(2,1)S(1)}, bf16[64,2176]{1,0:T(8,128)(2,1)S(1)}, u32[]{:S(2)}, u32[]{:S(2)}) collective-permute-start(bf16[64,2176]{1,0:T(8,128)(2,1)S(1)} %join_kernel.4.refs_2_.refs_1_.refs_5_), channel_id=1, source_target_pairs={{0,4},{1,3},{2,6},{3,1},{4,0},{5,7},{6,2},{7,5},{8,12},{9,11},{10,... | collective-permute-start | bytes 835592 | tf_op jit(solution)/shard_map/ppermute | solution.py:294
  13.6 5.1 %collective-permute-start.2 = (bf16[32,2176]{1,0:T(8,128)(2,1)S(1)}, bf16[32,2176]{1,0:T(8,128)(2,1)S(1)}, u32[]{:S(2)}, u32[]{:S(2)}) collective-permute-start(bf16[32,2176]{1,0:T(8,128)(2,1)S(1)} %collective-permute-done.1.refs_1_.refs_0_), channel_id=1, source_target_pairs={{0,2},{1,5},{2,0},{3,7},{4,6},{5,1},{6,4},{7,3},{8,10},{9,13},{10,... | collective-permute-start | bytes 417800 | tf_op jit(solution)/shard_map/ppermute | solution.py:294
  15.1 12.6 %copy-start.1 = (bf16[1,512,384]{2,1,0:T(8,128)(2,1)S(1)}, bf16[1,512,384]{2,1,0:T(8,128)(2,1)}, u32[]{:S(2)}) copy-start(bf16[1,512,384]{2,1,0:T(8,128)(2,1)} %param.11) | copy-start | bytes 1179652
  15.2 12.6 %copy-start.2 = (bf16[1,512,384]{2,1,0:T(8,128)(2,1)S(1)}, bf16[1,512,384]{2,1,0:T(8,128)(2,1)}, u32[]{:S(2)}) copy-start(bf16[1,512,384]{2,1,0:T(8,128)(2,1)} %param.12) | copy-start | bytes 1179652
  15.2 12.6 %copy-start.3 = (bf16[1,384,512]{2,1,0:T(8,128)(2,1)S(1)}, bf16[1,384,512]{2,1,0:T(8,128)(2,1)}, u32[]{:S(2)}) copy-start(bf16[1,384,512]{2,1,0:T(8,128)(2,1)} %param.13) | copy-start | bytes 1179652
  15.2 7.4 %collective-permute-start.7 = (bf16[64,2176]{1,0:T(8,128)(2,1)S(1)}, bf16[64,2176]{1,0:T(8,128)(2,1)S(1)}, u32[]{:S(2)}, u32[]{:S(2)}) collective-permute-start(bf16[64,2176]{1,0:T(8,128)(2,1)S(1)} %join_kernel.5.refs_1_), channel_id=1, source_target_pairs={{0,8},{1,9},{2,10},{3,11},{4,12},{5,13},{6,14},{7,15},{8,0},{9,1},... | collective-permute-start | bytes 835592 | tf_op jit(solution)/shard_map/ppermute | solution.py:294
  18.7 9.1 %collective-permute-start.9 = (bf16[64,2176]{1,0:T(8,128)(2,1)S(1)}, bf16[64,2176]{1,0:T(8,128)(2,1)}, u32[]{:S(2)}, u32[]{:S(2)}) collective-permute-start(bf16[64,2176]{1,0:T(8,128)(2,1)S(1)} %join_kernel.6.refs_1_.refs_2_.refs_6_), channel_id=1, source_target_pairs={{0,4},{1,3},{2,6},{3,1},{4,0},{5,7},{6,2},{7,5},{8,12},{9,11},{10,... | collective-permute-start | bytes 835592 | tf_op jit(solution)/shard_map/ppermute | solution.py:294
  22.6 7.6 %collective-permute-start.8 = (bf16[64,2176]{1,0:T(8,128)(2,1)S(1)}, bf16[64,2176]{1,0:T(8,128)(2,1)S(1)}, u32[]{:S(2)}, u32[]{:S(2)}) collective-permute-start(bf16[64,2176]{1,0:T(8,128)(2,1)S(1)} %pass_kernel.3.refs_9_.refs_0_), channel_id=1, source_target_pairs={{0,2},{1,5},{2,0},{3,7},{4,6},{5,1},{6,4},{7,3},{8,10},{9,13},{10,... | collective-permute-start | bytes 835592 | tf_op jit(solution)/shard_map/ppermute | solution.py:294
  30.1 8.4 %collective-permute-start.10 = (bf16[128,1152]{1,0:T(8,128)(2,1)S(1)}, bf16[128,1152]{1,0:T(8,128)(2,1)S(1)}, u32[]{:S(2)}, u32[]{:S(2)}) collective-permute-start(bf16[128,1152]{1,0:T(8,128)(2,1)S(1)} %get-tuple-element.38), channel_id=1, source_target_pairs={{0,4},{1,3},{2,6},{3,1},{4,0},{5,7},{6,2},{7,5},{8,12},{9,11},{10,... | collective-permute-start | bytes 884744 | tf_op jit(solution)/shard_map/ppermute | solution.py:294
  30.2 14.2 %collective-permute-start.12 = (bf16[128,2176]{1,0:T(8,128)(2,1)S(1)}, bf16[128,2176]{1,0:T(8,128)(2,1)S(1)}, u32[]{:S(2)}, u32[]{:S(2)}) collective-permute-start(bf16[128,2176]{1,0:T(8,128)(2,1)S(1)} %join_kernel.7.refs_9_.refs_1_), channel_id=1, source_target_pairs={{0,4},{1,3},{2,6},{3,1},{4,0},{5,7},{6,2},{7,5},{8,12},{9,11},{10,... | collective-permute-start | bytes 1671176 | tf_op jit(solution)/shard_map/ppermute | solution.py:294
  38.5 8.2 %collective-permute-start.11 = (bf16[64,1152]{1,0:T(8,128)(2,1)S(1)}, bf16[64,1152]{1,0:T(8,128)(2,1)S(1)}, u32[]{:S(2)}, u32[]{:S(2)}) collective-permute-start(bf16[64,1152]{1,0:T(8,128)(2,1)S(1)} %get-tuple-element.41.refs_8_), channel_id=1, source_target_pairs={{0,2},{1,5},{2,0},{3,7},{4,6},{5,1},{6,4},{7,3},{8,10},{9,13},{10,... | collective-permute-start | bytes 442376 | tf_op jit(solution)/shard_map/ppermute | solution.py:294
  46.6 6.8 %collective-permute-start.14 = (bf16[128,1152]{1,0:T(8,128)(2,1)S(1)}, bf16[128,1152]{1,0:T(8,128)(2,1)S(1)}, u32[]{:S(2)}, u32[]{:S(2)}) collective-permute-start(bf16[128,1152]{1,0:T(8,128)(2,1)S(1)} %get-tuple-element.47), channel_id=1, source_target_pairs={{0,4},{1,3},{2,6},{3,1},{4,0},{5,7},{6,2},{7,5},{8,12},{9,11},{10,... | collective-permute-start | bytes 884744 | tf_op jit(solution)/shard_map/ppermute | solution.py:294
  49.2 14.8 %collective-permute-start.17 = (bf16[512,384]{1,0:T(8,128)(2,1)S(1)}, bf16[512,384]{1,0:T(8,128)(2,1)S(1)}, u32[]{:S(2)}, u32[]{:S(2)}) collective-permute-start(bf16[512,384]{1,0:T(8,128)(2,1)S(1)} %get-tuple-element.59), channel_id=1, source_target_pairs={{0,1},{1,0},{2,3},{3,2},{4,5},{5,4},{6,7},{7,6},{8,9},{9,8},{10,11... | collective-permute-start | bytes 1179656 | tf_op jit(solution)/shard_map/ppermute | solution.py:21
  49.3 14.7 %collective-permute-start.18 = (bf16[512,384]{1,0:T(8,128)(2,1)S(1)}, bf16[512,384]{1,0:T(8,128)(2,1)S(1)}, u32[]{:S(2)}, u32[]{:S(2)}) collective-permute-start(bf16[512,384]{1,0:T(8,128)(2,1)S(1)} %get-tuple-element.60), channel_id=1, source_target_pairs={{0,1},{1,0},{2,3},{3,2},{4,5},{5,4},{6,7},{7,6},{8,9},{9,8},{10,11... | collective-permute-start | bytes 1179656 | tf_op jit(solution)/shard_map/ppermute | solution.py:21
  49.8 14.2 %collective-permute-start.19 = (bf16[384,512]{1,0:T(8,128)(2,1)S(1)}, bf16[384,512]{1,0:T(8,128)(2,1)S(1)}, u32[]{:S(2)}, u32[]{:S(2)}) collective-permute-start(bf16[384,512]{1,0:T(8,128)(2,1)S(1)} %get-tuple-element.52.refs_2_), channel_id=1, source_target_pairs={{0,1},{1,0},{2,3},{3,2},{4,5},{5,4},{6,7},{7,6},{8,9},{9,8},{10,11... | collective-permute-start | bytes 1179656 | tf_op jit(solution)/shard_map/ppermute | solution.py:21
  53.5 5.2 %collective-permute-start.15 = (bf16[64,1152]{1,0:T(8,128)(2,1)S(1)}, bf16[64,1152]{1,0:T(8,128)(2,1)S(1)}, u32[]{:S(2)}, u32[]{:S(2)}) collective-permute-start(bf16[64,1152]{1,0:T(8,128)(2,1)S(1)} %get-tuple-element.54.refs_2_), channel_id=1, source_target_pairs={{0,2},{1,5},{2,0},{3,7},{4,6},{5,1},{6,4},{7,3},{8,10},{9,13},{10,... | collective-permute-start | bytes 442376 | tf_op jit(solution)/shard_map/ppermute | solution.py:294
  54.8 6.5 %collective-permute-start.13 = (bf16[32,1152]{1,0:T(8,128)(2,1)S(1)}, bf16[32,1152]{1,0:T(8,128)(2,1)S(1)}, u32[]{:S(2)}, u32[]{:S(2)}) collective-permute-start(bf16[32,1152]{1,0:T(8,128)(2,1)S(1)} %get-tuple-element.45.refs_15_), channel_id=1, source_target_pairs={{0,16},{1,17},{2,18},{3,19},{4,20},{5,21},{6,22},{7,23},{8,24},{9,... | collective-permute-start | bytes 221192 | tf_op jit(solution)/shard_map/ppermute | solution.py:294
  58.8 6.5 %collective-permute-start.16 = (bf16[32,1152]{1,0:T(8,128)(2,1)S(1)}, bf16[32,1152]{1,0:T(8,128)(2,1)S(1)}, u32[]{:S(2)}, u32[]{:S(2)}) collective-permute-start(bf16[32,1152]{1,0:T(8,128)(2,1)S(1)} %get-tuple-element.56), channel_id=1, source_target_pairs={{0,8},{1,9},{2,10},{3,11},{4,12},{5,13},{6,14},{7,15},{8,0},{9,1},... | collective-permute-start | bytes 221192 | tf_op jit(solution)/shard_map/ppermute | solution.py:294
  61.3 6.2 %collective-permute-start.20 = (bf16[32,1152]{1,0:T(8,128)(2,1)S(1)}, bf16[32,1152]{1,0:T(8,128)(2,1)S(1)}, u32[]{:S(2)}, u32[]{:S(2)}) collective-permute-start(bf16[32,1152]{1,0:T(8,128)(2,1)S(1)} %get-tuple-element.55.refs_2_), channel_id=1, source_target_pairs={{0,24},{1,25},{2,26},{3,27},{4,28},{5,29},{6,30},{7,31},{8,16},{9,... | collective-permute-start | bytes 221192 | tf_op jit(solution)/shard_map/ppermute | solution.py:294
  64.0 3.4 %copy-start = (s32[32,8]{0,1:T(8,128)S(1)}, s32[32,8]{0,1:T(8,128)}, u32[]{:S(2)}) copy-start(s32[32,8]{0,1:T(8,128)} %param.9) | copy-start | bytes 3076

commit v9 on v8

--- a/solution.py
+++ b/solution.py
@@ -328,7 +328,7 @@
 
     gate_own, up_own, down_own = gate_half[0], up_half[0], down_half[0]
     gate_other, up_other, down_other = swap_core(gate_own), swap_core(up_own), swap_core(down_own)
-    weights = (gate_own, gate_other, up_own, up_other, down_own, down_other)
+    weights = [gate_own, gate_other, up_own, up_other, down_own, down_other]
     numbers, saved = [], []
 
     def at_offset(x, i):
@@ -373,16 +373,16 @@
     second_two = exchange(first_two, near_b)
     near_1 = after_all(near_1)
     got_near = exchange(near_1, near_a)
-    got_0 = exchange(expert(second_own, second_two), near_b)
+    weights[-1] = after_all(weights[-1])
+    kept_0 = expert(first_own, first_two)
     first_1 = join(near_1, got_near)
     second_1 = exchange(first_1, near_b)
-    kept_0 = expert(first_own, first_two)
+    give_0 = expert(second_own, second_two)
+    kept_1 = expert(first_1)
+    got_0 = exchange(after_all(give_0, second_1), near_b)
+    got_1 = exchange(expert(second_1), near_b)
     kept_0, give = split(kept_0, got_0, (F32, BF16))
     got_0 = exchange(give, near_a)
-    kept_1 = expert(first_1)
-    got_1 = exchange(expert(second_1), near_b)
-    total, give = split(kept_0, got_0, (F32, BF16))
-    back_two = at_offset(give, 0)
     keep_in, keep_down, *gives = run(
         lambda *refs: weight_kernel(tuple(numbers), *refs),
         [
@@ -397,14 +397,16 @@
     gots = [swap_core(give) for give in gives]
     kept_1, give = split(kept_1, got_1, (F32, BF16))
     got_1 = exchange(give, near_a)
+    total, give = split(kept_0, got_0, (F32, BF16))
+    back_two = at_offset(give, 0)
     give_one, give_both = split(kept_1, got_1, (BF16, BF16))
     back_one, back_both = at_offset(give_one, 1), at_offset(give_both, 2)
-    total = collect(total, back_two)
     grad_gate, grad_up, grad_down, _ = run(
         settle_kernel,
         [((half, width), BF16), ((half, width), BF16), ((width, half), BF16), ((8, 128), F32)],
         None, keep_in, keep_down, *gots, leaves=3, limit=6,
     )
+    total = collect(total, back_two)
     total = collect(total, back_one)
 
     parts = (total, back_both)

time: 69.1 us -> 65.3 us (0.945)
  waiting for transfers between devices: 29.5 us -> 24.6 us
  starting transfers between devices: 23.2 us -> 26.5 us
  Pallas kernels: 15.2 us -> 13 us
    ppermute x15, waiting for transfers between devices: 29.4 us -> 24.6 us  [exchange(): return lax.ppermute(x, DEVICES, pairs)]
    ppermute x15, starting transfers between devices: 22 us -> 25.4 us  [exchange(): return lax.ppermute(x, DEVICES, pairs)]
    pallas_call x19 -> x21, Pallas kernels: 14.3 us -> 12 us  [call(): pl.pallas_call(run, out_shape=out_shape, in_specs=[pl.BlockSpec(memory_sp...]
  transfers between devices with their start and end apart: 21 -> 21, of which waited for: 10 -> 8; matrix products, arithmetic and copies ran while one was open for 0% -> 0% of each run, Pallas kernels for 19% -> 16%
where the time goes in v9:
time: 65.3 us; the launch traced here: 65.1 us
  starting transfers between devices  26.5 us (41%)
  waiting for transfers between devices  24.6 us (38%)
  Pallas kernels  13 us (20%)
  between operations  0.84 us (1%)
    ppermute x15, starting transfers between devices, exchange(): return lax.ppermute(x, DEVICES, pairs)  25.4 us
    ppermute x15, waiting for transfers between devices, exchange(): return lax.ppermute(x, DEVICES, pairs)  24.6 us
    pallas_call x21, Pallas kernels, call(): pl.pallas_call(run, out_shape=out_shape, in_specs=[pl.BlockSpec(memory_sp...  12 us
  transfers between devices with their start and end apart: 21, of which 8 were waited for; matrix products, arithmetic and copies ran while one was open for 0% of the time, Pallas kernels for 16%

profile of v9, /device:TPU:0, one launch (start us, length us, event | category | flops | bytes accessed | tf_op | source)
XLA Modules:
  0.0 65.1 jit_solution(8013203850211633334)
XLA Ops:
  0.6 0.9 %prepare_kernel.1.refs_0_ = bf16[32,2176]{1,0:T(8,128)(2,1)S(1)} custom-call(bf16[32,1024]{1,0:T(8,128)(2,1)} %tokens.1, bf16[32,1024]{1,0:T(8,128)(2,1)} %cotangent.1, s32[8,32]{1,0:T(8,128)} %bitcast.11, bf16[8,32]{1,0:T(8,128)(2,1)} %bitcast.28), custom_call_target="tpu_custom_call" | custom-call | tf_op jit(solution)/shard_map/prepare_kernel/pallas_call | solution.py:309
  1.6 3.0 %collective-permute-start = (bf16[32,2176]{1,0:T(8,128)(2,1)S(1)}, bf16[32,2176]{1,0:T(8,128)(2,1)S(1)}, u32[]{:S(2)}, u32[]{:S(2)}) collective-permute-start(bf16[32,2176]{1,0:T(8,128)(2,1)S(1)} %prepare_kernel.1.refs_0_), channel_id=1, source_target_pairs={{0,2},{1,5},{2,0},{3,7},{4,6},{5,1},{6,4},{7,3},{8,10},{9,13},{10,... | collective-permute-start | bytes 417800 | tf_op jit(solution)/shard_map/ppermute | solution.py:294
  4.6 2.6 %collective-permute-start.1 = (bf16[32,2176]{1,0:T(8,128)(2,1)S(1)}, bf16[32,2176]{1,0:T(8,128)(2,1)S(1)}, u32[]{:S(2)}, u32[]{:S(2)}) collective-permute-start(bf16[32,2176]{1,0:T(8,128)(2,1)S(1)} %prepare_kernel.1.refs_0_), channel_id=1, source_target_pairs={{0,16},{1,17},{2,18},{3,19},{4,20},{5,21},{6,22},{7,23},{8,24},{9,... | collective-permute-start | bytes 417800 | tf_op jit(solution)/shard_map/ppermute | solution.py:294
  7.2 0.5 collective-permute-start.5
  7.7 2.0 %collective-permute-start.3 = (bf16[64,2176]{1,0:T(8,128)(2,1)S(1)}, bf16[64,2176]{1,0:T(8,128)(2,1)S(1)}, u32[]{:S(2)}, u32[]{:S(2)}) collective-permute-start(bf16[64,2176]{1,0:T(8,128)(2,1)S(1)} %join_kernel.4.refs_2_.refs_1_), channel_id=1, source_target_pairs={{0,4},{1,3},{2,6},{3,1},{4,0},{5,7},{6,2},{7,5},{8,12},{9,11},{10,... | collective-permute-start | bytes 835592 | tf_op jit(solution)/shard_map/ppermute | solution.py:294
  9.8 3.9 %collective-permute-done.1.refs_1_.refs_0_ = bf16[32,2176]{1,0:T(8,128)(2,1)S(1)} collective-permute-done((bf16[32,2176]{1,0:T(8,128)(2,1)S(1)}, bf16[32,2176]{1,0:T(8,128)(2,1)S(1)}, u32[]{:S(2)}, u32[]{:S(2)}) %collective-permute-start.1) | collective-permute-done | bytes 139296 | tf_op jit(solution)/shard_map/ppermute | solution.py:294
  13.7 0.7 %collective-permute-start.7 = (bf16[64,2176]{1,0:T(8,128)(2,1)S(1)}, bf16[64,2176]{1,0:T(8,128)(2,1)S(1)}, u32[]{:S(2)}, u32[]{:S(2)}) collective-permute-start(bf16[64,2176]{1,0:T(8,128)(2,1)S(1)} %join_kernel.5.refs_1_), channel_id=1, source_target_pairs={{0,8},{1,9},{2,10},{3,11},{4,12},{5,13},{6,14},{7,15},{8,0},{9,1},... | collective-permute-start | bytes 835592 | tf_op jit(solution)/shard_map/ppermute | solution.py:294
  14.4 1.9 %collective-permute-start.2 = (bf16[32,2176]{1,0:T(8,128)(2,1)S(1)}, bf16[32,2176]{1,0:T(8,128)(2,1)S(1)}, u32[]{:S(2)}, u32[]{:S(2)}) collective-permute-start(bf16[32,2176]{1,0:T(8,128)(2,1)S(1)} %collective-permute-done.1.refs_1_.refs_0_), channel_id=1, source_target_pairs={{0,2},{1,5},{2,0},{3,7},{4,6},{5,1},{6,4},{7,3},{8,10},{9,13},{10,... | collective-permute-start | bytes 417800 | tf_op jit(solution)/shard_map/ppermute | solution.py:294
  16.4 3.0 %collective-permute-done.2.refs_1_ = bf16[32,2176]{1,0:T(8,128)(2,1)S(1)} collective-permute-done((bf16[32,2176]{1,0:T(8,128)(2,1)S(1)}, bf16[32,2176]{1,0:T(8,128)(2,1)S(1)}, u32[]{:S(2)}, u32[]{:S(2)}) %collective-permute-start.2) | collective-permute-done | bytes 139296 | tf_op jit(solution)/shard_map/ppermute | solution.py:294
  19.5 2.0 %collective-permute-start.8 = (bf16[64,2176]{1,0:T(8,128)(2,1)S(1)}, bf16[64,2176]{1,0:T(8,128)(2,1)S(1)}, u32[]{:S(2)}, u32[]{:S(2)}) collective-permute-start(bf16[64,2176]{1,0:T(8,128)(2,1)S(1)} %join_kernel.6.refs_1_.refs_2_), channel_id=1, source_target_pairs={{0,4},{1,3},{2,6},{3,1},{4,0},{5,7},{6,2},{7,5},{8,12},{9,11},{10,... | collective-permute-start | bytes 835592 | tf_op jit(solution)/shard_map/ppermute | solution.py:294
  21.5 2.4 %collective-permute-start.9 = (bf16[64,2176]{1,0:T(8,128)(2,1)S(1)}, bf16[64,2176]{1,0:T(8,128)(2,1)S(1)}, u32[]{:S(2)}, u32[]{:S(2)}) collective-permute-start(bf16[64,2176]{1,0:T(8,128)(2,1)S(1)} %pass_kernel.5.refs_1_.refs_0_), channel_id=1, source_target_pairs={{0,2},{1,5},{2,0},{3,7},{4,6},{5,1},{6,4},{7,3},{8,10},{9,13},{10,... | collective-permute-start | bytes 835592 | tf_op jit(solution)/shard_map/ppermute | solution.py:294
  24.0 1.7 %expert_kernel.4 = (bf16[128,1152]{1,0:T(8,128)(2,1)S(1)}, bf16[2,64,768]{2,1,0:T(8,128)(2,1)S(1)}, bf16[2,64,384]{2,1,0:T(8,128)(2,1)S(1)}) custom-call(s32[2]{0:T(128)S(1)} %pad_add_fusion.refs_0_, bf16[64,2176]{1,0:T(8,128)(2,1)S(1)} %join_kernel.4.refs_2_.refs_1_, bf16[64,2176]{1,0:T(8,128)(2,1)S(1)} %join_kernel.6.refs_1_.refs_2_, ...), custom_call_target="tpu_custom_call" | custom-call | flops 6000000000 | tf_op jit(solution)/shard_map/expert_kernel/pallas_call | solution.py:253
  25.7 2.7 %collective-permute-done.9.refs_1_ = bf16[64,2176]{1,0:T(8,128)(2,1)S(1)} collective-permute-done((bf16[64,2176]{1,0:T(8,128)(2,1)S(1)}, bf16[64,2176]{1,0:T(8,128)(2,1)S(1)}, u32[]{:S(2)}, u32[]{:S(2)}) %collective-permute-start.9) | collective-permute-done | bytes 278560 | tf_op jit(solution)/shard_map/ppermute | solution.py:294
  28.5 1.7 %expert_kernel.5 = (bf16[128,1152]{1,0:T(8,128)(2,1)S(1)}, bf16[2,64,768]{2,1,0:T(8,128)(2,1)S(1)}, bf16[2,64,384]{2,1,0:T(8,128)(2,1)S(1)}) custom-call(s32[2]{0:T(128)S(1)} %pad_add_fusion.refs_0_, bf16[64,2176]{1,0:T(8,128)(2,1)S(1)} %pass_kernel.4.refs_2_.refs_1_.refs_5_, bf16[64,2176]{1,0:T(8,128)(2,1)S(1)} %collective-permute-done.8.refs_2_.refs_6_, ...), custom_call_target="tpu_custom_call" | custom-call | flops 6000000000 | tf_op jit(solution)/shard_map/expert_kernel/pallas_call | solution.py:253
  30.3 1.8 %expert_kernel.6 = (bf16[128,1152]{1,0:T(8,128)(2,1)S(1)}, bf16[1,128,768]{2,1,0:T(8,128)(2,1)S(1)}, bf16[1,128,384]{2,1,0:T(8,128)(2,1)S(1)}) custom-call(s32[2]{0:T(128)S(1)} %pad_add_fusion.refs_0_, bf16[128,2176]{1,0:T(8,128)(2,1)S(1)} %join_kernel.7.refs_9_.refs_1_, bf16[512,384]{1,0:T(8,128)(2,1)S(1)} %bitcast.16, ...), custom_call_target="tpu_custom_call" | custom-call | flops 6000000000 | tf_op jit(solution)/shard_map/expert_kernel/pallas_call | solution.py:253
  32.1 6.0 %collective-permute-done.10.refs_2_.refs_1_.refs_12_ = bf16[128,2176]{1,0:T(8,128)(2,1)S(1)} collective-permute-done((bf16[128,2176]{1,0:T(8,128)(2,1)S(1)}, bf16[128,2176]{1,0:T(8,128)(2,1)S(1)}, u32[]{:S(2)}, u32[]{:S(2)}) %collective-permute-start.10) | collective-permute-done | bytes 557088 | tf_op jit(solution)/shard_map/ppermute | solution.py:294
  38.1 1.8 %expert_kernel.7 = (bf16[128,1152]{1,0:T(8,128)(2,1)S(1)}, bf16[1,128,768]{2,1,0:T(8,128)(2,1)S(1)}, bf16[1,128,384]{2,1,0:T(8,128)(2,1)S(1)}) custom-call(s32[2]{0:T(128)S(1)} %pad_add_fusion.refs_0_, bf16[128,2176]{1,0:T(8,128)(2,1)S(1)} %collective-permute-done.10.refs_2_.refs_1_.refs_12_, bf16[512,384]{1,0:T(8,128)(2,1)S(1)} %bitcast.17, ...), custom_call_target="tpu_custom_call" | custom-call | flops 6000000000 | tf_op jit(solution)/shard_map/expert_kernel/pallas_call | solution.py:253
  39.9 2.1 %collective-permute-start.13 = (bf16[128,1152]{1,0:T(8,128)(2,1)S(1)}, bf16[128,1152]{1,0:T(8,128)(2,1)S(1)}, u32[]{:S(2)}, u32[]{:S(2)}) collective-permute-start(bf16[128,1152]{1,0:T(8,128)(2,1)S(1)} %get-tuple-element.45), channel_id=1, source_target_pairs={{0,4},{1,3},{2,6},{3,1},{4,0},{5,7},{6,2},{7,5},{8,12},{9,11},{10,... | collective-permute-start | bytes 884744 | tf_op jit(solution)/shard_map/ppermute | solution.py:294
  42.0 2.9 %collective-permute-done.11.refs_1_ = bf16[128,1152]{1,0:T(8,128)(2,1)S(1)} collective-permute-done((bf16[128,1152]{1,0:T(8,128)(2,1)S(1)}, bf16[128,1152]{1,0:T(8,128)(2,1)S(1)}, u32[]{:S(2)}, u32[]{:S(2)}) %collective-permute-start.11) | collective-permute-done | bytes 294944 | tf_op jit(solution)/shard_map/ppermute | solution.py:294
  44.9 2.0 %weight_kernel.1 = (f32[512,768]{1,0:T(8,128)S(1)}, f32[384,512]{1,0:T(8,128)S(1)}, bf16[512,384]{1,0:T(8,128)(2,1)S(1)}, bf16[512,384]{1,0:T(8,128)(2,1)S(1)}, bf16[384,512]{1,0:T(8,128)(2,1)S(1)}) custom-call(s32[2]{0:T(128)S(1)} %pad_add_fusion.refs_0_, bf16[64,2176]{1,0:T(8,128)(2,1)S(1)} %join_kernel.4.refs_2_.refs_1_, ...), custom_call_target="tpu_custom_call" | custom-call | flops 6000000000 | tf_op jit(solution)/shard_map/weight_kernel/pallas_call | solution.py:253
  47.0 0.5 collective-permute-start.16
  47.5 0.1 collective-permute-start.17
  47.6 2.0 %collective-permute-start.12 = (bf16[64,1152]{1,0:T(8,128)(2,1)S(1)}, bf16[64,1152]{1,0:T(8,128)(2,1)S(1)}, u32[]{:S(2)}, u32[]{:S(2)}) collective-permute-start(bf16[64,1152]{1,0:T(8,128)(2,1)S(1)} %get-tuple-element.43.refs_15_), channel_id=1, source_target_pairs={{0,2},{1,5},{2,0},{3,7},{4,6},{5,1},{6,4},{7,3},{8,10},{9,13},{10,... | collective-permute-start | bytes 442376 | tf_op jit(solution)/shard_map/ppermute | solution.py:294
  49.7 0.5 collective-permute-start.18
  50.2 2.6 %collective-permute-done.12.refs_1_ = bf16[64,1152]{1,0:T(8,128)(2,1)S(1)} collective-permute-done((bf16[64,1152]{1,0:T(8,128)(2,1)S(1)}, bf16[64,1152]{1,0:T(8,128)(2,1)S(1)}, u32[]{:S(2)}, u32[]{:S(2)}) %collective-permute-start.12) | collective-permute-done | bytes 147488 | tf_op jit(solution)/shard_map/ppermute | solution.py:294
  52.8 2.9 %collective-permute-start.14 = (bf16[32,1152]{1,0:T(8,128)(2,1)S(1)}, bf16[32,1152]{1,0:T(8,128)(2,1)S(1)}, u32[]{:S(2)}, u32[]{:S(2)}) collective-permute-start(bf16[32,1152]{1,0:T(8,128)(2,1)S(1)} %get-tuple-element.53.refs_2_), channel_id=1, source_target_pairs={{0,16},{1,17},{2,18},{3,19},{4,20},{5,21},{6,22},{7,23},{8,24},{9,... | collective-permute-start | bytes 221192 | tf_op jit(solution)/shard_map/ppermute | solution.py:294
  55.7 1.8 %collective-permute-start.19 = (bf16[32,1152]{1,0:T(8,128)(2,1)S(1)}, bf16[32,1152]{1,0:T(8,128)(2,1)S(1)}, u32[]{:S(2)}, u32[]{:S(2)}) collective-permute-start(bf16[32,1152]{1,0:T(8,128)(2,1)S(1)} %get-tuple-element.61), channel_id=1, source_target_pairs={{0,8},{1,9},{2,10},{3,11},{4,12},{5,13},{6,14},{7,15},{8,0},{9,1},... | collective-permute-start | bytes 221192 | tf_op jit(solution)/shard_map/ppermute | solution.py:294
  57.5 1.3 %collective-permute-start.20 = (bf16[32,1152]{1,0:T(8,128)(2,1)S(1)}, bf16[32,1152]{1,0:T(8,128)(2,1)S(1)}, u32[]{:S(2)}, u32[]{:S(2)}) collective-permute-start(bf16[32,1152]{1,0:T(8,128)(2,1)S(1)} %get-tuple-element.59.refs_5_), channel_id=1, source_target_pairs={{0,24},{1,25},{2,26},{3,27},{4,28},{5,29},{6,30},{7,31},{8,16},{9,... | collective-permute-start | bytes 221192 | tf_op jit(solution)/shard_map/ppermute | solution.py:294
  58.9 1.2 %settle_kernel.1 = (bf16[512,384]{1,0:T(8,128)(2,1)}, bf16[512,384]{1,0:T(8,128)(2,1)}, bf16[384,512]{1,0:T(8,128)(2,1)}, f32[8,128]{1,0:T(8,128)S(1)}) custom-call(f32[512,768]{1,0:T(8,128)S(1)} %get-tuple-element.54.refs_0_, f32[384,512]{1,0:T(8,128)S(1)} %get-tuple-element.55.refs_1_, bf16[512,384]{1,0:T(8,128)(2,1)S(1)} %collective-permute-done.15.refs_2_, ...), custom_call_target="tpu_custom_call" | custom-call | tf_op jit(solution)/shard_map/settle_kernel/pallas_call | solution.py:253
  60.1 0.3 collective-permute-done.19.refs_1_
  60.4 3.3 %collective-permute-done.20.refs_2_ = bf16[32,1152]{1,0:T(8,128)(2,1)S(1)} collective-permute-done((bf16[32,1152]{1,0:T(8,128)(2,1)S(1)}, bf16[32,1152]{1,0:T(8,128)(2,1)S(1)}, u32[]{:S(2)}, u32[]{:S(2)}) %collective-permute-start.20) | collective-permute-done | bytes 73760 | tf_op jit(solution)/shard_map/ppermute | solution.py:294
  63.7 1.4 %finish_kernel.1 = (bf16[32,1024]{1,0:T(8,128)(2,1)}, bf16[8,32]{1,0:T(8,128)(2,1)}) custom-call(s32[2]{0:T(128)S(1)} %pad_add_fusion.refs_0_, f32[32,1152]{1,0:T(8,128)S(1)} %add_kernel.3.refs_1_.refs_4_, bf16[32,1152]{1,0:T(8,128)(2,1)S(1)} %collective-permute-done.20.refs_2_, s32[8,32]{1,0:T(8,128)S(1)} %bitcast.12, f32[32,1152]{1,0:T(8,128)S(1)} %add_kernel.3.refs_1_.refs_4_), custom_call_target="tpu_custom_call" | custom-call | tf_op jit(solution)/shard_map/finish_kernel/pallas_call | solution.py:253
  (41 shorter events, 0.8 us)
Async XLA Ops:
  1.6 6.1 %collective-permute-start = (bf16[32,2176]{1,0:T(8,128)(2,1)S(1)}, bf16[32,2176]{1,0:T(8,128)(2,1)S(1)}, u32[]{:S(2)}, u32[]{:S(2)}) collective-permute-start(bf16[32,2176]{1,0:T(8,128)(2,1)S(1)} %prepare_kernel.1.refs_0_), channel_id=1, source_target_pairs={{0,2},{1,5},{2,0},{3,7},{4,6},{5,1},{6,4},{7,3},{8,10},{9,13},{10,... | collective-permute-start | bytes 417800 | tf_op jit(solution)/shard_map/ppermute | solution.py:294
  4.6 9.0 %collective-permute-start.1 = (bf16[32,2176]{1,0:T(8,128)(2,1)S(1)}, bf16[32,2176]{1,0:T(8,128)(2,1)S(1)}, u32[]{:S(2)}, u32[]{:S(2)}) collective-permute-start(bf16[32,2176]{1,0:T(8,128)(2,1)S(1)} %prepare_kernel.1.refs_0_), channel_id=1, source_target_pairs={{0,16},{1,17},{2,18},{3,19},{4,20},{5,21},{6,22},{7,23},{8,24},{9,... | collective-permute-start | bytes 417800 | tf_op jit(solution)/shard_map/ppermute | solution.py:294
  7.2 16.7 %collective-permute-start.4 = (bf16[512,384]{1,0:T(8,128)(2,1)}, bf16[512,384]{1,0:T(8,128)(2,1)S(1)}, u32[]{:S(2)}, u32[]{:S(2)}) collective-permute-start(bf16[512,384]{1,0:T(8,128)(2,1)} %bitcast.13), channel_id=1, source_target_pairs={{0,1},{1,0},{2,3},{3,2},{4,5},{5,4},{6,7},{7,6},{8,9},{9,8},{10,11... | collective-permute-start | bytes 1179656 | tf_op jit(solution)/shard_map/ppermute | solution.py:21
  7.2 16.7 %collective-permute-start.5 = (bf16[512,384]{1,0:T(8,128)(2,1)}, bf16[512,384]{1,0:T(8,128)(2,1)S(1)}, u32[]{:S(2)}, u32[]{:S(2)}) collective-permute-start(bf16[512,384]{1,0:T(8,128)(2,1)} %bitcast.18), channel_id=1, source_target_pairs={{0,1},{1,0},{2,3},{3,2},{4,5},{5,4},{6,7},{7,6},{8,9},{9,8},{10,11... | collective-permute-start | bytes 1179656 | tf_op jit(solution)/shard_map/ppermute | solution.py:21
  7.7 16.2 %collective-permute-start.6 = (bf16[384,512]{1,0:T(8,128)(2,1)}, bf16[384,512]{1,0:T(8,128)(2,1)S(1)}, u32[]{:S(2)}, u32[]{:S(2)}) collective-permute-start(bf16[384,512]{1,0:T(8,128)(2,1)} %bitcast.23), channel_id=1, source_target_pairs={{0,1},{1,0},{2,3},{3,2},{4,5},{5,4},{6,7},{7,6},{8,9},{9,8},{10,11... | collective-permute-start | bytes 1179656 | tf_op jit(solution)/shard_map/ppermute | solution.py:21
  7.7 6.7 %collective-permute-start.3 = (bf16[64,2176]{1,0:T(8,128)(2,1)S(1)}, bf16[64,2176]{1,0:T(8,128)(2,1)S(1)}, u32[]{:S(2)}, u32[]{:S(2)}) collective-permute-start(bf16[64,2176]{1,0:T(8,128)(2,1)S(1)} %join_kernel.4.refs_2_.refs_1_), channel_id=1, source_target_pairs={{0,4},{1,3},{2,6},{3,1},{4,0},{5,7},{6,2},{7,5},{8,12},{9,11},{10,... | collective-permute-start | bytes 835592 | tf_op jit(solution)/shard_map/ppermute | solution.py:294
  13.7 7.8 %collective-permute-start.7 = (bf16[64,2176]{1,0:T(8,128)(2,1)S(1)}, bf16[64,2176]{1,0:T(8,128)(2,1)S(1)}, u32[]{:S(2)}, u32[]{:S(2)}) collective-permute-start(bf16[64,2176]{1,0:T(8,128)(2,1)S(1)} %join_kernel.5.refs_1_), channel_id=1, source_target_pairs={{0,8},{1,9},{2,10},{3,11},{4,12},{5,13},{6,14},{7,15},{8,0},{9,1},... | collective-permute-start | bytes 835592 | tf_op jit(solution)/shard_map/ppermute | solution.py:294
  14.4 5.1 %collective-permute-start.2 = (bf16[32,2176]{1,0:T(8,128)(2,1)S(1)}, bf16[32,2176]{1,0:T(8,128)(2,1)S(1)}, u32[]{:S(2)}, u32[]{:S(2)}) collective-permute-start(bf16[32,2176]{1,0:T(8,128)(2,1)S(1)} %collective-permute-done.1.refs_1_.refs_0_), channel_id=1, source_target_pairs={{0,2},{1,5},{2,0},{3,7},{4,6},{5,1},{6,4},{7,3},{8,10},{9,13},{10,... | collective-permute-start | bytes 417800 | tf_op jit(solution)/shard_map/ppermute | solution.py:294
  16.4 7.6 %copy-start.1 = (bf16[1,512,384]{2,1,0:T(8,128)(2,1)S(1)}, bf16[1,512,384]{2,1,0:T(8,128)(2,1)}, u32[]{:S(2)}) copy-start(bf16[1,512,384]{2,1,0:T(8,128)(2,1)} %param.11) | copy-start | bytes 1179652
  16.4 7.6 %copy-start.2 = (bf16[1,512,384]{2,1,0:T(8,128)(2,1)S(1)}, bf16[1,512,384]{2,1,0:T(8,128)(2,1)}, u32[]{:S(2)}) copy-start(bf16[1,512,384]{2,1,0:T(8,128)(2,1)} %param.12) | copy-start | bytes 1179652
  16.4 7.6 %copy-start.3 = (bf16[1,384,512]{2,1,0:T(8,128)(2,1)S(1)}, bf16[1,384,512]{2,1,0:T(8,128)(2,1)}, u32[]{:S(2)}) copy-start(bf16[1,384,512]{2,1,0:T(8,128)(2,1)} %param.13) | copy-start | bytes 1179652
  19.5 9.1 %collective-permute-start.8 = (bf16[64,2176]{1,0:T(8,128)(2,1)S(1)}, bf16[64,2176]{1,0:T(8,128)(2,1)S(1)}, u32[]{:S(2)}, u32[]{:S(2)}) collective-permute-start(bf16[64,2176]{1,0:T(8,128)(2,1)S(1)} %join_kernel.6.refs_1_.refs_2_), channel_id=1, source_target_pairs={{0,4},{1,3},{2,6},{3,1},{4,0},{5,7},{6,2},{7,5},{8,12},{9,11},{10,... | collective-permute-start | bytes 835592 | tf_op jit(solution)/shard_map/ppermute | solution.py:294
  21.5 6.9 %collective-permute-start.9 = (bf16[64,2176]{1,0:T(8,128)(2,1)S(1)}, bf16[64,2176]{1,0:T(8,128)(2,1)S(1)}, u32[]{:S(2)}, u32[]{:S(2)}) collective-permute-start(bf16[64,2176]{1,0:T(8,128)(2,1)S(1)} %pass_kernel.5.refs_1_.refs_0_), channel_id=1, source_target_pairs={{0,2},{1,5},{2,0},{3,7},{4,6},{5,1},{6,4},{7,3},{8,10},{9,13},{10,... | collective-permute-start | bytes 835592 | tf_op jit(solution)/shard_map/ppermute | solution.py:294
  28.4 9.6 %collective-permute-start.10 = (bf16[128,2176]{1,0:T(8,128)(2,1)S(1)}, bf16[128,2176]{1,0:T(8,128)(2,1)S(1)}, u32[]{:S(2)}, u32[]{:S(2)}) collective-permute-start(bf16[128,2176]{1,0:T(8,128)(2,1)S(1)} %join_kernel.7.refs_9_.refs_1_), channel_id=1, source_target_pairs={{0,4},{1,3},{2,6},{3,1},{4,0},{5,7},{6,2},{7,5},{8,12},{9,11},{10,... | collective-permute-start | bytes 1671176 | tf_op jit(solution)/shard_map/ppermute | solution.py:294
  38.1 6.8 %collective-permute-start.11 = (bf16[128,1152]{1,0:T(8,128)(2,1)S(1)}, bf16[128,1152]{1,0:T(8,128)(2,1)S(1)}, u32[]{:S(2)}, u32[]{:S(2)}) collective-permute-start(bf16[128,1152]{1,0:T(8,128)(2,1)S(1)} %pass_kernel.7.refs_8_), channel_id=1, source_target_pairs={{0,4},{1,3},{2,6},{3,1},{4,0},{5,7},{6,2},{7,5},{8,12},{9,11},{10,... | collective-permute-start | bytes 884744 | tf_op jit(solution)/shard_map/ppermute | solution.py:294
  39.9 9.7 %collective-permute-start.13 = (bf16[128,1152]{1,0:T(8,128)(2,1)S(1)}, bf16[128,1152]{1,0:T(8,128)(2,1)S(1)}, u32[]{:S(2)}, u32[]{:S(2)}) collective-permute-start(bf16[128,1152]{1,0:T(8,128)(2,1)S(1)} %get-tuple-element.45), channel_id=1, source_target_pairs={{0,4},{1,3},{2,6},{3,1},{4,0},{5,7},{6,2},{7,5},{8,12},{9,11},{10,... | collective-permute-start | bytes 884744 | tf_op jit(solution)/shard_map/ppermute | solution.py:294
  46.9 10.6 %collective-permute-start.15 = (bf16[512,384]{1,0:T(8,128)(2,1)S(1)}, bf16[512,384]{1,0:T(8,128)(2,1)S(1)}, u32[]{:S(2)}, u32[]{:S(2)}) collective-permute-start(bf16[512,384]{1,0:T(8,128)(2,1)S(1)} %get-tuple-element.56), channel_id=1, source_target_pairs={{0,1},{1,0},{2,3},{3,2},{4,5},{5,4},{6,7},{7,6},{8,9},{9,8},{10,11... | collective-permute-start | bytes 1179656 | tf_op jit(solution)/shard_map/ppermute | solution.py:21
  47.0 11.8 %collective-permute-start.16 = (bf16[512,384]{1,0:T(8,128)(2,1)S(1)}, bf16[512,384]{1,0:T(8,128)(2,1)S(1)}, u32[]{:S(2)}, u32[]{:S(2)}) collective-permute-start(bf16[512,384]{1,0:T(8,128)(2,1)S(1)} %get-tuple-element.57), channel_id=1, source_target_pairs={{0,1},{1,0},{2,3},{3,2},{4,5},{5,4},{6,7},{7,6},{8,9},{9,8},{10,11... | collective-permute-start | bytes 1179656 | tf_op jit(solution)/shard_map/ppermute | solution.py:21
  47.5 11.3 %collective-permute-start.17 = (bf16[384,512]{1,0:T(8,128)(2,1)S(1)}, bf16[384,512]{1,0:T(8,128)(2,1)S(1)}, u32[]{:S(2)}, u32[]{:S(2)}) collective-permute-start(bf16[384,512]{1,0:T(8,128)(2,1)S(1)} %get-tuple-element.50.refs_2_), channel_id=1, source_target_pairs={{0,1},{1,0},{2,3},{3,2},{4,5},{5,4},{6,7},{7,6},{8,9},{9,8},{10,11... | collective-permute-start | bytes 1179656 | tf_op jit(solution)/shard_map/ppermute | solution.py:21
  47.6 5.1 %collective-permute-start.12 = (bf16[64,1152]{1,0:T(8,128)(2,1)S(1)}, bf16[64,1152]{1,0:T(8,128)(2,1)S(1)}, u32[]{:S(2)}, u32[]{:S(2)}) collective-permute-start(bf16[64,1152]{1,0:T(8,128)(2,1)S(1)} %get-tuple-element.43.refs_15_), channel_id=1, source_target_pairs={{0,2},{1,5},{2,0},{3,7},{4,6},{5,1},{6,4},{7,3},{8,10},{9,13},{10,... | collective-permute-start | bytes 442376 | tf_op jit(solution)/shard_map/ppermute | solution.py:294
  49.7 6.0 %collective-permute-start.18 = (bf16[64,1152]{1,0:T(8,128)(2,1)S(1)}, bf16[64,1152]{1,0:T(8,128)(2,1)S(1)}, u32[]{:S(2)}, u32[]{:S(2)}) collective-permute-start(bf16[64,1152]{1,0:T(8,128)(2,1)S(1)} %get-tuple-element.51.refs_2_), channel_id=1, source_target_pairs={{0,2},{1,5},{2,0},{3,7},{4,6},{5,1},{6,4},{7,3},{8,10},{9,13},{10,... | collective-permute-start | bytes 442376 | tf_op jit(solution)/shard_map/ppermute | solution.py:294
  52.8 7.3 %collective-permute-start.14 = (bf16[32,1152]{1,0:T(8,128)(2,1)S(1)}, bf16[32,1152]{1,0:T(8,128)(2,1)S(1)}, u32[]{:S(2)}, u32[]{:S(2)}) collective-permute-start(bf16[32,1152]{1,0:T(8,128)(2,1)S(1)} %get-tuple-element.53.refs_2_), channel_id=1, source_target_pairs={{0,16},{1,17},{2,18},{3,19},{4,20},{5,21},{6,22},{7,23},{8,24},{9,... | collective-permute-start | bytes 221192 | tf_op jit(solution)/shard_map/ppermute | solution.py:294
  55.7 4.6 %collective-permute-start.19 = (bf16[32,1152]{1,0:T(8,128)(2,1)S(1)}, bf16[32,1152]{1,0:T(8,128)(2,1)S(1)}, u32[]{:S(2)}, u32[]{:S(2)}) collective-permute-start(bf16[32,1152]{1,0:T(8,128)(2,1)S(1)} %get-tuple-element.61), channel_id=1, source_target_pairs={{0,8},{1,9},{2,10},{3,11},{4,12},{5,13},{6,14},{7,15},{8,0},{9,1},... | collective-permute-start | bytes 221192 | tf_op jit(solution)/shard_map/ppermute | solution.py:294
  57.5 6.2 %collective-permute-start.20 = (bf16[32,1152]{1,0:T(8,128)(2,1)S(1)}, bf16[32,1152]{1,0:T(8,128)(2,1)S(1)}, u32[]{:S(2)}, u32[]{:S(2)}) collective-permute-start(bf16[32,1152]{1,0:T(8,128)(2,1)S(1)} %get-tuple-element.59.refs_5_), channel_id=1, source_target_pairs={{0,24},{1,25},{2,26},{3,27},{4,28},{5,29},{6,30},{7,31},{8,16},{9,... | collective-permute-start | bytes 221192 | tf_op jit(solution)/shard_map/ppermute | solution.py:294
  58.9 4.8 %copy-start = (s32[32,8]{0,1:T(8,128)S(1)}, s32[32,8]{0,1:T(8,128)}, u32[]{:S(2)}) copy-start(s32[32,8]{0,1:T(8,128)} %param.9) | copy-start | bytes 3076

commit v10 on v9

--- a/solution.py
+++ b/solution.py
@@ -357,9 +357,9 @@
         saved.extend([*blocks, grads, hidden])
         return row_grads
 
-    def split(kept, got, types):
+    def split(kept, got, types, flops=0):
         shape = (kept.shape[0] // 2, columns)
-        return run(split_kernel, [(shape, t) for t in types], None, kept, got)
+        return run(split_kernel, [(shape, t) for t in types], None, kept, got, flops=flops)
 
     def collect(total, part):
         return run(add_kernel, [(total.shape, F32)], None, total, part)[0]
@@ -383,6 +383,10 @@
     got_1 = exchange(expert(second_1), near_b)
     kept_0, give = split(kept_0, got_0, (F32, BF16))
     got_0 = exchange(give, near_a)
+    kept_1, give = split(kept_1, got_1, (F32, BF16))
+    got_1 = exchange(give, near_a)
+    total, give = split(kept_0, got_0, (F32, BF16))
+    back_two = at_offset(give, 0)
     keep_in, keep_down, *gives = run(
         lambda *refs: weight_kernel(tuple(numbers), *refs),
         [
@@ -395,11 +399,7 @@
         place, *saved, limit=10, flops=6 * 10**9,
     )
     gots = [swap_core(give) for give in gives]
-    kept_1, give = split(kept_1, got_1, (F32, BF16))
-    got_1 = exchange(give, near_a)
-    total, give = split(kept_0, got_0, (F32, BF16))
-    back_two = at_offset(give, 0)
-    give_one, give_both = split(kept_1, got_1, (BF16, BF16))
+    give_one, give_both = split(kept_1, got_1, (BF16, BF16), flops=6 * 10**9)
     back_one, back_both = at_offset(give_one, 1), at_offset(give_both, 2)
     grad_gate, grad_up, grad_down, _ = run(
         settle_kernel,

time: 65.3 us -> 66.6 us (1.020)
  waiting for transfers between devices: 24.6 us -> 25.4 us
    ppermute x15, waiting for transfers between devices: 24.6 us -> 25.4 us  [exchange(): return lax.ppermute(x, DEVICES, pairs)]
where the time goes in v10:
time: 66.6 us; the launch traced here: 66.4 us
  starting transfers between devices  27.1 us (41%)
  waiting for transfers between devices  25.4 us (38%)
  Pallas kernels  12.9 us (19%)
  between operations  0.85 us (1%)
    ppermute x15, starting transfers between devices, exchange(): return lax.ppermute(x, DEVICES, pairs)  26 us
    ppermute x15, waiting for transfers between devices, exchange(): return lax.ppermute(x, DEVICES, pairs)  25.4 us
    pallas_call x21, Pallas kernels, call(): pl.pallas_call(run, out_shape=out_shape, in_specs=[pl.BlockSpec(memory_sp...  12 us
  transfers between devices with their start and end apart: 21, of which 8 were waited for; matrix products, arithmetic and copies ran while one was open for 0% of the time, Pallas kernels for 16%

profile of v10, /device:TPU:0, one launch (start us, length us, event | category | flops | bytes accessed | tf_op | source)
XLA Modules:
  0.0 66.4 jit_solution(7976620323809821397)
XLA Ops:
  0.6 0.9 %prepare_kernel.1.refs_0_ = bf16[32,2176]{1,0:T(8,128)(2,1)S(1)} custom-call(bf16[32,1024]{1,0:T(8,128)(2,1)} %tokens.1, bf16[32,1024]{1,0:T(8,128)(2,1)} %cotangent.1, s32[8,32]{1,0:T(8,128)} %bitcast.11, bf16[8,32]{1,0:T(8,128)(2,1)} %bitcast.28), custom_call_target="tpu_custom_call" | custom-call | tf_op jit(solution)/shard_map/prepare_kernel/pallas_call | solution.py:309
  1.6 3.0 %collective-permute-start = (bf16[32,2176]{1,0:T(8,128)(2,1)S(1)}, bf16[32,2176]{1,0:T(8,128)(2,1)S(1)}, u32[]{:S(2)}, u32[]{:S(2)}) collective-permute-start(bf16[32,2176]{1,0:T(8,128)(2,1)S(1)} %prepare_kernel.1.refs_0_), channel_id=1, source_target_pairs={{0,2},{1,5},{2,0},{3,7},{4,6},{5,1},{6,4},{7,3},{8,10},{9,13},{10,... | collective-permute-start | bytes 417800 | tf_op jit(solution)/shard_map/ppermute | solution.py:294
  4.6 2.6 %collective-permute-start.1 = (bf16[32,2176]{1,0:T(8,128)(2,1)S(1)}, bf16[32,2176]{1,0:T(8,128)(2,1)S(1)}, u32[]{:S(2)}, u32[]{:S(2)}) collective-permute-start(bf16[32,2176]{1,0:T(8,128)(2,1)S(1)} %prepare_kernel.1.refs_0_), channel_id=1, source_target_pairs={{0,16},{1,17},{2,18},{3,19},{4,20},{5,21},{6,22},{7,23},{8,24},{9,... | collective-permute-start | bytes 417800 | tf_op jit(solution)/shard_map/ppermute | solution.py:294
  7.2 0.5 collective-permute-start.4
  7.7 2.0 %collective-permute-start.3 = (bf16[64,2176]{1,0:T(8,128)(2,1)S(1)}, bf16[64,2176]{1,0:T(8,128)(2,1)S(1)}, u32[]{:S(2)}, u32[]{:S(2)}) collective-permute-start(bf16[64,2176]{1,0:T(8,128)(2,1)S(1)} %join_kernel.4.refs_2_.refs_1_), channel_id=1, source_target_pairs={{0,4},{1,3},{2,6},{3,1},{4,0},{5,7},{6,2},{7,5},{8,12},{9,11},{10,... | collective-permute-start | bytes 835592 | tf_op jit(solution)/shard_map/ppermute | solution.py:294
  9.8 3.9 %collective-permute-done.1.refs_1_.refs_0_ = bf16[32,2176]{1,0:T(8,128)(2,1)S(1)} collective-permute-done((bf16[32,2176]{1,0:T(8,128)(2,1)S(1)}, bf16[32,2176]{1,0:T(8,128)(2,1)S(1)}, u32[]{:S(2)}, u32[]{:S(2)}) %collective-permute-start.1) | collective-permute-done | bytes 139296 | tf_op jit(solution)/shard_map/ppermute | solution.py:294
  13.7 0.7 %collective-permute-start.7 = (bf16[64,2176]{1,0:T(8,128)(2,1)S(1)}, bf16[64,2176]{1,0:T(8,128)(2,1)S(1)}, u32[]{:S(2)}, u32[]{:S(2)}) collective-permute-start(bf16[64,2176]{1,0:T(8,128)(2,1)S(1)} %join_kernel.5.refs_1_), channel_id=1, source_target_pairs={{0,8},{1,9},{2,10},{3,11},{4,12},{5,13},{6,14},{7,15},{8,0},{9,1},... | collective-permute-start | bytes 835592 | tf_op jit(solution)/shard_map/ppermute | solution.py:294
  14.4 1.9 %collective-permute-start.2 = (bf16[32,2176]{1,0:T(8,128)(2,1)S(1)}, bf16[32,2176]{1,0:T(8,128)(2,1)S(1)}, u32[]{:S(2)}, u32[]{:S(2)}) collective-permute-start(bf16[32,2176]{1,0:T(8,128)(2,1)S(1)} %collective-permute-done.1.refs_1_.refs_0_), channel_id=1, source_target_pairs={{0,2},{1,5},{2,0},{3,7},{4,6},{5,1},{6,4},{7,3},{8,10},{9,13},{10,... | collective-permute-start | bytes 417800 | tf_op jit(solution)/shard_map/ppermute | solution.py:294
  16.4 3.0 %collective-permute-done.2.refs_1_ = bf16[32,2176]{1,0:T(8,128)(2,1)S(1)} collective-permute-done((bf16[32,2176]{1,0:T(8,128)(2,1)S(1)}, bf16[32,2176]{1,0:T(8,128)(2,1)S(1)}, u32[]{:S(2)}, u32[]{:S(2)}) %collective-permute-start.2) | collective-permute-done | bytes 139296 | tf_op jit(solution)/shard_map/ppermute | solution.py:294
  19.5 2.0 %collective-permute-start.8 = (bf16[64,2176]{1,0:T(8,128)(2,1)S(1)}, bf16[64,2176]{1,0:T(8,128)(2,1)S(1)}, u32[]{:S(2)}, u32[]{:S(2)}) collective-permute-start(bf16[64,2176]{1,0:T(8,128)(2,1)S(1)} %join_kernel.6.refs_1_.refs_2_), channel_id=1, source_target_pairs={{0,4},{1,3},{2,6},{3,1},{4,0},{5,7},{6,2},{7,5},{8,12},{9,11},{10,... | collective-permute-start | bytes 835592 | tf_op jit(solution)/shard_map/ppermute | solution.py:294
  21.5 2.4 %collective-permute-start.9 = (bf16[64,2176]{1,0:T(8,128)(2,1)S(1)}, bf16[64,2176]{1,0:T(8,128)(2,1)S(1)}, u32[]{:S(2)}, u32[]{:S(2)}) collective-permute-start(bf16[64,2176]{1,0:T(8,128)(2,1)S(1)} %pass_kernel.5.refs_1_.refs_0_), channel_id=1, source_target_pairs={{0,2},{1,5},{2,0},{3,7},{4,6},{5,1},{6,4},{7,3},{8,10},{9,13},{10,... | collective-permute-start | bytes 835592 | tf_op jit(solution)/shard_map/ppermute | solution.py:294
  24.0 1.7 %expert_kernel.4 = (bf16[128,1152]{1,0:T(8,128)(2,1)S(1)}, bf16[2,64,768]{2,1,0:T(8,128)(2,1)S(1)}, bf16[2,64,384]{2,1,0:T(8,128)(2,1)S(1)}) custom-call(s32[2]{0:T(128)S(1)} %pad_add_fusion.refs_0_, bf16[64,2176]{1,0:T(8,128)(2,1)S(1)} %join_kernel.4.refs_2_.refs_1_, bf16[64,2176]{1,0:T(8,128)(2,1)S(1)} %join_kernel.6.refs_1_.refs_2_, ...), custom_call_target="tpu_custom_call" | custom-call | flops 6000000000 | tf_op jit(solution)/shard_map/expert_kernel/pallas_call | solution.py:253
  25.7 2.7 %collective-permute-done.9.refs_1_ = bf16[64,2176]{1,0:T(8,128)(2,1)S(1)} collective-permute-done((bf16[64,2176]{1,0:T(8,128)(2,1)S(1)}, bf16[64,2176]{1,0:T(8,128)(2,1)S(1)}, u32[]{:S(2)}, u32[]{:S(2)}) %collective-permute-start.9) | collective-permute-done | bytes 278560 | tf_op jit(solution)/shard_map/ppermute | solution.py:294
  28.5 1.8 %expert_kernel.5 = (bf16[128,1152]{1,0:T(8,128)(2,1)S(1)}, bf16[2,64,768]{2,1,0:T(8,128)(2,1)S(1)}, bf16[2,64,384]{2,1,0:T(8,128)(2,1)S(1)}) custom-call(s32[2]{0:T(128)S(1)} %pad_add_fusion.refs_0_, bf16[64,2176]{1,0:T(8,128)(2,1)S(1)} %pass_kernel.4.refs_2_.refs_1_.refs_5_, bf16[64,2176]{1,0:T(8,128)(2,1)S(1)} %collective-permute-done.8.refs_2_.refs_6_, ...), custom_call_target="tpu_custom_call" | custom-call | flops 6000000000 | tf_op jit(solution)/shard_map/expert_kernel/pallas_call | solution.py:253
  30.3 1.8 %expert_kernel.6 = (bf16[128,1152]{1,0:T(8,128)(2,1)S(1)}, bf16[1,128,768]{2,1,0:T(8,128)(2,1)S(1)}, bf16[1,128,384]{2,1,0:T(8,128)(2,1)S(1)}) custom-call(s32[2]{0:T(128)S(1)} %pad_add_fusion.refs_0_, bf16[128,2176]{1,0:T(8,128)(2,1)S(1)} %join_kernel.7.refs_9_.refs_1_, bf16[512,384]{1,0:T(8,128)(2,1)S(1)} %bitcast.16, ...), custom_call_target="tpu_custom_call" | custom-call | flops 6000000000 | tf_op jit(solution)/shard_map/expert_kernel/pallas_call | solution.py:253
  32.1 6.0 %collective-permute-done.10.refs_2_.refs_1_.refs_12_ = bf16[128,2176]{1,0:T(8,128)(2,1)S(1)} collective-permute-done((bf16[128,2176]{1,0:T(8,128)(2,1)S(1)}, bf16[128,2176]{1,0:T(8,128)(2,1)S(1)}, u32[]{:S(2)}, u32[]{:S(2)}) %collective-permute-start.10) | collective-permute-done | bytes 557088 | tf_op jit(solution)/shard_map/ppermute | solution.py:294
  38.1 1.8 %expert_kernel.7 = (bf16[128,1152]{1,0:T(8,128)(2,1)S(1)}, bf16[1,128,768]{2,1,0:T(8,128)(2,1)S(1)}, bf16[1,128,384]{2,1,0:T(8,128)(2,1)S(1)}) custom-call(s32[2]{0:T(128)S(1)} %pad_add_fusion.refs_0_, bf16[128,2176]{1,0:T(8,128)(2,1)S(1)} %collective-permute-done.10.refs_2_.refs_1_.refs_12_, bf16[512,384]{1,0:T(8,128)(2,1)S(1)} %bitcast.17, ...), custom_call_target="tpu_custom_call" | custom-call | flops 6000000000 | tf_op jit(solution)/shard_map/expert_kernel/pallas_call | solution.py:253
  39.9 2.1 %collective-permute-start.13 = (bf16[128,1152]{1,0:T(8,128)(2,1)S(1)}, bf16[128,1152]{1,0:T(8,128)(2,1)S(1)}, u32[]{:S(2)}, u32[]{:S(2)}) collective-permute-start(bf16[128,1152]{1,0:T(8,128)(2,1)S(1)} %get-tuple-element.45), channel_id=1, source_target_pairs={{0,4},{1,3},{2,6},{3,1},{4,0},{5,7},{6,2},{7,5},{8,12},{9,11},{10,... | collective-permute-start | bytes 884744 | tf_op jit(solution)/shard_map/ppermute | solution.py:294
  42.0 2.9 %collective-permute-done.11.refs_1_ = bf16[128,1152]{1,0:T(8,128)(2,1)S(1)} collective-permute-done((bf16[128,1152]{1,0:T(8,128)(2,1)S(1)}, bf16[128,1152]{1,0:T(8,128)(2,1)S(1)}, u32[]{:S(2)}, u32[]{:S(2)}) %collective-permute-start.11) | collective-permute-done | bytes 294944 | tf_op jit(solution)/shard_map/ppermute | solution.py:294
  44.9 2.1 %collective-permute-start.12 = (bf16[64,1152]{1,0:T(8,128)(2,1)S(1)}, bf16[64,1152]{1,0:T(8,128)(2,1)S(1)}, u32[]{:S(2)}, u32[]{:S(2)}) collective-permute-start(bf16[64,1152]{1,0:T(8,128)(2,1)S(1)} %get-tuple-element.43.refs_2_), channel_id=1, source_target_pairs={{0,2},{1,5},{2,0},{3,7},{4,6},{5,1},{6,4},{7,3},{8,10},{9,13},{10,... | collective-permute-start | bytes 442376 | tf_op jit(solution)/shard_map/ppermute | solution.py:294
  47.0 2.4 %collective-permute-done.13.refs_1_ = bf16[128,1152]{1,0:T(8,128)(2,1)S(1)} collective-permute-done((bf16[128,1152]{1,0:T(8,128)(2,1)S(1)}, bf16[128,1152]{1,0:T(8,128)(2,1)S(1)}, u32[]{:S(2)}, u32[]{:S(2)}) %collective-permute-start.13) | collective-permute-done | bytes 294944 | tf_op jit(solution)/shard_map/ppermute | solution.py:294
  49.5 2.4 %collective-permute-start.18 = (bf16[64,1152]{1,0:T(8,128)(2,1)S(1)}, bf16[64,1152]{1,0:T(8,128)(2,1)S(1)}, u32[]{:S(2)}, u32[]{:S(2)}) collective-permute-start(bf16[64,1152]{1,0:T(8,128)(2,1)S(1)} %get-tuple-element.46.refs_2_), channel_id=1, source_target_pairs={{0,2},{1,5},{2,0},{3,7},{4,6},{5,1},{6,4},{7,3},{8,10},{9,13},{10,... | collective-permute-start | bytes 442376 | tf_op jit(solution)/shard_map/ppermute | solution.py:294
  51.9 1.8 %collective-permute-start.14 = (bf16[32,1152]{1,0:T(8,128)(2,1)S(1)}, bf16[32,1152]{1,0:T(8,128)(2,1)S(1)}, u32[]{:S(2)}, u32[]{:S(2)}) collective-permute-start(bf16[32,1152]{1,0:T(8,128)(2,1)S(1)} %get-tuple-element.48.refs_15_), channel_id=1, source_target_pairs={{0,16},{1,17},{2,18},{3,19},{4,20},{5,21},{6,22},{7,23},{8,24},{9,... | collective-permute-start | bytes 221192 | tf_op jit(solution)/shard_map/ppermute | solution.py:294
  53.7 2.0 %weight_kernel.1 = (f32[512,768]{1,0:T(8,128)S(1)}, f32[384,512]{1,0:T(8,128)S(1)}, bf16[512,384]{1,0:T(8,128)(2,1)S(1)}, bf16[512,384]{1,0:T(8,128)(2,1)S(1)}, bf16[384,512]{1,0:T(8,128)(2,1)S(1)}) custom-call(s32[2]{0:T(128)S(1)} %pad_add_fusion.refs_0_, bf16[64,2176]{1,0:T(8,128)(2,1)S(1)} %join_kernel.4.refs_2_.refs_1_, ...), custom_call_target="tpu_custom_call" | custom-call | flops 6000000000 | tf_op jit(solution)/shard_map/weight_kernel/pallas_call | solution.py:253
  55.8 0.5 collective-permute-start.16
  56.3 0.1 collective-permute-start.17
  56.5 2.4 %collective-permute-start.19 = (bf16[32,1152]{1,0:T(8,128)(2,1)S(1)}, bf16[32,1152]{1,0:T(8,128)(2,1)S(1)}, u32[]{:S(2)}, u32[]{:S(2)}) collective-permute-start(bf16[32,1152]{1,0:T(8,128)(2,1)S(1)} %get-tuple-element.61), channel_id=1, source_target_pairs={{0,8},{1,9},{2,10},{3,11},{4,12},{5,13},{6,14},{7,15},{8,0},{9,1},... | collective-permute-start | bytes 221192 | tf_op jit(solution)/shard_map/ppermute | solution.py:294
  58.8 0.5 collective-permute-start.20
  59.3 1.2 %settle_kernel.1 = (bf16[512,384]{1,0:T(8,128)(2,1)}, bf16[512,384]{1,0:T(8,128)(2,1)}, bf16[384,512]{1,0:T(8,128)(2,1)}, f32[8,128]{1,0:T(8,128)S(1)}) custom-call(f32[512,768]{1,0:T(8,128)S(1)} %get-tuple-element.53.refs_0_, f32[384,512]{1,0:T(8,128)S(1)} %get-tuple-element.54.refs_1_, bf16[512,384]{1,0:T(8,128)(2,1)S(1)} %collective-permute-done.15.refs_2_, ...), custom_call_target="tpu_custom_call" | custom-call | tf_op jit(solution)/shard_map/settle_kernel/pallas_call | solution.py:253
  60.5 1.1 %collective-permute-done.19.refs_1_ = bf16[32,1152]{1,0:T(8,128)(2,1)S(1)} collective-permute-done((bf16[32,1152]{1,0:T(8,128)(2,1)S(1)}, bf16[32,1152]{1,0:T(8,128)(2,1)S(1)}, u32[]{:S(2)}, u32[]{:S(2)}) %collective-permute-start.19) | collective-permute-done | bytes 73760 | tf_op jit(solution)/shard_map/ppermute | solution.py:294
  61.7 3.4 %collective-permute-done.20.refs_2_ = bf16[32,1152]{1,0:T(8,128)(2,1)S(1)} collective-permute-done((bf16[32,1152]{1,0:T(8,128)(2,1)S(1)}, bf16[32,1152]{1,0:T(8,128)(2,1)S(1)}, u32[]{:S(2)}, u32[]{:S(2)}) %collective-permute-start.20) | collective-permute-done | bytes 73760 | tf_op jit(solution)/shard_map/ppermute | solution.py:294
  65.1 1.4 %finish_kernel.1 = (bf16[32,1024]{1,0:T(8,128)(2,1)}, bf16[8,32]{1,0:T(8,128)(2,1)}) custom-call(s32[2]{0:T(128)S(1)} %pad_add_fusion.refs_0_, f32[32,1152]{1,0:T(8,128)S(1)} %add_kernel.3.refs_1_.refs_4_, bf16[32,1152]{1,0:T(8,128)(2,1)S(1)} %collective-permute-done.20.refs_2_, s32[8,32]{1,0:T(8,128)S(1)} %bitcast.12, f32[32,1152]{1,0:T(8,128)S(1)} %add_kernel.3.refs_1_.refs_4_), custom_call_target="tpu_custom_call" | custom-call | tf_op jit(solution)/shard_map/finish_kernel/pallas_call | solution.py:253
  (41 shorter events, 0.8 us)
Async XLA Ops:
  1.6 6.1 %collective-permute-start = (bf16[32,2176]{1,0:T(8,128)(2,1)S(1)}, bf16[32,2176]{1,0:T(8,128)(2,1)S(1)}, u32[]{:S(2)}, u32[]{:S(2)}) collective-permute-start(bf16[32,2176]{1,0:T(8,128)(2,1)S(1)} %prepare_kernel.1.refs_0_), channel_id=1, source_target_pairs={{0,2},{1,5},{2,0},{3,7},{4,6},{5,1},{6,4},{7,3},{8,10},{9,13},{10,... | collective-permute-start | bytes 417800 | tf_op jit(solution)/shard_map/ppermute | solution.py:294
  4.6 9.0 %collective-permute-start.1 = (bf16[32,2176]{1,0:T(8,128)(2,1)S(1)}, bf16[32,2176]{1,0:T(8,128)(2,1)S(1)}, u32[]{:S(2)}, u32[]{:S(2)}) collective-permute-start(bf16[32,2176]{1,0:T(8,128)(2,1)S(1)} %prepare_kernel.1.refs_0_), channel_id=1, source_target_pairs={{0,16},{1,17},{2,18},{3,19},{4,20},{5,21},{6,22},{7,23},{8,24},{9,... | collective-permute-start | bytes 417800 | tf_op jit(solution)/shard_map/ppermute | solution.py:294
  7.2 16.7 %collective-permute-start.6 = (bf16[384,512]{1,0:T(8,128)(2,1)}, bf16[384,512]{1,0:T(8,128)(2,1)S(1)}, u32[]{:S(2)}, u32[]{:S(2)}) collective-permute-start(bf16[384,512]{1,0:T(8,128)(2,1)} %bitcast.23), channel_id=1, source_target_pairs={{0,1},{1,0},{2,3},{3,2},{4,5},{5,4},{6,7},{7,6},{8,9},{9,8},{10,11... | collective-permute-start | bytes 1179656 | tf_op jit(solution)/shard_map/ppermute | solution.py:21
  7.2 16.7 %collective-permute-start.4 = (bf16[512,384]{1,0:T(8,128)(2,1)}, bf16[512,384]{1,0:T(8,128)(2,1)S(1)}, u32[]{:S(2)}, u32[]{:S(2)}) collective-permute-start(bf16[512,384]{1,0:T(8,128)(2,1)} %bitcast.13), channel_id=1, source_target_pairs={{0,1},{1,0},{2,3},{3,2},{4,5},{5,4},{6,7},{7,6},{8,9},{9,8},{10,11... | collective-permute-start | bytes 1179656 | tf_op jit(solution)/shard_map/ppermute | solution.py:21
  7.7 16.2 %collective-permute-start.5 = (bf16[512,384]{1,0:T(8,128)(2,1)}, bf16[512,384]{1,0:T(8,128)(2,1)S(1)}, u32[]{:S(2)}, u32[]{:S(2)}) collective-permute-start(bf16[512,384]{1,0:T(8,128)(2,1)} %bitcast.18), channel_id=1, source_target_pairs={{0,1},{1,0},{2,3},{3,2},{4,5},{5,4},{6,7},{7,6},{8,9},{9,8},{10,11... | collective-permute-start | bytes 1179656 | tf_op jit(solution)/shard_map/ppermute | solution.py:21
  7.7 6.7 %collective-permute-start.3 = (bf16[64,2176]{1,0:T(8,128)(2,1)S(1)}, bf16[64,2176]{1,0:T(8,128)(2,1)S(1)}, u32[]{:S(2)}, u32[]{:S(2)}) collective-permute-start(bf16[64,2176]{1,0:T(8,128)(2,1)S(1)} %join_kernel.4.refs_2_.refs_1_), channel_id=1, source_target_pairs={{0,4},{1,3},{2,6},{3,1},{4,0},{5,7},{6,2},{7,5},{8,12},{9,11},{10,... | collective-permute-start | bytes 835592 | tf_op jit(solution)/shard_map/ppermute | solution.py:294
  13.7 7.8 %collective-permute-start.7 = (bf16[64,2176]{1,0:T(8,128)(2,1)S(1)}, bf16[64,2176]{1,0:T(8,128)(2,1)S(1)}, u32[]{:S(2)}, u32[]{:S(2)}) collective-permute-start(bf16[64,2176]{1,0:T(8,128)(2,1)S(1)} %join_kernel.5.refs_1_), channel_id=1, source_target_pairs={{0,8},{1,9},{2,10},{3,11},{4,12},{5,13},{6,14},{7,15},{8,0},{9,1},... | collective-permute-start | bytes 835592 | tf_op jit(solution)/shard_map/ppermute | solution.py:294
  14.4 5.1 %collective-permute-start.2 = (bf16[32,2176]{1,0:T(8,128)(2,1)S(1)}, bf16[32,2176]{1,0:T(8,128)(2,1)S(1)}, u32[]{:S(2)}, u32[]{:S(2)}) collective-permute-start(bf16[32,2176]{1,0:T(8,128)(2,1)S(1)} %collective-permute-done.1.refs_1_.refs_0_), channel_id=1, source_target_pairs={{0,2},{1,5},{2,0},{3,7},{4,6},{5,1},{6,4},{7,3},{8,10},{9,13},{10,... | collective-permute-start | bytes 417800 | tf_op jit(solution)/shard_map/ppermute | solution.py:294
  16.4 7.6 %copy-start.1 = (bf16[1,512,384]{2,1,0:T(8,128)(2,1)S(1)}, bf16[1,512,384]{2,1,0:T(8,128)(2,1)}, u32[]{:S(2)}) copy-start(bf16[1,512,384]{2,1,0:T(8,128)(2,1)} %param.11) | copy-start | bytes 1179652
  16.4 7.6 %copy-start.2 = (bf16[1,512,384]{2,1,0:T(8,128)(2,1)S(1)}, bf16[1,512,384]{2,1,0:T(8,128)(2,1)}, u32[]{:S(2)}) copy-start(bf16[1,512,384]{2,1,0:T(8,128)(2,1)} %param.12) | copy-start | bytes 1179652
  16.4 7.6 %copy-start.3 = (bf16[1,384,512]{2,1,0:T(8,128)(2,1)S(1)}, bf16[1,384,512]{2,1,0:T(8,128)(2,1)}, u32[]{:S(2)}) copy-start(bf16[1,384,512]{2,1,0:T(8,128)(2,1)} %param.13) | copy-start | bytes 1179652
  19.5 9.1 %collective-permute-start.8 = (bf16[64,2176]{1,0:T(8,128)(2,1)S(1)}, bf16[64,2176]{1,0:T(8,128)(2,1)S(1)}, u32[]{:S(2)}, u32[]{:S(2)}) collective-permute-start(bf16[64,2176]{1,0:T(8,128)(2,1)S(1)} %join_kernel.6.refs_1_.refs_2_), channel_id=1, source_target_pairs={{0,4},{1,3},{2,6},{3,1},{4,0},{5,7},{6,2},{7,5},{8,12},{9,11},{10,... | collective-permute-start | bytes 835592 | tf_op jit(solution)/shard_map/ppermute | solution.py:294
  21.5 6.9 %collective-permute-start.9 = (bf16[64,2176]{1,0:T(8,128)(2,1)S(1)}, bf16[64,2176]{1,0:T(8,128)(2,1)S(1)}, u32[]{:S(2)}, u32[]{:S(2)}) collective-permute-start(bf16[64,2176]{1,0:T(8,128)(2,1)S(1)} %pass_kernel.5.refs_1_.refs_0_), channel_id=1, source_target_pairs={{0,2},{1,5},{2,0},{3,7},{4,6},{5,1},{6,4},{7,3},{8,10},{9,13},{10,... | collective-permute-start | bytes 835592 | tf_op jit(solution)/shard_map/ppermute | solution.py:294
  28.4 9.6 %collective-permute-start.10 = (bf16[128,2176]{1,0:T(8,128)(2,1)S(1)}, bf16[128,2176]{1,0:T(8,128)(2,1)S(1)}, u32[]{:S(2)}, u32[]{:S(2)}) collective-permute-start(bf16[128,2176]{1,0:T(8,128)(2,1)S(1)} %join_kernel.7.refs_9_.refs_1_), channel_id=1, source_target_pairs={{0,4},{1,3},{2,6},{3,1},{4,0},{5,7},{6,2},{7,5},{8,12},{9,11},{10,... | collective-permute-start | bytes 1671176 | tf_op jit(solution)/shard_map/ppermute | solution.py:294
  38.1 6.8 %collective-permute-start.11 = (bf16[128,1152]{1,0:T(8,128)(2,1)S(1)}, bf16[128,1152]{1,0:T(8,128)(2,1)S(1)}, u32[]{:S(2)}, u32[]{:S(2)}) collective-permute-start(bf16[128,1152]{1,0:T(8,128)(2,1)S(1)} %pass_kernel.7.refs_8_), channel_id=1, source_target_pairs={{0,4},{1,3},{2,6},{3,1},{4,0},{5,7},{6,2},{7,5},{8,12},{9,11},{10,... | collective-permute-start | bytes 884744 | tf_op jit(solution)/shard_map/ppermute | solution.py:294
  39.9 9.5 %collective-permute-start.13 = (bf16[128,1152]{1,0:T(8,128)(2,1)S(1)}, bf16[128,1152]{1,0:T(8,128)(2,1)S(1)}, u32[]{:S(2)}, u32[]{:S(2)}) collective-permute-start(bf16[128,1152]{1,0:T(8,128)(2,1)S(1)} %get-tuple-element.45), channel_id=1, source_target_pairs={{0,4},{1,3},{2,6},{3,1},{4,0},{5,7},{6,2},{7,5},{8,12},{9,11},{10,... | collective-permute-start | bytes 884744 | tf_op jit(solution)/shard_map/ppermute | solution.py:294
  44.9 7.0 %collective-permute-start.12 = (bf16[64,1152]{1,0:T(8,128)(2,1)S(1)}, bf16[64,1152]{1,0:T(8,128)(2,1)S(1)}, u32[]{:S(2)}, u32[]{:S(2)}) collective-permute-start(bf16[64,1152]{1,0:T(8,128)(2,1)S(1)} %get-tuple-element.43.refs_2_), channel_id=1, source_target_pairs={{0,2},{1,5},{2,0},{3,7},{4,6},{5,1},{6,4},{7,3},{8,10},{9,13},{10,... | collective-permute-start | bytes 442376 | tf_op jit(solution)/shard_map/ppermute | solution.py:294
  49.5 6.9 %collective-permute-start.18 = (bf16[64,1152]{1,0:T(8,128)(2,1)S(1)}, bf16[64,1152]{1,0:T(8,128)(2,1)S(1)}, u32[]{:S(2)}, u32[]{:S(2)}) collective-permute-start(bf16[64,1152]{1,0:T(8,128)(2,1)S(1)} %get-tuple-element.46.refs_2_), channel_id=1, source_target_pairs={{0,2},{1,5},{2,0},{3,7},{4,6},{5,1},{6,4},{7,3},{8,10},{9,13},{10,... | collective-permute-start | bytes 442376 | tf_op jit(solution)/shard_map/ppermute | solution.py:294
  51.9 8.6 %collective-permute-start.14 = (bf16[32,1152]{1,0:T(8,128)(2,1)S(1)}, bf16[32,1152]{1,0:T(8,128)(2,1)S(1)}, u32[]{:S(2)}, u32[]{:S(2)}) collective-permute-start(bf16[32,1152]{1,0:T(8,128)(2,1)S(1)} %get-tuple-element.48.refs_15_), channel_id=1, source_target_pairs={{0,16},{1,17},{2,18},{3,19},{4,20},{5,21},{6,22},{7,23},{8,24},{9,... | collective-permute-start | bytes 221192 | tf_op jit(solution)/shard_map/ppermute | solution.py:294
  55.8 3.1 %collective-permute-start.15 = (bf16[512,384]{1,0:T(8,128)(2,1)S(1)}, bf16[512,384]{1,0:T(8,128)(2,1)S(1)}, u32[]{:S(2)}, u32[]{:S(2)}) collective-permute-start(bf16[512,384]{1,0:T(8,128)(2,1)S(1)} %get-tuple-element.55), channel_id=1, source_target_pairs={{0,1},{1,0},{2,3},{3,2},{4,5},{5,4},{6,7},{7,6},{8,9},{9,8},{10,11... | collective-permute-start | bytes 1179656 | tf_op jit(solution)/shard_map/ppermute | solution.py:21
  55.8 3.5 %collective-permute-start.16 = (bf16[512,384]{1,0:T(8,128)(2,1)S(1)}, bf16[512,384]{1,0:T(8,128)(2,1)S(1)}, u32[]{:S(2)}, u32[]{:S(2)}) collective-permute-start(bf16[512,384]{1,0:T(8,128)(2,1)S(1)} %get-tuple-element.56), channel_id=1, source_target_pairs={{0,1},{1,0},{2,3},{3,2},{4,5},{5,4},{6,7},{7,6},{8,9},{9,8},{10,11... | collective-permute-start | bytes 1179656 | tf_op jit(solution)/shard_map/ppermute | solution.py:21
  56.3 3.0 %collective-permute-start.17 = (bf16[384,512]{1,0:T(8,128)(2,1)S(1)}, bf16[384,512]{1,0:T(8,128)(2,1)S(1)}, u32[]{:S(2)}, u32[]{:S(2)}) collective-permute-start(bf16[384,512]{1,0:T(8,128)(2,1)S(1)} %get-tuple-element.57.refs_2_), channel_id=1, source_target_pairs={{0,1},{1,0},{2,3},{3,2},{4,5},{5,4},{6,7},{7,6},{8,9},{9,8},{10,11... | collective-permute-start | bytes 1179656 | tf_op jit(solution)/shard_map/ppermute | solution.py:21
  56.5 5.2 %collective-permute-start.19 = (bf16[32,1152]{1,0:T(8,128)(2,1)S(1)}, bf16[32,1152]{1,0:T(8,128)(2,1)S(1)}, u32[]{:S(2)}, u32[]{:S(2)}) collective-permute-start(bf16[32,1152]{1,0:T(8,128)(2,1)S(1)} %get-tuple-element.61), channel_id=1, source_target_pairs={{0,8},{1,9},{2,10},{3,11},{4,12},{5,13},{6,14},{7,15},{8,0},{9,1},... | collective-permute-start | bytes 221192 | tf_op jit(solution)/shard_map/ppermute | solution.py:294
  58.8 6.2 %collective-permute-start.20 = (bf16[32,1152]{1,0:T(8,128)(2,1)S(1)}, bf16[32,1152]{1,0:T(8,128)(2,1)S(1)}, u32[]{:S(2)}, u32[]{:S(2)}) collective-permute-start(bf16[32,1152]{1,0:T(8,128)(2,1)S(1)} %get-tuple-element.59.refs_5_), channel_id=1, source_target_pairs={{0,24},{1,25},{2,26},{3,27},{4,28},{5,29},{6,30},{7,31},{8,16},{9,... | collective-permute-start | bytes 221192 | tf_op jit(solution)/shard_map/ppermute | solution.py:294
  59.3 5.8 %copy-start = (s32[32,8]{0,1:T(8,128)S(1)}, s32[32,8]{0,1:T(8,128)}, u32[]{:S(2)}) copy-start(s32[32,8]{0,1:T(8,128)} %param.9) | copy-start | bytes 3076

commit v11 on v10

--- a/solution.py
+++ b/solution.py
@@ -383,10 +383,6 @@
     got_1 = exchange(expert(second_1), near_b)
     kept_0, give = split(kept_0, got_0, (F32, BF16))
     got_0 = exchange(give, near_a)
-    kept_1, give = split(kept_1, got_1, (F32, BF16))
-    got_1 = exchange(give, near_a)
-    total, give = split(kept_0, got_0, (F32, BF16))
-    back_two = at_offset(give, 0)
     keep_in, keep_down, *gives = run(
         lambda *refs: weight_kernel(tuple(numbers), *refs),
         [
@@ -398,6 +394,10 @@
         ],
         place, *saved, limit=10, flops=6 * 10**9,
     )
+    kept_1, give = split(kept_1, got_1, (F32, BF16))
+    got_1 = exchange(give, near_a)
+    total, give = split(kept_0, got_0, (F32, BF16))
+    back_two = at_offset(give, 0)
     gots = [swap_core(give) for give in gives]
     give_one, give_both = split(kept_1, got_1, (BF16, BF16), flops=6 * 10**9)
     back_one, back_both = at_offset(give_one, 1), at_offset(give_both, 2)

time: 66.6 us -> 64.6 us (0.970)
  waiting for transfers between devices: 25.4 us -> 22.3 us
  starting transfers between devices: 27.1 us -> 28.2 us
    ppermute x15, waiting for transfers between devices: 25.4 us -> 22.3 us  [exchange(): return lax.ppermute(x, DEVICES, pairs)]
    ppermute x15, starting transfers between devices: 26 us -> 27.2 us  [exchange(): return lax.ppermute(x, DEVICES, pairs)]
where the time goes in v11:
time: 64.6 us; the launch traced here: 64.4 us
  starting transfers between devices  28.2 us (44%)
  waiting for transfers between devices  22.3 us (35%)
  Pallas kernels  12.9 us (20%)
  between operations  0.85 us (1%)
    ppermute x15, starting transfers between devices, exchange(): return lax.ppermute(x, DEVICES, pairs)  27.2 us
    ppermute x15, waiting for transfers between devices, exchange(): return lax.ppermute(x, DEVICES, pairs)  22.3 us
    pallas_call x21, Pallas kernels, call(): pl.pallas_call(run, out_shape=out_shape, in_specs=[pl.BlockSpec(memory_sp...  12 us
  transfers between devices with their start and end apart: 21, of which 8 were waited for; matrix products, arithmetic and copies ran while one was open for 0% of the time, Pallas kernels for 16%

profile of v11, /device:TPU:0, one launch (start us, length us, event | category | flops | bytes accessed | tf_op | source)
XLA Modules:
  0.0 64.4 jit_solution(9241887687686907715)
XLA Ops:
  0.6 0.9 %prepare_kernel.1.refs_0_ = bf16[32,2176]{1,0:T(8,128)(2,1)S(1)} custom-call(bf16[32,1024]{1,0:T(8,128)(2,1)} %tokens.1, bf16[32,1024]{1,0:T(8,128)(2,1)} %cotangent.1, s32[8,32]{1,0:T(8,128)} %bitcast.11, bf16[8,32]{1,0:T(8,128)(2,1)} %bitcast.28), custom_call_target="tpu_custom_call" | custom-call | tf_op jit(solution)/shard_map/prepare_kernel/pallas_call | solution.py:309
  1.6 3.0 %collective-permute-start = (bf16[32,2176]{1,0:T(8,128)(2,1)S(1)}, bf16[32,2176]{1,0:T(8,128)(2,1)S(1)}, u32[]{:S(2)}, u32[]{:S(2)}) collective-permute-start(bf16[32,2176]{1,0:T(8,128)(2,1)S(1)} %prepare_kernel.1.refs_0_), channel_id=1, source_target_pairs={{0,2},{1,5},{2,0},{3,7},{4,6},{5,1},{6,4},{7,3},{8,10},{9,13},{10,... | collective-permute-start | bytes 417800 | tf_op jit(solution)/shard_map/ppermute | solution.py:294
  4.6 2.6 %collective-permute-start.1 = (bf16[32,2176]{1,0:T(8,128)(2,1)S(1)}, bf16[32,2176]{1,0:T(8,128)(2,1)S(1)}, u32[]{:S(2)}, u32[]{:S(2)}) collective-permute-start(bf16[32,2176]{1,0:T(8,128)(2,1)S(1)} %prepare_kernel.1.refs_0_), channel_id=1, source_target_pairs={{0,16},{1,17},{2,18},{3,19},{4,20},{5,21},{6,22},{7,23},{8,24},{9,... | collective-permute-start | bytes 417800 | tf_op jit(solution)/shard_map/ppermute | solution.py:294
  7.2 0.5 collective-permute-start.5
  7.7 2.0 %collective-permute-start.3 = (bf16[64,2176]{1,0:T(8,128)(2,1)S(1)}, bf16[64,2176]{1,0:T(8,128)(2,1)S(1)}, u32[]{:S(2)}, u32[]{:S(2)}) collective-permute-start(bf16[64,2176]{1,0:T(8,128)(2,1)S(1)} %join_kernel.4.refs_2_.refs_1_), channel_id=1, source_target_pairs={{0,4},{1,3},{2,6},{3,1},{4,0},{5,7},{6,2},{7,5},{8,12},{9,11},{10,... | collective-permute-start | bytes 835592 | tf_op jit(solution)/shard_map/ppermute | solution.py:294
  9.8 3.9 %collective-permute-done.1.refs_1_.refs_0_ = bf16[32,2176]{1,0:T(8,128)(2,1)S(1)} collective-permute-done((bf16[32,2176]{1,0:T(8,128)(2,1)S(1)}, bf16[32,2176]{1,0:T(8,128)(2,1)S(1)}, u32[]{:S(2)}, u32[]{:S(2)}) %collective-permute-start.1) | collective-permute-done | bytes 139296 | tf_op jit(solution)/shard_map/ppermute | solution.py:294
  13.7 0.7 %collective-permute-start.7 = (bf16[64,2176]{1,0:T(8,128)(2,1)S(1)}, bf16[64,2176]{1,0:T(8,128)(2,1)S(1)}, u32[]{:S(2)}, u32[]{:S(2)}) collective-permute-start(bf16[64,2176]{1,0:T(8,128)(2,1)S(1)} %join_kernel.5.refs_1_), channel_id=1, source_target_pairs={{0,8},{1,9},{2,10},{3,11},{4,12},{5,13},{6,14},{7,15},{8,0},{9,1},... | collective-permute-start | bytes 835592 | tf_op jit(solution)/shard_map/ppermute | solution.py:294
  14.4 1.9 %collective-permute-start.2 = (bf16[32,2176]{1,0:T(8,128)(2,1)S(1)}, bf16[32,2176]{1,0:T(8,128)(2,1)S(1)}, u32[]{:S(2)}, u32[]{:S(2)}) collective-permute-start(bf16[32,2176]{1,0:T(8,128)(2,1)S(1)} %collective-permute-done.1.refs_1_.refs_0_), channel_id=1, source_target_pairs={{0,2},{1,5},{2,0},{3,7},{4,6},{5,1},{6,4},{7,3},{8,10},{9,13},{10,... | collective-permute-start | bytes 417800 | tf_op jit(solution)/shard_map/ppermute | solution.py:294
  16.3 0.1 pad_add_fusion.refs_0_
  16.4 3.0 %collective-permute-done.2.refs_1_ = bf16[32,2176]{1,0:T(8,128)(2,1)S(1)} collective-permute-done((bf16[32,2176]{1,0:T(8,128)(2,1)S(1)}, bf16[32,2176]{1,0:T(8,128)(2,1)S(1)}, u32[]{:S(2)}, u32[]{:S(2)}) %collective-permute-start.2) | collective-permute-done | bytes 139296 | tf_op jit(solution)/shard_map/ppermute | solution.py:294
  19.5 2.0 %collective-permute-start.8 = (bf16[64,2176]{1,0:T(8,128)(2,1)S(1)}, bf16[64,2176]{1,0:T(8,128)(2,1)S(1)}, u32[]{:S(2)}, u32[]{:S(2)}) collective-permute-start(bf16[64,2176]{1,0:T(8,128)(2,1)S(1)} %join_kernel.6.refs_1_.refs_2_), channel_id=1, source_target_pairs={{0,4},{1,3},{2,6},{3,1},{4,0},{5,7},{6,2},{7,5},{8,12},{9,11},{10,... | collective-permute-start | bytes 835592 | tf_op jit(solution)/shard_map/ppermute | solution.py:294
  21.5 2.4 %collective-permute-start.9 = (bf16[64,2176]{1,0:T(8,128)(2,1)S(1)}, bf16[64,2176]{1,0:T(8,128)(2,1)S(1)}, u32[]{:S(2)}, u32[]{:S(2)}) collective-permute-start(bf16[64,2176]{1,0:T(8,128)(2,1)S(1)} %pass_kernel.5.refs_1_.refs_0_), channel_id=1, source_target_pairs={{0,2},{1,5},{2,0},{3,7},{4,6},{5,1},{6,4},{7,3},{8,10},{9,13},{10,... | collective-permute-start | bytes 835592 | tf_op jit(solution)/shard_map/ppermute | solution.py:294
  24.0 1.7 %expert_kernel.4 = (bf16[128,1152]{1,0:T(8,128)(2,1)S(1)}, bf16[2,64,768]{2,1,0:T(8,128)(2,1)S(1)}, bf16[2,64,384]{2,1,0:T(8,128)(2,1)S(1)}) custom-call(s32[2]{0:T(128)S(1)} %pad_add_fusion.refs_0_, bf16[64,2176]{1,0:T(8,128)(2,1)S(1)} %join_kernel.4.refs_2_.refs_1_, bf16[64,2176]{1,0:T(8,128)(2,1)S(1)} %join_kernel.6.refs_1_.refs_2_, ...), custom_call_target="tpu_custom_call" | custom-call | flops 6000000000 | tf_op jit(solution)/shard_map/expert_kernel/pallas_call | solution.py:253
  25.7 2.7 %collective-permute-done.9.refs_1_ = bf16[64,2176]{1,0:T(8,128)(2,1)S(1)} collective-permute-done((bf16[64,2176]{1,0:T(8,128)(2,1)S(1)}, bf16[64,2176]{1,0:T(8,128)(2,1)S(1)}, u32[]{:S(2)}, u32[]{:S(2)}) %collective-permute-start.9) | collective-permute-done | bytes 278560 | tf_op jit(solution)/shard_map/ppermute | solution.py:294
  28.5 1.7 %expert_kernel.5 = (bf16[128,1152]{1,0:T(8,128)(2,1)S(1)}, bf16[2,64,768]{2,1,0:T(8,128)(2,1)S(1)}, bf16[2,64,384]{2,1,0:T(8,128)(2,1)S(1)}) custom-call(s32[2]{0:T(128)S(1)} %pad_add_fusion.refs_0_, bf16[64,2176]{1,0:T(8,128)(2,1)S(1)} %pass_kernel.4.refs_2_.refs_1_.refs_5_, bf16[64,2176]{1,0:T(8,128)(2,1)S(1)} %collective-permute-done.8.refs_2_.refs_6_, ...), custom_call_target="tpu_custom_call" | custom-call | flops 6000000000 | tf_op jit(solution)/shard_map/expert_kernel/pallas_call | solution.py:253
  30.3 1.8 %expert_kernel.6 = (bf16[128,1152]{1,0:T(8,128)(2,1)S(1)}, bf16[1,128,768]{2,1,0:T(8,128)(2,1)S(1)}, bf16[1,128,384]{2,1,0:T(8,128)(2,1)S(1)}) custom-call(s32[2]{0:T(128)S(1)} %pad_add_fusion.refs_0_, bf16[128,2176]{1,0:T(8,128)(2,1)S(1)} %join_kernel.7.refs_9_.refs_1_, bf16[512,384]{1,0:T(8,128)(2,1)S(1)} %bitcast.16, ...), custom_call_target="tpu_custom_call" | custom-call | flops 6000000000 | tf_op jit(solution)/shard_map/expert_kernel/pallas_call | solution.py:253
  32.1 6.0 %collective-permute-done.10.refs_2_.refs_1_.refs_12_ = bf16[128,2176]{1,0:T(8,128)(2,1)S(1)} collective-permute-done((bf16[128,2176]{1,0:T(8,128)(2,1)S(1)}, bf16[128,2176]{1,0:T(8,128)(2,1)S(1)}, u32[]{:S(2)}, u32[]{:S(2)}) %collective-permute-start.10) | collective-permute-done | bytes 557088 | tf_op jit(solution)/shard_map/ppermute | solution.py:294
  38.1 1.8 %expert_kernel.7 = (bf16[128,1152]{1,0:T(8,128)(2,1)S(1)}, bf16[1,128,768]{2,1,0:T(8,128)(2,1)S(1)}, bf16[1,128,384]{2,1,0:T(8,128)(2,1)S(1)}) custom-call(s32[2]{0:T(128)S(1)} %pad_add_fusion.refs_0_, bf16[128,2176]{1,0:T(8,128)(2,1)S(1)} %collective-permute-done.10.refs_2_.refs_1_.refs_12_, bf16[512,384]{1,0:T(8,128)(2,1)S(1)} %bitcast.17, ...), custom_call_target="tpu_custom_call" | custom-call | flops 6000000000 | tf_op jit(solution)/shard_map/expert_kernel/pallas_call | solution.py:253
  39.9 2.1 %collective-permute-start.13 = (bf16[128,1152]{1,0:T(8,128)(2,1)S(1)}, bf16[128,1152]{1,0:T(8,128)(2,1)S(1)}, u32[]{:S(2)}, u32[]{:S(2)}) collective-permute-start(bf16[128,1152]{1,0:T(8,128)(2,1)S(1)} %get-tuple-element.45), channel_id=1, source_target_pairs={{0,4},{1,3},{2,6},{3,1},{4,0},{5,7},{6,2},{7,5},{8,12},{9,11},{10,... | collective-permute-start | bytes 884744 | tf_op jit(solution)/shard_map/ppermute | solution.py:294
  42.0 2.9 %collective-permute-done.11.refs_1_ = bf16[128,1152]{1,0:T(8,128)(2,1)S(1)} collective-permute-done((bf16[128,1152]{1,0:T(8,128)(2,1)S(1)}, bf16[128,1152]{1,0:T(8,128)(2,1)S(1)}, u32[]{:S(2)}, u32[]{:S(2)}) %collective-permute-start.11) | collective-permute-done | bytes 294944 | tf_op jit(solution)/shard_map/ppermute | solution.py:294
  44.9 2.1 %collective-permute-start.12 = (bf16[64,1152]{1,0:T(8,128)(2,1)S(1)}, bf16[64,1152]{1,0:T(8,128)(2,1)S(1)}, u32[]{:S(2)}, u32[]{:S(2)}) collective-permute-start(bf16[64,1152]{1,0:T(8,128)(2,1)S(1)} %get-tuple-element.43.refs_15_), channel_id=1, source_target_pairs={{0,2},{1,5},{2,0},{3,7},{4,6},{5,1},{6,4},{7,3},{8,10},{9,13},{10,... | collective-permute-start | bytes 442376 | tf_op jit(solution)/shard_map/ppermute | solution.py:294
  47.0 2.0 %weight_kernel.1 = (f32[512,768]{1,0:T(8,128)S(1)}, f32[384,512]{1,0:T(8,128)S(1)}, bf16[512,384]{1,0:T(8,128)(2,1)S(1)}, bf16[512,384]{1,0:T(8,128)(2,1)S(1)}, bf16[384,512]{1,0:T(8,128)(2,1)S(1)}) custom-call(s32[2]{0:T(128)S(1)} %pad_add_fusion.refs_0_, bf16[64,2176]{1,0:T(8,128)(2,1)S(1)} %join_kernel.4.refs_2_.refs_1_, ...), custom_call_target="tpu_custom_call" | custom-call | flops 6000000000 | tf_op jit(solution)/shard_map/weight_kernel/pallas_call | solution.py:253
  49.0 0.4 collective-permute-done.13.refs_1_
  49.5 2.4 %collective-permute-start.18 = (bf16[64,1152]{1,0:T(8,128)(2,1)S(1)}, bf16[64,1152]{1,0:T(8,128)(2,1)S(1)}, u32[]{:S(2)}, u32[]{:S(2)}) collective-permute-start(bf16[64,1152]{1,0:T(8,128)(2,1)S(1)} %get-tuple-element.51.refs_2_), channel_id=1, source_target_pairs={{0,2},{1,5},{2,0},{3,7},{4,6},{5,1},{6,4},{7,3},{8,10},{9,13},{10,... | collective-permute-start | bytes 442376 | tf_op jit(solution)/shard_map/ppermute | solution.py:294
  51.9 0.5 collective-permute-start.15
  52.4 1.8 %collective-permute-start.14 = (bf16[32,1152]{1,0:T(8,128)(2,1)S(1)}, bf16[32,1152]{1,0:T(8,128)(2,1)S(1)}, u32[]{:S(2)}, u32[]{:S(2)}) collective-permute-start(bf16[32,1152]{1,0:T(8,128)(2,1)S(1)} %get-tuple-element.53.refs_2_), channel_id=1, source_target_pairs={{0,16},{1,17},{2,18},{3,19},{4,20},{5,21},{6,22},{7,23},{8,24},{9,... | collective-permute-start | bytes 221192 | tf_op jit(solution)/shard_map/ppermute | solution.py:294
  54.3 0.8 %collective-permute-done.18.refs_1_ = bf16[64,1152]{1,0:T(8,128)(2,1)S(1)} collective-permute-done((bf16[64,1152]{1,0:T(8,128)(2,1)S(1)}, bf16[64,1152]{1,0:T(8,128)(2,1)S(1)}, u32[]{:S(2)}, u32[]{:S(2)}) %collective-permute-start.18) | collective-permute-done | bytes 147488 | tf_op jit(solution)/shard_map/ppermute | solution.py:294
  55.1 1.6 %collective-permute-start.19 = (bf16[32,1152]{1,0:T(8,128)(2,1)S(1)}, bf16[32,1152]{1,0:T(8,128)(2,1)S(1)}, u32[]{:S(2)}, u32[]{:S(2)}) collective-permute-start(bf16[32,1152]{1,0:T(8,128)(2,1)S(1)} %get-tuple-element.61), channel_id=1, source_target_pairs={{0,8},{1,9},{2,10},{3,11},{4,12},{5,13},{6,14},{7,15},{8,0},{9,1},... | collective-permute-start | bytes 221192 | tf_op jit(solution)/shard_map/ppermute | solution.py:294
  56.7 2.4 %collective-permute-start.20 = (bf16[32,1152]{1,0:T(8,128)(2,1)S(1)}, bf16[32,1152]{1,0:T(8,128)(2,1)S(1)}, u32[]{:S(2)}, u32[]{:S(2)}) collective-permute-start(bf16[32,1152]{1,0:T(8,128)(2,1)S(1)} %get-tuple-element.59.refs_5_), channel_id=1, source_target_pairs={{0,24},{1,25},{2,26},{3,27},{4,28},{5,29},{6,30},{7,31},{8,16},{9,... | collective-permute-start | bytes 221192 | tf_op jit(solution)/shard_map/ppermute | solution.py:294
  59.1 1.2 %settle_kernel.1 = (bf16[512,384]{1,0:T(8,128)(2,1)}, bf16[512,384]{1,0:T(8,128)(2,1)}, bf16[384,512]{1,0:T(8,128)(2,1)}, f32[8,128]{1,0:T(8,128)S(1)}) custom-call(f32[512,768]{1,0:T(8,128)S(1)} %get-tuple-element.54.refs_0_, f32[384,512]{1,0:T(8,128)S(1)} %get-tuple-element.55.refs_1_, bf16[512,384]{1,0:T(8,128)(2,1)S(1)} %collective-permute-done.15.refs_2_, ...), custom_call_target="tpu_custom_call" | custom-call | tf_op jit(solution)/shard_map/settle_kernel/pallas_call | solution.py:253
  60.4 2.7 %collective-permute-done.20.refs_2_ = bf16[32,1152]{1,0:T(8,128)(2,1)S(1)} collective-permute-done((bf16[32,1152]{1,0:T(8,128)(2,1)S(1)}, bf16[32,1152]{1,0:T(8,128)(2,1)S(1)}, u32[]{:S(2)}, u32[]{:S(2)}) %collective-permute-start.20) | collective-permute-done | bytes 73760 | tf_op jit(solution)/shard_map/ppermute | solution.py:294
  63.0 1.4 %finish_kernel.1 = (bf16[32,1024]{1,0:T(8,128)(2,1)}, bf16[8,32]{1,0:T(8,128)(2,1)}) custom-call(s32[2]{0:T(128)S(1)} %pad_add_fusion.refs_0_, f32[32,1152]{1,0:T(8,128)S(1)} %add_kernel.3.refs_1_.refs_4_, bf16[32,1152]{1,0:T(8,128)(2,1)S(1)} %collective-permute-done.20.refs_2_, s32[8,32]{1,0:T(8,128)S(1)} %bitcast.12, f32[32,1152]{1,0:T(8,128)S(1)} %add_kernel.3.refs_1_.refs_4_), custom_call_target="tpu_custom_call" | custom-call | tf_op jit(solution)/shard_map/finish_kernel/pallas_call | solution.py:253
  (41 shorter events, 0.6 us)
Async XLA Ops:
  1.6 6.1 %collective-permute-start = (bf16[32,2176]{1,0:T(8,128)(2,1)S(1)}, bf16[32,2176]{1,0:T(8,128)(2,1)S(1)}, u32[]{:S(2)}, u32[]{:S(2)}) collective-permute-start(bf16[32,2176]{1,0:T(8,128)(2,1)S(1)} %prepare_kernel.1.refs_0_), channel_id=1, source_target_pairs={{0,2},{1,5},{2,0},{3,7},{4,6},{5,1},{6,4},{7,3},{8,10},{9,13},{10,... | collective-permute-start | bytes 417800 | tf_op jit(solution)/shard_map/ppermute | solution.py:294
  4.6 9.0 %collective-permute-start.1 = (bf16[32,2176]{1,0:T(8,128)(2,1)S(1)}, bf16[32,2176]{1,0:T(8,128)(2,1)S(1)}, u32[]{:S(2)}, u32[]{:S(2)}) collective-permute-start(bf16[32,2176]{1,0:T(8,128)(2,1)S(1)} %prepare_kernel.1.refs_0_), channel_id=1, source_target_pairs={{0,16},{1,17},{2,18},{3,19},{4,20},{5,21},{6,22},{7,23},{8,24},{9,... | collective-permute-start | bytes 417800 | tf_op jit(solution)/shard_map/ppermute | solution.py:294
  7.2 16.7 %collective-permute-start.4 = (bf16[512,384]{1,0:T(8,128)(2,1)}, bf16[512,384]{1,0:T(8,128)(2,1)S(1)}, u32[]{:S(2)}, u32[]{:S(2)}) collective-permute-start(bf16[512,384]{1,0:T(8,128)(2,1)} %bitcast.13), channel_id=1, source_target_pairs={{0,1},{1,0},{2,3},{3,2},{4,5},{5,4},{6,7},{7,6},{8,9},{9,8},{10,11... | collective-permute-start | bytes 1179656 | tf_op jit(solution)/shard_map/ppermute | solution.py:21
  7.2 16.7 %collective-permute-start.5 = (bf16[512,384]{1,0:T(8,128)(2,1)}, bf16[512,384]{1,0:T(8,128)(2,1)S(1)}, u32[]{:S(2)}, u32[]{:S(2)}) collective-permute-start(bf16[512,384]{1,0:T(8,128)(2,1)} %bitcast.18), channel_id=1, source_target_pairs={{0,1},{1,0},{2,3},{3,2},{4,5},{5,4},{6,7},{7,6},{8,9},{9,8},{10,11... | collective-permute-start | bytes 1179656 | tf_op jit(solution)/shard_map/ppermute | solution.py:21
  7.7 16.2 %collective-permute-start.6 = (bf16[384,512]{1,0:T(8,128)(2,1)}, bf16[384,512]{1,0:T(8,128)(2,1)S(1)}, u32[]{:S(2)}, u32[]{:S(2)}) collective-permute-start(bf16[384,512]{1,0:T(8,128)(2,1)} %bitcast.23), channel_id=1, source_target_pairs={{0,1},{1,0},{2,3},{3,2},{4,5},{5,4},{6,7},{7,6},{8,9},{9,8},{10,11... | collective-permute-start | bytes 1179656 | tf_op jit(solution)/shard_map/ppermute | solution.py:21
  7.7 6.7 %collective-permute-start.3 = (bf16[64,2176]{1,0:T(8,128)(2,1)S(1)}, bf16[64,2176]{1,0:T(8,128)(2,1)S(1)}, u32[]{:S(2)}, u32[]{:S(2)}) collective-permute-start(bf16[64,2176]{1,0:T(8,128)(2,1)S(1)} %join_kernel.4.refs_2_.refs_1_), channel_id=1, source_target_pairs={{0,4},{1,3},{2,6},{3,1},{4,0},{5,7},{6,2},{7,5},{8,12},{9,11},{10,... | collective-permute-start | bytes 835592 | tf_op jit(solution)/shard_map/ppermute | solution.py:294
  13.7 7.8 %collective-permute-start.7 = (bf16[64,2176]{1,0:T(8,128)(2,1)S(1)}, bf16[64,2176]{1,0:T(8,128)(2,1)S(1)}, u32[]{:S(2)}, u32[]{:S(2)}) collective-permute-start(bf16[64,2176]{1,0:T(8,128)(2,1)S(1)} %join_kernel.5.refs_1_), channel_id=1, source_target_pairs={{0,8},{1,9},{2,10},{3,11},{4,12},{5,13},{6,14},{7,15},{8,0},{9,1},... | collective-permute-start | bytes 835592 | tf_op jit(solution)/shard_map/ppermute | solution.py:294
  14.4 5.1 %collective-permute-start.2 = (bf16[32,2176]{1,0:T(8,128)(2,1)S(1)}, bf16[32,2176]{1,0:T(8,128)(2,1)S(1)}, u32[]{:S(2)}, u32[]{:S(2)}) collective-permute-start(bf16[32,2176]{1,0:T(8,128)(2,1)S(1)} %collective-permute-done.1.refs_1_.refs_0_), channel_id=1, source_target_pairs={{0,2},{1,5},{2,0},{3,7},{4,6},{5,1},{6,4},{7,3},{8,10},{9,13},{10,... | collective-permute-start | bytes 417800 | tf_op jit(solution)/shard_map/ppermute | solution.py:294
  16.4 7.6 %copy-start.1 = (bf16[1,512,384]{2,1,0:T(8,128)(2,1)S(1)}, bf16[1,512,384]{2,1,0:T(8,128)(2,1)}, u32[]{:S(2)}) copy-start(bf16[1,512,384]{2,1,0:T(8,128)(2,1)} %param.11) | copy-start | bytes 1179652
  16.4 7.6 %copy-start.2 = (bf16[1,512,384]{2,1,0:T(8,128)(2,1)S(1)}, bf16[1,512,384]{2,1,0:T(8,128)(2,1)}, u32[]{:S(2)}) copy-start(bf16[1,512,384]{2,1,0:T(8,128)(2,1)} %param.12) | copy-start | bytes 1179652
  16.4 7.6 %copy-start.3 = (bf16[1,384,512]{2,1,0:T(8,128)(2,1)S(1)}, bf16[1,384,512]{2,1,0:T(8,128)(2,1)}, u32[]{:S(2)}) copy-start(bf16[1,384,512]{2,1,0:T(8,128)(2,1)} %param.13) | copy-start | bytes 1179652
  19.5 9.1 %collective-permute-start.8 = (bf16[64,2176]{1,0:T(8,128)(2,1)S(1)}, bf16[64,2176]{1,0:T(8,128)(2,1)S(1)}, u32[]{:S(2)}, u32[]{:S(2)}) collective-permute-start(bf16[64,2176]{1,0:T(8,128)(2,1)S(1)} %join_kernel.6.refs_1_.refs_2_), channel_id=1, source_target_pairs={{0,4},{1,3},{2,6},{3,1},{4,0},{5,7},{6,2},{7,5},{8,12},{9,11},{10,... | collective-permute-start | bytes 835592 | tf_op jit(solution)/shard_map/ppermute | solution.py:294
  21.5 6.9 %collective-permute-start.9 = (bf16[64,2176]{1,0:T(8,128)(2,1)S(1)}, bf16[64,2176]{1,0:T(8,128)(2,1)S(1)}, u32[]{:S(2)}, u32[]{:S(2)}) collective-permute-start(bf16[64,2176]{1,0:T(8,128)(2,1)S(1)} %pass_kernel.5.refs_1_.refs_0_), channel_id=1, source_target_pairs={{0,2},{1,5},{2,0},{3,7},{4,6},{5,1},{6,4},{7,3},{8,10},{9,13},{10,... | collective-permute-start | bytes 835592 | tf_op jit(solution)/shard_map/ppermute | solution.py:294
  28.4 9.6 %collective-permute-start.10 = (bf16[128,2176]{1,0:T(8,128)(2,1)S(1)}, bf16[128,2176]{1,0:T(8,128)(2,1)S(1)}, u32[]{:S(2)}, u32[]{:S(2)}) collective-permute-start(bf16[128,2176]{1,0:T(8,128)(2,1)S(1)} %join_kernel.7.refs_9_.refs_1_), channel_id=1, source_target_pairs={{0,4},{1,3},{2,6},{3,1},{4,0},{5,7},{6,2},{7,5},{8,12},{9,11},{10,... | collective-permute-start | bytes 1671176 | tf_op jit(solution)/shard_map/ppermute | solution.py:294
  38.1 6.8 %collective-permute-start.11 = (bf16[128,1152]{1,0:T(8,128)(2,1)S(1)}, bf16[128,1152]{1,0:T(8,128)(2,1)S(1)}, u32[]{:S(2)}, u32[]{:S(2)}) collective-permute-start(bf16[128,1152]{1,0:T(8,128)(2,1)S(1)} %pass_kernel.7.refs_8_), channel_id=1, source_target_pairs={{0,4},{1,3},{2,6},{3,1},{4,0},{5,7},{6,2},{7,5},{8,12},{9,11},{10,... | collective-permute-start | bytes 884744 | tf_op jit(solution)/shard_map/ppermute | solution.py:294
  39.9 9.5 %collective-permute-start.13 = (bf16[128,1152]{1,0:T(8,128)(2,1)S(1)}, bf16[128,1152]{1,0:T(8,128)(2,1)S(1)}, u32[]{:S(2)}, u32[]{:S(2)}) collective-permute-start(bf16[128,1152]{1,0:T(8,128)(2,1)S(1)} %get-tuple-element.45), channel_id=1, source_target_pairs={{0,4},{1,3},{2,6},{3,1},{4,0},{5,7},{6,2},{7,5},{8,12},{9,11},{10,... | collective-permute-start | bytes 884744 | tf_op jit(solution)/shard_map/ppermute | solution.py:294
  44.9 7.5 %collective-permute-start.12 = (bf16[64,1152]{1,0:T(8,128)(2,1)S(1)}, bf16[64,1152]{1,0:T(8,128)(2,1)S(1)}, u32[]{:S(2)}, u32[]{:S(2)}) collective-permute-start(bf16[64,1152]{1,0:T(8,128)(2,1)S(1)} %get-tuple-element.43.refs_15_), channel_id=1, source_target_pairs={{0,2},{1,5},{2,0},{3,7},{4,6},{5,1},{6,4},{7,3},{8,10},{9,13},{10,... | collective-permute-start | bytes 442376 | tf_op jit(solution)/shard_map/ppermute | solution.py:294
  49.5 5.5 %collective-permute-start.18 = (bf16[64,1152]{1,0:T(8,128)(2,1)S(1)}, bf16[64,1152]{1,0:T(8,128)(2,1)S(1)}, u32[]{:S(2)}, u32[]{:S(2)}) collective-permute-start(bf16[64,1152]{1,0:T(8,128)(2,1)S(1)} %get-tuple-element.51.refs_2_), channel_id=1, source_target_pairs={{0,2},{1,5},{2,0},{3,7},{4,6},{5,1},{6,4},{7,3},{8,10},{9,13},{10,... | collective-permute-start | bytes 442376 | tf_op jit(solution)/shard_map/ppermute | solution.py:294
  51.9 7.2 %collective-permute-start.17 = (bf16[384,512]{1,0:T(8,128)(2,1)S(1)}, bf16[384,512]{1,0:T(8,128)(2,1)S(1)}, u32[]{:S(2)}, u32[]{:S(2)}) collective-permute-start(bf16[384,512]{1,0:T(8,128)(2,1)S(1)} %get-tuple-element.50.refs_2_), channel_id=1, source_target_pairs={{0,1},{1,0},{2,3},{3,2},{4,5},{5,4},{6,7},{7,6},{8,9},{9,8},{10,11... | collective-permute-start | bytes 1179656 | tf_op jit(solution)/shard_map/ppermute | solution.py:21
  51.9 4.8 %collective-permute-start.15 = (bf16[512,384]{1,0:T(8,128)(2,1)S(1)}, bf16[512,384]{1,0:T(8,128)(2,1)S(1)}, u32[]{:S(2)}, u32[]{:S(2)}) collective-permute-start(bf16[512,384]{1,0:T(8,128)(2,1)S(1)} %get-tuple-element.56), channel_id=1, source_target_pairs={{0,1},{1,0},{2,3},{3,2},{4,5},{5,4},{6,7},{7,6},{8,9},{9,8},{10,11... | collective-permute-start | bytes 1179656 | tf_op jit(solution)/shard_map/ppermute | solution.py:21
  52.4 6.7 %collective-permute-start.16 = (bf16[512,384]{1,0:T(8,128)(2,1)S(1)}, bf16[512,384]{1,0:T(8,128)(2,1)S(1)}, u32[]{:S(2)}, u32[]{:S(2)}) collective-permute-start(bf16[512,384]{1,0:T(8,128)(2,1)S(1)} %get-tuple-element.57), channel_id=1, source_target_pairs={{0,1},{1,0},{2,3},{3,2},{4,5},{5,4},{6,7},{7,6},{8,9},{9,8},{10,11... | collective-permute-start | bytes 1179656 | tf_op jit(solution)/shard_map/ppermute | solution.py:21
  52.4 7.9 %collective-permute-start.14 = (bf16[32,1152]{1,0:T(8,128)(2,1)S(1)}, bf16[32,1152]{1,0:T(8,128)(2,1)S(1)}, u32[]{:S(2)}, u32[]{:S(2)}) collective-permute-start(bf16[32,1152]{1,0:T(8,128)(2,1)S(1)} %get-tuple-element.53.refs_2_), channel_id=1, source_target_pairs={{0,16},{1,17},{2,18},{3,19},{4,20},{5,21},{6,22},{7,23},{8,24},{9,... | collective-permute-start | bytes 221192 | tf_op jit(solution)/shard_map/ppermute | solution.py:294
  55.1 5.3 %collective-permute-start.19 = (bf16[32,1152]{1,0:T(8,128)(2,1)S(1)}, bf16[32,1152]{1,0:T(8,128)(2,1)S(1)}, u32[]{:S(2)}, u32[]{:S(2)}) collective-permute-start(bf16[32,1152]{1,0:T(8,128)(2,1)S(1)} %get-tuple-element.61), channel_id=1, source_target_pairs={{0,8},{1,9},{2,10},{3,11},{4,12},{5,13},{6,14},{7,15},{8,0},{9,1},... | collective-permute-start | bytes 221192 | tf_op jit(solution)/shard_map/ppermute | solution.py:294
  56.7 6.4 %collective-permute-start.20 = (bf16[32,1152]{1,0:T(8,128)(2,1)S(1)}, bf16[32,1152]{1,0:T(8,128)(2,1)S(1)}, u32[]{:S(2)}, u32[]{:S(2)}) collective-permute-start(bf16[32,1152]{1,0:T(8,128)(2,1)S(1)} %get-tuple-element.59.refs_5_), channel_id=1, source_target_pairs={{0,24},{1,25},{2,26},{3,27},{4,28},{5,29},{6,30},{7,31},{8,16},{9,... | collective-permute-start | bytes 221192 | tf_op jit(solution)/shard_map/ppermute | solution.py:294
  59.1 3.9 %copy-start = (s32[32,8]{0,1:T(8,128)S(1)}, s32[32,8]{0,1:T(8,128)}, u32[]{:S(2)}) copy-start(s32[32,8]{0,1:T(8,128)} %param.9) | copy-start | bytes 3076

commit v12 on v11

--- a/solution.py
+++ b/solution.py
@@ -361,8 +361,8 @@
         shape = (kept.shape[0] // 2, columns)
         return run(split_kernel, [(shape, t) for t in types], None, kept, got, flops=flops)
 
-    def collect(total, part):
-        return run(add_kernel, [(total.shape, F32)], None, total, part)[0]
+    def collect(total, part, flops=0):
+        return run(add_kernel, [(total.shape, F32)], None, total, part, flops=flops)[0]
 
     far_two = at_offset(block, 0)
     first_own = join(block, exchange(block, near_a))
@@ -394,11 +394,12 @@
         ],
         place, *saved, limit=10, flops=6 * 10**9,
     )
+    total, give = split(kept_0, got_0, (F32, BF16))
+    back_two = at_offset(give, 0)
     kept_1, give = split(kept_1, got_1, (F32, BF16))
     got_1 = exchange(give, near_a)
-    total, give = split(kept_0, got_0, (F32, BF16))
-    back_two = at_offset(give, 0)
     gots = [swap_core(give) for give in gives]
+    total = collect(total, back_two, flops=6 * 10**9)
     give_one, give_both = split(kept_1, got_1, (BF16, BF16), flops=6 * 10**9)
     back_one, back_both = at_offset(give_one, 1), at_offset(give_both, 2)
     grad_gate, grad_up, grad_down, _ = run(
@@ -406,7 +407,6 @@
         [((half, width), BF16), ((half, width), BF16), ((width, half), BF16), ((8, 128), F32)],
         None, keep_in, keep_down, *gots, leaves=3, limit=6,
     )
-    total = collect(total, back_two)
     total = collect(total, back_one)
 
     parts = (total, back_both)

time: 64.6 us -> 68.4 us (1.059)
  waiting for transfers between devices: 22.3 us -> 28.1 us
  starting transfers between devices: 28.2 us -> 26.3 us
    ppermute x15, waiting for transfers between devices: 22.3 us -> 28 us  [exchange(): return lax.ppermute(x, DEVICES, pairs)]
    ppermute x15, starting transfers between devices: 27.2 us -> 25.3 us  [exchange(): return lax.ppermute(x, DEVICES, pairs)]
  transfers between devices with their start and end apart: 21 -> 21, of which waited for: 8 -> 10; matrix products, arithmetic and copies ran while one was open for 0% -> 0% of each run, Pallas kernels for 16% -> 16%
where the time goes in v12:
time: 68.4 us; the launch traced here: 68.2 us
  waiting for transfers between devices  28.1 us (41%)
  starting transfers between devices  26.3 us (38%)
  Pallas kernels  12.9 us (19%)
  between operations  0.85 us (1%)
    ppermute x15, waiting for transfers between devices, exchange(): return lax.ppermute(x, DEVICES, pairs)  28 us
    ppermute x15, starting transfers between devices, exchange(): return lax.ppermute(x, DEVICES, pairs)  25.3 us
    pallas_call x21, Pallas kernels, call(): pl.pallas_call(run, out_shape=out_shape, in_specs=[pl.BlockSpec(memory_sp...  12 us
  transfers between devices with their start and end apart: 21, of which 10 were waited for; matrix products, arithmetic and copies ran while one was open for 0% of the time, Pallas kernels for 16%

profile of v12, /device:TPU:0, one launch (start us, length us, event | category | flops | bytes accessed | tf_op | source)
XLA Modules:
  0.0 68.2 jit_solution(1852702325361796317)
XLA Ops:
  0.6 0.9 %prepare_kernel.1.refs_0_ = bf16[32,2176]{1,0:T(8,128)(2,1)S(1)} custom-call(bf16[32,1024]{1,0:T(8,128)(2,1)} %tokens.1, bf16[32,1024]{1,0:T(8,128)(2,1)} %cotangent.1, s32[8,32]{1,0:T(8,128)} %bitcast.11, bf16[8,32]{1,0:T(8,128)(2,1)} %bitcast.28), custom_call_target="tpu_custom_call" | custom-call | tf_op jit(solution)/shard_map/prepare_kernel/pallas_call | solution.py:309
  1.6 3.0 %collective-permute-start = (bf16[32,2176]{1,0:T(8,128)(2,1)S(1)}, bf16[32,2176]{1,0:T(8,128)(2,1)S(1)}, u32[]{:S(2)}, u32[]{:S(2)}) collective-permute-start(bf16[32,2176]{1,0:T(8,128)(2,1)S(1)} %prepare_kernel.1.refs_0_), channel_id=1, source_target_pairs={{0,2},{1,5},{2,0},{3,7},{4,6},{5,1},{6,4},{7,3},{8,10},{9,13},{10,... | collective-permute-start | bytes 417800 | tf_op jit(solution)/shard_map/ppermute | solution.py:294
  4.6 2.6 %collective-permute-start.1 = (bf16[32,2176]{1,0:T(8,128)(2,1)S(1)}, bf16[32,2176]{1,0:T(8,128)(2,1)S(1)}, u32[]{:S(2)}, u32[]{:S(2)}) collective-permute-start(bf16[32,2176]{1,0:T(8,128)(2,1)S(1)} %prepare_kernel.1.refs_0_), channel_id=1, source_target_pairs={{0,16},{1,17},{2,18},{3,19},{4,20},{5,21},{6,22},{7,23},{8,24},{9,... | collective-permute-start | bytes 417800 | tf_op jit(solution)/shard_map/ppermute | solution.py:294
  7.2 0.5 collective-permute-start.5
  7.7 2.0 %collective-permute-start.3 = (bf16[64,2176]{1,0:T(8,128)(2,1)S(1)}, bf16[64,2176]{1,0:T(8,128)(2,1)S(1)}, u32[]{:S(2)}, u32[]{:S(2)}) collective-permute-start(bf16[64,2176]{1,0:T(8,128)(2,1)S(1)} %join_kernel.4.refs_2_.refs_1_), channel_id=1, source_target_pairs={{0,4},{1,3},{2,6},{3,1},{4,0},{5,7},{6,2},{7,5},{8,12},{9,11},{10,... | collective-permute-start | bytes 835592 | tf_op jit(solution)/shard_map/ppermute | solution.py:294
  9.8 3.9 %collective-permute-done.1.refs_1_.refs_0_ = bf16[32,2176]{1,0:T(8,128)(2,1)S(1)} collective-permute-done((bf16[32,2176]{1,0:T(8,128)(2,1)S(1)}, bf16[32,2176]{1,0:T(8,128)(2,1)S(1)}, u32[]{:S(2)}, u32[]{:S(2)}) %collective-permute-start.1) | collective-permute-done | bytes 139296 | tf_op jit(solution)/shard_map/ppermute | solution.py:294
  13.7 0.7 %collective-permute-start.7 = (bf16[64,2176]{1,0:T(8,128)(2,1)S(1)}, bf16[64,2176]{1,0:T(8,128)(2,1)S(1)}, u32[]{:S(2)}, u32[]{:S(2)}) collective-permute-start(bf16[64,2176]{1,0:T(8,128)(2,1)S(1)} %join_kernel.5.refs_1_), channel_id=1, source_target_pairs={{0,8},{1,9},{2,10},{3,11},{4,12},{5,13},{6,14},{7,15},{8,0},{9,1},... | collective-permute-start | bytes 835592 | tf_op jit(solution)/shard_map/ppermute | solution.py:294
  14.4 1.9 %collective-permute-start.2 = (bf16[32,2176]{1,0:T(8,128)(2,1)S(1)}, bf16[32,2176]{1,0:T(8,128)(2,1)S(1)}, u32[]{:S(2)}, u32[]{:S(2)}) collective-permute-start(bf16[32,2176]{1,0:T(8,128)(2,1)S(1)} %collective-permute-done.1.refs_1_.refs_0_), channel_id=1, source_target_pairs={{0,2},{1,5},{2,0},{3,7},{4,6},{5,1},{6,4},{7,3},{8,10},{9,13},{10,... | collective-permute-start | bytes 417800 | tf_op jit(solution)/shard_map/ppermute | solution.py:294
  16.4 3.0 %collective-permute-done.2.refs_1_ = bf16[32,2176]{1,0:T(8,128)(2,1)S(1)} collective-permute-done((bf16[32,2176]{1,0:T(8,128)(2,1)S(1)}, bf16[32,2176]{1,0:T(8,128)(2,1)S(1)}, u32[]{:S(2)}, u32[]{:S(2)}) %collective-permute-start.2) | collective-permute-done | bytes 139296 | tf_op jit(solution)/shard_map/ppermute | solution.py:294
  19.5 2.0 %collective-permute-start.8 = (bf16[64,2176]{1,0:T(8,128)(2,1)S(1)}, bf16[64,2176]{1,0:T(8,128)(2,1)S(1)}, u32[]{:S(2)}, u32[]{:S(2)}) collective-permute-start(bf16[64,2176]{1,0:T(8,128)(2,1)S(1)} %join_kernel.6.refs_1_.refs_2_), channel_id=1, source_target_pairs={{0,4},{1,3},{2,6},{3,1},{4,0},{5,7},{6,2},{7,5},{8,12},{9,11},{10,... | collective-permute-start | bytes 835592 | tf_op jit(solution)/shard_map/ppermute | solution.py:294
  21.5 2.4 %collective-permute-start.9 = (bf16[64,2176]{1,0:T(8,128)(2,1)S(1)}, bf16[64,2176]{1,0:T(8,128)(2,1)S(1)}, u32[]{:S(2)}, u32[]{:S(2)}) collective-permute-start(bf16[64,2176]{1,0:T(8,128)(2,1)S(1)} %pass_kernel.5.refs_1_.refs_0_), channel_id=1, source_target_pairs={{0,2},{1,5},{2,0},{3,7},{4,6},{5,1},{6,4},{7,3},{8,10},{9,13},{10,... | collective-permute-start | bytes 835592 | tf_op jit(solution)/shard_map/ppermute | solution.py:294
  24.0 1.7 %expert_kernel.4 = (bf16[128,1152]{1,0:T(8,128)(2,1)S(1)}, bf16[2,64,768]{2,1,0:T(8,128)(2,1)S(1)}, bf16[2,64,384]{2,1,0:T(8,128)(2,1)S(1)}) custom-call(s32[2]{0:T(128)S(1)} %pad_add_fusion.refs_0_, bf16[64,2176]{1,0:T(8,128)(2,1)S(1)} %join_kernel.4.refs_2_.refs_1_, bf16[64,2176]{1,0:T(8,128)(2,1)S(1)} %join_kernel.6.refs_1_.refs_2_, ...), custom_call_target="tpu_custom_call" | custom-call | flops 6000000000 | tf_op jit(solution)/shard_map/expert_kernel/pallas_call | solution.py:253
  25.7 2.7 %collective-permute-done.9.refs_1_ = bf16[64,2176]{1,0:T(8,128)(2,1)S(1)} collective-permute-done((bf16[64,2176]{1,0:T(8,128)(2,1)S(1)}, bf16[64,2176]{1,0:T(8,128)(2,1)S(1)}, u32[]{:S(2)}, u32[]{:S(2)}) %collective-permute-start.9) | collective-permute-done | bytes 278560 | tf_op jit(solution)/shard_map/ppermute | solution.py:294
  28.5 1.7 %expert_kernel.5 = (bf16[128,1152]{1,0:T(8,128)(2,1)S(1)}, bf16[2,64,768]{2,1,0:T(8,128)(2,1)S(1)}, bf16[2,64,384]{2,1,0:T(8,128)(2,1)S(1)}) custom-call(s32[2]{0:T(128)S(1)} %pad_add_fusion.refs_0_, bf16[64,2176]{1,0:T(8,128)(2,1)S(1)} %pass_kernel.4.refs_2_.refs_1_.refs_5_, bf16[64,2176]{1,0:T(8,128)(2,1)S(1)} %collective-permute-done.8.refs_2_.refs_6_, ...), custom_call_target="tpu_custom_call" | custom-call | flops 6000000000 | tf_op jit(solution)/shard_map/expert_kernel/pallas_call | solution.py:253
  30.3 1.8 %expert_kernel.6 = (bf16[128,1152]{1,0:T(8,128)(2,1)S(1)}, bf16[1,128,768]{2,1,0:T(8,128)(2,1)S(1)}, bf16[1,128,384]{2,1,0:T(8,128)(2,1)S(1)}) custom-call(s32[2]{0:T(128)S(1)} %pad_add_fusion.refs_0_, bf16[128,2176]{1,0:T(8,128)(2,1)S(1)} %join_kernel.7.refs_9_.refs_1_, bf16[512,384]{1,0:T(8,128)(2,1)S(1)} %bitcast.16, ...), custom_call_target="tpu_custom_call" | custom-call | flops 6000000000 | tf_op jit(solution)/shard_map/expert_kernel/pallas_call | solution.py:253
  32.1 6.0 %collective-permute-done.10.refs_2_.refs_1_.refs_12_ = bf16[128,2176]{1,0:T(8,128)(2,1)S(1)} collective-permute-done((bf16[128,2176]{1,0:T(8,128)(2,1)S(1)}, bf16[128,2176]{1,0:T(8,128)(2,1)S(1)}, u32[]{:S(2)}, u32[]{:S(2)}) %collective-permute-start.10) | collective-permute-done | bytes 557088 | tf_op jit(solution)/shard_map/ppermute | solution.py:294
  38.1 1.8 %expert_kernel.7 = (bf16[128,1152]{1,0:T(8,128)(2,1)S(1)}, bf16[1,128,768]{2,1,0:T(8,128)(2,1)S(1)}, bf16[1,128,384]{2,1,0:T(8,128)(2,1)S(1)}) custom-call(s32[2]{0:T(128)S(1)} %pad_add_fusion.refs_0_, bf16[128,2176]{1,0:T(8,128)(2,1)S(1)} %collective-permute-done.10.refs_2_.refs_1_.refs_12_, bf16[512,384]{1,0:T(8,128)(2,1)S(1)} %bitcast.17, ...), custom_call_target="tpu_custom_call" | custom-call | flops 6000000000 | tf_op jit(solution)/shard_map/expert_kernel/pallas_call | solution.py:253
  39.9 2.1 %collective-permute-start.14 = (bf16[128,1152]{1,0:T(8,128)(2,1)S(1)}, bf16[128,1152]{1,0:T(8,128)(2,1)S(1)}, u32[]{:S(2)}, u32[]{:S(2)}) collective-permute-start(bf16[128,1152]{1,0:T(8,128)(2,1)S(1)} %get-tuple-element.52), channel_id=1, source_target_pairs={{0,4},{1,3},{2,6},{3,1},{4,0},{5,7},{6,2},{7,5},{8,12},{9,11},{10,... | collective-permute-start | bytes 884744 | tf_op jit(solution)/shard_map/ppermute | solution.py:294
  42.0 2.9 %collective-permute-done.11.refs_1_ = bf16[128,1152]{1,0:T(8,128)(2,1)S(1)} collective-permute-done((bf16[128,1152]{1,0:T(8,128)(2,1)S(1)}, bf16[128,1152]{1,0:T(8,128)(2,1)S(1)}, u32[]{:S(2)}, u32[]{:S(2)}) %collective-permute-start.11) | collective-permute-done | bytes 294944 | tf_op jit(solution)/shard_map/ppermute | solution.py:294
  44.9 2.1 %collective-permute-start.12 = (bf16[64,1152]{1,0:T(8,128)(2,1)S(1)}, bf16[64,1152]{1,0:T(8,128)(2,1)S(1)}, u32[]{:S(2)}, u32[]{:S(2)}) collective-permute-start(bf16[64,1152]{1,0:T(8,128)(2,1)S(1)} %get-tuple-element.43.refs_15_), channel_id=1, source_target_pairs={{0,2},{1,5},{2,0},{3,7},{4,6},{5,1},{6,4},{7,3},{8,10},{9,13},{10,... | collective-permute-start | bytes 442376 | tf_op jit(solution)/shard_map/ppermute | solution.py:294
  47.0 2.0 %weight_kernel.1 = (f32[512,768]{1,0:T(8,128)S(1)}, f32[384,512]{1,0:T(8,128)S(1)}, bf16[512,384]{1,0:T(8,128)(2,1)S(1)}, bf16[512,384]{1,0:T(8,128)(2,1)S(1)}, bf16[384,512]{1,0:T(8,128)(2,1)S(1)}) custom-call(s32[2]{0:T(128)S(1)} %pad_add_fusion.refs_0_, bf16[64,2176]{1,0:T(8,128)(2,1)S(1)} %join_kernel.4.refs_2_.refs_1_, ...), custom_call_target="tpu_custom_call" | custom-call | flops 6000000000 | tf_op jit(solution)/shard_map/weight_kernel/pallas_call | solution.py:253
  49.0 1.1 %collective-permute-done.12.refs_1_ = bf16[64,1152]{1,0:T(8,128)(2,1)S(1)} collective-permute-done((bf16[64,1152]{1,0:T(8,128)(2,1)S(1)}, bf16[64,1152]{1,0:T(8,128)(2,1)S(1)}, u32[]{:S(2)}, u32[]{:S(2)}) %collective-permute-start.12) | collective-permute-done | bytes 147488 | tf_op jit(solution)/shard_map/ppermute | solution.py:294
  50.2 2.9 %collective-permute-start.13 = (bf16[32,1152]{1,0:T(8,128)(2,1)S(1)}, bf16[32,1152]{1,0:T(8,128)(2,1)S(1)}, u32[]{:S(2)}, u32[]{:S(2)}) collective-permute-start(bf16[32,1152]{1,0:T(8,128)(2,1)S(1)} %get-tuple-element.50.refs_2_), channel_id=1, source_target_pairs={{0,16},{1,17},{2,18},{3,19},{4,20},{5,21},{6,22},{7,23},{8,24},{9,... | collective-permute-start | bytes 221192 | tf_op jit(solution)/shard_map/ppermute | solution.py:294
  53.1 0.5 collective-permute-start.17
  53.7 1.6 %collective-permute-start.15 = (bf16[64,1152]{1,0:T(8,128)(2,1)S(1)}, bf16[64,1152]{1,0:T(8,128)(2,1)S(1)}, u32[]{:S(2)}, u32[]{:S(2)}) collective-permute-start(bf16[64,1152]{1,0:T(8,128)(2,1)S(1)} %get-tuple-element.53.refs_2_), channel_id=1, source_target_pairs={{0,2},{1,5},{2,0},{3,7},{4,6},{5,1},{6,4},{7,3},{8,10},{9,13},{10,... | collective-permute-start | bytes 442376 | tf_op jit(solution)/shard_map/ppermute | solution.py:294
  55.3 1.7 %collective-permute-done.13.refs_1_ = bf16[32,1152]{1,0:T(8,128)(2,1)S(1)} collective-permute-done((bf16[32,1152]{1,0:T(8,128)(2,1)S(1)}, bf16[32,1152]{1,0:T(8,128)(2,1)S(1)}, u32[]{:S(2)}, u32[]{:S(2)}) %collective-permute-start.13) | collective-permute-done | bytes 73760 | tf_op jit(solution)/shard_map/ppermute | solution.py:294
  57.0 1.8 %collective-permute-done.15.refs_1_ = bf16[64,1152]{1,0:T(8,128)(2,1)S(1)} collective-permute-done((bf16[64,1152]{1,0:T(8,128)(2,1)S(1)}, bf16[64,1152]{1,0:T(8,128)(2,1)S(1)}, u32[]{:S(2)}, u32[]{:S(2)}) %collective-permute-start.15) | collective-permute-done | bytes 147488 | tf_op jit(solution)/shard_map/ppermute | solution.py:294
  58.9 1.8 %collective-permute-start.16 = (bf16[32,1152]{1,0:T(8,128)(2,1)S(1)}, bf16[32,1152]{1,0:T(8,128)(2,1)S(1)}, u32[]{:S(2)}, u32[]{:S(2)}) collective-permute-start(bf16[32,1152]{1,0:T(8,128)(2,1)S(1)} %get-tuple-element.55), channel_id=1, source_target_pairs={{0,8},{1,9},{2,10},{3,11},{4,12},{5,13},{6,14},{7,15},{8,0},{9,1},... | collective-permute-start | bytes 221192 | tf_op jit(solution)/shard_map/ppermute | solution.py:294
  60.7 1.2 %settle_kernel.1 = (bf16[512,384]{1,0:T(8,128)(2,1)}, bf16[512,384]{1,0:T(8,128)(2,1)}, bf16[384,512]{1,0:T(8,128)(2,1)}, f32[8,128]{1,0:T(8,128)S(1)}) custom-call(f32[512,768]{1,0:T(8,128)S(1)} %get-tuple-element.56.refs_0_, f32[384,512]{1,0:T(8,128)S(1)} %get-tuple-element.57.refs_1_, bf16[512,384]{1,0:T(8,128)(2,1)S(1)} %collective-permute-done.17.refs_2_, ...), custom_call_target="tpu_custom_call" | custom-call | tf_op jit(solution)/shard_map/settle_kernel/pallas_call | solution.py:253
  61.9 1.4 %collective-permute-done.16.refs_1_ = bf16[32,1152]{1,0:T(8,128)(2,1)S(1)} collective-permute-done((bf16[32,1152]{1,0:T(8,128)(2,1)S(1)}, bf16[32,1152]{1,0:T(8,128)(2,1)S(1)}, u32[]{:S(2)}, u32[]{:S(2)}) %collective-permute-start.16) | collective-permute-done | bytes 73760 | tf_op jit(solution)/shard_map/ppermute | solution.py:294
  63.3 3.5 %collective-permute-done.20.refs_2_ = bf16[32,1152]{1,0:T(8,128)(2,1)S(1)} collective-permute-done((bf16[32,1152]{1,0:T(8,128)(2,1)S(1)}, bf16[32,1152]{1,0:T(8,128)(2,1)S(1)}, u32[]{:S(2)}, u32[]{:S(2)}) %collective-permute-start.20) | collective-permute-done | bytes 73760 | tf_op jit(solution)/shard_map/ppermute | solution.py:294
  66.9 1.4 %finish_kernel.1 = (bf16[32,1024]{1,0:T(8,128)(2,1)}, bf16[8,32]{1,0:T(8,128)(2,1)}) custom-call(s32[2]{0:T(128)S(1)} %pad_add_fusion.refs_0_, f32[32,1152]{1,0:T(8,128)S(1)} %add_kernel.3.refs_1_.refs_4_, bf16[32,1152]{1,0:T(8,128)(2,1)S(1)} %collective-permute-done.20.refs_2_, s32[8,32]{1,0:T(8,128)S(1)} %bitcast.12, f32[32,1152]{1,0:T(8,128)S(1)} %add_kernel.3.refs_1_.refs_4_), custom_call_target="tpu_custom_call" | custom-call | tf_op jit(solution)/shard_map/finish_kernel/pallas_call | solution.py:253
  (41 shorter events, 0.7 us)
Async XLA Ops:
  1.6 6.1 %collective-permute-start = (bf16[32,2176]{1,0:T(8,128)(2,1)S(1)}, bf16[32,2176]{1,0:T(8,128)(2,1)S(1)}, u32[]{:S(2)}, u32[]{:S(2)}) collective-permute-start(bf16[32,2176]{1,0:T(8,128)(2,1)S(1)} %prepare_kernel.1.refs_0_), channel_id=1, source_target_pairs={{0,2},{1,5},{2,0},{3,7},{4,6},{5,1},{6,4},{7,3},{8,10},{9,13},{10,... | collective-permute-start | bytes 417800 | tf_op jit(solution)/shard_map/ppermute | solution.py:294
  4.6 9.0 %collective-permute-start.1 = (bf16[32,2176]{1,0:T(8,128)(2,1)S(1)}, bf16[32,2176]{1,0:T(8,128)(2,1)S(1)}, u32[]{:S(2)}, u32[]{:S(2)}) collective-permute-start(bf16[32,2176]{1,0:T(8,128)(2,1)S(1)} %prepare_kernel.1.refs_0_), channel_id=1, source_target_pairs={{0,16},{1,17},{2,18},{3,19},{4,20},{5,21},{6,22},{7,23},{8,24},{9,... | collective-permute-start | bytes 417800 | tf_op jit(solution)/shard_map/ppermute | solution.py:294
  7.2 16.7 %collective-permute-start.4 = (bf16[512,384]{1,0:T(8,128)(2,1)}, bf16[512,384]{1,0:T(8,128)(2,1)S(1)}, u32[]{:S(2)}, u32[]{:S(2)}) collective-permute-start(bf16[512,384]{1,0:T(8,128)(2,1)} %bitcast.13), channel_id=1, source_target_pairs={{0,1},{1,0},{2,3},{3,2},{4,5},{5,4},{6,7},{7,6},{8,9},{9,8},{10,11... | collective-permute-start | bytes 1179656 | tf_op jit(solution)/shard_map/ppermute | solution.py:21
  7.2 16.7 %collective-permute-start.5 = (bf16[512,384]{1,0:T(8,128)(2,1)}, bf16[512,384]{1,0:T(8,128)(2,1)S(1)}, u32[]{:S(2)}, u32[]{:S(2)}) collective-permute-start(bf16[512,384]{1,0:T(8,128)(2,1)} %bitcast.18), channel_id=1, source_target_pairs={{0,1},{1,0},{2,3},{3,2},{4,5},{5,4},{6,7},{7,6},{8,9},{9,8},{10,11... | collective-permute-start | bytes 1179656 | tf_op jit(solution)/shard_map/ppermute | solution.py:21
  7.7 16.2 %collective-permute-start.6 = (bf16[384,512]{1,0:T(8,128)(2,1)}, bf16[384,512]{1,0:T(8,128)(2,1)S(1)}, u32[]{:S(2)}, u32[]{:S(2)}) collective-permute-start(bf16[384,512]{1,0:T(8,128)(2,1)} %bitcast.23), channel_id=1, source_target_pairs={{0,1},{1,0},{2,3},{3,2},{4,5},{5,4},{6,7},{7,6},{8,9},{9,8},{10,11... | collective-permute-start | bytes 1179656 | tf_op jit(solution)/shard_map/ppermute | solution.py:21
  7.7 6.7 %collective-permute-start.3 = (bf16[64,2176]{1,0:T(8,128)(2,1)S(1)}, bf16[64,2176]{1,0:T(8,128)(2,1)S(1)}, u32[]{:S(2)}, u32[]{:S(2)}) collective-permute-start(bf16[64,2176]{1,0:T(8,128)(2,1)S(1)} %join_kernel.4.refs_2_.refs_1_), channel_id=1, source_target_pairs={{0,4},{1,3},{2,6},{3,1},{4,0},{5,7},{6,2},{7,5},{8,12},{9,11},{10,... | collective-permute-start | bytes 835592 | tf_op jit(solution)/shard_map/ppermute | solution.py:294
  13.7 7.8 %collective-permute-start.7 = (bf16[64,2176]{1,0:T(8,128)(2,1)S(1)}, bf16[64,2176]{1,0:T(8,128)(2,1)S(1)}, u32[]{:S(2)}, u32[]{:S(2)}) collective-permute-start(bf16[64,2176]{1,0:T(8,128)(2,1)S(1)} %join_kernel.5.refs_1_), channel_id=1, source_target_pairs={{0,8},{1,9},{2,10},{3,11},{4,12},{5,13},{6,14},{7,15},{8,0},{9,1},... | collective-permute-start | bytes 835592 | tf_op jit(solution)/shard_map/ppermute | solution.py:294
  14.4 5.1 %collective-permute-start.2 = (bf16[32,2176]{1,0:T(8,128)(2,1)S(1)}, bf16[32,2176]{1,0:T(8,128)(2,1)S(1)}, u32[]{:S(2)}, u32[]{:S(2)}) collective-permute-start(bf16[32,2176]{1,0:T(8,128)(2,1)S(1)} %collective-permute-done.1.refs_1_.refs_0_), channel_id=1, source_target_pairs={{0,2},{1,5},{2,0},{3,7},{4,6},{5,1},{6,4},{7,3},{8,10},{9,13},{10,... | collective-permute-start | bytes 417800 | tf_op jit(solution)/shard_map/ppermute | solution.py:294
  16.4 7.6 %copy-start.1 = (bf16[1,512,384]{2,1,0:T(8,128)(2,1)S(1)}, bf16[1,512,384]{2,1,0:T(8,128)(2,1)}, u32[]{:S(2)}) copy-start(bf16[1,512,384]{2,1,0:T(8,128)(2,1)} %param.11) | copy-start | bytes 1179652
  16.4 7.6 %copy-start.2 = (bf16[1,512,384]{2,1,0:T(8,128)(2,1)S(1)}, bf16[1,512,384]{2,1,0:T(8,128)(2,1)}, u32[]{:S(2)}) copy-start(bf16[1,512,384]{2,1,0:T(8,128)(2,1)} %param.12) | copy-start | bytes 1179652
  16.4 7.6 %copy-start.3 = (bf16[1,384,512]{2,1,0:T(8,128)(2,1)S(1)}, bf16[1,384,512]{2,1,0:T(8,128)(2,1)}, u32[]{:S(2)}) copy-start(bf16[1,384,512]{2,1,0:T(8,128)(2,1)} %param.13) | copy-start | bytes 1179652
  19.5 9.1 %collective-permute-start.8 = (bf16[64,2176]{1,0:T(8,128)(2,1)S(1)}, bf16[64,2176]{1,0:T(8,128)(2,1)S(1)}, u32[]{:S(2)}, u32[]{:S(2)}) collective-permute-start(bf16[64,2176]{1,0:T(8,128)(2,1)S(1)} %join_kernel.6.refs_1_.refs_2_), channel_id=1, source_target_pairs={{0,4},{1,3},{2,6},{3,1},{4,0},{5,7},{6,2},{7,5},{8,12},{9,11},{10,... | collective-permute-start | bytes 835592 | tf_op jit(solution)/shard_map/ppermute | solution.py:294
  21.5 6.9 %collective-permute-start.9 = (bf16[64,2176]{1,0:T(8,128)(2,1)S(1)}, bf16[64,2176]{1,0:T(8,128)(2,1)S(1)}, u32[]{:S(2)}, u32[]{:S(2)}) collective-permute-start(bf16[64,2176]{1,0:T(8,128)(2,1)S(1)} %pass_kernel.5.refs_1_.refs_0_), channel_id=1, source_target_pairs={{0,2},{1,5},{2,0},{3,7},{4,6},{5,1},{6,4},{7,3},{8,10},{9,13},{10,... | collective-permute-start | bytes 835592 | tf_op jit(solution)/shard_map/ppermute | solution.py:294
  28.4 9.6 %collective-permute-start.10 = (bf16[128,2176]{1,0:T(8,128)(2,1)S(1)}, bf16[128,2176]{1,0:T(8,128)(2,1)S(1)}, u32[]{:S(2)}, u32[]{:S(2)}) collective-permute-start(bf16[128,2176]{1,0:T(8,128)(2,1)S(1)} %join_kernel.7.refs_9_.refs_1_), channel_id=1, source_target_pairs={{0,4},{1,3},{2,6},{3,1},{4,0},{5,7},{6,2},{7,5},{8,12},{9,11},{10,... | collective-permute-start | bytes 1671176 | tf_op jit(solution)/shard_map/ppermute | solution.py:294
  38.1 6.8 %collective-permute-start.11 = (bf16[128,1152]{1,0:T(8,128)(2,1)S(1)}, bf16[128,1152]{1,0:T(8,128)(2,1)S(1)}, u32[]{:S(2)}, u32[]{:S(2)}) collective-permute-start(bf16[128,1152]{1,0:T(8,128)(2,1)S(1)} %pass_kernel.7.refs_8_), channel_id=1, source_target_pairs={{0,4},{1,3},{2,6},{3,1},{4,0},{5,7},{6,2},{7,5},{8,12},{9,11},{10,... | collective-permute-start | bytes 884744 | tf_op jit(solution)/shard_map/ppermute | solution.py:294
  39.9 13.7 %collective-permute-start.14 = (bf16[128,1152]{1,0:T(8,128)(2,1)S(1)}, bf16[128,1152]{1,0:T(8,128)(2,1)S(1)}, u32[]{:S(2)}, u32[]{:S(2)}) collective-permute-start(bf16[128,1152]{1,0:T(8,128)(2,1)S(1)} %get-tuple-element.52), channel_id=1, source_target_pairs={{0,4},{1,3},{2,6},{3,1},{4,0},{5,7},{6,2},{7,5},{8,12},{9,11},{10,... | collective-permute-start | bytes 884744 | tf_op jit(solution)/shard_map/ppermute | solution.py:294
  44.9 5.2 %collective-permute-start.12 = (bf16[64,1152]{1,0:T(8,128)(2,1)S(1)}, bf16[64,1152]{1,0:T(8,128)(2,1)S(1)}, u32[]{:S(2)}, u32[]{:S(2)}) collective-permute-start(bf16[64,1152]{1,0:T(8,128)(2,1)S(1)} %get-tuple-element.43.refs_15_), channel_id=1, source_target_pairs={{0,2},{1,5},{2,0},{3,7},{4,6},{5,1},{6,4},{7,3},{8,10},{9,13},{10,... | collective-permute-start | bytes 442376 | tf_op jit(solution)/shard_map/ppermute | solution.py:294
  50.2 6.8 %collective-permute-start.13 = (bf16[32,1152]{1,0:T(8,128)(2,1)S(1)}, bf16[32,1152]{1,0:T(8,128)(2,1)S(1)}, u32[]{:S(2)}, u32[]{:S(2)}) collective-permute-start(bf16[32,1152]{1,0:T(8,128)(2,1)S(1)} %get-tuple-element.50.refs_2_), channel_id=1, source_target_pairs={{0,16},{1,17},{2,18},{3,19},{4,20},{5,21},{6,22},{7,23},{8,24},{9,... | collective-permute-start | bytes 221192 | tf_op jit(solution)/shard_map/ppermute | solution.py:294
  53.1 7.6 %collective-permute-start.19 = (bf16[384,512]{1,0:T(8,128)(2,1)S(1)}, bf16[384,512]{1,0:T(8,128)(2,1)S(1)}, u32[]{:S(2)}, u32[]{:S(2)}) collective-permute-start(bf16[384,512]{1,0:T(8,128)(2,1)S(1)} %get-tuple-element.48.refs_2_), channel_id=1, source_target_pairs={{0,1},{1,0},{2,3},{3,2},{4,5},{5,4},{6,7},{7,6},{8,9},{9,8},{10,11... | collective-permute-start | bytes 1179656 | tf_op jit(solution)/shard_map/ppermute | solution.py:21
  53.1 7.6 %collective-permute-start.17 = (bf16[512,384]{1,0:T(8,128)(2,1)S(1)}, bf16[512,384]{1,0:T(8,128)(2,1)S(1)}, u32[]{:S(2)}, u32[]{:S(2)}) collective-permute-start(bf16[512,384]{1,0:T(8,128)(2,1)S(1)} %get-tuple-element.58), channel_id=1, source_target_pairs={{0,1},{1,0},{2,3},{3,2},{4,5},{5,4},{6,7},{7,6},{8,9},{9,8},{10,11... | collective-permute-start | bytes 1179656 | tf_op jit(solution)/shard_map/ppermute | solution.py:21
  53.6 7.1 %collective-permute-start.18 = (bf16[512,384]{1,0:T(8,128)(2,1)S(1)}, bf16[512,384]{1,0:T(8,128)(2,1)S(1)}, u32[]{:S(2)}, u32[]{:S(2)}) collective-permute-start(bf16[512,384]{1,0:T(8,128)(2,1)S(1)} %get-tuple-element.59), channel_id=1, source_target_pairs={{0,1},{1,0},{2,3},{3,2},{4,5},{5,4},{6,7},{7,6},{8,9},{9,8},{10,11... | collective-permute-start | bytes 1179656 | tf_op jit(solution)/shard_map/ppermute | solution.py:21
  53.7 5.2 %collective-permute-start.15 = (bf16[64,1152]{1,0:T(8,128)(2,1)S(1)}, bf16[64,1152]{1,0:T(8,128)(2,1)S(1)}, u32[]{:S(2)}, u32[]{:S(2)}) collective-permute-start(bf16[64,1152]{1,0:T(8,128)(2,1)S(1)} %get-tuple-element.53.refs_2_), channel_id=1, source_target_pairs={{0,2},{1,5},{2,0},{3,7},{4,6},{5,1},{6,4},{7,3},{8,10},{9,13},{10,... | collective-permute-start | bytes 442376 | tf_op jit(solution)/shard_map/ppermute | solution.py:294
  58.9 4.4 %collective-permute-start.16 = (bf16[32,1152]{1,0:T(8,128)(2,1)S(1)}, bf16[32,1152]{1,0:T(8,128)(2,1)S(1)}, u32[]{:S(2)}, u32[]{:S(2)}) collective-permute-start(bf16[32,1152]{1,0:T(8,128)(2,1)S(1)} %get-tuple-element.55), channel_id=1, source_target_pairs={{0,8},{1,9},{2,10},{3,11},{4,12},{5,13},{6,14},{7,15},{8,0},{9,1},... | collective-permute-start | bytes 221192 | tf_op jit(solution)/shard_map/ppermute | solution.py:294
  60.7 6.2 %collective-permute-start.20 = (bf16[32,1152]{1,0:T(8,128)(2,1)S(1)}, bf16[32,1152]{1,0:T(8,128)(2,1)S(1)}, u32[]{:S(2)}, u32[]{:S(2)}) collective-permute-start(bf16[32,1152]{1,0:T(8,128)(2,1)S(1)} %get-tuple-element.60.refs_5_), channel_id=1, source_target_pairs={{0,24},{1,25},{2,26},{3,27},{4,28},{5,29},{6,30},{7,31},{8,16},{9,... | collective-permute-start | bytes 221192 | tf_op jit(solution)/shard_map/ppermute | solution.py:294
  60.7 6.1 %copy-start = (s32[32,8]{0,1:T(8,128)S(1)}, s32[32,8]{0,1:T(8,128)}, u32[]{:S(2)}) copy-start(s32[32,8]{0,1:T(8,128)} %param.9) | copy-start | bytes 3076

commit v13 on v11

--- a/solution.py
+++ b/solution.py
@@ -379,10 +379,8 @@
     second_1 = exchange(first_1, near_b)
     give_0 = expert(second_own, second_two)
     kept_1 = expert(first_1)
-    got_0 = exchange(after_all(give_0, second_1), near_b)
     got_1 = exchange(expert(second_1), near_b)
-    kept_0, give = split(kept_0, got_0, (F32, BF16))
-    got_0 = exchange(give, near_a)
+    got_0 = exchange(after_all(give_0), near_b)
     keep_in, keep_down, *gives = run(
         lambda *refs: weight_kernel(tuple(numbers), *refs),
         [
@@ -396,8 +394,8 @@
     )
     kept_1, give = split(kept_1, got_1, (F32, BF16))
     got_1 = exchange(give, near_a)
-    total, give = split(kept_0, got_0, (F32, BF16))
-    back_two = at_offset(give, 0)
+    kept_0, give = split(kept_0, got_0, (F32, BF16))
+    got_0 = exchange(give, near_a)
     gots = [swap_core(give) for give in gives]
     give_one, give_both = split(kept_1, got_1, (BF16, BF16), flops=6 * 10**9)
     back_one, back_both = at_offset(give_one, 1), at_offset(give_both, 2)
@@ -406,12 +404,14 @@
         [((half, width), BF16), ((half, width), BF16), ((width, half), BF16), ((8, 128), F32)],
         None, keep_in, keep_down, *gots, leaves=3, limit=6,
     )
-    total = collect(total, back_two)
+    total, give = split(kept_0, got_0, (F32, BF16))
+    back_two = at_offset(give, 0)
     total = collect(total, back_one)
-
-    parts = (total, back_both)
+    total = collect(total, back_both)
+
+    parts = (total, back_two)
     if far:
-        total = total + back_both.astype(F32)
+        total = total + back_two.astype(F32)
         for step in reversed(steps[:far]):
             middle = total.shape[0] // 2
             total = total[:middle] + exchange(total[middle:].astype(BF16), step).astype(F32)

time: 64.6 us -> 66.2 us (1.025)
  waiting for transfers between devices: 22.3 us -> 25.6 us
  starting transfers between devices: 28.2 us -> 26.6 us
    ppermute x15, waiting for transfers between devices: 22.3 us -> 25.6 us  [exchange(): return lax.ppermute(x, DEVICES, pairs)]
    ppermute x15, starting transfers between devices: 27.2 us -> 25.5 us  [exchange(): return lax.ppermute(x, DEVICES, pairs)]
  transfers between devices with their start and end apart: 21 -> 21, of which waited for: 8 -> 8; matrix products, arithmetic and copies ran while one was open for 0% -> 0% of each run, Pallas kernels for 16% -> 13%
where the time goes in v13:
time: 66.2 us; the launch traced here: 66 us
  starting transfers between devices  26.6 us (40%)
  waiting for transfers between devices  25.6 us (39%)
  Pallas kernels  12.9 us (19%)
  between operations  0.83 us (1%)
    ppermute x15, waiting for transfers between devices, exchange(): return lax.ppermute(x, DEVICES, pairs)  25.6 us
    ppermute x15, starting transfers between devices, exchange(): return lax.ppermute(x, DEVICES, pairs)  25.5 us
    pallas_call x21, Pallas kernels, call(): pl.pallas_call(run, out_shape=out_shape, in_specs=[pl.BlockSpec(memory_sp...  12 us
  transfers between devices with their start and end apart: 21, of which 8 were waited for; matrix products, arithmetic and copies ran while one was open for 0% of the time, Pallas kernels for 13%

profile of v13, /device:TPU:0, one launch (start us, length us, event | category | flops | bytes accessed | tf_op | source)
XLA Modules:
  0.0 66.0 jit_solution(11682269263904518283)
XLA Ops:
  0.6 0.9 %prepare_kernel.1.refs_0_ = bf16[32,2176]{1,0:T(8,128)(2,1)S(1)} custom-call(bf16[32,1024]{1,0:T(8,128)(2,1)} %tokens.1, bf16[32,1024]{1,0:T(8,128)(2,1)} %cotangent.1, s32[8,32]{1,0:T(8,128)} %bitcast.11, bf16[8,32]{1,0:T(8,128)(2,1)} %bitcast.28), custom_call_target="tpu_custom_call" | custom-call | tf_op jit(solution)/shard_map/prepare_kernel/pallas_call | solution.py:309
  1.6 3.0 %collective-permute-start = (bf16[32,2176]{1,0:T(8,128)(2,1)S(1)}, bf16[32,2176]{1,0:T(8,128)(2,1)S(1)}, u32[]{:S(2)}, u32[]{:S(2)}) collective-permute-start(bf16[32,2176]{1,0:T(8,128)(2,1)S(1)} %prepare_kernel.1.refs_0_), channel_id=1, source_target_pairs={{0,2},{1,5},{2,0},{3,7},{4,6},{5,1},{6,4},{7,3},{8,10},{9,13},{10,... | collective-permute-start | bytes 417800 | tf_op jit(solution)/shard_map/ppermute | solution.py:294
  4.6 2.6 %collective-permute-start.1 = (bf16[32,2176]{1,0:T(8,128)(2,1)S(1)}, bf16[32,2176]{1,0:T(8,128)(2,1)S(1)}, u32[]{:S(2)}, u32[]{:S(2)}) collective-permute-start(bf16[32,2176]{1,0:T(8,128)(2,1)S(1)} %prepare_kernel.1.refs_0_), channel_id=1, source_target_pairs={{0,16},{1,17},{2,18},{3,19},{4,20},{5,21},{6,22},{7,23},{8,24},{9,... | collective-permute-start | bytes 417800 | tf_op jit(solution)/shard_map/ppermute | solution.py:294
  7.2 0.5 collective-permute-start.4
  7.7 2.0 %collective-permute-start.3 = (bf16[64,2176]{1,0:T(8,128)(2,1)S(1)}, bf16[64,2176]{1,0:T(8,128)(2,1)S(1)}, u32[]{:S(2)}, u32[]{:S(2)}) collective-permute-start(bf16[64,2176]{1,0:T(8,128)(2,1)S(1)} %join_kernel.4.refs_2_.refs_1_), channel_id=1, source_target_pairs={{0,4},{1,3},{2,6},{3,1},{4,0},{5,7},{6,2},{7,5},{8,12},{9,11},{10,... | collective-permute-start | bytes 835592 | tf_op jit(solution)/shard_map/ppermute | solution.py:294
  9.8 3.9 %collective-permute-done.1.refs_1_.refs_0_ = bf16[32,2176]{1,0:T(8,128)(2,1)S(1)} collective-permute-done((bf16[32,2176]{1,0:T(8,128)(2,1)S(1)}, bf16[32,2176]{1,0:T(8,128)(2,1)S(1)}, u32[]{:S(2)}, u32[]{:S(2)}) %collective-permute-start.1) | collective-permute-done | bytes 139296 | tf_op jit(solution)/shard_map/ppermute | solution.py:294
  13.7 0.7 %collective-permute-start.7 = (bf16[64,2176]{1,0:T(8,128)(2,1)S(1)}, bf16[64,2176]{1,0:T(8,128)(2,1)S(1)}, u32[]{:S(2)}, u32[]{:S(2)}) collective-permute-start(bf16[64,2176]{1,0:T(8,128)(2,1)S(1)} %join_kernel.5.refs_1_), channel_id=1, source_target_pairs={{0,8},{1,9},{2,10},{3,11},{4,12},{5,13},{6,14},{7,15},{8,0},{9,1},... | collective-permute-start | bytes 835592 | tf_op jit(solution)/shard_map/ppermute | solution.py:294
  14.4 1.9 %collective-permute-start.2 = (bf16[32,2176]{1,0:T(8,128)(2,1)S(1)}, bf16[32,2176]{1,0:T(8,128)(2,1)S(1)}, u32[]{:S(2)}, u32[]{:S(2)}) collective-permute-start(bf16[32,2176]{1,0:T(8,128)(2,1)S(1)} %collective-permute-done.1.refs_1_.refs_0_), channel_id=1, source_target_pairs={{0,2},{1,5},{2,0},{3,7},{4,6},{5,1},{6,4},{7,3},{8,10},{9,13},{10,... | collective-permute-start | bytes 417800 | tf_op jit(solution)/shard_map/ppermute | solution.py:294
  16.4 3.0 %collective-permute-done.2.refs_1_ = bf16[32,2176]{1,0:T(8,128)(2,1)S(1)} collective-permute-done((bf16[32,2176]{1,0:T(8,128)(2,1)S(1)}, bf16[32,2176]{1,0:T(8,128)(2,1)S(1)}, u32[]{:S(2)}, u32[]{:S(2)}) %collective-permute-start.2) | collective-permute-done | bytes 139296 | tf_op jit(solution)/shard_map/ppermute | solution.py:294
  19.5 2.0 %collective-permute-start.8 = (bf16[64,2176]{1,0:T(8,128)(2,1)S(1)}, bf16[64,2176]{1,0:T(8,128)(2,1)S(1)}, u32[]{:S(2)}, u32[]{:S(2)}) collective-permute-start(bf16[64,2176]{1,0:T(8,128)(2,1)S(1)} %join_kernel.6.refs_1_.refs_2_), channel_id=1, source_target_pairs={{0,4},{1,3},{2,6},{3,1},{4,0},{5,7},{6,2},{7,5},{8,12},{9,11},{10,... | collective-permute-start | bytes 835592 | tf_op jit(solution)/shard_map/ppermute | solution.py:294
  21.5 2.4 %collective-permute-start.9 = (bf16[64,2176]{1,0:T(8,128)(2,1)S(1)}, bf16[64,2176]{1,0:T(8,128)(2,1)S(1)}, u32[]{:S(2)}, u32[]{:S(2)}) collective-permute-start(bf16[64,2176]{1,0:T(8,128)(2,1)S(1)} %pass_kernel.5.refs_1_.refs_0_), channel_id=1, source_target_pairs={{0,2},{1,5},{2,0},{3,7},{4,6},{5,1},{6,4},{7,3},{8,10},{9,13},{10,... | collective-permute-start | bytes 835592 | tf_op jit(solution)/shard_map/ppermute | solution.py:294
  24.0 1.8 %expert_kernel.4 = (bf16[128,1152]{1,0:T(8,128)(2,1)S(1)}, bf16[2,64,768]{2,1,0:T(8,128)(2,1)S(1)}, bf16[2,64,384]{2,1,0:T(8,128)(2,1)S(1)}) custom-call(s32[2]{0:T(128)S(1)} %pad_add_fusion.refs_0_, bf16[64,2176]{1,0:T(8,128)(2,1)S(1)} %join_kernel.4.refs_2_.refs_1_, bf16[64,2176]{1,0:T(8,128)(2,1)S(1)} %join_kernel.6.refs_1_.refs_2_, ...), custom_call_target="tpu_custom_call" | custom-call | flops 6000000000 | tf_op jit(solution)/shard_map/expert_kernel/pallas_call | solution.py:253
  25.7 2.7 %collective-permute-done.9.refs_1_ = bf16[64,2176]{1,0:T(8,128)(2,1)S(1)} collective-permute-done((bf16[64,2176]{1,0:T(8,128)(2,1)S(1)}, bf16[64,2176]{1,0:T(8,128)(2,1)S(1)}, u32[]{:S(2)}, u32[]{:S(2)}) %collective-permute-start.9) | collective-permute-done | bytes 278560 | tf_op jit(solution)/shard_map/ppermute | solution.py:294
  28.5 1.7 %expert_kernel.5 = (bf16[128,1152]{1,0:T(8,128)(2,1)S(1)}, bf16[2,64,768]{2,1,0:T(8,128)(2,1)S(1)}, bf16[2,64,384]{2,1,0:T(8,128)(2,1)S(1)}) custom-call(s32[2]{0:T(128)S(1)} %pad_add_fusion.refs_0_, bf16[64,2176]{1,0:T(8,128)(2,1)S(1)} %pass_kernel.4.refs_2_.refs_1_.refs_5_, bf16[64,2176]{1,0:T(8,128)(2,1)S(1)} %collective-permute-done.8.refs_2_.refs_6_, ...), custom_call_target="tpu_custom_call" | custom-call | flops 6000000000 | tf_op jit(solution)/shard_map/expert_kernel/pallas_call | solution.py:253
  30.3 1.8 %expert_kernel.6 = (bf16[128,1152]{1,0:T(8,128)(2,1)S(1)}, bf16[1,128,768]{2,1,0:T(8,128)(2,1)S(1)}, bf16[1,128,384]{2,1,0:T(8,128)(2,1)S(1)}) custom-call(s32[2]{0:T(128)S(1)} %pad_add_fusion.refs_0_, bf16[128,2176]{1,0:T(8,128)(2,1)S(1)} %join_kernel.7.refs_9_.refs_1_, bf16[512,384]{1,0:T(8,128)(2,1)S(1)} %bitcast.16, ...), custom_call_target="tpu_custom_call" | custom-call | flops 6000000000 | tf_op jit(solution)/shard_map/expert_kernel/pallas_call | solution.py:253
  32.1 6.0 %collective-permute-done.10.refs_1_.refs_12_ = bf16[128,2176]{1,0:T(8,128)(2,1)S(1)} collective-permute-done((bf16[128,2176]{1,0:T(8,128)(2,1)S(1)}, bf16[128,2176]{1,0:T(8,128)(2,1)S(1)}, u32[]{:S(2)}, u32[]{:S(2)}) %collective-permute-start.10) | collective-permute-done | bytes 557088 | tf_op jit(solution)/shard_map/ppermute | solution.py:294
  38.0 1.7 %expert_kernel.7 = (bf16[128,1152]{1,0:T(8,128)(2,1)S(1)}, bf16[1,128,768]{2,1,0:T(8,128)(2,1)S(1)}, bf16[1,128,384]{2,1,0:T(8,128)(2,1)S(1)}) custom-call(s32[2]{0:T(128)S(1)} %pad_add_fusion.refs_0_, bf16[128,2176]{1,0:T(8,128)(2,1)S(1)} %collective-permute-done.10.refs_1_.refs_12_, bf16[512,384]{1,0:T(8,128)(2,1)S(1)} %bitcast.17, ...), custom_call_target="tpu_custom_call" | custom-call | flops 6000000000 | tf_op jit(solution)/shard_map/expert_kernel/pallas_call | solution.py:253
  39.8 0.1 collective-permute-start.12
  39.9 2.1 %collective-permute-start.11 = (bf16[128,1152]{1,0:T(8,128)(2,1)S(1)}, bf16[128,1152]{1,0:T(8,128)(2,1)S(1)}, u32[]{:S(2)}, u32[]{:S(2)}) collective-permute-start(bf16[128,1152]{1,0:T(8,128)(2,1)S(1)} %pass_kernel.7.refs_15_), channel_id=1, source_target_pairs={{0,4},{1,3},{2,6},{3,1},{4,0},{5,7},{6,2},{7,5},{8,12},{9,11},{10,... | collective-permute-start | bytes 884744 | tf_op jit(solution)/shard_map/ppermute | solution.py:294
  42.0 2.0 %weight_kernel.1 = (f32[512,768]{1,0:T(8,128)S(1)}, f32[384,512]{1,0:T(8,128)S(1)}, bf16[512,384]{1,0:T(8,128)(2,1)S(1)}, bf16[512,384]{1,0:T(8,128)(2,1)S(1)}, bf16[384,512]{1,0:T(8,128)(2,1)S(1)}) custom-call(s32[2]{0:T(128)S(1)} %pad_add_fusion.refs_0_, bf16[64,2176]{1,0:T(8,128)(2,1)S(1)} %join_kernel.4.refs_2_.refs_1_, ...), custom_call_target="tpu_custom_call" | custom-call | flops 6000000000 | tf_op jit(solution)/shard_map/weight_kernel/pallas_call | solution.py:253
  44.0 2.6 %collective-permute-done.12.refs_1_ = bf16[128,1152]{1,0:T(8,128)(2,1)S(1)} collective-permute-done((bf16[128,1152]{1,0:T(8,128)(2,1)S(1)}, bf16[128,1152]{1,0:T(8,128)(2,1)S(1)}, u32[]{:S(2)}, u32[]{:S(2)}) %collective-permute-start.12) | collective-permute-done | bytes 294944 | tf_op jit(solution)/shard_map/ppermute | solution.py:294
  46.7 2.1 %collective-permute-start.17 = (bf16[64,1152]{1,0:T(8,128)(2,1)S(1)}, bf16[64,1152]{1,0:T(8,128)(2,1)S(1)}, u32[]{:S(2)}, u32[]{:S(2)}) collective-permute-start(bf16[64,1152]{1,0:T(8,128)(2,1)S(1)} %get-tuple-element.49.refs_2_), channel_id=1, source_target_pairs={{0,2},{1,5},{2,0},{3,7},{4,6},{5,1},{6,4},{7,3},{8,10},{9,13},{10,... | collective-permute-start | bytes 442376 | tf_op jit(solution)/shard_map/ppermute | solution.py:294
  48.7 0.5 collective-permute-start.14
  49.3 1.9 %collective-permute-done.11.refs_1_ = bf16[128,1152]{1,0:T(8,128)(2,1)S(1)} collective-permute-done((bf16[128,1152]{1,0:T(8,128)(2,1)S(1)}, bf16[128,1152]{1,0:T(8,128)(2,1)S(1)}, u32[]{:S(2)}, u32[]{:S(2)}) %collective-permute-start.11) | collective-permute-done | bytes 294944 | tf_op jit(solution)/shard_map/ppermute | solution.py:294
  51.3 2.4 %collective-permute-start.13 = (bf16[64,1152]{1,0:T(8,128)(2,1)S(1)}, bf16[64,1152]{1,0:T(8,128)(2,1)S(1)}, u32[]{:S(2)}, u32[]{:S(2)}) collective-permute-start(bf16[64,1152]{1,0:T(8,128)(2,1)S(1)} %get-tuple-element.51.refs_2_), channel_id=1, source_target_pairs={{0,2},{1,5},{2,0},{3,7},{4,6},{5,1},{6,4},{7,3},{8,10},{9,13},{10,... | collective-permute-start | bytes 442376 | tf_op jit(solution)/shard_map/ppermute | solution.py:294
  53.7 0.2 collective-permute-start.18
  53.8 3.5 %collective-permute-start.19 = (bf16[32,1152]{1,0:T(8,128)(2,1)S(1)}, bf16[32,1152]{1,0:T(8,128)(2,1)S(1)}, u32[]{:S(2)}, u32[]{:S(2)}) collective-permute-start(bf16[32,1152]{1,0:T(8,128)(2,1)S(1)} %get-tuple-element.57.refs_5_), channel_id=1, source_target_pairs={{0,24},{1,25},{2,26},{3,27},{4,28},{5,29},{6,30},{7,31},{8,16},{9,... | collective-permute-start | bytes 221192 | tf_op jit(solution)/shard_map/ppermute | solution.py:294
  57.3 1.2 %settle_kernel.1 = (bf16[512,384]{1,0:T(8,128)(2,1)}, bf16[512,384]{1,0:T(8,128)(2,1)}, bf16[384,512]{1,0:T(8,128)(2,1)}, f32[8,128]{1,0:T(8,128)S(1)}) custom-call(f32[512,768]{1,0:T(8,128)S(1)} %get-tuple-element.52.refs_0_, f32[384,512]{1,0:T(8,128)S(1)} %get-tuple-element.53.refs_1_, bf16[512,384]{1,0:T(8,128)(2,1)S(1)} %collective-permute-done.14.refs_2_, ...), custom_call_target="tpu_custom_call" | custom-call | tf_op jit(solution)/shard_map/settle_kernel/pallas_call | solution.py:253
  58.6 0.6 collective-permute-start.20
  59.2 1.3 %collective-permute-done.19.refs_1_ = bf16[32,1152]{1,0:T(8,128)(2,1)S(1)} collective-permute-done((bf16[32,1152]{1,0:T(8,128)(2,1)S(1)}, bf16[32,1152]{1,0:T(8,128)(2,1)S(1)}, u32[]{:S(2)}, u32[]{:S(2)}) %collective-permute-start.19) | collective-permute-done | bytes 73760 | tf_op jit(solution)/shard_map/ppermute | solution.py:294
  60.5 4.2 %collective-permute-done.20.refs_2_ = bf16[32,1152]{1,0:T(8,128)(2,1)S(1)} collective-permute-done((bf16[32,1152]{1,0:T(8,128)(2,1)S(1)}, bf16[32,1152]{1,0:T(8,128)(2,1)S(1)}, u32[]{:S(2)}, u32[]{:S(2)}) %collective-permute-start.20) | collective-permute-done | bytes 73760 | tf_op jit(solution)/shard_map/ppermute | solution.py:294
  64.7 1.4 %finish_kernel.1 = (bf16[32,1024]{1,0:T(8,128)(2,1)}, bf16[8,32]{1,0:T(8,128)(2,1)}) custom-call(s32[2]{0:T(128)S(1)} %pad_add_fusion.refs_0_, f32[32,1152]{1,0:T(8,128)S(1)} %add_kernel.3.refs_1_.refs_4_, bf16[32,1152]{1,0:T(8,128)(2,1)S(1)} %collective-permute-done.20.refs_2_, s32[8,32]{1,0:T(8,128)S(1)} %bitcast.12, f32[32,1152]{1,0:T(8,128)S(1)} %add_kernel.3.refs_1_.refs_4_), custom_call_target="tpu_custom_call" | custom-call | tf_op jit(solution)/shard_map/finish_kernel/pallas_call | solution.py:253
  (41 shorter events, 0.6 us)
Async XLA Ops:
  1.6 6.1 %collective-permute-start = (bf16[32,2176]{1,0:T(8,128)(2,1)S(1)}, bf16[32,2176]{1,0:T(8,128)(2,1)S(1)}, u32[]{:S(2)}, u32[]{:S(2)}) collective-permute-start(bf16[32,2176]{1,0:T(8,128)(2,1)S(1)} %prepare_kernel.1.refs_0_), channel_id=1, source_target_pairs={{0,2},{1,5},{2,0},{3,7},{4,6},{5,1},{6,4},{7,3},{8,10},{9,13},{10,... | collective-permute-start | bytes 417800 | tf_op jit(solution)/shard_map/ppermute | solution.py:294
  4.6 9.0 %collective-permute-start.1 = (bf16[32,2176]{1,0:T(8,128)(2,1)S(1)}, bf16[32,2176]{1,0:T(8,128)(2,1)S(1)}, u32[]{:S(2)}, u32[]{:S(2)}) collective-permute-start(bf16[32,2176]{1,0:T(8,128)(2,1)S(1)} %prepare_kernel.1.refs_0_), channel_id=1, source_target_pairs={{0,16},{1,17},{2,18},{3,19},{4,20},{5,21},{6,22},{7,23},{8,24},{9,... | collective-permute-start | bytes 417800 | tf_op jit(solution)/shard_map/ppermute | solution.py:294
  7.2 16.7 %collective-permute-start.6 = (bf16[384,512]{1,0:T(8,128)(2,1)}, bf16[384,512]{1,0:T(8,128)(2,1)S(1)}, u32[]{:S(2)}, u32[]{:S(2)}) collective-permute-start(bf16[384,512]{1,0:T(8,128)(2,1)} %bitcast.23), channel_id=1, source_target_pairs={{0,1},{1,0},{2,3},{3,2},{4,5},{5,4},{6,7},{7,6},{8,9},{9,8},{10,11... | collective-permute-start | bytes 1179656 | tf_op jit(solution)/shard_map/ppermute | solution.py:21
  7.2 16.7 %collective-permute-start.4 = (bf16[512,384]{1,0:T(8,128)(2,1)}, bf16[512,384]{1,0:T(8,128)(2,1)S(1)}, u32[]{:S(2)}, u32[]{:S(2)}) collective-permute-start(bf16[512,384]{1,0:T(8,128)(2,1)} %bitcast.13), channel_id=1, source_target_pairs={{0,1},{1,0},{2,3},{3,2},{4,5},{5,4},{6,7},{7,6},{8,9},{9,8},{10,11... | collective-permute-start | bytes 1179656 | tf_op jit(solution)/shard_map/ppermute | solution.py:21
  7.7 16.2 %collective-permute-start.5 = (bf16[512,384]{1,0:T(8,128)(2,1)}, bf16[512,384]{1,0:T(8,128)(2,1)S(1)}, u32[]{:S(2)}, u32[]{:S(2)}) collective-permute-start(bf16[512,384]{1,0:T(8,128)(2,1)} %bitcast.18), channel_id=1, source_target_pairs={{0,1},{1,0},{2,3},{3,2},{4,5},{5,4},{6,7},{7,6},{8,9},{9,8},{10,11... | collective-permute-start | bytes 1179656 | tf_op jit(solution)/shard_map/ppermute | solution.py:21
  7.7 6.7 %collective-permute-start.3 = (bf16[64,2176]{1,0:T(8,128)(2,1)S(1)}, bf16[64,2176]{1,0:T(8,128)(2,1)S(1)}, u32[]{:S(2)}, u32[]{:S(2)}) collective-permute-start(bf16[64,2176]{1,0:T(8,128)(2,1)S(1)} %join_kernel.4.refs_2_.refs_1_), channel_id=1, source_target_pairs={{0,4},{1,3},{2,6},{3,1},{4,0},{5,7},{6,2},{7,5},{8,12},{9,11},{10,... | collective-permute-start | bytes 835592 | tf_op jit(solution)/shard_map/ppermute | solution.py:294
  13.7 7.8 %collective-permute-start.7 = (bf16[64,2176]{1,0:T(8,128)(2,1)S(1)}, bf16[64,2176]{1,0:T(8,128)(2,1)S(1)}, u32[]{:S(2)}, u32[]{:S(2)}) collective-permute-start(bf16[64,2176]{1,0:T(8,128)(2,1)S(1)} %join_kernel.5.refs_1_), channel_id=1, source_target_pairs={{0,8},{1,9},{2,10},{3,11},{4,12},{5,13},{6,14},{7,15},{8,0},{9,1},... | collective-permute-start | bytes 835592 | tf_op jit(solution)/shard_map/ppermute | solution.py:294
  14.4 5.1 %collective-permute-start.2 = (bf16[32,2176]{1,0:T(8,128)(2,1)S(1)}, bf16[32,2176]{1,0:T(8,128)(2,1)S(1)}, u32[]{:S(2)}, u32[]{:S(2)}) collective-permute-start(bf16[32,2176]{1,0:T(8,128)(2,1)S(1)} %collective-permute-done.1.refs_1_.refs_0_), channel_id=1, source_target_pairs={{0,2},{1,5},{2,0},{3,7},{4,6},{5,1},{6,4},{7,3},{8,10},{9,13},{10,... | collective-permute-start | bytes 417800 | tf_op jit(solution)/shard_map/ppermute | solution.py:294
  16.4 7.6 %copy-start.1 = (bf16[1,512,384]{2,1,0:T(8,128)(2,1)S(1)}, bf16[1,512,384]{2,1,0:T(8,128)(2,1)}, u32[]{:S(2)}) copy-start(bf16[1,512,384]{2,1,0:T(8,128)(2,1)} %param.11) | copy-start | bytes 1179652
  16.4 7.6 %copy-start.2 = (bf16[1,512,384]{2,1,0:T(8,128)(2,1)S(1)}, bf16[1,512,384]{2,1,0:T(8,128)(2,1)}, u32[]{:S(2)}) copy-start(bf16[1,512,384]{2,1,0:T(8,128)(2,1)} %param.12) | copy-start | bytes 1179652
  16.4 7.6 %copy-start.3 = (bf16[1,384,512]{2,1,0:T(8,128)(2,1)S(1)}, bf16[1,384,512]{2,1,0:T(8,128)(2,1)}, u32[]{:S(2)}) copy-start(bf16[1,384,512]{2,1,0:T(8,128)(2,1)} %param.13) | copy-start | bytes 1179652
  19.5 9.1 %collective-permute-start.8 = (bf16[64,2176]{1,0:T(8,128)(2,1)S(1)}, bf16[64,2176]{1,0:T(8,128)(2,1)S(1)}, u32[]{:S(2)}, u32[]{:S(2)}) collective-permute-start(bf16[64,2176]{1,0:T(8,128)(2,1)S(1)} %join_kernel.6.refs_1_.refs_2_), channel_id=1, source_target_pairs={{0,4},{1,3},{2,6},{3,1},{4,0},{5,7},{6,2},{7,5},{8,12},{9,11},{10,... | collective-permute-start | bytes 835592 | tf_op jit(solution)/shard_map/ppermute | solution.py:294
  21.5 6.9 %collective-permute-start.9 = (bf16[64,2176]{1,0:T(8,128)(2,1)S(1)}, bf16[64,2176]{1,0:T(8,128)(2,1)S(1)}, u32[]{:S(2)}, u32[]{:S(2)}) collective-permute-start(bf16[64,2176]{1,0:T(8,128)(2,1)S(1)} %pass_kernel.5.refs_1_.refs_0_), channel_id=1, source_target_pairs={{0,2},{1,5},{2,0},{3,7},{4,6},{5,1},{6,4},{7,3},{8,10},{9,13},{10,... | collective-permute-start | bytes 835592 | tf_op jit(solution)/shard_map/ppermute | solution.py:294
  28.4 9.6 %collective-permute-start.10 = (bf16[128,2176]{1,0:T(8,128)(2,1)S(1)}, bf16[128,2176]{1,0:T(8,128)(2,1)S(1)}, u32[]{:S(2)}, u32[]{:S(2)}) collective-permute-start(bf16[128,2176]{1,0:T(8,128)(2,1)S(1)} %join_kernel.7.refs_9_.refs_1_), channel_id=1, source_target_pairs={{0,4},{1,3},{2,6},{3,1},{4,0},{5,7},{6,2},{7,5},{8,12},{9,11},{10,... | collective-permute-start | bytes 1671176 | tf_op jit(solution)/shard_map/ppermute | solution.py:294
  39.8 6.8 %collective-permute-start.12 = (bf16[128,1152]{1,0:T(8,128)(2,1)S(1)}, bf16[128,1152]{1,0:T(8,128)(2,1)S(1)}, u32[]{:S(2)}, u32[]{:S(2)}) collective-permute-start(bf16[128,1152]{1,0:T(8,128)(2,1)S(1)} %get-tuple-element.43), channel_id=1, source_target_pairs={{0,4},{1,3},{2,6},{3,1},{4,0},{5,7},{6,2},{7,5},{8,12},{9,11},{10,... | collective-permute-start | bytes 884744 | tf_op jit(solution)/shard_map/ppermute | solution.py:294
  39.9 11.3 %collective-permute-start.11 = (bf16[128,1152]{1,0:T(8,128)(2,1)S(1)}, bf16[128,1152]{1,0:T(8,128)(2,1)S(1)}, u32[]{:S(2)}, u32[]{:S(2)}) collective-permute-start(bf16[128,1152]{1,0:T(8,128)(2,1)S(1)} %pass_kernel.7.refs_15_), channel_id=1, source_target_pairs={{0,4},{1,3},{2,6},{3,1},{4,0},{5,7},{6,2},{7,5},{8,12},{9,11},{10,... | collective-permute-start | bytes 884744 | tf_op jit(solution)/shard_map/ppermute | solution.py:294
  46.7 7.0 %collective-permute-start.17 = (bf16[64,1152]{1,0:T(8,128)(2,1)S(1)}, bf16[64,1152]{1,0:T(8,128)(2,1)S(1)}, u32[]{:S(2)}, u32[]{:S(2)}) collective-permute-start(bf16[64,1152]{1,0:T(8,128)(2,1)S(1)} %get-tuple-element.49.refs_2_), channel_id=1, source_target_pairs={{0,2},{1,5},{2,0},{3,7},{4,6},{5,1},{6,4},{7,3},{8,10},{9,13},{10,... | collective-permute-start | bytes 442376 | tf_op jit(solution)/shard_map/ppermute | solution.py:294
  48.7 8.6 %collective-permute-start.16 = (bf16[384,512]{1,0:T(8,128)(2,1)S(1)}, bf16[384,512]{1,0:T(8,128)(2,1)S(1)}, u32[]{:S(2)}, u32[]{:S(2)}) collective-permute-start(bf16[384,512]{1,0:T(8,128)(2,1)S(1)} %get-tuple-element.48.refs_2_), channel_id=1, source_target_pairs={{0,1},{1,0},{2,3},{3,2},{4,5},{5,4},{6,7},{7,6},{8,9},{9,8},{10,11... | collective-permute-start | bytes 1179656 | tf_op jit(solution)/shard_map/ppermute | solution.py:21
  48.7 5.1 %collective-permute-start.14 = (bf16[512,384]{1,0:T(8,128)(2,1)S(1)}, bf16[512,384]{1,0:T(8,128)(2,1)S(1)}, u32[]{:S(2)}, u32[]{:S(2)}) collective-permute-start(bf16[512,384]{1,0:T(8,128)(2,1)S(1)} %get-tuple-element.54), channel_id=1, source_target_pairs={{0,1},{1,0},{2,3},{3,2},{4,5},{5,4},{6,7},{7,6},{8,9},{9,8},{10,11... | collective-permute-start | bytes 1179656 | tf_op jit(solution)/shard_map/ppermute | solution.py:21
  49.3 8.1 %collective-permute-start.15 = (bf16[512,384]{1,0:T(8,128)(2,1)S(1)}, bf16[512,384]{1,0:T(8,128)(2,1)S(1)}, u32[]{:S(2)}, u32[]{:S(2)}) collective-permute-start(bf16[512,384]{1,0:T(8,128)(2,1)S(1)} %get-tuple-element.55), channel_id=1, source_target_pairs={{0,1},{1,0},{2,3},{3,2},{4,5},{5,4},{6,7},{7,6},{8,9},{9,8},{10,11... | collective-permute-start | bytes 1179656 | tf_op jit(solution)/shard_map/ppermute | solution.py:21
  51.3 7.3 %collective-permute-start.13 = (bf16[64,1152]{1,0:T(8,128)(2,1)S(1)}, bf16[64,1152]{1,0:T(8,128)(2,1)S(1)}, u32[]{:S(2)}, u32[]{:S(2)}) collective-permute-start(bf16[64,1152]{1,0:T(8,128)(2,1)S(1)} %get-tuple-element.51.refs_2_), channel_id=1, source_target_pairs={{0,2},{1,5},{2,0},{3,7},{4,6},{5,1},{6,4},{7,3},{8,10},{9,13},{10,... | collective-permute-start | bytes 442376 | tf_op jit(solution)/shard_map/ppermute | solution.py:294
  53.7 5.5 %collective-permute-start.18 = (bf16[32,1152]{1,0:T(8,128)(2,1)S(1)}, bf16[32,1152]{1,0:T(8,128)(2,1)S(1)}, u32[]{:S(2)}, u32[]{:S(2)}) collective-permute-start(bf16[32,1152]{1,0:T(8,128)(2,1)S(1)} %get-tuple-element.60), channel_id=1, source_target_pairs={{0,8},{1,9},{2,10},{3,11},{4,12},{5,13},{6,14},{7,15},{8,0},{9,1},... | collective-permute-start | bytes 221192 | tf_op jit(solution)/shard_map/ppermute | solution.py:294
  53.8 6.6 %collective-permute-start.19 = (bf16[32,1152]{1,0:T(8,128)(2,1)S(1)}, bf16[32,1152]{1,0:T(8,128)(2,1)S(1)}, u32[]{:S(2)}, u32[]{:S(2)}) collective-permute-start(bf16[32,1152]{1,0:T(8,128)(2,1)S(1)} %get-tuple-element.57.refs_5_), channel_id=1, source_target_pairs={{0,24},{1,25},{2,26},{3,27},{4,28},{5,29},{6,30},{7,31},{8,16},{9,... | collective-permute-start | bytes 221192 | tf_op jit(solution)/shard_map/ppermute | solution.py:294
  57.3 7.4 %copy-start = (s32[32,8]{0,1:T(8,128)S(1)}, s32[32,8]{0,1:T(8,128)}, u32[]{:S(2)}) copy-start(s32[32,8]{0,1:T(8,128)} %param.9) | copy-start | bytes 3076
  58.6 6.1 %collective-permute-start.20 = (bf16[32,1152]{1,0:T(8,128)(2,1)S(1)}, bf16[32,1152]{1,0:T(8,128)(2,1)S(1)}, u32[]{:S(2)}, u32[]{:S(2)}) collective-permute-start(bf16[32,1152]{1,0:T(8,128)(2,1)S(1)} %get-tuple-element.61.refs_2_), channel_id=1, source_target_pairs={{0,16},{1,17},{2,18},{3,19},{4,20},{5,21},{6,22},{7,23},{8,24},{9,... | collective-permute-start | bytes 221192 | tf_op jit(solution)/shard_map/ppermute | solution.py:294

commit v14 on v11

--- a/solution.py
+++ b/solution.py
@@ -367,7 +367,7 @@
     far_two = at_offset(block, 0)
     first_own = join(block, exchange(block, near_a))
     second_own = exchange(first_own, near_b)
-    near_1 = at_offset(join(block, far_two, flops=4 * 10**9), 1)
+    near_1 = at_offset(join(block, far_two, flops=1 * 10**9), 1)
     second_own = after_all(second_own)
     first_two = join(far_two, exchange(far_two, near_a))
     second_two = exchange(first_two, near_b)

time: 64.6 us -> 64.6 us (level)
  transfers between devices with their start and end apart: 21 -> 21, of which waited for: 8 -> 9; matrix products, arithmetic and copies ran while one was open for 0% -> 0% of each run, Pallas kernels for 16% -> 16%
where the time goes in v14:
time: 64.6 us; the launch traced here: 64.4 us
  starting transfers between devices  28.3 us (44%)
  waiting for transfers between devices  22.3 us (35%)
  Pallas kernels  12.9 us (20%)
  between operations  0.85 us (1%)
    ppermute x15, starting transfers between devices, exchange(): return lax.ppermute(x, DEVICES, pairs)  27.2 us
    ppermute x15, waiting for transfers between devices, exchange(): return lax.ppermute(x, DEVICES, pairs)  22.3 us
    pallas_call x21, Pallas kernels, call(): pl.pallas_call(run, out_shape=out_shape, in_specs=[pl.BlockSpec(memory_sp...  12 us
  transfers between devices with their start and end apart: 21, of which 9 were waited for; matrix products, arithmetic and copies ran while one was open for 0% of the time, Pallas kernels for 16%

profile of v14, /device:TPU:0, one launch (start us, length us, event | category | flops | bytes accessed | tf_op | source)
XLA Modules:
  0.0 64.4 jit_solution(5575649654877349991)
XLA Ops:
  0.6 0.9 %prepare_kernel.1.refs_0_ = bf16[32,2176]{1,0:T(8,128)(2,1)S(1)} custom-call(bf16[32,1024]{1,0:T(8,128)(2,1)} %tokens.1, bf16[32,1024]{1,0:T(8,128)(2,1)} %cotangent.1, s32[8,32]{1,0:T(8,128)} %bitcast.11, bf16[8,32]{1,0:T(8,128)(2,1)} %bitcast.28), custom_call_target="tpu_custom_call" | custom-call | tf_op jit(solution)/shard_map/prepare_kernel/pallas_call | solution.py:309
  1.6 3.0 %collective-permute-start = (bf16[32,2176]{1,0:T(8,128)(2,1)S(1)}, bf16[32,2176]{1,0:T(8,128)(2,1)S(1)}, u32[]{:S(2)}, u32[]{:S(2)}) collective-permute-start(bf16[32,2176]{1,0:T(8,128)(2,1)S(1)} %prepare_kernel.1.refs_0_), channel_id=1, source_target_pairs={{0,2},{1,5},{2,0},{3,7},{4,6},{5,1},{6,4},{7,3},{8,10},{9,13},{10,... | collective-permute-start | bytes 417800 | tf_op jit(solution)/shard_map/ppermute | solution.py:294
  4.6 2.6 %collective-permute-start.1 = (bf16[32,2176]{1,0:T(8,128)(2,1)S(1)}, bf16[32,2176]{1,0:T(8,128)(2,1)S(1)}, u32[]{:S(2)}, u32[]{:S(2)}) collective-permute-start(bf16[32,2176]{1,0:T(8,128)(2,1)S(1)} %prepare_kernel.1.refs_0_), channel_id=1, source_target_pairs={{0,16},{1,17},{2,18},{3,19},{4,20},{5,21},{6,22},{7,23},{8,24},{9,... | collective-permute-start | bytes 417800 | tf_op jit(solution)/shard_map/ppermute | solution.py:294
  7.2 0.4 collective-permute-done.refs_1_
  7.6 2.1 %collective-permute-start.3 = (bf16[64,2176]{1,0:T(8,128)(2,1)S(1)}, bf16[64,2176]{1,0:T(8,128)(2,1)S(1)}, u32[]{:S(2)}, u32[]{:S(2)}) collective-permute-start(bf16[64,2176]{1,0:T(8,128)(2,1)S(1)} %join_kernel.4.refs_2_.refs_1_), channel_id=1, source_target_pairs={{0,4},{1,3},{2,6},{3,1},{4,0},{5,7},{6,2},{7,5},{8,12},{9,11},{10,... | collective-permute-start | bytes 835592 | tf_op jit(solution)/shard_map/ppermute | solution.py:294
  9.8 0.5 collective-permute-start.6
  10.3 3.4 %collective-permute-done.1.refs_1_.refs_0_ = bf16[32,2176]{1,0:T(8,128)(2,1)S(1)} collective-permute-done((bf16[32,2176]{1,0:T(8,128)(2,1)S(1)}, bf16[32,2176]{1,0:T(8,128)(2,1)S(1)}, u32[]{:S(2)}, u32[]{:S(2)}) %collective-permute-start.1) | collective-permute-done | bytes 139296 | tf_op jit(solution)/shard_map/ppermute | solution.py:294
  13.7 0.7 %collective-permute-start.7 = (bf16[64,2176]{1,0:T(8,128)(2,1)S(1)}, bf16[64,2176]{1,0:T(8,128)(2,1)S(1)}, u32[]{:S(2)}, u32[]{:S(2)}) collective-permute-start(bf16[64,2176]{1,0:T(8,128)(2,1)S(1)} %join_kernel.5.refs_1_), channel_id=1, source_target_pairs={{0,8},{1,9},{2,10},{3,11},{4,12},{5,13},{6,14},{7,15},{8,0},{9,1},... | collective-permute-start | bytes 835592 | tf_op jit(solution)/shard_map/ppermute | solution.py:294
  14.4 1.9 %collective-permute-start.2 = (bf16[32,2176]{1,0:T(8,128)(2,1)S(1)}, bf16[32,2176]{1,0:T(8,128)(2,1)S(1)}, u32[]{:S(2)}, u32[]{:S(2)}) collective-permute-start(bf16[32,2176]{1,0:T(8,128)(2,1)S(1)} %collective-permute-done.1.refs_1_.refs_0_), channel_id=1, source_target_pairs={{0,2},{1,5},{2,0},{3,7},{4,6},{5,1},{6,4},{7,3},{8,10},{9,13},{10,... | collective-permute-start | bytes 417800 | tf_op jit(solution)/shard_map/ppermute | solution.py:294
  16.4 3.0 %collective-permute-done.2.refs_1_ = bf16[32,2176]{1,0:T(8,128)(2,1)S(1)} collective-permute-done((bf16[32,2176]{1,0:T(8,128)(2,1)S(1)}, bf16[32,2176]{1,0:T(8,128)(2,1)S(1)}, u32[]{:S(2)}, u32[]{:S(2)}) %collective-permute-start.2) | collective-permute-done | bytes 139296 | tf_op jit(solution)/shard_map/ppermute | solution.py:294
  19.5 2.0 %collective-permute-start.8 = (bf16[64,2176]{1,0:T(8,128)(2,1)S(1)}, bf16[64,2176]{1,0:T(8,128)(2,1)S(1)}, u32[]{:S(2)}, u32[]{:S(2)}) collective-permute-start(bf16[64,2176]{1,0:T(8,128)(2,1)S(1)} %join_kernel.6.refs_1_.refs_2_), channel_id=1, source_target_pairs={{0,4},{1,3},{2,6},{3,1},{4,0},{5,7},{6,2},{7,5},{8,12},{9,11},{10,... | collective-permute-start | bytes 835592 | tf_op jit(solution)/shard_map/ppermute | solution.py:294
  21.5 2.4 %collective-permute-start.9 = (bf16[64,2176]{1,0:T(8,128)(2,1)S(1)}, bf16[64,2176]{1,0:T(8,128)(2,1)S(1)}, u32[]{:S(2)}, u32[]{:S(2)}) collective-permute-start(bf16[64,2176]{1,0:T(8,128)(2,1)S(1)} %pass_kernel.5.refs_1_.refs_0_), channel_id=1, source_target_pairs={{0,2},{1,5},{2,0},{3,7},{4,6},{5,1},{6,4},{7,3},{8,10},{9,13},{10,... | collective-permute-start | bytes 835592 | tf_op jit(solution)/shard_map/ppermute | solution.py:294
  24.0 1.7 %expert_kernel.4 = (bf16[128,1152]{1,0:T(8,128)(2,1)S(1)}, bf16[2,64,768]{2,1,0:T(8,128)(2,1)S(1)}, bf16[2,64,384]{2,1,0:T(8,128)(2,1)S(1)}) custom-call(s32[2]{0:T(128)S(1)} %pad_add_fusion.refs_0_, bf16[64,2176]{1,0:T(8,128)(2,1)S(1)} %join_kernel.4.refs_2_.refs_1_, bf16[64,2176]{1,0:T(8,128)(2,1)S(1)} %join_kernel.6.refs_1_.refs_2_, ...), custom_call_target="tpu_custom_call" | custom-call | flops 6000000000 | tf_op jit(solution)/shard_map/expert_kernel/pallas_call | solution.py:253
  25.7 2.7 %collective-permute-done.9.refs_1_ = bf16[64,2176]{1,0:T(8,128)(2,1)S(1)} collective-permute-done((bf16[64,2176]{1,0:T(8,128)(2,1)S(1)}, bf16[64,2176]{1,0:T(8,128)(2,1)S(1)}, u32[]{:S(2)}, u32[]{:S(2)}) %collective-permute-start.9) | collective-permute-done | bytes 278560 | tf_op jit(solution)/shard_map/ppermute | solution.py:294
  28.5 1.7 %expert_kernel.5 = (bf16[128,1152]{1,0:T(8,128)(2,1)S(1)}, bf16[2,64,768]{2,1,0:T(8,128)(2,1)S(1)}, bf16[2,64,384]{2,1,0:T(8,128)(2,1)S(1)}) custom-call(s32[2]{0:T(128)S(1)} %pad_add_fusion.refs_0_, bf16[64,2176]{1,0:T(8,128)(2,1)S(1)} %pass_kernel.4.refs_2_.refs_1_.refs_5_, bf16[64,2176]{1,0:T(8,128)(2,1)S(1)} %collective-permute-done.8.refs_2_.refs_6_, ...), custom_call_target="tpu_custom_call" | custom-call | flops 6000000000 | tf_op jit(solution)/shard_map/expert_kernel/pallas_call | solution.py:253
  30.3 1.8 %expert_kernel.6 = (bf16[128,1152]{1,0:T(8,128)(2,1)S(1)}, bf16[1,128,768]{2,1,0:T(8,128)(2,1)S(1)}, bf16[1,128,384]{2,1,0:T(8,128)(2,1)S(1)}) custom-call(s32[2]{0:T(128)S(1)} %pad_add_fusion.refs_0_, bf16[128,2176]{1,0:T(8,128)(2,1)S(1)} %join_kernel.7.refs_9_.refs_1_, bf16[512,384]{1,0:T(8,128)(2,1)S(1)} %bitcast.16, ...), custom_call_target="tpu_custom_call" | custom-call | flops 6000000000 | tf_op jit(solution)/shard_map/expert_kernel/pallas_call | solution.py:253
  32.1 6.0 %collective-permute-done.10.refs_2_.refs_1_.refs_12_ = bf16[128,2176]{1,0:T(8,128)(2,1)S(1)} collective-permute-done((bf16[128,2176]{1,0:T(8,128)(2,1)S(1)}, bf16[128,2176]{1,0:T(8,128)(2,1)S(1)}, u32[]{:S(2)}, u32[]{:S(2)}) %collective-permute-start.10) | collective-permute-done | bytes 557088 | tf_op jit(solution)/shard_map/ppermute | solution.py:294
  38.1 1.8 %expert_kernel.7 = (bf16[128,1152]{1,0:T(8,128)(2,1)S(1)}, bf16[1,128,768]{2,1,0:T(8,128)(2,1)S(1)}, bf16[1,128,384]{2,1,0:T(8,128)(2,1)S(1)}) custom-call(s32[2]{0:T(128)S(1)} %pad_add_fusion.refs_0_, bf16[128,2176]{1,0:T(8,128)(2,1)S(1)} %collective-permute-done.10.refs_2_.refs_1_.refs_12_, bf16[512,384]{1,0:T(8,128)(2,1)S(1)} %bitcast.17, ...), custom_call_target="tpu_custom_call" | custom-call | flops 6000000000 | tf_op jit(solution)/shard_map/expert_kernel/pallas_call | solution.py:253
  39.9 2.1 %collective-permute-start.13 = (bf16[128,1152]{1,0:T(8,128)(2,1)S(1)}, bf16[128,1152]{1,0:T(8,128)(2,1)S(1)}, u32[]{:S(2)}, u32[]{:S(2)}) collective-permute-start(bf16[128,1152]{1,0:T(8,128)(2,1)S(1)} %get-tuple-element.45), channel_id=1, source_target_pairs={{0,4},{1,3},{2,6},{3,1},{4,0},{5,7},{6,2},{7,5},{8,12},{9,11},{10,... | collective-permute-start | bytes 884744 | tf_op jit(solution)/shard_map/ppermute | solution.py:294
  42.0 2.9 %collective-permute-done.11.refs_1_ = bf16[128,1152]{1,0:T(8,128)(2,1)S(1)} collective-permute-done((bf16[128,1152]{1,0:T(8,128)(2,1)S(1)}, bf16[128,1152]{1,0:T(8,128)(2,1)S(1)}, u32[]{:S(2)}, u32[]{:S(2)}) %collective-permute-start.11) | collective-permute-done | bytes 294944 | tf_op jit(solution)/shard_map/ppermute | solution.py:294
  44.9 2.1 %collective-permute-start.12 = (bf16[64,1152]{1,0:T(8,128)(2,1)S(1)}, bf16[64,1152]{1,0:T(8,128)(2,1)S(1)}, u32[]{:S(2)}, u32[]{:S(2)}) collective-permute-start(bf16[64,1152]{1,0:T(8,128)(2,1)S(1)} %get-tuple-element.43.refs_15_), channel_id=1, source_target_pairs={{0,2},{1,5},{2,0},{3,7},{4,6},{5,1},{6,4},{7,3},{8,10},{9,13},{10,... | collective-permute-start | bytes 442376 | tf_op jit(solution)/shard_map/ppermute | solution.py:294
  47.0 2.0 %weight_kernel.1 = (f32[512,768]{1,0:T(8,128)S(1)}, f32[384,512]{1,0:T(8,128)S(1)}, bf16[512,384]{1,0:T(8,128)(2,1)S(1)}, bf16[512,384]{1,0:T(8,128)(2,1)S(1)}, bf16[384,512]{1,0:T(8,128)(2,1)S(1)}) custom-call(s32[2]{0:T(128)S(1)} %pad_add_fusion.refs_0_, bf16[64,2176]{1,0:T(8,128)(2,1)S(1)} %join_kernel.4.refs_2_.refs_1_, ...), custom_call_target="tpu_custom_call" | custom-call | flops 6000000000 | tf_op jit(solution)/shard_map/weight_kernel/pallas_call | solution.py:253
  49.0 0.4 collective-permute-done.13.refs_1_
  49.5 2.4 %collective-permute-start.18 = (bf16[64,1152]{1,0:T(8,128)(2,1)S(1)}, bf16[64,1152]{1,0:T(8,128)(2,1)S(1)}, u32[]{:S(2)}, u32[]{:S(2)}) collective-permute-start(bf16[64,1152]{1,0:T(8,128)(2,1)S(1)} %get-tuple-element.51.refs_2_), channel_id=1, source_target_pairs={{0,2},{1,5},{2,0},{3,7},{4,6},{5,1},{6,4},{7,3},{8,10},{9,13},{10,... | collective-permute-start | bytes 442376 | tf_op jit(solution)/shard_map/ppermute | solution.py:294
  51.9 0.5 collective-permute-start.15
  52.4 1.8 %collective-permute-start.14 = (bf16[32,1152]{1,0:T(8,128)(2,1)S(1)}, bf16[32,1152]{1,0:T(8,128)(2,1)S(1)}, u32[]{:S(2)}, u32[]{:S(2)}) collective-permute-start(bf16[32,1152]{1,0:T(8,128)(2,1)S(1)} %get-tuple-element.53.refs_2_), channel_id=1, source_target_pairs={{0,16},{1,17},{2,18},{3,19},{4,20},{5,21},{6,22},{7,23},{8,24},{9,... | collective-permute-start | bytes 221192 | tf_op jit(solution)/shard_map/ppermute | solution.py:294
  54.3 0.8 %collective-permute-done.18.refs_1_ = bf16[64,1152]{1,0:T(8,128)(2,1)S(1)} collective-permute-done((bf16[64,1152]{1,0:T(8,128)(2,1)S(1)}, bf16[64,1152]{1,0:T(8,128)(2,1)S(1)}, u32[]{:S(2)}, u32[]{:S(2)}) %collective-permute-start.18) | collective-permute-done | bytes 147488 | tf_op jit(solution)/shard_map/ppermute | solution.py:294
  55.1 1.6 %collective-permute-start.19 = (bf16[32,1152]{1,0:T(8,128)(2,1)S(1)}, bf16[32,1152]{1,0:T(8,128)(2,1)S(1)}, u32[]{:S(2)}, u32[]{:S(2)}) collective-permute-start(bf16[32,1152]{1,0:T(8,128)(2,1)S(1)} %get-tuple-element.61), channel_id=1, source_target_pairs={{0,8},{1,9},{2,10},{3,11},{4,12},{5,13},{6,14},{7,15},{8,0},{9,1},... | collective-permute-start | bytes 221192 | tf_op jit(solution)/shard_map/ppermute | solution.py:294
  56.7 2.4 %collective-permute-start.20 = (bf16[32,1152]{1,0:T(8,128)(2,1)S(1)}, bf16[32,1152]{1,0:T(8,128)(2,1)S(1)}, u32[]{:S(2)}, u32[]{:S(2)}) collective-permute-start(bf16[32,1152]{1,0:T(8,128)(2,1)S(1)} %get-tuple-element.59.refs_5_), channel_id=1, source_target_pairs={{0,24},{1,25},{2,26},{3,27},{4,28},{5,29},{6,30},{7,31},{8,16},{9,... | collective-permute-start | bytes 221192 | tf_op jit(solution)/shard_map/ppermute | solution.py:294
  59.1 1.2 %settle_kernel.1 = (bf16[512,384]{1,0:T(8,128)(2,1)}, bf16[512,384]{1,0:T(8,128)(2,1)}, bf16[384,512]{1,0:T(8,128)(2,1)}, f32[8,128]{1,0:T(8,128)S(1)}) custom-call(f32[512,768]{1,0:T(8,128)S(1)} %get-tuple-element.54.refs_0_, f32[384,512]{1,0:T(8,128)S(1)} %get-tuple-element.55.refs_1_, bf16[512,384]{1,0:T(8,128)(2,1)S(1)} %collective-permute-done.15.refs_2_, ...), custom_call_target="tpu_custom_call" | custom-call | tf_op jit(solution)/shard_map/settle_kernel/pallas_call | solution.py:253
  60.4 2.7 %collective-permute-done.20.refs_2_ = bf16[32,1152]{1,0:T(8,128)(2,1)S(1)} collective-permute-done((bf16[32,1152]{1,0:T(8,128)(2,1)S(1)}, bf16[32,1152]{1,0:T(8,128)(2,1)S(1)}, u32[]{:S(2)}, u32[]{:S(2)}) %collective-permute-start.20) | collective-permute-done | bytes 73760 | tf_op jit(solution)/shard_map/ppermute | solution.py:294
  63.0 1.4 %finish_kernel.1 = (bf16[32,1024]{1,0:T(8,128)(2,1)}, bf16[8,32]{1,0:T(8,128)(2,1)}) custom-call(s32[2]{0:T(128)S(1)} %pad_add_fusion.refs_0_, f32[32,1152]{1,0:T(8,128)S(1)} %add_kernel.3.refs_1_.refs_4_, bf16[32,1152]{1,0:T(8,128)(2,1)S(1)} %collective-permute-done.20.refs_2_, s32[8,32]{1,0:T(8,128)S(1)} %bitcast.12, f32[32,1152]{1,0:T(8,128)S(1)} %add_kernel.3.refs_1_.refs_4_), custom_call_target="tpu_custom_call" | custom-call | tf_op jit(solution)/shard_map/finish_kernel/pallas_call | solution.py:253
  (41 shorter events, 0.7 us)
Async XLA Ops:
  1.6 6.0 %collective-permute-start = (bf16[32,2176]{1,0:T(8,128)(2,1)S(1)}, bf16[32,2176]{1,0:T(8,128)(2,1)S(1)}, u32[]{:S(2)}, u32[]{:S(2)}) collective-permute-start(bf16[32,2176]{1,0:T(8,128)(2,1)S(1)} %prepare_kernel.1.refs_0_), channel_id=1, source_target_pairs={{0,2},{1,5},{2,0},{3,7},{4,6},{5,1},{6,4},{7,3},{8,10},{9,13},{10,... | collective-permute-start | bytes 417800 | tf_op jit(solution)/shard_map/ppermute | solution.py:294
  4.6 9.0 %collective-permute-start.1 = (bf16[32,2176]{1,0:T(8,128)(2,1)S(1)}, bf16[32,2176]{1,0:T(8,128)(2,1)S(1)}, u32[]{:S(2)}, u32[]{:S(2)}) collective-permute-start(bf16[32,2176]{1,0:T(8,128)(2,1)S(1)} %prepare_kernel.1.refs_0_), channel_id=1, source_target_pairs={{0,16},{1,17},{2,18},{3,19},{4,20},{5,21},{6,22},{7,23},{8,24},{9,... | collective-permute-start | bytes 417800 | tf_op jit(solution)/shard_map/ppermute | solution.py:294
  7.6 6.7 %collective-permute-start.3 = (bf16[64,2176]{1,0:T(8,128)(2,1)S(1)}, bf16[64,2176]{1,0:T(8,128)(2,1)S(1)}, u32[]{:S(2)}, u32[]{:S(2)}) collective-permute-start(bf16[64,2176]{1,0:T(8,128)(2,1)S(1)} %join_kernel.4.refs_2_.refs_1_), channel_id=1, source_target_pairs={{0,4},{1,3},{2,6},{3,1},{4,0},{5,7},{6,2},{7,5},{8,12},{9,11},{10,... | collective-permute-start | bytes 835592 | tf_op jit(solution)/shard_map/ppermute | solution.py:294
  9.8 14.2 %collective-permute-start.4 = (bf16[512,384]{1,0:T(8,128)(2,1)}, bf16[512,384]{1,0:T(8,128)(2,1)S(1)}, u32[]{:S(2)}, u32[]{:S(2)}) collective-permute-start(bf16[512,384]{1,0:T(8,128)(2,1)} %bitcast.13), channel_id=1, source_target_pairs={{0,1},{1,0},{2,3},{3,2},{4,5},{5,4},{6,7},{7,6},{8,9},{9,8},{10,11... | collective-permute-start | bytes 1179656 | tf_op jit(solution)/shard_map/ppermute | solution.py:21
  9.8 14.1 %collective-permute-start.6 = (bf16[384,512]{1,0:T(8,128)(2,1)}, bf16[384,512]{1,0:T(8,128)(2,1)S(1)}, u32[]{:S(2)}, u32[]{:S(2)}) collective-permute-start(bf16[384,512]{1,0:T(8,128)(2,1)} %bitcast.23), channel_id=1, source_target_pairs={{0,1},{1,0},{2,3},{3,2},{4,5},{5,4},{6,7},{7,6},{8,9},{9,8},{10,11... | collective-permute-start | bytes 1179656 | tf_op jit(solution)/shard_map/ppermute | solution.py:21
  10.3 13.7 %collective-permute-start.5 = (bf16[512,384]{1,0:T(8,128)(2,1)}, bf16[512,384]{1,0:T(8,128)(2,1)S(1)}, u32[]{:S(2)}, u32[]{:S(2)}) collective-permute-start(bf16[512,384]{1,0:T(8,128)(2,1)} %bitcast.18), channel_id=1, source_target_pairs={{0,1},{1,0},{2,3},{3,2},{4,5},{5,4},{6,7},{7,6},{8,9},{9,8},{10,11... | collective-permute-start | bytes 1179656 | tf_op jit(solution)/shard_map/ppermute | solution.py:21
  13.7 7.8 %collective-permute-start.7 = (bf16[64,2176]{1,0:T(8,128)(2,1)S(1)}, bf16[64,2176]{1,0:T(8,128)(2,1)S(1)}, u32[]{:S(2)}, u32[]{:S(2)}) collective-permute-start(bf16[64,2176]{1,0:T(8,128)(2,1)S(1)} %join_kernel.5.refs_1_), channel_id=1, source_target_pairs={{0,8},{1,9},{2,10},{3,11},{4,12},{5,13},{6,14},{7,15},{8,0},{9,1},... | collective-permute-start | bytes 835592 | tf_op jit(solution)/shard_map/ppermute | solution.py:294
  14.4 5.1 %collective-permute-start.2 = (bf16[32,2176]{1,0:T(8,128)(2,1)S(1)}, bf16[32,2176]{1,0:T(8,128)(2,1)S(1)}, u32[]{:S(2)}, u32[]{:S(2)}) collective-permute-start(bf16[32,2176]{1,0:T(8,128)(2,1)S(1)} %collective-permute-done.1.refs_1_.refs_0_), channel_id=1, source_target_pairs={{0,2},{1,5},{2,0},{3,7},{4,6},{5,1},{6,4},{7,3},{8,10},{9,13},{10,... | collective-permute-start | bytes 417800 | tf_op jit(solution)/shard_map/ppermute | solution.py:294
  16.4 7.6 %copy-start.1 = (bf16[1,512,384]{2,1,0:T(8,128)(2,1)S(1)}, bf16[1,512,384]{2,1,0:T(8,128)(2,1)}, u32[]{:S(2)}) copy-start(bf16[1,512,384]{2,1,0:T(8,128)(2,1)} %param.11) | copy-start | bytes 1179652
  16.4 7.6 %copy-start.2 = (bf16[1,512,384]{2,1,0:T(8,128)(2,1)S(1)}, bf16[1,512,384]{2,1,0:T(8,128)(2,1)}, u32[]{:S(2)}) copy-start(bf16[1,512,384]{2,1,0:T(8,128)(2,1)} %param.12) | copy-start | bytes 1179652
  16.4 7.6 %copy-start.3 = (bf16[1,384,512]{2,1,0:T(8,128)(2,1)S(1)}, bf16[1,384,512]{2,1,0:T(8,128)(2,1)}, u32[]{:S(2)}) copy-start(bf16[1,384,512]{2,1,0:T(8,128)(2,1)} %param.13) | copy-start | bytes 1179652
  19.5 9.1 %collective-permute-start.8 = (bf16[64,2176]{1,0:T(8,128)(2,1)S(1)}, bf16[64,2176]{1,0:T(8,128)(2,1)S(1)}, u32[]{:S(2)}, u32[]{:S(2)}) collective-permute-start(bf16[64,2176]{1,0:T(8,128)(2,1)S(1)} %join_kernel.6.refs_1_.refs_2_), channel_id=1, source_target_pairs={{0,4},{1,3},{2,6},{3,1},{4,0},{5,7},{6,2},{7,5},{8,12},{9,11},{10,... | collective-permute-start | bytes 835592 | tf_op jit(solution)/shard_map/ppermute | solution.py:294
  21.5 6.9 %collective-permute-start.9 = (bf16[64,2176]{1,0:T(8,128)(2,1)S(1)}, bf16[64,2176]{1,0:T(8,128)(2,1)S(1)}, u32[]{:S(2)}, u32[]{:S(2)}) collective-permute-start(bf16[64,2176]{1,0:T(8,128)(2,1)S(1)} %pass_kernel.5.refs_1_.refs_0_), channel_id=1, source_target_pairs={{0,2},{1,5},{2,0},{3,7},{4,6},{5,1},{6,4},{7,3},{8,10},{9,13},{10,... | collective-permute-start | bytes 835592 | tf_op jit(solution)/shard_map/ppermute | solution.py:294
  28.4 9.6 %collective-permute-start.10 = (bf16[128,2176]{1,0:T(8,128)(2,1)S(1)}, bf16[128,2176]{1,0:T(8,128)(2,1)S(1)}, u32[]{:S(2)}, u32[]{:S(2)}) collective-permute-start(bf16[128,2176]{1,0:T(8,128)(2,1)S(1)} %join_kernel.7.refs_9_.refs_1_), channel_id=1, source_target_pairs={{0,4},{1,3},{2,6},{3,1},{4,0},{5,7},{6,2},{7,5},{8,12},{9,11},{10,... | collective-permute-start | bytes 1671176 | tf_op jit(solution)/shard_map/ppermute | solution.py:294
  38.1 6.8 %collective-permute-start.11 = (bf16[128,1152]{1,0:T(8,128)(2,1)S(1)}, bf16[128,1152]{1,0:T(8,128)(2,1)S(1)}, u32[]{:S(2)}, u32[]{:S(2)}) collective-permute-start(bf16[128,1152]{1,0:T(8,128)(2,1)S(1)} %pass_kernel.7.refs_8_), channel_id=1, source_target_pairs={{0,4},{1,3},{2,6},{3,1},{4,0},{5,7},{6,2},{7,5},{8,12},{9,11},{10,... | collective-permute-start | bytes 884744 | tf_op jit(solution)/shard_map/ppermute | solution.py:294
  39.9 9.5 %collective-permute-start.13 = (bf16[128,1152]{1,0:T(8,128)(2,1)S(1)}, bf16[128,1152]{1,0:T(8,128)(2,1)S(1)}, u32[]{:S(2)}, u32[]{:S(2)}) collective-permute-start(bf16[128,1152]{1,0:T(8,128)(2,1)S(1)} %get-tuple-element.45), channel_id=1, source_target_pairs={{0,4},{1,3},{2,6},{3,1},{4,0},{5,7},{6,2},{7,5},{8,12},{9,11},{10,... | collective-permute-start | bytes 884744 | tf_op jit(solution)/shard_map/ppermute | solution.py:294
  44.9 7.5 %collective-permute-start.12 = (bf16[64,1152]{1,0:T(8,128)(2,1)S(1)}, bf16[64,1152]{1,0:T(8,128)(2,1)S(1)}, u32[]{:S(2)}, u32[]{:S(2)}) collective-permute-start(bf16[64,1152]{1,0:T(8,128)(2,1)S(1)} %get-tuple-element.43.refs_15_), channel_id=1, source_target_pairs={{0,2},{1,5},{2,0},{3,7},{4,6},{5,1},{6,4},{7,3},{8,10},{9,13},{10,... | collective-permute-start | bytes 442376 | tf_op jit(solution)/shard_map/ppermute | solution.py:294
  49.5 5.5 %collective-permute-start.18 = (bf16[64,1152]{1,0:T(8,128)(2,1)S(1)}, bf16[64,1152]{1,0:T(8,128)(2,1)S(1)}, u32[]{:S(2)}, u32[]{:S(2)}) collective-permute-start(bf16[64,1152]{1,0:T(8,128)(2,1)S(1)} %get-tuple-element.51.refs_2_), channel_id=1, source_target_pairs={{0,2},{1,5},{2,0},{3,7},{4,6},{5,1},{6,4},{7,3},{8,10},{9,13},{10,... | collective-permute-start | bytes 442376 | tf_op jit(solution)/shard_map/ppermute | solution.py:294
  51.9 7.2 %collective-permute-start.17 = (bf16[384,512]{1,0:T(8,128)(2,1)S(1)}, bf16[384,512]{1,0:T(8,128)(2,1)S(1)}, u32[]{:S(2)}, u32[]{:S(2)}) collective-permute-start(bf16[384,512]{1,0:T(8,128)(2,1)S(1)} %get-tuple-element.50.refs_2_), channel_id=1, source_target_pairs={{0,1},{1,0},{2,3},{3,2},{4,5},{5,4},{6,7},{7,6},{8,9},{9,8},{10,11... | collective-permute-start | bytes 1179656 | tf_op jit(solution)/shard_map/ppermute | solution.py:21
  51.9 4.8 %collective-permute-start.15 = (bf16[512,384]{1,0:T(8,128)(2,1)S(1)}, bf16[512,384]{1,0:T(8,128)(2,1)S(1)}, u32[]{:S(2)}, u32[]{:S(2)}) collective-permute-start(bf16[512,384]{1,0:T(8,128)(2,1)S(1)} %get-tuple-element.56), channel_id=1, source_target_pairs={{0,1},{1,0},{2,3},{3,2},{4,5},{5,4},{6,7},{7,6},{8,9},{9,8},{10,11... | collective-permute-start | bytes 1179656 | tf_op jit(solution)/shard_map/ppermute | solution.py:21
  52.4 6.7 %collective-permute-start.16 = (bf16[512,384]{1,0:T(8,128)(2,1)S(1)}, bf16[512,384]{1,0:T(8,128)(2,1)S(1)}, u32[]{:S(2)}, u32[]{:S(2)}) collective-permute-start(bf16[512,384]{1,0:T(8,128)(2,1)S(1)} %get-tuple-element.57), channel_id=1, source_target_pairs={{0,1},{1,0},{2,3},{3,2},{4,5},{5,4},{6,7},{7,6},{8,9},{9,8},{10,11... | collective-permute-start | bytes 1179656 | tf_op jit(solution)/shard_map/ppermute | solution.py:21
  52.4 7.9 %collective-permute-start.14 = (bf16[32,1152]{1,0:T(8,128)(2,1)S(1)}, bf16[32,1152]{1,0:T(8,128)(2,1)S(1)}, u32[]{:S(2)}, u32[]{:S(2)}) collective-permute-start(bf16[32,1152]{1,0:T(8,128)(2,1)S(1)} %get-tuple-element.53.refs_2_), channel_id=1, source_target_pairs={{0,16},{1,17},{2,18},{3,19},{4,20},{5,21},{6,22},{7,23},{8,24},{9,... | collective-permute-start | bytes 221192 | tf_op jit(solution)/shard_map/ppermute | solution.py:294
  55.1 5.3 %collective-permute-start.19 = (bf16[32,1152]{1,0:T(8,128)(2,1)S(1)}, bf16[32,1152]{1,0:T(8,128)(2,1)S(1)}, u32[]{:S(2)}, u32[]{:S(2)}) collective-permute-start(bf16[32,1152]{1,0:T(8,128)(2,1)S(1)} %get-tuple-element.61), channel_id=1, source_target_pairs={{0,8},{1,9},{2,10},{3,11},{4,12},{5,13},{6,14},{7,15},{8,0},{9,1},... | collective-permute-start | bytes 221192 | tf_op jit(solution)/shard_map/ppermute | solution.py:294
  56.7 6.4 %collective-permute-start.20 = (bf16[32,1152]{1,0:T(8,128)(2,1)S(1)}, bf16[32,1152]{1,0:T(8,128)(2,1)S(1)}, u32[]{:S(2)}, u32[]{:S(2)}) collective-permute-start(bf16[32,1152]{1,0:T(8,128)(2,1)S(1)} %get-tuple-element.59.refs_5_), channel_id=1, source_target_pairs={{0,24},{1,25},{2,26},{3,27},{4,28},{5,29},{6,30},{7,31},{8,16},{9,... | collective-permute-start | bytes 221192 | tf_op jit(solution)/shard_map/ppermute | solution.py:294
  59.1 3.9 %copy-start = (s32[32,8]{0,1:T(8,128)S(1)}, s32[32,8]{0,1:T(8,128)}, u32[]{:S(2)}) copy-start(s32[32,8]{0,1:T(8,128)} %param.9) | copy-start | bytes 3076

commit v15 on v14

--- a/solution.py
+++ b/solution.py
@@ -269,7 +269,7 @@
     while bit:
         bits.append(bit)
         bit //= 2
-    return (bits[:-2] + bits[-2:][::-1], bits)
+    return (bits, bits[:-2] + bits[-2:][::-1])
 
 
 def body(tokens, cotangent, expert_ids, gate_probs, gate_half, up_half, down_half):

time: 64.6 us -> 64.5 us (level)
  no operation moved by 1% of the time
where the time goes in v15:
time: 64.5 us; the launch traced here: 64.3 us
  starting transfers between devices  28.3 us (44%)
  waiting for transfers between devices  22.2 us (34%)
  Pallas kernels  12.9 us (20%)
  between operations  0.85 us (1%)
    ppermute x15, starting transfers between devices, exchange(): return lax.ppermute(x, DEVICES, pairs)  27.3 us
    ppermute x15, waiting for transfers between devices, exchange(): return lax.ppermute(x, DEVICES, pairs)  22.2 us
    pallas_call x21, Pallas kernels, call(): pl.pallas_call(run, out_shape=out_shape, in_specs=[pl.BlockSpec(memory_sp...  12 us
  transfers between devices with their start and end apart: 21, of which 9 were waited for; matrix products, arithmetic and copies ran while one was open for 0% of the time, Pallas kernels for 16%

profile of v15, /device:TPU:0, one launch (start us, length us, event | category | flops | bytes accessed | tf_op | source)
XLA Modules:
  0.0 64.3 jit_solution(952619111720471029)
XLA Ops:
  0.6 0.9 %prepare_kernel.1.refs_0_ = bf16[32,2176]{1,0:T(8,128)(2,1)S(1)} custom-call(bf16[32,1024]{1,0:T(8,128)(2,1)} %tokens.1, bf16[32,1024]{1,0:T(8,128)(2,1)} %cotangent.1, s32[8,32]{1,0:T(8,128)} %bitcast.11, bf16[8,32]{1,0:T(8,128)(2,1)} %bitcast.28), custom_call_target="tpu_custom_call" | custom-call | tf_op jit(solution)/shard_map/prepare_kernel/pallas_call | solution.py:309
  1.6 3.0 %collective-permute-start = (bf16[32,2176]{1,0:T(8,128)(2,1)S(1)}, bf16[32,2176]{1,0:T(8,128)(2,1)S(1)}, u32[]{:S(2)}, u32[]{:S(2)}) collective-permute-start(bf16[32,2176]{1,0:T(8,128)(2,1)S(1)} %prepare_kernel.1.refs_0_), channel_id=1, source_target_pairs={{0,4},{1,3},{2,6},{3,1},{4,0},{5,7},{6,2},{7,5},{8,12},{9,11},{10,... | collective-permute-start | bytes 417800 | tf_op jit(solution)/shard_map/ppermute | solution.py:294
  4.6 2.6 %collective-permute-start.1 = (bf16[32,2176]{1,0:T(8,128)(2,1)S(1)}, bf16[32,2176]{1,0:T(8,128)(2,1)S(1)}, u32[]{:S(2)}, u32[]{:S(2)}) collective-permute-start(bf16[32,2176]{1,0:T(8,128)(2,1)S(1)} %prepare_kernel.1.refs_0_), channel_id=1, source_target_pairs={{0,16},{1,17},{2,18},{3,19},{4,20},{5,21},{6,22},{7,23},{8,24},{9,... | collective-permute-start | bytes 417800 | tf_op jit(solution)/shard_map/ppermute | solution.py:294
  7.2 0.4 collective-permute-done.refs_1_
  7.7 2.1 %collective-permute-start.3 = (bf16[64,2176]{1,0:T(8,128)(2,1)S(1)}, bf16[64,2176]{1,0:T(8,128)(2,1)S(1)}, u32[]{:S(2)}, u32[]{:S(2)}) collective-permute-start(bf16[64,2176]{1,0:T(8,128)(2,1)S(1)} %join_kernel.4.refs_2_.refs_1_), channel_id=1, source_target_pairs={{0,2},{1,5},{2,0},{3,7},{4,6},{5,1},{6,4},{7,3},{8,10},{9,13},{10,... | collective-permute-start | bytes 835592 | tf_op jit(solution)/shard_map/ppermute | solution.py:294
  9.7 0.5 collective-permute-start.6
  10.2 3.4 %collective-permute-done.1.refs_1_.refs_0_ = bf16[32,2176]{1,0:T(8,128)(2,1)S(1)} collective-permute-done((bf16[32,2176]{1,0:T(8,128)(2,1)S(1)}, bf16[32,2176]{1,0:T(8,128)(2,1)S(1)}, u32[]{:S(2)}, u32[]{:S(2)}) %collective-permute-start.1) | collective-permute-done | bytes 139296 | tf_op jit(solution)/shard_map/ppermute | solution.py:294
  13.6 0.7 %collective-permute-start.7 = (bf16[64,2176]{1,0:T(8,128)(2,1)S(1)}, bf16[64,2176]{1,0:T(8,128)(2,1)S(1)}, u32[]{:S(2)}, u32[]{:S(2)}) collective-permute-start(bf16[64,2176]{1,0:T(8,128)(2,1)S(1)} %join_kernel.5.refs_1_), channel_id=1, source_target_pairs={{0,8},{1,9},{2,10},{3,11},{4,12},{5,13},{6,14},{7,15},{8,0},{9,1},... | collective-permute-start | bytes 835592 | tf_op jit(solution)/shard_map/ppermute | solution.py:294
  14.4 1.9 %collective-permute-start.2 = (bf16[32,2176]{1,0:T(8,128)(2,1)S(1)}, bf16[32,2176]{1,0:T(8,128)(2,1)S(1)}, u32[]{:S(2)}, u32[]{:S(2)}) collective-permute-start(bf16[32,2176]{1,0:T(8,128)(2,1)S(1)} %collective-permute-done.1.refs_1_.refs_0_), channel_id=1, source_target_pairs={{0,4},{1,3},{2,6},{3,1},{4,0},{5,7},{6,2},{7,5},{8,12},{9,11},{10,... | collective-permute-start | bytes 417800 | tf_op jit(solution)/shard_map/ppermute | solution.py:294
  16.4 3.0 %collective-permute-done.2.refs_1_ = bf16[32,2176]{1,0:T(8,128)(2,1)S(1)} collective-permute-done((bf16[32,2176]{1,0:T(8,128)(2,1)S(1)}, bf16[32,2176]{1,0:T(8,128)(2,1)S(1)}, u32[]{:S(2)}, u32[]{:S(2)}) %collective-permute-start.2) | collective-permute-done | bytes 139296 | tf_op jit(solution)/shard_map/ppermute | solution.py:294
  19.4 2.0 %collective-permute-start.8 = (bf16[64,2176]{1,0:T(8,128)(2,1)S(1)}, bf16[64,2176]{1,0:T(8,128)(2,1)S(1)}, u32[]{:S(2)}, u32[]{:S(2)}) collective-permute-start(bf16[64,2176]{1,0:T(8,128)(2,1)S(1)} %join_kernel.6.refs_1_.refs_2_), channel_id=1, source_target_pairs={{0,2},{1,5},{2,0},{3,7},{4,6},{5,1},{6,4},{7,3},{8,10},{9,13},{10,... | collective-permute-start | bytes 835592 | tf_op jit(solution)/shard_map/ppermute | solution.py:294
  21.4 2.4 %collective-permute-start.9 = (bf16[64,2176]{1,0:T(8,128)(2,1)S(1)}, bf16[64,2176]{1,0:T(8,128)(2,1)S(1)}, u32[]{:S(2)}, u32[]{:S(2)}) collective-permute-start(bf16[64,2176]{1,0:T(8,128)(2,1)S(1)} %pass_kernel.5.refs_1_.refs_0_), channel_id=1, source_target_pairs={{0,4},{1,3},{2,6},{3,1},{4,0},{5,7},{6,2},{7,5},{8,12},{9,11},{10,... | collective-permute-start | bytes 835592 | tf_op jit(solution)/shard_map/ppermute | solution.py:294
  24.0 1.7 %expert_kernel.4 = (bf16[128,1152]{1,0:T(8,128)(2,1)S(1)}, bf16[2,64,768]{2,1,0:T(8,128)(2,1)S(1)}, bf16[2,64,384]{2,1,0:T(8,128)(2,1)S(1)}) custom-call(s32[2]{0:T(128)S(1)} %pad_add_fusion.refs_0_, bf16[64,2176]{1,0:T(8,128)(2,1)S(1)} %join_kernel.4.refs_2_.refs_1_, bf16[64,2176]{1,0:T(8,128)(2,1)S(1)} %join_kernel.6.refs_1_.refs_2_, ...), custom_call_target="tpu_custom_call" | custom-call | flops 6000000000 | tf_op jit(solution)/shard_map/expert_kernel/pallas_call | solution.py:253
  25.7 2.7 %collective-permute-done.9.refs_1_ = bf16[64,2176]{1,0:T(8,128)(2,1)S(1)} collective-permute-done((bf16[64,2176]{1,0:T(8,128)(2,1)S(1)}, bf16[64,2176]{1,0:T(8,128)(2,1)S(1)}, u32[]{:S(2)}, u32[]{:S(2)}) %collective-permute-start.9) | collective-permute-done | bytes 278560 | tf_op jit(solution)/shard_map/ppermute | solution.py:294
  28.5 1.7 %expert_kernel.5 = (bf16[128,1152]{1,0:T(8,128)(2,1)S(1)}, bf16[2,64,768]{2,1,0:T(8,128)(2,1)S(1)}, bf16[2,64,384]{2,1,0:T(8,128)(2,1)S(1)}) custom-call(s32[2]{0:T(128)S(1)} %pad_add_fusion.refs_0_, bf16[64,2176]{1,0:T(8,128)(2,1)S(1)} %pass_kernel.4.refs_2_.refs_1_.refs_5_, bf16[64,2176]{1,0:T(8,128)(2,1)S(1)} %collective-permute-done.8.refs_2_.refs_6_, ...), custom_call_target="tpu_custom_call" | custom-call | flops 6000000000 | tf_op jit(solution)/shard_map/expert_kernel/pallas_call | solution.py:253
  30.3 1.8 %expert_kernel.6 = (bf16[128,1152]{1,0:T(8,128)(2,1)S(1)}, bf16[1,128,768]{2,1,0:T(8,128)(2,1)S(1)}, bf16[1,128,384]{2,1,0:T(8,128)(2,1)S(1)}) custom-call(s32[2]{0:T(128)S(1)} %pad_add_fusion.refs_0_, bf16[128,2176]{1,0:T(8,128)(2,1)S(1)} %join_kernel.7.refs_9_.refs_1_, bf16[512,384]{1,0:T(8,128)(2,1)S(1)} %bitcast.16, ...), custom_call_target="tpu_custom_call" | custom-call | flops 6000000000 | tf_op jit(solution)/shard_map/expert_kernel/pallas_call | solution.py:253
  32.1 6.0 %collective-permute-done.10.refs_2_.refs_1_.refs_12_ = bf16[128,2176]{1,0:T(8,128)(2,1)S(1)} collective-permute-done((bf16[128,2176]{1,0:T(8,128)(2,1)S(1)}, bf16[128,2176]{1,0:T(8,128)(2,1)S(1)}, u32[]{:S(2)}, u32[]{:S(2)}) %collective-permute-start.10) | collective-permute-done | bytes 557088 | tf_op jit(solution)/shard_map/ppermute | solution.py:294
  38.1 1.8 %expert_kernel.7 = (bf16[128,1152]{1,0:T(8,128)(2,1)S(1)}, bf16[1,128,768]{2,1,0:T(8,128)(2,1)S(1)}, bf16[1,128,384]{2,1,0:T(8,128)(2,1)S(1)}) custom-call(s32[2]{0:T(128)S(1)} %pad_add_fusion.refs_0_, bf16[128,2176]{1,0:T(8,128)(2,1)S(1)} %collective-permute-done.10.refs_2_.refs_1_.refs_12_, bf16[512,384]{1,0:T(8,128)(2,1)S(1)} %bitcast.17, ...), custom_call_target="tpu_custom_call" | custom-call | flops 6000000000 | tf_op jit(solution)/shard_map/expert_kernel/pallas_call | solution.py:253
  39.9 2.1 %collective-permute-start.13 = (bf16[128,1152]{1,0:T(8,128)(2,1)S(1)}, bf16[128,1152]{1,0:T(8,128)(2,1)S(1)}, u32[]{:S(2)}, u32[]{:S(2)}) collective-permute-start(bf16[128,1152]{1,0:T(8,128)(2,1)S(1)} %get-tuple-element.45), channel_id=1, source_target_pairs={{0,2},{1,5},{2,0},{3,7},{4,6},{5,1},{6,4},{7,3},{8,10},{9,13},{10,... | collective-permute-start | bytes 884744 | tf_op jit(solution)/shard_map/ppermute | solution.py:294
  42.0 2.9 %collective-permute-done.11.refs_1_ = bf16[128,1152]{1,0:T(8,128)(2,1)S(1)} collective-permute-done((bf16[128,1152]{1,0:T(8,128)(2,1)S(1)}, bf16[128,1152]{1,0:T(8,128)(2,1)S(1)}, u32[]{:S(2)}, u32[]{:S(2)}) %collective-permute-start.11) | collective-permute-done | bytes 294944 | tf_op jit(solution)/shard_map/ppermute | solution.py:294
  44.9 2.1 %collective-permute-start.12 = (bf16[64,1152]{1,0:T(8,128)(2,1)S(1)}, bf16[64,1152]{1,0:T(8,128)(2,1)S(1)}, u32[]{:S(2)}, u32[]{:S(2)}) collective-permute-start(bf16[64,1152]{1,0:T(8,128)(2,1)S(1)} %get-tuple-element.43.refs_15_), channel_id=1, source_target_pairs={{0,4},{1,3},{2,6},{3,1},{4,0},{5,7},{6,2},{7,5},{8,12},{9,11},{10,... | collective-permute-start | bytes 442376 | tf_op jit(solution)/shard_map/ppermute | solution.py:294
  47.0 2.0 %weight_kernel.1 = (f32[512,768]{1,0:T(8,128)S(1)}, f32[384,512]{1,0:T(8,128)S(1)}, bf16[512,384]{1,0:T(8,128)(2,1)S(1)}, bf16[512,384]{1,0:T(8,128)(2,1)S(1)}, bf16[384,512]{1,0:T(8,128)(2,1)S(1)}) custom-call(s32[2]{0:T(128)S(1)} %pad_add_fusion.refs_0_, bf16[64,2176]{1,0:T(8,128)(2,1)S(1)} %join_kernel.4.refs_2_.refs_1_, ...), custom_call_target="tpu_custom_call" | custom-call | flops 6000000000 | tf_op jit(solution)/shard_map/weight_kernel/pallas_call | solution.py:253
  49.0 0.4 collective-permute-done.13.refs_1_
  49.5 2.4 %collective-permute-start.18 = (bf16[64,1152]{1,0:T(8,128)(2,1)S(1)}, bf16[64,1152]{1,0:T(8,128)(2,1)S(1)}, u32[]{:S(2)}, u32[]{:S(2)}) collective-permute-start(bf16[64,1152]{1,0:T(8,128)(2,1)S(1)} %get-tuple-element.51.refs_2_), channel_id=1, source_target_pairs={{0,4},{1,3},{2,6},{3,1},{4,0},{5,7},{6,2},{7,5},{8,12},{9,11},{10,... | collective-permute-start | bytes 442376 | tf_op jit(solution)/shard_map/ppermute | solution.py:294
  51.9 0.5 collective-permute-start.15
  52.4 1.9 %collective-permute-start.14 = (bf16[32,1152]{1,0:T(8,128)(2,1)S(1)}, bf16[32,1152]{1,0:T(8,128)(2,1)S(1)}, u32[]{:S(2)}, u32[]{:S(2)}) collective-permute-start(bf16[32,1152]{1,0:T(8,128)(2,1)S(1)} %get-tuple-element.53.refs_2_), channel_id=1, source_target_pairs={{0,16},{1,17},{2,18},{3,19},{4,20},{5,21},{6,22},{7,23},{8,24},{9,... | collective-permute-start | bytes 221192 | tf_op jit(solution)/shard_map/ppermute | solution.py:294
  54.3 0.7 %collective-permute-done.18.refs_1_ = bf16[64,1152]{1,0:T(8,128)(2,1)S(1)} collective-permute-done((bf16[64,1152]{1,0:T(8,128)(2,1)S(1)}, bf16[64,1152]{1,0:T(8,128)(2,1)S(1)}, u32[]{:S(2)}, u32[]{:S(2)}) %collective-permute-start.18) | collective-permute-done | bytes 147488 | tf_op jit(solution)/shard_map/ppermute | solution.py:294
  55.0 1.6 %collective-permute-start.19 = (bf16[32,1152]{1,0:T(8,128)(2,1)S(1)}, bf16[32,1152]{1,0:T(8,128)(2,1)S(1)}, u32[]{:S(2)}, u32[]{:S(2)}) collective-permute-start(bf16[32,1152]{1,0:T(8,128)(2,1)S(1)} %get-tuple-element.61), channel_id=1, source_target_pairs={{0,8},{1,9},{2,10},{3,11},{4,12},{5,13},{6,14},{7,15},{8,0},{9,1},... | collective-permute-start | bytes 221192 | tf_op jit(solution)/shard_map/ppermute | solution.py:294
  56.6 2.4 %collective-permute-start.20 = (bf16[32,1152]{1,0:T(8,128)(2,1)S(1)}, bf16[32,1152]{1,0:T(8,128)(2,1)S(1)}, u32[]{:S(2)}, u32[]{:S(2)}) collective-permute-start(bf16[32,1152]{1,0:T(8,128)(2,1)S(1)} %get-tuple-element.59.refs_5_), channel_id=1, source_target_pairs={{0,24},{1,25},{2,26},{3,27},{4,28},{5,29},{6,30},{7,31},{8,16},{9,... | collective-permute-start | bytes 221192 | tf_op jit(solution)/shard_map/ppermute | solution.py:294
  59.1 1.2 %settle_kernel.1 = (bf16[512,384]{1,0:T(8,128)(2,1)}, bf16[512,384]{1,0:T(8,128)(2,1)}, bf16[384,512]{1,0:T(8,128)(2,1)}, f32[8,128]{1,0:T(8,128)S(1)}) custom-call(f32[512,768]{1,0:T(8,128)S(1)} %get-tuple-element.54.refs_0_, f32[384,512]{1,0:T(8,128)S(1)} %get-tuple-element.55.refs_1_, bf16[512,384]{1,0:T(8,128)(2,1)S(1)} %collective-permute-done.15.refs_2_, ...), custom_call_target="tpu_custom_call" | custom-call | tf_op jit(solution)/shard_map/settle_kernel/pallas_call | solution.py:253
  60.3 2.7 %collective-permute-done.20.refs_2_ = bf16[32,1152]{1,0:T(8,128)(2,1)S(1)} collective-permute-done((bf16[32,1152]{1,0:T(8,128)(2,1)S(1)}, bf16[32,1152]{1,0:T(8,128)(2,1)S(1)}, u32[]{:S(2)}, u32[]{:S(2)}) %collective-permute-start.20) | collective-permute-done | bytes 73760 | tf_op jit(solution)/shard_map/ppermute | solution.py:294
  63.0 1.4 %finish_kernel.1 = (bf16[32,1024]{1,0:T(8,128)(2,1)}, bf16[8,32]{1,0:T(8,128)(2,1)}) custom-call(s32[2]{0:T(128)S(1)} %pad_add_fusion.refs_0_, f32[32,1152]{1,0:T(8,128)S(1)} %add_kernel.3.refs_1_.refs_4_, bf16[32,1152]{1,0:T(8,128)(2,1)S(1)} %collective-permute-done.20.refs_2_, s32[8,32]{1,0:T(8,128)S(1)} %bitcast.12, f32[32,1152]{1,0:T(8,128)S(1)} %add_kernel.3.refs_1_.refs_4_), custom_call_target="tpu_custom_call" | custom-call | tf_op jit(solution)/shard_map/finish_kernel/pallas_call | solution.py:253
  (41 shorter events, 0.7 us)
Async XLA Ops:
  1.6 6.1 %collective-permute-start = (bf16[32,2176]{1,0:T(8,128)(2,1)S(1)}, bf16[32,2176]{1,0:T(8,128)(2,1)S(1)}, u32[]{:S(2)}, u32[]{:S(2)}) collective-permute-start(bf16[32,2176]{1,0:T(8,128)(2,1)S(1)} %prepare_kernel.1.refs_0_), channel_id=1, source_target_pairs={{0,4},{1,3},{2,6},{3,1},{4,0},{5,7},{6,2},{7,5},{8,12},{9,11},{10,... | collective-permute-start | bytes 417800 | tf_op jit(solution)/shard_map/ppermute | solution.py:294
  4.6 9.0 %collective-permute-start.1 = (bf16[32,2176]{1,0:T(8,128)(2,1)S(1)}, bf16[32,2176]{1,0:T(8,128)(2,1)S(1)}, u32[]{:S(2)}, u32[]{:S(2)}) collective-permute-start(bf16[32,2176]{1,0:T(8,128)(2,1)S(1)} %prepare_kernel.1.refs_0_), channel_id=1, source_target_pairs={{0,16},{1,17},{2,18},{3,19},{4,20},{5,21},{6,22},{7,23},{8,24},{9,... | collective-permute-start | bytes 417800 | tf_op jit(solution)/shard_map/ppermute | solution.py:294
  7.7 6.7 %collective-permute-start.3 = (bf16[64,2176]{1,0:T(8,128)(2,1)S(1)}, bf16[64,2176]{1,0:T(8,128)(2,1)S(1)}, u32[]{:S(2)}, u32[]{:S(2)}) collective-permute-start(bf16[64,2176]{1,0:T(8,128)(2,1)S(1)} %join_kernel.4.refs_2_.refs_1_), channel_id=1, source_target_pairs={{0,2},{1,5},{2,0},{3,7},{4,6},{5,1},{6,4},{7,3},{8,10},{9,13},{10,... | collective-permute-start | bytes 835592 | tf_op jit(solution)/shard_map/ppermute | solution.py:294
  9.7 14.2 %collective-permute-start.4 = (bf16[512,384]{1,0:T(8,128)(2,1)}, bf16[512,384]{1,0:T(8,128)(2,1)S(1)}, u32[]{:S(2)}, u32[]{:S(2)}) collective-permute-start(bf16[512,384]{1,0:T(8,128)(2,1)} %bitcast.13), channel_id=1, source_target_pairs={{0,1},{1,0},{2,3},{3,2},{4,5},{5,4},{6,7},{7,6},{8,9},{9,8},{10,11... | collective-permute-start | bytes 1179656 | tf_op jit(solution)/shard_map/ppermute | solution.py:21
  9.7 14.1 %collective-permute-start.6 = (bf16[384,512]{1,0:T(8,128)(2,1)}, bf16[384,512]{1,0:T(8,128)(2,1)S(1)}, u32[]{:S(2)}, u32[]{:S(2)}) collective-permute-start(bf16[384,512]{1,0:T(8,128)(2,1)} %bitcast.23), channel_id=1, source_target_pairs={{0,1},{1,0},{2,3},{3,2},{4,5},{5,4},{6,7},{7,6},{8,9},{9,8},{10,11... | collective-permute-start | bytes 1179656 | tf_op jit(solution)/shard_map/ppermute | solution.py:21
  10.2 13.7 %collective-permute-start.5 = (bf16[512,384]{1,0:T(8,128)(2,1)}, bf16[512,384]{1,0:T(8,128)(2,1)S(1)}, u32[]{:S(2)}, u32[]{:S(2)}) collective-permute-start(bf16[512,384]{1,0:T(8,128)(2,1)} %bitcast.18), channel_id=1, source_target_pairs={{0,1},{1,0},{2,3},{3,2},{4,5},{5,4},{6,7},{7,6},{8,9},{9,8},{10,11... | collective-permute-start | bytes 1179656 | tf_op jit(solution)/shard_map/ppermute | solution.py:21
  13.6 7.8 %collective-permute-start.7 = (bf16[64,2176]{1,0:T(8,128)(2,1)S(1)}, bf16[64,2176]{1,0:T(8,128)(2,1)S(1)}, u32[]{:S(2)}, u32[]{:S(2)}) collective-permute-start(bf16[64,2176]{1,0:T(8,128)(2,1)S(1)} %join_kernel.5.refs_1_), channel_id=1, source_target_pairs={{0,8},{1,9},{2,10},{3,11},{4,12},{5,13},{6,14},{7,15},{8,0},{9,1},... | collective-permute-start | bytes 835592 | tf_op jit(solution)/shard_map/ppermute | solution.py:294
  14.4 5.1 %collective-permute-start.2 = (bf16[32,2176]{1,0:T(8,128)(2,1)S(1)}, bf16[32,2176]{1,0:T(8,128)(2,1)S(1)}, u32[]{:S(2)}, u32[]{:S(2)}) collective-permute-start(bf16[32,2176]{1,0:T(8,128)(2,1)S(1)} %collective-permute-done.1.refs_1_.refs_0_), channel_id=1, source_target_pairs={{0,4},{1,3},{2,6},{3,1},{4,0},{5,7},{6,2},{7,5},{8,12},{9,11},{10,... | collective-permute-start | bytes 417800 | tf_op jit(solution)/shard_map/ppermute | solution.py:294
  16.4 7.5 %copy-start.1 = (bf16[1,512,384]{2,1,0:T(8,128)(2,1)S(1)}, bf16[1,512,384]{2,1,0:T(8,128)(2,1)}, u32[]{:S(2)}) copy-start(bf16[1,512,384]{2,1,0:T(8,128)(2,1)} %param.11) | copy-start | bytes 1179652
  16.4 7.5 %copy-start.2 = (bf16[1,512,384]{2,1,0:T(8,128)(2,1)S(1)}, bf16[1,512,384]{2,1,0:T(8,128)(2,1)}, u32[]{:S(2)}) copy-start(bf16[1,512,384]{2,1,0:T(8,128)(2,1)} %param.12) | copy-start | bytes 1179652
  16.4 7.5 %copy-start.3 = (bf16[1,384,512]{2,1,0:T(8,128)(2,1)S(1)}, bf16[1,384,512]{2,1,0:T(8,128)(2,1)}, u32[]{:S(2)}) copy-start(bf16[1,384,512]{2,1,0:T(8,128)(2,1)} %param.13) | copy-start | bytes 1179652
  19.4 9.1 %collective-permute-start.8 = (bf16[64,2176]{1,0:T(8,128)(2,1)S(1)}, bf16[64,2176]{1,0:T(8,128)(2,1)S(1)}, u32[]{:S(2)}, u32[]{:S(2)}) collective-permute-start(bf16[64,2176]{1,0:T(8,128)(2,1)S(1)} %join_kernel.6.refs_1_.refs_2_), channel_id=1, source_target_pairs={{0,2},{1,5},{2,0},{3,7},{4,6},{5,1},{6,4},{7,3},{8,10},{9,13},{10,... | collective-permute-start | bytes 835592 | tf_op jit(solution)/shard_map/ppermute | solution.py:294
  21.4 7.0 %collective-permute-start.9 = (bf16[64,2176]{1,0:T(8,128)(2,1)S(1)}, bf16[64,2176]{1,0:T(8,128)(2,1)S(1)}, u32[]{:S(2)}, u32[]{:S(2)}) collective-permute-start(bf16[64,2176]{1,0:T(8,128)(2,1)S(1)} %pass_kernel.5.refs_1_.refs_0_), channel_id=1, source_target_pairs={{0,4},{1,3},{2,6},{3,1},{4,0},{5,7},{6,2},{7,5},{8,12},{9,11},{10,... | collective-permute-start | bytes 835592 | tf_op jit(solution)/shard_map/ppermute | solution.py:294
  28.4 9.6 %collective-permute-start.10 = (bf16[128,2176]{1,0:T(8,128)(2,1)S(1)}, bf16[128,2176]{1,0:T(8,128)(2,1)S(1)}, u32[]{:S(2)}, u32[]{:S(2)}) collective-permute-start(bf16[128,2176]{1,0:T(8,128)(2,1)S(1)} %join_kernel.7.refs_9_.refs_1_), channel_id=1, source_target_pairs={{0,2},{1,5},{2,0},{3,7},{4,6},{5,1},{6,4},{7,3},{8,10},{9,13},{10,... | collective-permute-start | bytes 1671176 | tf_op jit(solution)/shard_map/ppermute | solution.py:294
  38.1 6.8 %collective-permute-start.11 = (bf16[128,1152]{1,0:T(8,128)(2,1)S(1)}, bf16[128,1152]{1,0:T(8,128)(2,1)S(1)}, u32[]{:S(2)}, u32[]{:S(2)}) collective-permute-start(bf16[128,1152]{1,0:T(8,128)(2,1)S(1)} %pass_kernel.7.refs_8_), channel_id=1, source_target_pairs={{0,2},{1,5},{2,0},{3,7},{4,6},{5,1},{6,4},{7,3},{8,10},{9,13},{10,... | collective-permute-start | bytes 884744 | tf_op jit(solution)/shard_map/ppermute | solution.py:294
  39.9 9.5 %collective-permute-start.13 = (bf16[128,1152]{1,0:T(8,128)(2,1)S(1)}, bf16[128,1152]{1,0:T(8,128)(2,1)S(1)}, u32[]{:S(2)}, u32[]{:S(2)}) collective-permute-start(bf16[128,1152]{1,0:T(8,128)(2,1)S(1)} %get-tuple-element.45), channel_id=1, source_target_pairs={{0,2},{1,5},{2,0},{3,7},{4,6},{5,1},{6,4},{7,3},{8,10},{9,13},{10,... | collective-permute-start | bytes 884744 | tf_op jit(solution)/shard_map/ppermute | solution.py:294
  44.9 7.5 %collective-permute-start.12 = (bf16[64,1152]{1,0:T(8,128)(2,1)S(1)}, bf16[64,1152]{1,0:T(8,128)(2,1)S(1)}, u32[]{:S(2)}, u32[]{:S(2)}) collective-permute-start(bf16[64,1152]{1,0:T(8,128)(2,1)S(1)} %get-tuple-element.43.refs_15_), channel_id=1, source_target_pairs={{0,4},{1,3},{2,6},{3,1},{4,0},{5,7},{6,2},{7,5},{8,12},{9,11},{10,... | collective-permute-start | bytes 442376 | tf_op jit(solution)/shard_map/ppermute | solution.py:294
  49.5 5.5 %collective-permute-start.18 = (bf16[64,1152]{1,0:T(8,128)(2,1)S(1)}, bf16[64,1152]{1,0:T(8,128)(2,1)S(1)}, u32[]{:S(2)}, u32[]{:S(2)}) collective-permute-start(bf16[64,1152]{1,0:T(8,128)(2,1)S(1)} %get-tuple-element.51.refs_2_), channel_id=1, source_target_pairs={{0,4},{1,3},{2,6},{3,1},{4,0},{5,7},{6,2},{7,5},{8,12},{9,11},{10,... | collective-permute-start | bytes 442376 | tf_op jit(solution)/shard_map/ppermute | solution.py:294
  51.9 7.2 %collective-permute-start.17 = (bf16[384,512]{1,0:T(8,128)(2,1)S(1)}, bf16[384,512]{1,0:T(8,128)(2,1)S(1)}, u32[]{:S(2)}, u32[]{:S(2)}) collective-permute-start(bf16[384,512]{1,0:T(8,128)(2,1)S(1)} %get-tuple-element.50.refs_2_), channel_id=1, source_target_pairs={{0,1},{1,0},{2,3},{3,2},{4,5},{5,4},{6,7},{7,6},{8,9},{9,8},{10,11... | collective-permute-start | bytes 1179656 | tf_op jit(solution)/shard_map/ppermute | solution.py:21
  51.9 4.8 %collective-permute-start.15 = (bf16[512,384]{1,0:T(8,128)(2,1)S(1)}, bf16[512,384]{1,0:T(8,128)(2,1)S(1)}, u32[]{:S(2)}, u32[]{:S(2)}) collective-permute-start(bf16[512,384]{1,0:T(8,128)(2,1)S(1)} %get-tuple-element.56), channel_id=1, source_target_pairs={{0,1},{1,0},{2,3},{3,2},{4,5},{5,4},{6,7},{7,6},{8,9},{9,8},{10,11... | collective-permute-start | bytes 1179656 | tf_op jit(solution)/shard_map/ppermute | solution.py:21
  52.4 6.7 %collective-permute-start.16 = (bf16[512,384]{1,0:T(8,128)(2,1)S(1)}, bf16[512,384]{1,0:T(8,128)(2,1)S(1)}, u32[]{:S(2)}, u32[]{:S(2)}) collective-permute-start(bf16[512,384]{1,0:T(8,128)(2,1)S(1)} %get-tuple-element.57), channel_id=1, source_target_pairs={{0,1},{1,0},{2,3},{3,2},{4,5},{5,4},{6,7},{7,6},{8,9},{9,8},{10,11... | collective-permute-start | bytes 1179656 | tf_op jit(solution)/shard_map/ppermute | solution.py:21
  52.4 7.8 %collective-permute-start.14 = (bf16[32,1152]{1,0:T(8,128)(2,1)S(1)}, bf16[32,1152]{1,0:T(8,128)(2,1)S(1)}, u32[]{:S(2)}, u32[]{:S(2)}) collective-permute-start(bf16[32,1152]{1,0:T(8,128)(2,1)S(1)} %get-tuple-element.53.refs_2_), channel_id=1, source_target_pairs={{0,16},{1,17},{2,18},{3,19},{4,20},{5,21},{6,22},{7,23},{8,24},{9,... | collective-permute-start | bytes 221192 | tf_op jit(solution)/shard_map/ppermute | solution.py:294
  55.0 5.3 %collective-permute-start.19 = (bf16[32,1152]{1,0:T(8,128)(2,1)S(1)}, bf16[32,1152]{1,0:T(8,128)(2,1)S(1)}, u32[]{:S(2)}, u32[]{:S(2)}) collective-permute-start(bf16[32,1152]{1,0:T(8,128)(2,1)S(1)} %get-tuple-element.61), channel_id=1, source_target_pairs={{0,8},{1,9},{2,10},{3,11},{4,12},{5,13},{6,14},{7,15},{8,0},{9,1},... | collective-permute-start | bytes 221192 | tf_op jit(solution)/shard_map/ppermute | solution.py:294
  56.6 6.3 %collective-permute-start.20 = (bf16[32,1152]{1,0:T(8,128)(2,1)S(1)}, bf16[32,1152]{1,0:T(8,128)(2,1)S(1)}, u32[]{:S(2)}, u32[]{:S(2)}) collective-permute-start(bf16[32,1152]{1,0:T(8,128)(2,1)S(1)} %get-tuple-element.59.refs_5_), channel_id=1, source_target_pairs={{0,24},{1,25},{2,26},{3,27},{4,28},{5,29},{6,30},{7,31},{8,16},{9,... | collective-permute-start | bytes 221192 | tf_op jit(solution)/shard_map/ppermute | solution.py:294
  59.1 3.9 %copy-start = (s32[32,8]{0,1:T(8,128)S(1)}, s32[32,8]{0,1:T(8,128)}, u32[]{:S(2)}) copy-start(s32[32,8]{0,1:T(8,128)} %param.9) | copy-start | bytes 3076

commit v16 on v15

--- a/solution.py
+++ b/solution.py
@@ -407,11 +407,11 @@
         None, keep_in, keep_down, *gots, leaves=3, limit=6,
     )
     total = collect(total, back_two)
-    total = collect(total, back_one)
-
-    parts = (total, back_both)
+    total = collect(total, back_both)
+
+    parts = (total, back_one)
     if far:
-        total = total + back_both.astype(F32)
+        total = total + back_one.astype(F32)
         for step in reversed(steps[:far]):
             middle = total.shape[0] // 2
             total = total[:middle] + exchange(total[middle:].astype(BF16), step).astype(F32)

time: 64.5 us -> 64.9 us (level)
  transfers between devices with their start and end apart: 21 -> 21, of which waited for: 9 -> 11; matrix products, arithmetic and copies ran while one was open for 0% -> 0% of each run, Pallas kernels for 16% -> 16%
where the time goes in v16:
time: 64.9 us; the launch traced here: 64.7 us
  starting transfers between devices  28.2 us (43%)
  waiting for transfers between devices  22.6 us (35%)
  Pallas kernels  12.9 us (20%)
  between operations  0.85 us (1%)
    ppermute x15, starting transfers between devices, exchange(): return lax.ppermute(x, DEVICES, pairs)  27.2 us
    ppermute x15, waiting for transfers between devices, exchange(): return lax.ppermute(x, DEVICES, pairs)  22.6 us
    pallas_call x21, Pallas kernels, call(): pl.pallas_call(run, out_shape=out_shape, in_specs=[pl.BlockSpec(memory_sp...  12 us
  transfers between devices with their start and end apart: 21, of which 11 were waited for; matrix products, arithmetic and copies ran while one was open for 0% of the time, Pallas kernels for 16%

profile of v16, /device:TPU:0, one launch (start us, length us, event | category | flops | bytes accessed | tf_op | source)
XLA Modules:
  0.0 64.7 jit_solution(2885474420308403971)
XLA Ops:
  0.6 0.9 %prepare_kernel.1.refs_0_ = bf16[32,2176]{1,0:T(8,128)(2,1)S(1)} custom-call(bf16[32,1024]{1,0:T(8,128)(2,1)} %tokens.1, bf16[32,1024]{1,0:T(8,128)(2,1)} %cotangent.1, s32[8,32]{1,0:T(8,128)} %bitcast.11, bf16[8,32]{1,0:T(8,128)(2,1)} %bitcast.28), custom_call_target="tpu_custom_call" | custom-call | tf_op jit(solution)/shard_map/prepare_kernel/pallas_call | solution.py:309
  1.6 3.0 %collective-permute-start = (bf16[32,2176]{1,0:T(8,128)(2,1)S(1)}, bf16[32,2176]{1,0:T(8,128)(2,1)S(1)}, u32[]{:S(2)}, u32[]{:S(2)}) collective-permute-start(bf16[32,2176]{1,0:T(8,128)(2,1)S(1)} %prepare_kernel.1.refs_0_), channel_id=1, source_target_pairs={{0,4},{1,3},{2,6},{3,1},{4,0},{5,7},{6,2},{7,5},{8,12},{9,11},{10,... | collective-permute-start | bytes 417800 | tf_op jit(solution)/shard_map/ppermute | solution.py:294
  4.6 2.6 %collective-permute-start.1 = (bf16[32,2176]{1,0:T(8,128)(2,1)S(1)}, bf16[32,2176]{1,0:T(8,128)(2,1)S(1)}, u32[]{:S(2)}, u32[]{:S(2)}) collective-permute-start(bf16[32,2176]{1,0:T(8,128)(2,1)S(1)} %prepare_kernel.1.refs_0_), channel_id=1, source_target_pairs={{0,16},{1,17},{2,18},{3,19},{4,20},{5,21},{6,22},{7,23},{8,24},{9,... | collective-permute-start | bytes 417800 | tf_op jit(solution)/shard_map/ppermute | solution.py:294
  7.2 0.4 collective-permute-done.refs_1_
  7.7 2.1 %collective-permute-start.3 = (bf16[64,2176]{1,0:T(8,128)(2,1)S(1)}, bf16[64,2176]{1,0:T(8,128)(2,1)S(1)}, u32[]{:S(2)}, u32[]{:S(2)}) collective-permute-start(bf16[64,2176]{1,0:T(8,128)(2,1)S(1)} %join_kernel.4.refs_2_.refs_1_), channel_id=1, source_target_pairs={{0,2},{1,5},{2,0},{3,7},{4,6},{5,1},{6,4},{7,3},{8,10},{9,13},{10,... | collective-permute-start | bytes 835592 | tf_op jit(solution)/shard_map/ppermute | solution.py:294
  9.7 0.5 collective-permute-start.6
  10.2 3.4 %collective-permute-done.1.refs_1_.refs_0_ = bf16[32,2176]{1,0:T(8,128)(2,1)S(1)} collective-permute-done((bf16[32,2176]{1,0:T(8,128)(2,1)S(1)}, bf16[32,2176]{1,0:T(8,128)(2,1)S(1)}, u32[]{:S(2)}, u32[]{:S(2)}) %collective-permute-start.1) | collective-permute-done | bytes 139296 | tf_op jit(solution)/shard_map/ppermute | solution.py:294
  13.6 0.7 %collective-permute-start.7 = (bf16[64,2176]{1,0:T(8,128)(2,1)S(1)}, bf16[64,2176]{1,0:T(8,128)(2,1)S(1)}, u32[]{:S(2)}, u32[]{:S(2)}) collective-permute-start(bf16[64,2176]{1,0:T(8,128)(2,1)S(1)} %join_kernel.5.refs_1_), channel_id=1, source_target_pairs={{0,8},{1,9},{2,10},{3,11},{4,12},{5,13},{6,14},{7,15},{8,0},{9,1},... | collective-permute-start | bytes 835592 | tf_op jit(solution)/shard_map/ppermute | solution.py:294
  14.4 1.9 %collective-permute-start.2 = (bf16[32,2176]{1,0:T(8,128)(2,1)S(1)}, bf16[32,2176]{1,0:T(8,128)(2,1)S(1)}, u32[]{:S(2)}, u32[]{:S(2)}) collective-permute-start(bf16[32,2176]{1,0:T(8,128)(2,1)S(1)} %collective-permute-done.1.refs_1_.refs_0_), channel_id=1, source_target_pairs={{0,4},{1,3},{2,6},{3,1},{4,0},{5,7},{6,2},{7,5},{8,12},{9,11},{10,... | collective-permute-start | bytes 417800 | tf_op jit(solution)/shard_map/ppermute | solution.py:294
  16.4 3.0 %collective-permute-done.2.refs_1_ = bf16[32,2176]{1,0:T(8,128)(2,1)S(1)} collective-permute-done((bf16[32,2176]{1,0:T(8,128)(2,1)S(1)}, bf16[32,2176]{1,0:T(8,128)(2,1)S(1)}, u32[]{:S(2)}, u32[]{:S(2)}) %collective-permute-start.2) | collective-permute-done | bytes 139296 | tf_op jit(solution)/shard_map/ppermute | solution.py:294
  19.4 2.0 %collective-permute-start.8 = (bf16[64,2176]{1,0:T(8,128)(2,1)S(1)}, bf16[64,2176]{1,0:T(8,128)(2,1)S(1)}, u32[]{:S(2)}, u32[]{:S(2)}) collective-permute-start(bf16[64,2176]{1,0:T(8,128)(2,1)S(1)} %join_kernel.6.refs_1_.refs_2_), channel_id=1, source_target_pairs={{0,2},{1,5},{2,0},{3,7},{4,6},{5,1},{6,4},{7,3},{8,10},{9,13},{10,... | collective-permute-start | bytes 835592 | tf_op jit(solution)/shard_map/ppermute | solution.py:294
  21.4 2.4 %collective-permute-start.9 = (bf16[64,2176]{1,0:T(8,128)(2,1)S(1)}, bf16[64,2176]{1,0:T(8,128)(2,1)S(1)}, u32[]{:S(2)}, u32[]{:S(2)}) collective-permute-start(bf16[64,2176]{1,0:T(8,128)(2,1)S(1)} %pass_kernel.5.refs_1_.refs_0_), channel_id=1, source_target_pairs={{0,4},{1,3},{2,6},{3,1},{4,0},{5,7},{6,2},{7,5},{8,12},{9,11},{10,... | collective-permute-start | bytes 835592 | tf_op jit(solution)/shard_map/ppermute | solution.py:294
  24.0 1.7 %expert_kernel.4 = (bf16[128,1152]{1,0:T(8,128)(2,1)S(1)}, bf16[2,64,768]{2,1,0:T(8,128)(2,1)S(1)}, bf16[2,64,384]{2,1,0:T(8,128)(2,1)S(1)}) custom-call(s32[2]{0:T(128)S(1)} %pad_add_fusion.refs_0_, bf16[64,2176]{1,0:T(8,128)(2,1)S(1)} %join_kernel.4.refs_2_.refs_1_, bf16[64,2176]{1,0:T(8,128)(2,1)S(1)} %join_kernel.6.refs_1_.refs_2_, ...), custom_call_target="tpu_custom_call" | custom-call | flops 6000000000 | tf_op jit(solution)/shard_map/expert_kernel/pallas_call | solution.py:253
  25.7 2.7 %collective-permute-done.9.refs_1_ = bf16[64,2176]{1,0:T(8,128)(2,1)S(1)} collective-permute-done((bf16[64,2176]{1,0:T(8,128)(2,1)S(1)}, bf16[64,2176]{1,0:T(8,128)(2,1)S(1)}, u32[]{:S(2)}, u32[]{:S(2)}) %collective-permute-start.9) | collective-permute-done | bytes 278560 | tf_op jit(solution)/shard_map/ppermute | solution.py:294
  28.5 1.7 %expert_kernel.5 = (bf16[128,1152]{1,0:T(8,128)(2,1)S(1)}, bf16[2,64,768]{2,1,0:T(8,128)(2,1)S(1)}, bf16[2,64,384]{2,1,0:T(8,128)(2,1)S(1)}) custom-call(s32[2]{0:T(128)S(1)} %pad_add_fusion.refs_0_, bf16[64,2176]{1,0:T(8,128)(2,1)S(1)} %pass_kernel.4.refs_2_.refs_1_.refs_5_, bf16[64,2176]{1,0:T(8,128)(2,1)S(1)} %collective-permute-done.8.refs_2_.refs_6_, ...), custom_call_target="tpu_custom_call" | custom-call | flops 6000000000 | tf_op jit(solution)/shard_map/expert_kernel/pallas_call | solution.py:253
  30.3 1.8 %expert_kernel.6 = (bf16[128,1152]{1,0:T(8,128)(2,1)S(1)}, bf16[1,128,768]{2,1,0:T(8,128)(2,1)S(1)}, bf16[1,128,384]{2,1,0:T(8,128)(2,1)S(1)}) custom-call(s32[2]{0:T(128)S(1)} %pad_add_fusion.refs_0_, bf16[128,2176]{1,0:T(8,128)(2,1)S(1)} %join_kernel.7.refs_9_.refs_1_, bf16[512,384]{1,0:T(8,128)(2,1)S(1)} %bitcast.16, ...), custom_call_target="tpu_custom_call" | custom-call | flops 6000000000 | tf_op jit(solution)/shard_map/expert_kernel/pallas_call | solution.py:253
  32.1 6.0 %collective-permute-done.10.refs_2_.refs_1_.refs_12_ = bf16[128,2176]{1,0:T(8,128)(2,1)S(1)} collective-permute-done((bf16[128,2176]{1,0:T(8,128)(2,1)S(1)}, bf16[128,2176]{1,0:T(8,128)(2,1)S(1)}, u32[]{:S(2)}, u32[]{:S(2)}) %collective-permute-start.10) | collective-permute-done | bytes 557088 | tf_op jit(solution)/shard_map/ppermute | solution.py:294
  38.1 1.8 %expert_kernel.7 = (bf16[128,1152]{1,0:T(8,128)(2,1)S(1)}, bf16[1,128,768]{2,1,0:T(8,128)(2,1)S(1)}, bf16[1,128,384]{2,1,0:T(8,128)(2,1)S(1)}) custom-call(s32[2]{0:T(128)S(1)} %pad_add_fusion.refs_0_, bf16[128,2176]{1,0:T(8,128)(2,1)S(1)} %collective-permute-done.10.refs_2_.refs_1_.refs_12_, bf16[512,384]{1,0:T(8,128)(2,1)S(1)} %bitcast.17, ...), custom_call_target="tpu_custom_call" | custom-call | flops 6000000000 | tf_op jit(solution)/shard_map/expert_kernel/pallas_call | solution.py:253
  39.9 2.1 %collective-permute-start.13 = (bf16[128,1152]{1,0:T(8,128)(2,1)S(1)}, bf16[128,1152]{1,0:T(8,128)(2,1)S(1)}, u32[]{:S(2)}, u32[]{:S(2)}) collective-permute-start(bf16[128,1152]{1,0:T(8,128)(2,1)S(1)} %get-tuple-element.45), channel_id=1, source_target_pairs={{0,2},{1,5},{2,0},{3,7},{4,6},{5,1},{6,4},{7,3},{8,10},{9,13},{10,... | collective-permute-start | bytes 884744 | tf_op jit(solution)/shard_map/ppermute | solution.py:294
  42.0 2.9 %collective-permute-done.11.refs_1_ = bf16[128,1152]{1,0:T(8,128)(2,1)S(1)} collective-permute-done((bf16[128,1152]{1,0:T(8,128)(2,1)S(1)}, bf16[128,1152]{1,0:T(8,128)(2,1)S(1)}, u32[]{:S(2)}, u32[]{:S(2)}) %collective-permute-start.11) | collective-permute-done | bytes 294944 | tf_op jit(solution)/shard_map/ppermute | solution.py:294
  44.9 2.1 %collective-permute-start.12 = (bf16[64,1152]{1,0:T(8,128)(2,1)S(1)}, bf16[64,1152]{1,0:T(8,128)(2,1)S(1)}, u32[]{:S(2)}, u32[]{:S(2)}) collective-permute-start(bf16[64,1152]{1,0:T(8,128)(2,1)S(1)} %get-tuple-element.43.refs_15_), channel_id=1, source_target_pairs={{0,4},{1,3},{2,6},{3,1},{4,0},{5,7},{6,2},{7,5},{8,12},{9,11},{10,... | collective-permute-start | bytes 442376 | tf_op jit(solution)/shard_map/ppermute | solution.py:294
  47.0 2.0 %weight_kernel.1 = (f32[512,768]{1,0:T(8,128)S(1)}, f32[384,512]{1,0:T(8,128)S(1)}, bf16[512,384]{1,0:T(8,128)(2,1)S(1)}, bf16[512,384]{1,0:T(8,128)(2,1)S(1)}, bf16[384,512]{1,0:T(8,128)(2,1)S(1)}) custom-call(s32[2]{0:T(128)S(1)} %pad_add_fusion.refs_0_, bf16[64,2176]{1,0:T(8,128)(2,1)S(1)} %join_kernel.4.refs_2_.refs_1_, ...), custom_call_target="tpu_custom_call" | custom-call | flops 6000000000 | tf_op jit(solution)/shard_map/weight_kernel/pallas_call | solution.py:253
  49.0 0.4 collective-permute-done.13.refs_1_
  49.5 2.4 %collective-permute-start.18 = (bf16[64,1152]{1,0:T(8,128)(2,1)S(1)}, bf16[64,1152]{1,0:T(8,128)(2,1)S(1)}, u32[]{:S(2)}, u32[]{:S(2)}) collective-permute-start(bf16[64,1152]{1,0:T(8,128)(2,1)S(1)} %get-tuple-element.51.refs_2_), channel_id=1, source_target_pairs={{0,4},{1,3},{2,6},{3,1},{4,0},{5,7},{6,2},{7,5},{8,12},{9,11},{10,... | collective-permute-start | bytes 442376 | tf_op jit(solution)/shard_map/ppermute | solution.py:294
  51.9 0.5 collective-permute-start.15
  52.4 1.9 %collective-permute-start.14 = (bf16[32,1152]{1,0:T(8,128)(2,1)S(1)}, bf16[32,1152]{1,0:T(8,128)(2,1)S(1)}, u32[]{:S(2)}, u32[]{:S(2)}) collective-permute-start(bf16[32,1152]{1,0:T(8,128)(2,1)S(1)} %get-tuple-element.53.refs_2_), channel_id=1, source_target_pairs={{0,16},{1,17},{2,18},{3,19},{4,20},{5,21},{6,22},{7,23},{8,24},{9,... | collective-permute-start | bytes 221192 | tf_op jit(solution)/shard_map/ppermute | solution.py:294
  54.3 0.7 %collective-permute-done.18.refs_1_ = bf16[64,1152]{1,0:T(8,128)(2,1)S(1)} collective-permute-done((bf16[64,1152]{1,0:T(8,128)(2,1)S(1)}, bf16[64,1152]{1,0:T(8,128)(2,1)S(1)}, u32[]{:S(2)}, u32[]{:S(2)}) %collective-permute-start.18) | collective-permute-done | bytes 147488 | tf_op jit(solution)/shard_map/ppermute | solution.py:294
  55.0 3.9 %collective-permute-start.19 = (bf16[32,1152]{1,0:T(8,128)(2,1)S(1)}, bf16[32,1152]{1,0:T(8,128)(2,1)S(1)}, u32[]{:S(2)}, u32[]{:S(2)}) collective-permute-start(bf16[32,1152]{1,0:T(8,128)(2,1)S(1)} %get-tuple-element.59.refs_5_), channel_id=1, source_target_pairs={{0,24},{1,25},{2,26},{3,27},{4,28},{5,29},{6,30},{7,31},{8,16},{9,... | collective-permute-start | bytes 221192 | tf_op jit(solution)/shard_map/ppermute | solution.py:294
  59.0 1.2 %settle_kernel.1 = (bf16[512,384]{1,0:T(8,128)(2,1)}, bf16[512,384]{1,0:T(8,128)(2,1)}, bf16[384,512]{1,0:T(8,128)(2,1)}, f32[8,128]{1,0:T(8,128)S(1)}) custom-call(f32[512,768]{1,0:T(8,128)S(1)} %get-tuple-element.54.refs_0_, f32[384,512]{1,0:T(8,128)S(1)} %get-tuple-element.55.refs_1_, bf16[512,384]{1,0:T(8,128)(2,1)S(1)} %collective-permute-done.15.refs_2_, ...), custom_call_target="tpu_custom_call" | custom-call | tf_op jit(solution)/shard_map/settle_kernel/pallas_call | solution.py:253
  60.2 1.1 %collective-permute-done.14.refs_1_ = bf16[32,1152]{1,0:T(8,128)(2,1)S(1)} collective-permute-done((bf16[32,1152]{1,0:T(8,128)(2,1)S(1)}, bf16[32,1152]{1,0:T(8,128)(2,1)S(1)}, u32[]{:S(2)}, u32[]{:S(2)}) %collective-permute-start.14) | collective-permute-done | bytes 73760 | tf_op jit(solution)/shard_map/ppermute | solution.py:294
  61.7 1.6 %collective-permute-done.20.refs_2_ = bf16[32,1152]{1,0:T(8,128)(2,1)S(1)} collective-permute-done((bf16[32,1152]{1,0:T(8,128)(2,1)S(1)}, bf16[32,1152]{1,0:T(8,128)(2,1)S(1)}, u32[]{:S(2)}, u32[]{:S(2)}) %collective-permute-start.20) | collective-permute-done | bytes 73760 | tf_op jit(solution)/shard_map/ppermute | solution.py:294
  63.3 1.4 %finish_kernel.1 = (bf16[32,1024]{1,0:T(8,128)(2,1)}, bf16[8,32]{1,0:T(8,128)(2,1)}) custom-call(s32[2]{0:T(128)S(1)} %pad_add_fusion.refs_0_, f32[32,1152]{1,0:T(8,128)S(1)} %add_kernel.3.refs_1_.refs_4_, bf16[32,1152]{1,0:T(8,128)(2,1)S(1)} %collective-permute-done.20.refs_2_, s32[8,32]{1,0:T(8,128)S(1)} %bitcast.12, f32[32,1152]{1,0:T(8,128)S(1)} %add_kernel.3.refs_1_.refs_4_), custom_call_target="tpu_custom_call" | custom-call | tf_op jit(solution)/shard_map/finish_kernel/pallas_call | solution.py:253
  (41 shorter events, 1.1 us)
Async XLA Ops:
  1.6 6.1 %collective-permute-start = (bf16[32,2176]{1,0:T(8,128)(2,1)S(1)}, bf16[32,2176]{1,0:T(8,128)(2,1)S(1)}, u32[]{:S(2)}, u32[]{:S(2)}) collective-permute-start(bf16[32,2176]{1,0:T(8,128)(2,1)S(1)} %prepare_kernel.1.refs_0_), channel_id=1, source_target_pairs={{0,4},{1,3},{2,6},{3,1},{4,0},{5,7},{6,2},{7,5},{8,12},{9,11},{10,... | collective-permute-start | bytes 417800 | tf_op jit(solution)/shard_map/ppermute | solution.py:294
  4.6 9.0 %collective-permute-start.1 = (bf16[32,2176]{1,0:T(8,128)(2,1)S(1)}, bf16[32,2176]{1,0:T(8,128)(2,1)S(1)}, u32[]{:S(2)}, u32[]{:S(2)}) collective-permute-start(bf16[32,2176]{1,0:T(8,128)(2,1)S(1)} %prepare_kernel.1.refs_0_), channel_id=1, source_target_pairs={{0,16},{1,17},{2,18},{3,19},{4,20},{5,21},{6,22},{7,23},{8,24},{9,... | collective-permute-start | bytes 417800 | tf_op jit(solution)/shard_map/ppermute | solution.py:294
  7.7 6.7 %collective-permute-start.3 = (bf16[64,2176]{1,0:T(8,128)(2,1)S(1)}, bf16[64,2176]{1,0:T(8,128)(2,1)S(1)}, u32[]{:S(2)}, u32[]{:S(2)}) collective-permute-start(bf16[64,2176]{1,0:T(8,128)(2,1)S(1)} %join_kernel.4.refs_2_.refs_1_), channel_id=1, source_target_pairs={{0,2},{1,5},{2,0},{3,7},{4,6},{5,1},{6,4},{7,3},{8,10},{9,13},{10,... | collective-permute-start | bytes 835592 | tf_op jit(solution)/shard_map/ppermute | solution.py:294
  9.7 14.2 %collective-permute-start.4 = (bf16[512,384]{1,0:T(8,128)(2,1)}, bf16[512,384]{1,0:T(8,128)(2,1)S(1)}, u32[]{:S(2)}, u32[]{:S(2)}) collective-permute-start(bf16[512,384]{1,0:T(8,128)(2,1)} %bitcast.13), channel_id=1, source_target_pairs={{0,1},{1,0},{2,3},{3,2},{4,5},{5,4},{6,7},{7,6},{8,9},{9,8},{10,11... | collective-permute-start | bytes 1179656 | tf_op jit(solution)/shard_map/ppermute | solution.py:21
  9.7 14.1 %collective-permute-start.6 = (bf16[384,512]{1,0:T(8,128)(2,1)}, bf16[384,512]{1,0:T(8,128)(2,1)S(1)}, u32[]{:S(2)}, u32[]{:S(2)}) collective-permute-start(bf16[384,512]{1,0:T(8,128)(2,1)} %bitcast.23), channel_id=1, source_target_pairs={{0,1},{1,0},{2,3},{3,2},{4,5},{5,4},{6,7},{7,6},{8,9},{9,8},{10,11... | collective-permute-start | bytes 1179656 | tf_op jit(solution)/shard_map/ppermute | solution.py:21
  10.2 13.7 %collective-permute-start.5 = (bf16[512,384]{1,0:T(8,128)(2,1)}, bf16[512,384]{1,0:T(8,128)(2,1)S(1)}, u32[]{:S(2)}, u32[]{:S(2)}) collective-permute-start(bf16[512,384]{1,0:T(8,128)(2,1)} %bitcast.18), channel_id=1, source_target_pairs={{0,1},{1,0},{2,3},{3,2},{4,5},{5,4},{6,7},{7,6},{8,9},{9,8},{10,11... | collective-permute-start | bytes 1179656 | tf_op jit(solution)/shard_map/ppermute | solution.py:21
  13.6 7.8 %collective-permute-start.7 = (bf16[64,2176]{1,0:T(8,128)(2,1)S(1)}, bf16[64,2176]{1,0:T(8,128)(2,1)S(1)}, u32[]{:S(2)}, u32[]{:S(2)}) collective-permute-start(bf16[64,2176]{1,0:T(8,128)(2,1)S(1)} %join_kernel.5.refs_1_), channel_id=1, source_target_pairs={{0,8},{1,9},{2,10},{3,11},{4,12},{5,13},{6,14},{7,15},{8,0},{9,1},... | collective-permute-start | bytes 835592 | tf_op jit(solution)/shard_map/ppermute | solution.py:294
  14.4 5.1 %collective-permute-start.2 = (bf16[32,2176]{1,0:T(8,128)(2,1)S(1)}, bf16[32,2176]{1,0:T(8,128)(2,1)S(1)}, u32[]{:S(2)}, u32[]{:S(2)}) collective-permute-start(bf16[32,2176]{1,0:T(8,128)(2,1)S(1)} %collective-permute-done.1.refs_1_.refs_0_), channel_id=1, source_target_pairs={{0,4},{1,3},{2,6},{3,1},{4,0},{5,7},{6,2},{7,5},{8,12},{9,11},{10,... | collective-permute-start | bytes 417800 | tf_op jit(solution)/shard_map/ppermute | solution.py:294
  16.4 7.5 %copy-start.1 = (bf16[1,512,384]{2,1,0:T(8,128)(2,1)S(1)}, bf16[1,512,384]{2,1,0:T(8,128)(2,1)}, u32[]{:S(2)}) copy-start(bf16[1,512,384]{2,1,0:T(8,128)(2,1)} %param.11) | copy-start | bytes 1179652
  16.4 7.5 %copy-start.2 = (bf16[1,512,384]{2,1,0:T(8,128)(2,1)S(1)}, bf16[1,512,384]{2,1,0:T(8,128)(2,1)}, u32[]{:S(2)}) copy-start(bf16[1,512,384]{2,1,0:T(8,128)(2,1)} %param.12) | copy-start | bytes 1179652
  16.4 7.5 %copy-start.3 = (bf16[1,384,512]{2,1,0:T(8,128)(2,1)S(1)}, bf16[1,384,512]{2,1,0:T(8,128)(2,1)}, u32[]{:S(2)}) copy-start(bf16[1,384,512]{2,1,0:T(8,128)(2,1)} %param.13) | copy-start | bytes 1179652
  19.4 9.1 %collective-permute-start.8 = (bf16[64,2176]{1,0:T(8,128)(2,1)S(1)}, bf16[64,2176]{1,0:T(8,128)(2,1)S(1)}, u32[]{:S(2)}, u32[]{:S(2)}) collective-permute-start(bf16[64,2176]{1,0:T(8,128)(2,1)S(1)} %join_kernel.6.refs_1_.refs_2_), channel_id=1, source_target_pairs={{0,2},{1,5},{2,0},{3,7},{4,6},{5,1},{6,4},{7,3},{8,10},{9,13},{10,... | collective-permute-start | bytes 835592 | tf_op jit(solution)/shard_map/ppermute | solution.py:294
  21.4 7.0 %collective-permute-start.9 = (bf16[64,2176]{1,0:T(8,128)(2,1)S(1)}, bf16[64,2176]{1,0:T(8,128)(2,1)S(1)}, u32[]{:S(2)}, u32[]{:S(2)}) collective-permute-start(bf16[64,2176]{1,0:T(8,128)(2,1)S(1)} %pass_kernel.5.refs_1_.refs_0_), channel_id=1, source_target_pairs={{0,4},{1,3},{2,6},{3,1},{4,0},{5,7},{6,2},{7,5},{8,12},{9,11},{10,... | collective-permute-start | bytes 835592 | tf_op jit(solution)/shard_map/ppermute | solution.py:294
  28.4 9.6 %collective-permute-start.10 = (bf16[128,2176]{1,0:T(8,128)(2,1)S(1)}, bf16[128,2176]{1,0:T(8,128)(2,1)S(1)}, u32[]{:S(2)}, u32[]{:S(2)}) collective-permute-start(bf16[128,2176]{1,0:T(8,128)(2,1)S(1)} %join_kernel.7.refs_9_.refs_1_), channel_id=1, source_target_pairs={{0,2},{1,5},{2,0},{3,7},{4,6},{5,1},{6,4},{7,3},{8,10},{9,13},{10,... | collective-permute-start | bytes 1671176 | tf_op jit(solution)/shard_map/ppermute | solution.py:294
  38.1 6.8 %collective-permute-start.11 = (bf16[128,1152]{1,0:T(8,128)(2,1)S(1)}, bf16[128,1152]{1,0:T(8,128)(2,1)S(1)}, u32[]{:S(2)}, u32[]{:S(2)}) collective-permute-start(bf16[128,1152]{1,0:T(8,128)(2,1)S(1)} %pass_kernel.7.refs_8_), channel_id=1, source_target_pairs={{0,2},{1,5},{2,0},{3,7},{4,6},{5,1},{6,4},{7,3},{8,10},{9,13},{10,... | collective-permute-start | bytes 884744 | tf_op jit(solution)/shard_map/ppermute | solution.py:294
  39.9 9.5 %collective-permute-start.13 = (bf16[128,1152]{1,0:T(8,128)(2,1)S(1)}, bf16[128,1152]{1,0:T(8,128)(2,1)S(1)}, u32[]{:S(2)}, u32[]{:S(2)}) collective-permute-start(bf16[128,1152]{1,0:T(8,128)(2,1)S(1)} %get-tuple-element.45), channel_id=1, source_target_pairs={{0,2},{1,5},{2,0},{3,7},{4,6},{5,1},{6,4},{7,3},{8,10},{9,13},{10,... | collective-permute-start | bytes 884744 | tf_op jit(solution)/shard_map/ppermute | solution.py:294
  44.9 7.5 %collective-permute-start.12 = (bf16[64,1152]{1,0:T(8,128)(2,1)S(1)}, bf16[64,1152]{1,0:T(8,128)(2,1)S(1)}, u32[]{:S(2)}, u32[]{:S(2)}) collective-permute-start(bf16[64,1152]{1,0:T(8,128)(2,1)S(1)} %get-tuple-element.43.refs_15_), channel_id=1, source_target_pairs={{0,4},{1,3},{2,6},{3,1},{4,0},{5,7},{6,2},{7,5},{8,12},{9,11},{10,... | collective-permute-start | bytes 442376 | tf_op jit(solution)/shard_map/ppermute | solution.py:294
  49.5 5.5 %collective-permute-start.18 = (bf16[64,1152]{1,0:T(8,128)(2,1)S(1)}, bf16[64,1152]{1,0:T(8,128)(2,1)S(1)}, u32[]{:S(2)}, u32[]{:S(2)}) collective-permute-start(bf16[64,1152]{1,0:T(8,128)(2,1)S(1)} %get-tuple-element.51.refs_2_), channel_id=1, source_target_pairs={{0,4},{1,3},{2,6},{3,1},{4,0},{5,7},{6,2},{7,5},{8,12},{9,11},{10,... | collective-permute-start | bytes 442376 | tf_op jit(solution)/shard_map/ppermute | solution.py:294
  51.9 7.1 %collective-permute-start.17 = (bf16[384,512]{1,0:T(8,128)(2,1)S(1)}, bf16[384,512]{1,0:T(8,128)(2,1)S(1)}, u32[]{:S(2)}, u32[]{:S(2)}) collective-permute-start(bf16[384,512]{1,0:T(8,128)(2,1)S(1)} %get-tuple-element.50.refs_2_), channel_id=1, source_target_pairs={{0,1},{1,0},{2,3},{3,2},{4,5},{5,4},{6,7},{7,6},{8,9},{9,8},{10,11... | collective-permute-start | bytes 1179656 | tf_op jit(solution)/shard_map/ppermute | solution.py:21
  51.9 7.1 %collective-permute-start.15 = (bf16[512,384]{1,0:T(8,128)(2,1)S(1)}, bf16[512,384]{1,0:T(8,128)(2,1)S(1)}, u32[]{:S(2)}, u32[]{:S(2)}) collective-permute-start(bf16[512,384]{1,0:T(8,128)(2,1)S(1)} %get-tuple-element.56), channel_id=1, source_target_pairs={{0,1},{1,0},{2,3},{3,2},{4,5},{5,4},{6,7},{7,6},{8,9},{9,8},{10,11... | collective-permute-start | bytes 1179656 | tf_op jit(solution)/shard_map/ppermute | solution.py:21
  52.4 6.6 %collective-permute-start.16 = (bf16[512,384]{1,0:T(8,128)(2,1)S(1)}, bf16[512,384]{1,0:T(8,128)(2,1)S(1)}, u32[]{:S(2)}, u32[]{:S(2)}) collective-permute-start(bf16[512,384]{1,0:T(8,128)(2,1)S(1)} %get-tuple-element.57), channel_id=1, source_target_pairs={{0,1},{1,0},{2,3},{3,2},{4,5},{5,4},{6,7},{7,6},{8,9},{9,8},{10,11... | collective-permute-start | bytes 1179656 | tf_op jit(solution)/shard_map/ppermute | solution.py:21
  52.4 8.9 %collective-permute-start.14 = (bf16[32,1152]{1,0:T(8,128)(2,1)S(1)}, bf16[32,1152]{1,0:T(8,128)(2,1)S(1)}, u32[]{:S(2)}, u32[]{:S(2)}) collective-permute-start(bf16[32,1152]{1,0:T(8,128)(2,1)S(1)} %get-tuple-element.53.refs_2_), channel_id=1, source_target_pairs={{0,16},{1,17},{2,18},{3,19},{4,20},{5,21},{6,22},{7,23},{8,24},{9,... | collective-permute-start | bytes 221192 | tf_op jit(solution)/shard_map/ppermute | solution.py:294
  55.0 6.7 %collective-permute-start.19 = (bf16[32,1152]{1,0:T(8,128)(2,1)S(1)}, bf16[32,1152]{1,0:T(8,128)(2,1)S(1)}, u32[]{:S(2)}, u32[]{:S(2)}) collective-permute-start(bf16[32,1152]{1,0:T(8,128)(2,1)S(1)} %get-tuple-element.59.refs_5_), channel_id=1, source_target_pairs={{0,24},{1,25},{2,26},{3,27},{4,28},{5,29},{6,30},{7,31},{8,16},{9,... | collective-permute-start | bytes 221192 | tf_op jit(solution)/shard_map/ppermute | solution.py:294
  59.0 4.4 %collective-permute-start.20 = (bf16[32,1152]{1,0:T(8,128)(2,1)S(1)}, bf16[32,1152]{1,0:T(8,128)(2,1)S(1)}, u32[]{:S(2)}, u32[]{:S(2)}) collective-permute-start(bf16[32,1152]{1,0:T(8,128)(2,1)S(1)} %get-tuple-element.61), channel_id=1, source_target_pairs={{0,8},{1,9},{2,10},{3,11},{4,12},{5,13},{6,14},{7,15},{8,0},{9,1},... | collective-permute-start | bytes 221192 | tf_op jit(solution)/shard_map/ppermute | solution.py:294
  59.0 4.3 %copy-start = (s32[32,8]{0,1:T(8,128)S(1)}, s32[32,8]{0,1:T(8,128)}, u32[]{:S(2)}) copy-start(s32[32,8]{0,1:T(8,128)} %param.9) | copy-start | bytes 3076
